TPU v7x, 32 devices: a whole 2x2x4 slice. The times are simulated.
32 devices in a mesh: section: 4 (over x, core), fsdp: 2 (over y), ep: 4 (over z).
Axes of the slice: x: 2, y: 2, z: 4, core: 2. Of those that a mesh axis runs over, the one named last changes fastest.
Arguments:
- hidden: bfloat16 [2048, 7168], P(('section', 'fsdp'), 'ep'), may hold values from -6 to 6
- attn_gain: float32 [7168], replicated, may hold values from 0.25 to 1.75
- q_gain: float32 [1536], replicated, may hold values from 0.25 to 1.75
- kv_gain: float32 [512], replicated, may hold values from 0.25 to 1.75
- down_weight: bfloat16 [7168, 2112], P('fsdp', 'ep'), may hold values from -0.0625 to 0.0625
Outputs:
- q_latent: bfloat16 [2048, 1536], P(('section', 'fsdp', 'ep'))
- kv_cache: bfloat16 [2048, 576], P(('section', 'fsdp', 'ep'))
All inputs are finite; a program needn't handle non-finite values.
Results may differ from a plain program's by a relative error of at most 0.0049.
Values may be sent and summed in bfloat16 or wider, within the bound.
No kernel may reach another device: no remote copies, remote signals or barrier semaphores. Data moves between devices by JAX's collectives and lax.ppermute only.
A program may use at most 64 MiB of HBM per device.

v0:
```python
import jax
import jax.numpy as jnp
from jax import lax
from jax.sharding import PartitionSpec as P

QL = 1536
KVL = 512
ROPE = 64
LENGTH = 4096


epsilon = 1e-06
rope_base = 10000.0


def from_behind(x, axis, by):
    count = lax.axis_size(axis)
    return lax.ppermute(x, axis, [(i, (i + by) % count) for i in range(count)])


def root_scale(values, gain):
    mean_square = jnp.mean(values * values, axis=-1, keepdims=True)
    return values * lax.rsqrt(mean_square + epsilon) * gain


def rotate(latent, position):
    half_rope = ROPE // 2
    frequency = rope_base ** (-(jnp.arange(half_rope).astype(jnp.float32) / half_rope))
    angle = position.astype(jnp.float32)[:, None] * frequency[None, :]
    first = latent[:, QL + KVL : QL + KVL + half_rope]
    second = latent[:, QL + KVL + half_rope :]
    cosine = jnp.cos(angle)
    sine = jnp.sin(angle)
    return jnp.concatenate([first * cosine - second * sine, second * cosine + first * sine], axis=1)


def on_device(hidden, attn_gain, q_gain, kv_gain, down_weight):
    row_count = hidden.shape[0]
    sender = lax.all_gather(hidden, "ep", axis=1, tiled=True)
    whole = from_behind(sender, "section", 1)
    normed = root_scale(whole.astype(jnp.float32), attn_gain).astype(jnp.bfloat16)
    partial_latent = jnp.dot(
        normed,
        lax.all_gather(down_weight, "fsdp", axis=0, tiled=True),
        preferred_element_type=jnp.float32,
    )
    latent = lax.all_to_all(partial_latent, "ep", split_axis=0, concat_axis=1, tiled=True)
    quarter = latent.shape[0]
    query = root_scale(latent[:, :QL], q_gain).astype(jnp.bfloat16)
    key_value = root_scale(latent[:, QL : QL + KVL], kv_gain)
    row_index = (
        lax.axis_index("fsdp") * row_count + lax.axis_index("ep") * quarter + jnp.arange(quarter)
    )
    position = row_index % LENGTH
    cache = jnp.concatenate([key_value, rotate(latent, position)], axis=1).astype(jnp.bfloat16)
    return (query, cache)


def solution(mesh):
    placed = (P(("section", "fsdp"), "ep"), P(), P(), P(), P("fsdp", "ep"))
    return jax.shard_map(
        on_device,
        mesh=mesh,
        in_specs=placed,
        out_specs=(P(("section", "fsdp", "ep"), None), P(("section", "fsdp", "ep"), None)),
        check_vma=False,
    )
```

profile of v0, /device:TPU:0, one launch (start us, length us, event | category | flops | bytes accessed | tf_op | source)
XLA Modules:
  0.0 219.5 jit_solution(9590752783372481953)
XLA Ops:
  7.2 0.0 copy-start.3
  7.2 0.0 all-gather.3.cloned.1.call-start
  7.2 0.7 all-gather.3.cloned.1.call-update
  7.9 0.0 all-gather.5.cloned.1.call-start
  8.0 0.7 all-gather.5.cloned.1.call-update
  8.7 75.8 %all-gather.3.cloned.1.call-done = bf16[256,7168]{1,0:T(8,128)(2,1)} async-done(((bf16[256,1792]{1,0:T(8,128)(2,1)}), bf16[256,7168]{1,0:T(8,128)(2,1)}) %all-gather.3.cloned.1.call-update) | async-done | bytes 3670032 | tf_op jit(solution)/shard_map/all_gather | solution.py:39
  84.4 0.0 collective-permute-start
  84.4 42.5 %collective-permute-done = bf16[256,7168]{1,0:T(8,128)(2,1)S(1)} collective-permute-done((bf16[256,7168]{1,0:T(8,128)(2,1)}, bf16[256,7168]{1,0:T(8,128)(2,1)S(1)}, u32[]{:S(2)}, u32[]{:S(2)}) %collective-permute-start) | collective-permute-done | bytes 3670048 | tf_op jit(solution)/shard_map/ppermute | solution.py:18
  126.9 0.0 copy-start
  126.9 1.9 copy-done
  128.9 0.8 fusion
  129.7 0.0 copy-start.2
  129.7 0.0 copy-start.1
  129.7 49.7 %all-gather.5.cloned.1.call-done = bf16[7168,528]{0,1:T(8,128)(2,1)} async-done(((bf16[3584,528]{0,1:T(8,128)(2,1)}), bf16[7168,528]{0,1:T(8,128)(2,1)}) %all-gather.5.cloned.1.call-update) | async-done | bytes 7569424 | tf_op jit(solution)/shard_map/all_gather | solution.py:44
  179.4 0.0 copy-done.3
  179.4 8.2 %fusion.3 = f32[256,528]{1,0:T(8,128)} fusion(bf16[7168,528]{0,1:T(8,128)(2,1)} %all-gather.5.cloned.1.call-done, bf16[256,7168]{1,0:T(8,128)(2,1)} %copy-done, f32[7168]{0:T(1024)S(1)} %copy-done.3, f32[256]{0:T(256)S(1)} %add_rsqrt_fusion), kind=kOutput, calls=%fused_computation.5 | convolution fusion | flops 1945108480 | bytes 11809792 | tf_op jit(solution)/shard_map/dot_general | solution.py:42
  187.5 4.6 %all-to-all-start = ((f32[4,64,528]{2,1,0:T(8,128)}), f32[4,64,528]{2,1,0:T(8,128)S(1)}, u32[]{:S(2)}, u32[]{:S(2)}) async-start(f32[4,64,528]{2,1,0:T(8,128)} %bitcast), calls=%async_computation | async-start | bytes 1310720 | tf_op jit(solution)/shard_map/all_to_all | solution.py:47
  192.2 17.3 %all-to-all-done = f32[4,64,528]{2,1,0:T(8,128)S(1)} async-done(((f32[4,64,528]{2,1,0:T(8,128)}), f32[4,64,528]{2,1,0:T(8,128)S(1)}, u32[]{:S(2)}, u32[]{:S(2)}) %all-to-all-start) | async-done | bytes 540704 | tf_op jit(solution)/shard_map/all_to_all | solution.py:47
  209.4 0.4 copy.12
  209.9 0.3 all_to_all.17
  210.2 0.1 fusion.17
  210.3 0.1 multiply_reduce_fusion.1
  210.4 0.1 multiply_reduce_fusion
  210.5 0.1 copy.18
  210.6 0.1 copy.19
  210.7 0.2 fusion.12
  210.8 0.1 copy.15
  210.9 0.1 copy.16
  211.1 0.0 copy-done.2
  211.1 0.1 multiply_convert_fusion.1
  211.2 0.0 copy-done.1
  211.2 0.8 multiply_convert_fusion
  211.9 0.7 pad_maximum_fusion
  (5 shorter events, 0.0 us)
Async XLA Ops:
  7.2 172.2 %copy-start.3 = (f32[7168]{0:T(1024)S(1)}, f32[7168]{0:T(1024)}, u32[]{:S(2)}) copy-start(f32[7168]{0:T(1024)} %param.6) | copy-start | bytes 86020
  7.2 77.2 %all-gather.3.cloned.1.call-start = ((), (), s32[]{:S(2)}) async-start(), calls=%async_computation.1 | async-start | bytes 4587520 | tf_op jit(solution)/shard_map/all_gather | solution.py:39
  7.9 171.5 %all-gather.5.cloned.1.call-start = ((), (), s32[]{:S(2)}) async-start(), calls=%async_computation.2 | async-start | bytes 11354112 | tf_op jit(solution)/shard_map/all_gather | solution.py:44
  84.4 42.5 %collective-permute-start = (bf16[256,7168]{1,0:T(8,128)(2,1)}, bf16[256,7168]{1,0:T(8,128)(2,1)S(1)}, u32[]{:S(2)}, u32[]{:S(2)}) collective-permute-start(bf16[256,7168]{1,0:T(8,128)(2,1)} %all-gather.3.cloned.1.call-done), channel_id=1, source_target_pairs={{0,8},{8,16},{16,24},{24,0},{1,9},{9,17},{17,25},{25,1},{2,10},{10... | collective-permute-start | bytes 11010056 | tf_op jit(solution)/shard_map/ppermute | solution.py:18
  126.9 1.9 copy-start
  129.7 81.4 %copy-start.2 = (f32[512]{0:T(512)S(1)}, f32[512]{0:T(512)}, u32[]{:S(2)}) copy-start(f32[512]{0:T(512)} %param.8) | copy-start | bytes 6148
  129.7 81.5 %copy-start.1 = (f32[1536]{0:T(1024)S(1)}, f32[1536]{0:T(1024)}, u32[]{:S(2)}) copy-start(f32[1536]{0:T(1024)} %param.7) | copy-start | bytes 18436
  187.5 21.9 %all-to-all-start = ((f32[4,64,528]{2,1,0:T(8,128)}), f32[4,64,528]{2,1,0:T(8,128)S(1)}, u32[]{:S(2)}, u32[]{:S(2)}) async-start(f32[4,64,528]{2,1,0:T(8,128)} %bitcast), calls=%async_computation | async-start | bytes 1310720 | tf_op jit(solution)/shard_map/all_to_all | solution.py:47
Sparse Core Ops, SparseCore 0:
  9.6 74.7 all-gather.2
  86.0 93.3 all-gather.4
where the time goes:
time: 220 us
  waiting for transfers between devices  187 us (85%)
  between operations  14.1 us (6%)
  matrix products  8.15 us (4%)
  starting transfers between devices  4.67 us (2%)
  local copies, waits for them, and re-layouts  3.09 us (1%)
  other arithmetic  2.83 us (1%)
    all_gather x1, waiting for transfers between devices, on_device(): sender = lax.all_gather(hidden, 'ep', axis=1, tiled=True)  75.8 us
    all_gather x1, waiting for transfers between devices, on_device(): lax.all_gather(down_weight, 'fsdp', axis=0, tiled=True)  49.7 us
    ppermute x1, waiting for transfers between devices, from_behind(): return lax.ppermute(x, axis, [(i, (i + by) % count) for i in range(count)])  42.5 us
    all_to_all x1, waiting for transfers between devices, on_device(): lax.all_to_all(partial_latent, 'ep', split_axis=0, concat_axis=1, tiled=T...  17.3 us
    dot_general x1, matrix products, on_device(): jnp.dot(normed, lax.all_gather(down_weight, 'fsdp', axis=0, tiled=True),...  8.15 us
    all_to_all x1, starting transfers between devices, on_device(): lax.all_to_all(partial_latent, 'ep', split_axis=0, concat_axis=1, tiled=T...  4.59 us
  transfers between devices with their start and end apart: 4, of which 4 were waited for; matrix products, arithmetic and copies ran while one was open for 0% of the time, Pallas kernels for 0%

commit v1 on v0

--- a/solution.py
+++ b/solution.py
@@ -11,11 +11,8 @@
 
 epsilon = 1e-06
 rope_base = 10000.0
-
-
-def from_behind(x, axis, by):
-    count = lax.axis_size(axis)
-    return lax.ppermute(x, axis, [(i, (i + by) % count) for i in range(count)])
+ROW_CHUNKS = 2
+WEIGHT_CHUNKS = 2
 
 
 def root_scale(values, gain):
@@ -34,23 +31,80 @@
     return jnp.concatenate([first * cosine - second * sine, second * cosine + first * sine], axis=1)
 
 
+def whole_weight(weight):
+    fsdp, section = lax.axis_size("fsdp"), lax.axis_size("section")
+    columns, depth = weight.shape
+    if fsdp != 2 or section != 4:
+        return lax.all_gather(weight, "fsdp", axis=1, tiled=True)
+    section_index, fsdp_index = lax.axis_index("section"), lax.axis_index("fsdp")
+    quarter = depth // section
+    part = quarter // WEIGHT_CHUNKS
+    other = (1 - fsdp_index) * depth
+    full = jnp.zeros((columns, fsdp * depth), weight.dtype)
+    full = lax.dynamic_update_slice(full, weight, (0, fsdp_index * depth))
+    for chunk in range(WEIGHT_CHUNKS):
+        own = lax.dynamic_slice(weight, (0, section_index * quarter + chunk * part), (columns, part))
+        here = lax.ppermute(own, "fsdp", [(0, 1), (1, 0)])
+        across = lax.ppermute(here, "section", [(i, i ^ 2) for i in range(4)])
+        beside = lax.ppermute(here, "section", [(i, i ^ 1) for i in range(4)])
+        beside_across = lax.ppermute(across, "section", [(i, i ^ 1) for i in range(4)])
+        for flip, piece in ((0, here), (1, beside), (2, across), (3, beside_across)):
+            start = other + (section_index ^ flip) * quarter + chunk * part
+            full = lax.dynamic_update_slice(full, piece, (0, start))
+    return full
+
+
 def on_device(hidden, attn_gain, q_gain, kv_gain, down_weight):
-    row_count = hidden.shape[0]
-    sender = lax.all_gather(hidden, "ep", axis=1, tiled=True)
-    whole = from_behind(sender, "section", 1)
-    normed = root_scale(whole.astype(jnp.float32), attn_gain).astype(jnp.bfloat16)
-    partial_latent = jnp.dot(
-        normed,
-        lax.all_gather(down_weight, "fsdp", axis=0, tiled=True),
-        preferred_element_type=jnp.float32,
-    )
-    latent = lax.all_to_all(partial_latent, "ep", split_axis=0, concat_axis=1, tiled=True)
-    quarter = latent.shape[0]
+    row_count, width = hidden.shape
+    ep, section = lax.axis_size("ep"), lax.axis_size("section")
+    ep_index = lax.axis_index("ep")
+    rows = row_count // ROW_CHUNKS
+    own = [hidden[i * rows : (i + 1) * rows] for i in range(ROW_CHUNKS)]
+    up = [(i, i + 1) for i in range(ep - 1)]
+    down = [(i + 1, i) for i in range(ep - 1)]
+    arrivals = [[(block, 0)] for block in own]
+    rising, falling = list(own), list(own)
+    for step in range(1, ep):
+        for i in range(ROW_CHUNKS):
+            rising[i] = lax.ppermute(rising[i], "ep", up)
+            falling[i] = lax.ppermute(falling[i], "ep", down)
+            arrivals[i] += [(rising[i], -step), (falling[i], step)]
+    weight = whole_weight(down_weight.T)
+    latents = []
+    for i in range(ROW_CHUNKS):
+        total, squares = 0.0, 0.0
+        for block, offset in arrivals[i]:
+            place = jnp.clip(ep_index + offset, 0, ep - 1) * width
+            values = block.astype(jnp.float32)
+            squares = squares + jnp.sum(values * values, axis=1, keepdims=True)
+            gained = (values * lax.dynamic_slice(attn_gain, (place,), (width,))).astype(jnp.bfloat16)
+            total = total + lax.dot_general(
+                gained,
+                lax.dynamic_slice(weight, (0, place), (weight.shape[0], width)),
+                (((1,), (1,)), ((), ())),
+                preferred_element_type=jnp.float32,
+            )
+        scale = lax.rsqrt(squares / (ep * width) + epsilon)
+        latents.append((total * scale).astype(jnp.bfloat16))
+    mine = jnp.concatenate(latents, axis=0)
+    quarter = row_count // ep
+    columns = mine.shape[1]
+    latent = jnp.zeros((ep, quarter, columns), jnp.bfloat16)
+    for turn in range(ep):
+        target = (ep_index + turn) % ep
+        piece = lax.dynamic_slice(mine, (target * quarter, 0), (quarter, columns))
+        moves = [
+            (s * ep + e, (s + 1) % section * ep + (e + turn) % ep)
+            for s in range(section)
+            for e in range(ep)
+        ]
+        piece = lax.ppermute(piece, ("section", "ep"), moves)
+        source = (ep_index + ep - turn) % ep
+        latent = lax.dynamic_update_slice(latent, piece[None], (source, 0, 0))
+    latent = latent.astype(jnp.float32).transpose(1, 0, 2).reshape(quarter, ep * columns)
     query = root_scale(latent[:, :QL], q_gain).astype(jnp.bfloat16)
     key_value = root_scale(latent[:, QL : QL + KVL], kv_gain)
-    row_index = (
-        lax.axis_index("fsdp") * row_count + lax.axis_index("ep") * quarter + jnp.arange(quarter)
-    )
+    row_index = lax.axis_index("fsdp") * row_count + ep_index * quarter + jnp.arange(quarter)
     position = row_index % LENGTH
     cache = jnp.concatenate([key_value, rotate(latent, position)], axis=1).astype(jnp.bfloat16)
     return (query, cache)

time: 220 us -> 177 us (0.80)
  the two profiles are of different devices: /device:TPU:0 before, /device:TPU:13 now
where the time goes in v1:
time: 177 us; the launch traced here: 174 us
  local copies, waits for them, and re-layouts  69 us (39%)
  starting transfers between devices  46.1 us (26%)
  matrix products  31.7 us (18%)
  waiting for transfers between devices  15.4 us (9%)
  other arithmetic  11 us (6%)
    dynamic_update_slice x8, local copies, waits for them, and re-layouts, whole_weight(): full = lax.dynamic_update_slice(full, piece, (0, start))  56.2 us
    dot_general x14, matrix products, on_device(): lax.dot_general(gained, lax.dynamic_slice(weight, (0, place), (weight.sha...  31.7 us
    ppermute x6, starting transfers between devices, on_device(): rising[i] = lax.ppermute(rising[i], 'ep', up)  18.5 us
    ppermute x6, starting transfers between devices, on_device(): falling[i] = lax.ppermute(falling[i], 'ep', down)  15.5 us
    ppermute x4, waiting for transfers between devices, on_device(): piece = lax.ppermute(piece, ('section', 'ep'), moves)  11.2 us
    reduce_sum x13, other arithmetic, on_device(): squares = squares + jnp.sum(values * values, axis=1, keepdims=True)  9.5 us
    ppermute x2, starting transfers between devices, whole_weight(): beside = lax.ppermute(here, 'section', [(i, i ^ 1) for i in range(4)])  4.39 us
    ppermute x4, starting transfers between devices, on_device(): piece = lax.ppermute(piece, ('section', 'ep'), moves)  4.04 us
  transfers between devices with their start and end apart: 24, of which 5 were waited for; matrix products, arithmetic and copies ran while one was open for 39% of the time, Pallas kernels for 0%

profile of v1, /device:TPU:13, one launch (start us, length us, event | category | flops | bytes accessed | tf_op | source)
XLA Modules:
  0.0 174.3 jit_solution(8465377336778657371)
XLA Ops:
  0.6 2.0 %fusion.162 = (bf16[128,1792]{1,0:T(8,128)(2,1)S(1)}, bf16[128,1792]{1,0:T(8,128)(2,1)}) fusion(bf16[256,1792]{1,0:T(8,128)(2,1)} %param.5), kind=kLoop, calls=%fused_computation.174 | loop fusion | bytes 1835008 | tf_op jit(solution)/shard_map/slice | solution.py:62
  2.6 2.1 %collective-permute-start.15 = (bf16[128,1792]{1,0:T(8,128)(2,1)S(1)}, bf16[128,1792]{1,0:T(8,128)(2,1)S(1)}, u32[]{:S(2)}, u32[]{:S(2)}) collective-permute-start(bf16[128,1792]{1,0:T(8,128)(2,1)S(1)} %get-tuple-element.10), channel_id=1, source_target_pairs={{1,0},{2,1},{3,2},{5,4},{6,5},{7,6},{9,8},{10,9},{11,10},{13,12},{... | collective-permute-start | bytes 1376264 | tf_op jit(solution)/shard_map/ppermute | solution.py:70
  4.7 3.2 %collective-permute-start.14 = (bf16[128,1792]{1,0:T(8,128)(2,1)S(1)}, bf16[128,1792]{1,0:T(8,128)(2,1)S(1)}, u32[]{:S(2)}, u32[]{:S(2)}) collective-permute-start(bf16[128,1792]{1,0:T(8,128)(2,1)S(1)} %get-tuple-element.10), channel_id=1, source_target_pairs={{0,1},{1,2},{2,3},{4,5},{5,6},{6,7},{8,9},{9,10},{10,11},{12,13},{... | collective-permute-start | bytes 1376264 | tf_op jit(solution)/shard_map/ppermute | solution.py:69
  7.9 3.2 %collective-permute-start.8 = (bf16[128,1792]{1,0:T(8,128)(2,1)}, bf16[128,1792]{1,0:T(8,128)(2,1)S(1)}, u32[]{:S(2)}, u32[]{:S(2)}) collective-permute-start(bf16[128,1792]{1,0:T(8,128)(2,1)} %get-tuple-element.11), channel_id=1, source_target_pairs={{0,1},{1,2},{2,3},{4,5},{5,6},{6,7},{8,9},{9,10},{10,11},{12,13},{... | collective-permute-start | bytes 1376264 | tf_op jit(solution)/shard_map/ppermute | solution.py:69
  11.2 2.1 %collective-permute-start.9 = (bf16[128,1792]{1,0:T(8,128)(2,1)}, bf16[128,1792]{1,0:T(8,128)(2,1)S(1)}, u32[]{:S(2)}, u32[]{:S(2)}) collective-permute-start(bf16[128,1792]{1,0:T(8,128)(2,1)} %get-tuple-element.11), channel_id=1, source_target_pairs={{1,0},{2,1},{3,2},{5,4},{6,5},{7,6},{9,8},{10,9},{11,10},{13,12},{... | collective-permute-start | bytes 1376264 | tf_op jit(solution)/shard_map/ppermute | solution.py:70
  13.2 2.8 %dynamic-slice_bitcast_fusion = (bf16[528,448]{1,0:T(8,128)(2,1)}, bf16[528,448]{1,0:T(8,128)(2,1)}) fusion(bf16[3584,528]{0,1:T(8,128)(2,1)} %param.9, s32[]{:T(128)S(6)} %select_n.145, s32[]{:T(128)S(6)} %select_n.140), kind=kLoop, calls=%fused_computation.103 | loop fusion | bytes 1892360 | tf_op jit(solution)/shard_map/dynamic_slice | solution.py:46
  16.3 4.0 %broadcast_in_dim.13 = bf16[528,7168]{1,0:T(8,128)(2,1)} broadcast(bf16[]{:T(256)} %constant.99.clone.1), dimensions={} | broadcast | bytes 7569410 | tf_op jit(solution)/shard_map/broadcast_in_dim | solution.py:43
  20.3 2.1 %bitcast_dynamic-update-slice_fusion = bf16[528,7168]{1,0:T(8,128)(2,1)} fusion(bf16[528,7168]{1,0:T(8,128)(2,1)} %broadcast_in_dim.13, s32[]{:T(128)S(6)} %select_n.139, bf16[3584,528]{0,1:T(8,128)(2,1)S(1)} %copy-done.1), kind=kLoop, calls=%fused_computation | loop fusion | bytes 7569412 | tf_op jit(solution)/shard_map/dynamic_update_slice | solution.py:44
  22.5 0.3 fusion.91
  22.7 1.3 collective-permute-start.4
  24.1 1.9 %collective-permute-start.17 = (bf16[128,1792]{1,0:T(8,128)(2,1)S(1)}, bf16[128,1792]{1,0:T(8,128)(2,1)S(1)}, u32[]{:S(2)}, u32[]{:S(2)}) collective-permute-start(bf16[128,1792]{1,0:T(8,128)(2,1)S(1)} %collective-permute-done.15), channel_id=1, source_target_pairs={{1,0},{2,1},{3,2},{5,4},{6,5},{7,6},{9,8},{10,9},{11,10},{13,12},{... | collective-permute-start | bytes 1376264 | tf_op jit(solution)/shard_map/ppermute | solution.py:70
  26.2 1.4 collective-permute-done.8
  27.6 3.2 %collective-permute-start.16 = (bf16[128,1792]{1,0:T(8,128)(2,1)S(1)}, bf16[128,1792]{1,0:T(8,128)(2,1)}, u32[]{:S(2)}, u32[]{:S(2)}) collective-permute-start(bf16[128,1792]{1,0:T(8,128)(2,1)S(1)} %collective-permute-done.14), channel_id=1, source_target_pairs={{0,1},{1,2},{2,3},{4,5},{5,6},{6,7},{8,9},{9,10},{10,11},{12,13},{... | collective-permute-start | bytes 1376264 | tf_op jit(solution)/shard_map/ppermute | solution.py:69
  31.0 3.2 %collective-permute-start.10 = (bf16[128,1792]{1,0:T(8,128)(2,1)S(1)}, bf16[128,1792]{1,0:T(8,128)(2,1)}, u32[]{:S(2)}, u32[]{:S(2)}) collective-permute-start(bf16[128,1792]{1,0:T(8,128)(2,1)S(1)} %collective-permute-done.8), channel_id=1, source_target_pairs={{0,1},{1,2},{2,3},{4,5},{5,6},{6,7},{8,9},{9,10},{10,11},{12,13},{... | collective-permute-start | bytes 1376264 | tf_op jit(solution)/shard_map/ppermute | solution.py:69
  34.2 2.8 %collective-permute-start.11 = (bf16[128,1792]{1,0:T(8,128)(2,1)S(1)}, bf16[128,1792]{1,0:T(8,128)(2,1)}, u32[]{:S(2)}, u32[]{:S(2)}) collective-permute-start(bf16[128,1792]{1,0:T(8,128)(2,1)S(1)} %collective-permute-done.9), channel_id=1, source_target_pairs={{1,0},{2,1},{3,2},{5,4},{6,5},{7,6},{9,8},{10,9},{11,10},{13,12},{... | collective-permute-start | bytes 1376264 | tf_op jit(solution)/shard_map/ppermute | solution.py:70
  37.2 2.7 %collective-permute-done.4 = bf16[528,448]{1,0:T(8,128)(2,1)} collective-permute-done((bf16[528,448]{1,0:T(8,128)(2,1)}, bf16[528,448]{1,0:T(8,128)(2,1)}, u32[]{:S(2)}, u32[]{:S(2)}) %collective-permute-start.4) | collective-permute-done | bytes 473120 | tf_op jit(solution)/shard_map/ppermute | solution.py:47
  40.0 2.7 %collective-permute-start.1 = (bf16[528,448]{1,0:T(8,128)(2,1)}, bf16[528,448]{1,0:T(8,128)(2,1)}, u32[]{:S(2)}, u32[]{:S(2)}) collective-permute-start(bf16[528,448]{1,0:T(8,128)(2,1)} %collective-permute-done), channel_id=1, source_target_pairs={{0,8},{8,0},{16,24},{24,16},{1,9},{9,1},{17,25},{25,17},{2,10},{10... | collective-permute-start | bytes 1419272 | tf_op jit(solution)/shard_map/ppermute | solution.py:49
  42.9 1.3 collective-permute-start.2
  44.3 6.6 %dynamic_update_slice.40 = bf16[528,7168]{1,0:T(8,128)(2,1)} dynamic-update-slice(bf16[528,7168]{1,0:T(8,128)(2,1)} %bitcast_dynamic-update-slice_fusion, bf16[528,448]{1,0:T(8,128)(2,1)} %collective-permute-done, s32[]{:T(128)} %constant.101.clone.1, s32[]{:T(128)S(6)} %select_n.141) | dynamic-update-slice | bytes 946180 | tf_op jit(solution)/shard_map/dynamic_update_slice | solution.py:53
  50.9 3.2 %collective-permute-start.18 = (bf16[128,1792]{1,0:T(8,128)(2,1)}, bf16[128,1792]{1,0:T(8,128)(2,1)}, u32[]{:S(2)}, u32[]{:S(2)}) collective-permute-start(bf16[128,1792]{1,0:T(8,128)(2,1)} %collective-permute-done.16), channel_id=1, source_target_pairs={{0,1},{1,2},{2,3},{4,5},{5,6},{6,7},{8,9},{9,10},{10,11},{12,13},{... | collective-permute-start | bytes 1376264 | tf_op jit(solution)/shard_map/ppermute | solution.py:69
  54.1 1.2 fusion.97
  55.3 0.4 collective-permute-start.6
  55.7 2.8 %collective-permute-start.19 = (bf16[128,1792]{1,0:T(8,128)(2,1)S(1)}, bf16[128,1792]{1,0:T(8,128)(2,1)}, u32[]{:S(2)}, u32[]{:S(2)}) collective-permute-start(bf16[128,1792]{1,0:T(8,128)(2,1)S(1)} %collective-permute-done.17), channel_id=1, source_target_pairs={{1,0},{2,1},{3,2},{5,4},{6,5},{7,6},{9,8},{10,9},{11,10},{13,12},{... | collective-permute-start | bytes 1376264 | tf_op jit(solution)/shard_map/ppermute | solution.py:70
  58.7 2.5 %collective-permute-start.12 = (bf16[128,1792]{1,0:T(8,128)(2,1)}, bf16[128,1792]{1,0:T(8,128)(2,1)}, u32[]{:S(2)}, u32[]{:S(2)}) collective-permute-start(bf16[128,1792]{1,0:T(8,128)(2,1)} %collective-permute-done.10), channel_id=1, source_target_pairs={{0,1},{1,2},{2,3},{4,5},{5,6},{6,7},{8,9},{9,10},{10,11},{12,13},{... | collective-permute-start | bytes 1376264 | tf_op jit(solution)/shard_map/ppermute | solution.py:69
  61.2 1.2 fusion.83
  62.4 3.8 %collective-permute-start.13 = (bf16[128,1792]{1,0:T(8,128)(2,1)}, bf16[128,1792]{1,0:T(8,128)(2,1)}, u32[]{:S(2)}, u32[]{:S(2)}) collective-permute-start(bf16[128,1792]{1,0:T(8,128)(2,1)} %collective-permute-done.11), channel_id=1, source_target_pairs={{1,0},{2,1},{3,2},{5,4},{6,5},{7,6},{9,8},{10,9},{11,10},{13,12},{... | collective-permute-start | bytes 1376264 | tf_op jit(solution)/shard_map/ppermute | solution.py:70
  66.2 1.2 fusion.85
  67.4 6.6 %dynamic_update_slice.41 = bf16[528,7168]{1,0:T(8,128)(2,1)} dynamic-update-slice(bf16[528,7168]{1,0:T(8,128)(2,1)} %dynamic_update_slice.40, bf16[528,448]{1,0:T(8,128)(2,1)} %collective-permute-done.1, s32[]{:T(128)} %constant.101.clone.1, s32[]{:T(128)S(6)} %select_n.142) | dynamic-update-slice | bytes 946180 | tf_op jit(solution)/shard_map/dynamic_update_slice | solution.py:53
  74.0 6.6 %dynamic_update_slice.42 = bf16[528,7168]{1,0:T(8,128)(2,1)} dynamic-update-slice(bf16[528,7168]{1,0:T(8,128)(2,1)} %dynamic_update_slice.41, bf16[528,448]{1,0:T(8,128)(2,1)} %collective-permute-done.2, s32[]{:T(128)} %constant.101.clone.1, s32[]{:T(128)S(6)} %select_n.143) | dynamic-update-slice | bytes 946180 | tf_op jit(solution)/shard_map/dynamic_update_slice | solution.py:53
  80.7 1.7 collective-permute-start.5
  82.3 1.2 fusion.101
  83.6 0.5 collective-permute-start.7
  84.1 1.2 fusion.103
  85.3 1.2 fusion.87
  86.5 1.2 fusion.89
  87.7 6.7 %dynamic_update_slice.43 = bf16[528,7168]{1,0:T(8,128)(2,1)} dynamic-update-slice(bf16[528,7168]{1,0:T(8,128)(2,1)} %dynamic_update_slice.42, bf16[528,448]{1,0:T(8,128)(2,1)} %collective-permute-done.3, s32[]{:T(128)} %constant.101.clone.1, s32[]{:T(128)S(6)} %select_n.144) | dynamic-update-slice | bytes 946180 | tf_op jit(solution)/shard_map/dynamic_update_slice | solution.py:53
  94.4 7.4 %dynamic_update_slice.44 = bf16[528,7168]{1,0:T(8,128)(2,1)} dynamic-update-slice(bf16[528,7168]{1,0:T(8,128)(2,1)} %dynamic_update_slice.43, bf16[528,448]{1,0:T(8,128)(2,1)} %collective-permute-done.4, s32[]{:T(128)} %constant.101.clone.1, s32[]{:T(128)S(6)} %select_n.146) | dynamic-update-slice | bytes 946180 | tf_op jit(solution)/shard_map/dynamic_update_slice | solution.py:53
  101.8 7.4 %dynamic_update_slice.45 = bf16[528,7168]{1,0:T(8,128)(2,1)} dynamic-update-slice(bf16[528,7168]{1,0:T(8,128)(2,1)} %dynamic_update_slice.44, bf16[528,448]{1,0:T(8,128)(2,1)} %collective-permute-done.5, s32[]{:T(128)} %constant.101.clone.1, s32[]{:T(128)S(6)} %select_n.147) | dynamic-update-slice | bytes 946180 | tf_op jit(solution)/shard_map/dynamic_update_slice | solution.py:53
  109.2 7.4 %dynamic_update_slice.46 = bf16[528,7168]{1,0:T(8,128)(2,1)} dynamic-update-slice(bf16[528,7168]{1,0:T(8,128)(2,1)} %dynamic_update_slice.45, bf16[528,448]{1,0:T(8,128)(2,1)} %collective-permute-done.6, s32[]{:T(128)} %constant.101.clone.1, s32[]{:T(128)S(6)} %select_n.148) | dynamic-update-slice | bytes 946180 | tf_op jit(solution)/shard_map/dynamic_update_slice | solution.py:53
  116.6 7.4 %dynamic_update_slice.47 = bf16[528,7168]{1,0:T(8,128)(2,1)} dynamic-update-slice(bf16[528,7168]{1,0:T(8,128)(2,1)} %dynamic_update_slice.46, bf16[528,448]{1,0:T(8,128)(2,1)} %collective-permute-done.7, s32[]{:T(128)} %constant.101.clone.1, s32[]{:T(128)S(6)} %select_n.149) | dynamic-update-slice | bytes 946180 | tf_op jit(solution)/shard_map/dynamic_update_slice | solution.py:53
  124.0 2.3 %fusion = f32[128,528]{0,1:T(8,128)S(1)} fusion(bf16[528,7168]{1,0:T(8,128)(2,1)} %dynamic_update_slice.47, s32[]{:T(128)S(6)} %select_n.155, bf16[128,1792]{1,0:T(8,128)(2,1)} %collective-permute-done.19, f32[1792]{0:T(1024)S(1)} %get-tuple-element.21), kind=kOutput, calls=%fused_computation.1 | convolution fusion | flops 242909184 | bytes 2628612 | tf_op jit(solution)/shard_map/dot_general | solution.py:81
  126.3 2.3 %fusion.4 = f32[128,528]{0,1:T(8,128)S(1)} fusion(bf16[528,7168]{1,0:T(8,128)(2,1)} %dynamic_update_slice.47, s32[]{:T(128)S(6)} %select_n.154, bf16[128,1792]{1,0:T(8,128)(2,1)} %collective-permute-done.18, f32[1792]{0:T(1024)S(1)} %get-tuple-element.22), kind=kOutput, calls=%fused_computation.5 | convolution fusion | flops 242909184 | bytes 2628612 | tf_op jit(solution)/shard_map/dot_general | solution.py:81
  128.7 2.3 %fusion.12 = f32[128,528]{0,1:T(8,128)S(1)} fusion(bf16[528,7168]{1,0:T(8,128)(2,1)} %dynamic_update_slice.47, s32[]{:T(128)S(6)} %select_n.152, bf16[128,1792]{1,0:T(8,128)(2,1)} %collective-permute-done.16, f32[1792]{0:T(1024)S(1)} %get-tuple-element.18), kind=kOutput, calls=%fused_computation.13 | convolution fusion | flops 242909184 | bytes 2628612 | tf_op jit(solution)/shard_map/dot_general | solution.py:81
  131.0 2.2 %fusion.8 = f32[128,528]{0,1:T(8,128)S(1)} fusion(bf16[528,7168]{1,0:T(8,128)(2,1)} %dynamic_update_slice.47, s32[]{:T(128)S(6)} %select_n.153, bf16[128,1792]{1,0:T(8,128)(2,1)S(1)} %collective-permute-done.17, f32[1792]{0:T(1024)S(1)} %get-tuple-element.17), kind=kOutput, calls=%fused_computation.9 | convolution fusion | flops 242909184 | bytes 2628612 | tf_op jit(solution)/shard_map/dot_general | solution.py:81
  133.2 2.2 %fusion.16 = f32[128,528]{0,1:T(8,128)S(1)} fusion(bf16[528,7168]{1,0:T(8,128)(2,1)} %dynamic_update_slice.47, s32[]{:T(128)S(6)} %select_n.151, bf16[128,1792]{1,0:T(8,128)(2,1)S(1)} %collective-permute-done.15, f32[1792]{0:T(1024)S(1)} %get-tuple-element.19), kind=kOutput, calls=%fused_computation.17 | convolution fusion | flops 242909184 | bytes 2628612 | tf_op jit(solution)/shard_map/dot_general | solution.py:81
  135.4 2.2 %fusion.20 = f32[128,528]{0,1:T(8,128)S(1)} fusion(bf16[528,7168]{1,0:T(8,128)(2,1)} %dynamic_update_slice.47, s32[]{:T(128)S(6)} %select_n.150, bf16[128,1792]{1,0:T(8,128)(2,1)S(1)} %collective-permute-done.14, f32[1792]{0:T(1024)S(1)} %get-tuple-element.20), kind=kOutput, calls=%fused_computation.21 | convolution fusion | flops 242909184 | bytes 2628612 | tf_op jit(solution)/shard_map/dot_general | solution.py:81
  137.6 2.2 %fusion.70 = bf16[128,528]{0,1:T(8,128)(2,1)S(1)} fusion(f32[128,528]{0,1:T(8,128)S(1)} %fusion, f32[128,528]{0,1:T(8,128)S(1)} %fusion.4, f32[128,528]{0,1:T(8,128)S(1)} %fusion.8, f32[128,528]{0,1:T(8,128)S(1)} %fusion.12, f32[128,528]{0,1:T(8,128)S(1)} %fusion.16, f32[128,528]{0,1:T(8,128)S(1)} %fusion.20, bf16[528,7168]{1,0:T(8,128)(2,1)} %dynamic_update_slice.47, ...), kind=kOutput, calls=%fused_computation.43 | convolution fusion | flops 243449856 | bytes 4116996 | tf_op jit(solution)/shard_map/dot_general | solution.py:81
  139.8 2.3 %fusion.6 = f32[128,528]{0,1:T(8,128)S(1)} fusion(bf16[528,7168]{1,0:T(8,128)(2,1)} %dynamic_update_slice.47, s32[]{:T(128)S(6)} %select_n.154, bf16[128,1792]{1,0:T(8,128)(2,1)} %collective-permute-done.12, f32[1792]{0:T(1024)S(1)} %get-tuple-element.22), kind=kOutput, calls=%fused_computation.7 | convolution fusion | flops 242909184 | bytes 2628612 | tf_op jit(solution)/shard_map/dot_general | solution.py:81
  142.1 2.3 %fusion.2 = f32[128,528]{0,1:T(8,128)S(1)} fusion(bf16[528,7168]{1,0:T(8,128)(2,1)} %dynamic_update_slice.47, s32[]{:T(128)S(6)} %select_n.155, bf16[128,1792]{1,0:T(8,128)(2,1)} %collective-permute-done.13, f32[1792]{0:T(1024)S(1)} %get-tuple-element.21), kind=kOutput, calls=%fused_computation.3 | convolution fusion | flops 242909184 | bytes 2628612 | tf_op jit(solution)/shard_map/dot_general | solution.py:81
  144.5 2.3 %fusion.10 = f32[128,528]{0,1:T(8,128)S(1)} fusion(bf16[528,7168]{1,0:T(8,128)(2,1)} %dynamic_update_slice.47, s32[]{:T(128)S(6)} %select_n.153, bf16[128,1792]{1,0:T(8,128)(2,1)} %collective-permute-done.11, f32[1792]{0:T(1024)S(1)} %get-tuple-element.17), kind=kOutput, calls=%fused_computation.11 | convolution fusion | flops 242909184 | bytes 2628612 | tf_op jit(solution)/shard_map/dot_general | solution.py:81
  146.8 2.3 %fusion.14 = f32[128,528]{0,1:T(8,128)S(1)} fusion(bf16[528,7168]{1,0:T(8,128)(2,1)} %dynamic_update_slice.47, s32[]{:T(128)S(6)} %select_n.152, bf16[128,1792]{1,0:T(8,128)(2,1)} %collective-permute-done.10, f32[1792]{0:T(1024)S(1)} %get-tuple-element.18), kind=kOutput, calls=%fused_computation.15 | convolution fusion | flops 242909184 | bytes 2628612 | tf_op jit(solution)/shard_map/dot_general | solution.py:81
  149.2 2.2 %fusion.18 = f32[128,528]{0,1:T(8,128)S(1)} fusion(bf16[528,7168]{1,0:T(8,128)(2,1)} %dynamic_update_slice.47, s32[]{:T(128)S(6)} %select_n.151, bf16[128,1792]{1,0:T(8,128)(2,1)S(1)} %collective-permute-done.9, f32[1792]{0:T(1024)S(1)} %get-tuple-element.19), kind=kOutput, calls=%fused_computation.19 | convolution fusion | flops 242909184 | bytes 2628612 | tf_op jit(solution)/shard_map/dot_general | solution.py:81
  151.4 2.2 %fusion.22 = f32[128,528]{0,1:T(8,128)S(1)} fusion(bf16[528,7168]{1,0:T(8,128)(2,1)} %dynamic_update_slice.47, s32[]{:T(128)S(6)} %select_n.150, bf16[128,1792]{1,0:T(8,128)(2,1)S(1)} %collective-permute-done.8, f32[1792]{0:T(1024)S(1)} %get-tuple-element.20), kind=kOutput, calls=%fused_computation.23 | convolution fusion | flops 242909184 | bytes 2628612 | tf_op jit(solution)/shard_map/dot_general | solution.py:81
  153.6 2.2 %fusion.73 = bf16[128,528]{0,1:T(8,128)(2,1)S(1)} fusion(f32[128,528]{0,1:T(8,128)S(1)} %fusion.2, f32[128,528]{0,1:T(8,128)S(1)} %fusion.6, f32[128,528]{0,1:T(8,128)S(1)} %fusion.10, f32[128,528]{0,1:T(8,128)S(1)} %fusion.14, f32[128,528]{0,1:T(8,128)S(1)} %fusion.18, f32[128,528]{0,1:T(8,128)S(1)} %fusion.22, ...), kind=kOutput, calls=%fused_computation.44 | convolution fusion | flops 243449856 | bytes 4116996 | tf_op jit(solution)/shard_map/dot_general | solution.py:81
  155.8 0.4 fusion.132
  156.3 1.2 collective-permute-start.20
  157.5 1.5 collective-permute-start.22
  159.0 1.3 collective-permute-start.23
  160.4 3.2 %collective-permute-done.21 = bf16[64,528]{0,1:T(8,128)(2,1)S(1)} collective-permute-done((bf16[64,528]{0,1:T(8,128)(2,1)S(1)}, bf16[64,528]{0,1:T(8,128)(2,1)S(1)}, u32[]{:S(2)}, u32[]{:S(2)}) %collective-permute-start.21) | collective-permute-done | bytes 67616 | tf_op jit(solution)/shard_map/ppermute | solution.py:101
  163.6 5.7 %collective-permute-done.22 = bf16[64,528]{0,1:T(8,128)(2,1)S(1)} collective-permute-done((bf16[64,528]{0,1:T(8,128)(2,1)S(1)}, bf16[64,528]{0,1:T(8,128)(2,1)S(1)}, u32[]{:S(2)}, u32[]{:S(2)}) %collective-permute-start.22) | collective-permute-done | bytes 67616 | tf_op jit(solution)/shard_map/ppermute | solution.py:101
  169.3 2.4 %collective-permute-done.23 = bf16[64,528]{0,1:T(8,128)(2,1)S(1)} collective-permute-done((bf16[64,528]{0,1:T(8,128)(2,1)S(1)}, bf16[64,528]{0,1:T(8,128)(2,1)S(1)}, u32[]{:S(2)}, u32[]{:S(2)}) %collective-permute-start.23) | collective-permute-done | bytes 67616 | tf_op jit(solution)/shard_map/ppermute | solution.py:101
  172.4 0.8 copy.10
  173.2 0.3 multiply_convert_fusion
  173.5 0.8 copy.9
  (55 shorter events, 2.3 us)
Async XLA Ops:
  2.6 20.1 %collective-permute-start.15 = (bf16[128,1792]{1,0:T(8,128)(2,1)S(1)}, bf16[128,1792]{1,0:T(8,128)(2,1)S(1)}, u32[]{:S(2)}, u32[]{:S(2)}) collective-permute-start(bf16[128,1792]{1,0:T(8,128)(2,1)S(1)} %get-tuple-element.10), channel_id=1, source_target_pairs={{1,0},{2,1},{3,2},{5,4},{6,5},{7,6},{9,8},{10,9},{11,10},{13,12},{... | collective-permute-start | bytes 1376264 | tf_op jit(solution)/shard_map/ppermute | solution.py:70
  4.7 19.4 %collective-permute-start.14 = (bf16[128,1792]{1,0:T(8,128)(2,1)S(1)}, bf16[128,1792]{1,0:T(8,128)(2,1)S(1)}, u32[]{:S(2)}, u32[]{:S(2)}) collective-permute-start(bf16[128,1792]{1,0:T(8,128)(2,1)S(1)} %get-tuple-element.10), channel_id=1, source_target_pairs={{0,1},{1,2},{2,3},{4,5},{5,6},{6,7},{8,9},{9,10},{10,11},{12,13},{... | collective-permute-start | bytes 1376264 | tf_op jit(solution)/shard_map/ppermute | solution.py:69
  7.9 19.7 %collective-permute-start.8 = (bf16[128,1792]{1,0:T(8,128)(2,1)}, bf16[128,1792]{1,0:T(8,128)(2,1)S(1)}, u32[]{:S(2)}, u32[]{:S(2)}) collective-permute-start(bf16[128,1792]{1,0:T(8,128)(2,1)} %get-tuple-element.11), channel_id=1, source_target_pairs={{0,1},{1,2},{2,3},{4,5},{5,6},{6,7},{8,9},{9,10},{10,11},{12,13},{... | collective-permute-start | bytes 1376264 | tf_op jit(solution)/shard_map/ppermute | solution.py:69
  11.2 19.8 %collective-permute-start.9 = (bf16[128,1792]{1,0:T(8,128)(2,1)}, bf16[128,1792]{1,0:T(8,128)(2,1)S(1)}, u32[]{:S(2)}, u32[]{:S(2)}) collective-permute-start(bf16[128,1792]{1,0:T(8,128)(2,1)} %get-tuple-element.11), channel_id=1, source_target_pairs={{1,0},{2,1},{3,2},{5,4},{6,5},{7,6},{9,8},{10,9},{11,10},{13,12},{... | collective-permute-start | bytes 1376264 | tf_op jit(solution)/shard_map/ppermute | solution.py:70
  16.1 18.1 %collective-permute-start = (bf16[528,448]{1,0:T(8,128)(2,1)}, bf16[528,448]{1,0:T(8,128)(2,1)}, u32[]{:S(2)}, u32[]{:S(2)}) collective-permute-start(bf16[528,448]{1,0:T(8,128)(2,1)} %get-tuple-element.7), channel_id=1, source_target_pairs={{0,4},{4,0},{1,5},{5,1},{2,6},{6,2},{3,7},{7,3},{8,12},{12,8},{9,1... | collective-permute-start | bytes 1419272 | tf_op jit(solution)/shard_map/ppermute | solution.py:47
  16.3 4.0 %copy-start.1 = (bf16[3584,528]{0,1:T(8,128)(2,1)S(1)}, bf16[3584,528]{0,1:T(8,128)(2,1)}, u32[]{:S(2)}) copy-start(bf16[3584,528]{0,1:T(8,128)(2,1)} %param.9) | copy-start | bytes 11354116
  16.3 6.2 %copy-start = (bf16[256,1792]{1,0:T(8,128)(2,1)S(1)}, bf16[256,1792]{1,0:T(8,128)(2,1)}, u32[]{:S(2)}) copy-start(bf16[256,1792]{1,0:T(8,128)(2,1)} %param.5) | copy-start | bytes 2752516
  16.3 7.7 %copy-start.2 = (f32[7168]{0:T(1024)S(1)}, f32[7168]{0:T(1024)}, u32[]{:S(2)}) copy-start(f32[7168]{0:T(1024)} %param.6) | copy-start | bytes 86020
  22.7 17.2 %collective-permute-start.4 = (bf16[528,448]{1,0:T(8,128)(2,1)}, bf16[528,448]{1,0:T(8,128)(2,1)}, u32[]{:S(2)}, u32[]{:S(2)}) collective-permute-start(bf16[528,448]{1,0:T(8,128)(2,1)} %get-tuple-element.6), channel_id=1, source_target_pairs={{0,4},{4,0},{1,5},{5,1},{2,6},{6,2},{3,7},{7,3},{8,12},{12,8},{9,1... | collective-permute-start | bytes 1419272 | tf_op jit(solution)/shard_map/ppermute | solution.py:47
  24.1 18.7 %collective-permute-start.17 = (bf16[128,1792]{1,0:T(8,128)(2,1)S(1)}, bf16[128,1792]{1,0:T(8,128)(2,1)S(1)}, u32[]{:S(2)}, u32[]{:S(2)}) collective-permute-start(bf16[128,1792]{1,0:T(8,128)(2,1)S(1)} %collective-permute-done.15), channel_id=1, source_target_pairs={{1,0},{2,1},{3,2},{5,4},{6,5},{7,6},{9,8},{10,9},{11,10},{13,12},{... | collective-permute-start | bytes 1376264 | tf_op jit(solution)/shard_map/ppermute | solution.py:70
  27.6 23.3 %collective-permute-start.16 = (bf16[128,1792]{1,0:T(8,128)(2,1)S(1)}, bf16[128,1792]{1,0:T(8,128)(2,1)}, u32[]{:S(2)}, u32[]{:S(2)}) collective-permute-start(bf16[128,1792]{1,0:T(8,128)(2,1)S(1)} %collective-permute-done.14), channel_id=1, source_target_pairs={{0,1},{1,2},{2,3},{4,5},{5,6},{6,7},{8,9},{9,10},{10,11},{12,13},{... | collective-permute-start | bytes 1376264 | tf_op jit(solution)/shard_map/ppermute | solution.py:69
  31.0 24.4 %collective-permute-start.10 = (bf16[128,1792]{1,0:T(8,128)(2,1)S(1)}, bf16[128,1792]{1,0:T(8,128)(2,1)}, u32[]{:S(2)}, u32[]{:S(2)}) collective-permute-start(bf16[128,1792]{1,0:T(8,128)(2,1)S(1)} %collective-permute-done.8), channel_id=1, source_target_pairs={{0,1},{1,2},{2,3},{4,5},{5,6},{6,7},{8,9},{9,10},{10,11},{12,13},{... | collective-permute-start | bytes 1376264 | tf_op jit(solution)/shard_map/ppermute | solution.py:69
  34.2 21.5 %collective-permute-start.11 = (bf16[128,1792]{1,0:T(8,128)(2,1)S(1)}, bf16[128,1792]{1,0:T(8,128)(2,1)}, u32[]{:S(2)}, u32[]{:S(2)}) collective-permute-start(bf16[128,1792]{1,0:T(8,128)(2,1)S(1)} %collective-permute-done.9), channel_id=1, source_target_pairs={{1,0},{2,1},{3,2},{5,4},{6,5},{7,6},{9,8},{10,9},{11,10},{13,12},{... | collective-permute-start | bytes 1376264 | tf_op jit(solution)/shard_map/ppermute | solution.py:70
  40.0 18.8 %collective-permute-start.1 = (bf16[528,448]{1,0:T(8,128)(2,1)}, bf16[528,448]{1,0:T(8,128)(2,1)}, u32[]{:S(2)}, u32[]{:S(2)}) collective-permute-start(bf16[528,448]{1,0:T(8,128)(2,1)} %collective-permute-done), channel_id=1, source_target_pairs={{0,8},{8,0},{16,24},{24,16},{1,9},{9,1},{17,25},{25,17},{2,10},{10... | collective-permute-start | bytes 1419272 | tf_op jit(solution)/shard_map/ppermute | solution.py:49
  42.9 19.5 %collective-permute-start.2 = (bf16[528,448]{1,0:T(8,128)(2,1)}, bf16[528,448]{1,0:T(8,128)(2,1)}, u32[]{:S(2)}, u32[]{:S(2)}) collective-permute-start(bf16[528,448]{1,0:T(8,128)(2,1)} %collective-permute-done), channel_id=1, source_target_pairs={{0,16},{8,24},{16,0},{24,8},{1,17},{9,25},{17,1},{25,9},{2,18},{10... | collective-permute-start | bytes 1419272 | tf_op jit(solution)/shard_map/ppermute | solution.py:48
  50.9 29.7 %collective-permute-start.18 = (bf16[128,1792]{1,0:T(8,128)(2,1)}, bf16[128,1792]{1,0:T(8,128)(2,1)}, u32[]{:S(2)}, u32[]{:S(2)}) collective-permute-start(bf16[128,1792]{1,0:T(8,128)(2,1)} %collective-permute-done.16), channel_id=1, source_target_pairs={{0,1},{1,2},{2,3},{4,5},{5,6},{6,7},{8,9},{9,10},{10,11},{12,13},{... | collective-permute-start | bytes 1376264 | tf_op jit(solution)/shard_map/ppermute | solution.py:69
  55.3 28.2 %collective-permute-start.6 = (bf16[528,448]{1,0:T(8,128)(2,1)}, bf16[528,448]{1,0:T(8,128)(2,1)}, u32[]{:S(2)}, u32[]{:S(2)}) collective-permute-start(bf16[528,448]{1,0:T(8,128)(2,1)} %collective-permute-done.4), channel_id=1, source_target_pairs={{0,16},{8,24},{16,0},{24,8},{1,17},{9,25},{17,1},{25,9},{2,18},{10... | collective-permute-start | bytes 1419272 | tf_op jit(solution)/shard_map/ppermute | solution.py:48
  55.7 27.9 %collective-permute-start.19 = (bf16[128,1792]{1,0:T(8,128)(2,1)S(1)}, bf16[128,1792]{1,0:T(8,128)(2,1)}, u32[]{:S(2)}, u32[]{:S(2)}) collective-permute-start(bf16[128,1792]{1,0:T(8,128)(2,1)S(1)} %collective-permute-done.17), channel_id=1, source_target_pairs={{1,0},{2,1},{3,2},{5,4},{6,5},{7,6},{9,8},{10,9},{11,10},{13,12},{... | collective-permute-start | bytes 1376264 | tf_op jit(solution)/shard_map/ppermute | solution.py:70
  58.7 26.6 %collective-permute-start.12 = (bf16[128,1792]{1,0:T(8,128)(2,1)}, bf16[128,1792]{1,0:T(8,128)(2,1)}, u32[]{:S(2)}, u32[]{:S(2)}) collective-permute-start(bf16[128,1792]{1,0:T(8,128)(2,1)} %collective-permute-done.10), channel_id=1, source_target_pairs={{0,1},{1,2},{2,3},{4,5},{5,6},{6,7},{8,9},{9,10},{10,11},{12,13},{... | collective-permute-start | bytes 1376264 | tf_op jit(solution)/shard_map/ppermute | solution.py:69
  62.4 24.1 %collective-permute-start.13 = (bf16[128,1792]{1,0:T(8,128)(2,1)}, bf16[128,1792]{1,0:T(8,128)(2,1)}, u32[]{:S(2)}, u32[]{:S(2)}) collective-permute-start(bf16[128,1792]{1,0:T(8,128)(2,1)} %collective-permute-done.11), channel_id=1, source_target_pairs={{1,0},{2,1},{3,2},{5,4},{6,5},{7,6},{9,8},{10,9},{11,10},{13,12},{... | collective-permute-start | bytes 1376264 | tf_op jit(solution)/shard_map/ppermute | solution.py:70
  80.7 21.1 %collective-permute-start.5 = (bf16[528,448]{1,0:T(8,128)(2,1)}, bf16[528,448]{1,0:T(8,128)(2,1)}, u32[]{:S(2)}, u32[]{:S(2)}) collective-permute-start(bf16[528,448]{1,0:T(8,128)(2,1)} %collective-permute-done.4), channel_id=1, source_target_pairs={{0,8},{8,0},{16,24},{24,16},{1,9},{9,1},{17,25},{25,17},{2,10},{10... | collective-permute-start | bytes 1419272 | tf_op jit(solution)/shard_map/ppermute | solution.py:49
  83.5 4.2 %collective-permute-start.3 = (bf16[528,448]{1,0:T(8,128)(2,1)}, bf16[528,448]{1,0:T(8,128)(2,1)}, u32[]{:S(2)}, u32[]{:S(2)}) collective-permute-start(bf16[528,448]{1,0:T(8,128)(2,1)} %collective-permute-done.2), channel_id=1, source_target_pairs={{0,8},{8,0},{16,24},{24,16},{1,9},{9,1},{17,25},{25,17},{2,10},{10... | collective-permute-start | bytes 1419272 | tf_op jit(solution)/shard_map/ppermute | solution.py:50
  83.6 33.0 %collective-permute-start.7 = (bf16[528,448]{1,0:T(8,128)(2,1)}, bf16[528,448]{1,0:T(8,128)(2,1)}, u32[]{:S(2)}, u32[]{:S(2)}) collective-permute-start(bf16[528,448]{1,0:T(8,128)(2,1)} %collective-permute-done.6), channel_id=1, source_target_pairs={{0,8},{8,0},{16,24},{24,16},{1,9},{9,1},{17,25},{25,17},{2,10},{10... | collective-permute-start | bytes 1419272 | tf_op jit(solution)/shard_map/ppermute | solution.py:50
  149.2 22.9 %copy-start.4 = (f32[512]{0:T(512)S(1)}, f32[512]{0:T(512)}, u32[]{:S(2)}) copy-start(f32[512]{0:T(512)} %param.8) | copy-start | bytes 6148
  149.2 24.0 %copy-start.3 = (f32[1536]{0:T(1024)S(1)}, f32[1536]{0:T(1024)}, u32[]{:S(2)}) copy-start(f32[1536]{0:T(1024)} %param.7) | copy-start | bytes 18436
  156.3 4.1 %collective-permute-start.20 = (bf16[64,528]{0,1:T(8,128)(2,1)S(1)}, bf16[64,528]{0,1:T(8,128)(2,1)S(1)}, u32[]{:S(2)}, u32[]{:S(2)}) collective-permute-start(bf16[64,528]{0,1:T(8,128)(2,1)S(1)} %get-tuple-element.13), channel_id=1, source_target_pairs={{0,8},{1,9},{2,10},{3,11},{8,16},{9,17},{10,18},{11,19},{16,24},{1... | collective-permute-start | bytes 202760 | tf_op jit(solution)/shard_map/ppermute | solution.py:101
  157.5 6.1 %collective-permute-start.21 = (bf16[64,528]{0,1:T(8,128)(2,1)S(1)}, bf16[64,528]{0,1:T(8,128)(2,1)S(1)}, u32[]{:S(2)}, u32[]{:S(2)}) collective-permute-start(bf16[64,528]{0,1:T(8,128)(2,1)S(1)} %get-tuple-element.14), channel_id=1, source_target_pairs={{0,9},{1,10},{2,11},{3,8},{8,17},{9,18},{10,19},{11,16},{16,25},{1... | collective-permute-start | bytes 202760 | tf_op jit(solution)/shard_map/ppermute | solution.py:101
  157.5 11.8 %collective-permute-start.22 = (bf16[64,528]{0,1:T(8,128)(2,1)S(1)}, bf16[64,528]{0,1:T(8,128)(2,1)S(1)}, u32[]{:S(2)}, u32[]{:S(2)}) collective-permute-start(bf16[64,528]{0,1:T(8,128)(2,1)S(1)} %get-tuple-element.15), channel_id=1, source_target_pairs={{0,10},{1,11},{2,8},{3,9},{8,18},{9,19},{10,16},{11,17},{16,26},{1... | collective-permute-start | bytes 202760 | tf_op jit(solution)/shard_map/ppermute | solution.py:101
  159.0 12.7 %collective-permute-start.23 = (bf16[64,528]{0,1:T(8,128)(2,1)S(1)}, bf16[64,528]{0,1:T(8,128)(2,1)S(1)}, u32[]{:S(2)}, u32[]{:S(2)}) collective-permute-start(bf16[64,528]{0,1:T(8,128)(2,1)S(1)} %get-tuple-element.12), channel_id=1, source_target_pairs={{0,11},{1,8},{2,9},{3,10},{8,19},{9,16},{10,17},{11,18},{16,27},{1... | collective-permute-start | bytes 202760 | tf_op jit(solution)/shard_map/ppermute | solution.py:101

commit v2 on v0

v2 whole, which is shorter than its diff:
```python
import functools

import jax
import jax.numpy as jnp
from jax import lax
from jax.experimental import pallas as pl
from jax.experimental.pallas import tpu as pltpu
from jax.sharding import PartitionSpec as P

QL = 1536
KVL = 512
ROPE = 64
LENGTH = 4096


epsilon = 1e-06
rope_base = 10000.0
ROW_CHUNKS = 1
PACK = 16


def root_scale(values, gain):
    mean_square = jnp.mean(values * values, axis=-1, keepdims=True)
    return values * lax.rsqrt(mean_square + epsilon) * gain


def rotate(latent, position):
    half_rope = ROPE // 2
    frequency = rope_base ** (-(jnp.arange(half_rope).astype(jnp.float32) / half_rope))
    angle = position.astype(jnp.float32)[:, None] * frequency[None, :]
    first = latent[:, QL + KVL : QL + KVL + half_rope]
    second = latent[:, QL + KVL + half_rope :]
    cosine = jnp.cos(angle)
    sine = jnp.sin(angle)
    return jnp.concatenate([first * cosine - second * sine, second * cosine + first * sine], axis=1)


def weight_parts(weight, width):
    fsdp, section = lax.axis_size("fsdp"), lax.axis_size("section")
    columns, depth = weight.shape
    if fsdp != 2 or section != 4 or depth != 2 * width:
        full = lax.all_gather(weight, "fsdp", axis=1, tiled=True)
        return [[full]], lambda block: (0 * block, block)
    side, fsdp_index = lax.axis_index("section") % 2, lax.axis_index("fsdp")
    cut = (columns // 2 + PACK - 1) // PACK * PACK
    here, beside = [], []
    for low, high in ((0, cut), (cut, columns)):
        own = lax.dynamic_slice(weight, (low, side * width), (high - low, width))
        here.append(lax.ppermute(own, "fsdp", [(0, 1), (1, 0)]))
        beside.append(lax.ppermute(here[-1], "section", [(i, i ^ 1) for i in range(4)]))

    def place(block):
        local = block // 2 == fsdp_index
        return jnp.where(local, 0, jnp.where(block % 2 == side, 1, 2)), jnp.where(local, block % 2, 0)

    return [[weight], here, beside], place


def accumulate(layout, blocks, first, last, width, where, *refs):
    refs = list(refs)
    block_refs = [refs.pop(0) for _ in range(blocks)]
    part_refs = [[refs.pop(0) for _ in range(count)] for count in layout]
    gain_ref = refs.pop(0)
    if not first:
        total_in, squares_in = refs.pop(0), refs.pop(0)
    total_out, squares_out = refs.pop(0), refs.pop(0)
    weights, arrived = refs
    if first:
        total_out[...] = jnp.zeros_like(total_out)
        squares_out[...] = jnp.zeros_like(squares_out)
    else:
        total_out[...] = total_in[...]
        squares_out[...] = squares_in[...]

    def fetch(index, part):
        copies, row = [], 0
        for ref in part_refs[part]:
            rows = ref.shape[0]
            start = pl.multiple_of(where[3, index] * width, width)
            copies.append(
                pltpu.make_async_copy(
                    ref.at[:, pl.ds(start, width)],
                    weights.at[index, pl.ds(row, rows)],
                    arrived.at[index, len(copies)],
                )
            )
            row += rows
        return copies

    for index in range(blocks):
        for part in range(len(part_refs)):

            @pl.when((where[0, index] == 1) & (where[2, index] == part))
            def _():
                for copy in fetch(index, part):
                    copy.start()

    for index in range(blocks):

        @pl.when(where[0, index] == 1)
        def _():
            values = block_refs[index][...].astype(jnp.float32)
            squares_out[...] += jnp.sum(values * values, axis=1, keepdims=True)
            start = pl.multiple_of(where[1, index] * width, width)
            gained = (values * gain_ref[:, pl.ds(start, width)]).astype(jnp.bfloat16)
            for part in range(len(part_refs)):

                @pl.when(where[2, index] == part)
                def _():
                    for copy in fetch(index, part):
                        copy.wait()

            total_out[...] += lax.dot_general(
                gained,
                weights[index],
                (((1,), (1,)), ((), ())),
                preferred_element_type=jnp.float32,
            )


def multiply(blocks, where, parts, gain, carried):
    rows, width = blocks[0].shape
    columns = sum(array.shape[0] for array in parts[0])
    layout = tuple(len(part) for part in parts)
    vmem, anywhere = pl.BlockSpec(memory_space=pltpu.VMEM), pl.BlockSpec(memory_space=pl.ANY)
    flat = [array for part in parts for array in part]
    return pl.pallas_call(
        functools.partial(accumulate, layout, len(blocks), carried is None, False, width),
        out_shape=(
            jax.ShapeDtypeStruct((rows, columns), jnp.float32),
            jax.ShapeDtypeStruct((rows, 1), jnp.float32),
        ),
        in_specs=[pl.BlockSpec(memory_space=pltpu.SMEM)]
        + [vmem] * len(blocks)
        + [anywhere] * len(flat)
        + [vmem]
        + [vmem] * (0 if carried is None else 2),
        out_specs=(vmem, vmem),
        scratch_shapes=[
            pltpu.VMEM((len(blocks), columns, width), jnp.bfloat16),
            pltpu.SemaphoreType.DMA((len(blocks), max(layout))),
        ],
        compiler_params=pltpu.CompilerParams(vmem_limit_bytes=32 * 1024 * 1024),
        cost_estimate=pl.CostEstimate(
            flops=2 * rows * width * columns * len(blocks),
            bytes_accessed=2 * width * (rows + columns) * len(blocks),
            transcendentals=0,
        ),
    )(where, *blocks, *flat, gain, *(carried or ()))


def on_device(hidden, attn_gain, q_gain, kv_gain, down_weight):
    row_count, width = hidden.shape
    ep, section = lax.axis_size("ep"), lax.axis_size("section")
    ep_index = lax.axis_index("ep")
    up = [(i, i + 1) for i in range(ep - 1)]
    down = [(i + 1, i) for i in range(ep - 1)]
    rising, falling = [hidden], [hidden]
    for step in range(1, ep):
        rising.append(lax.ppermute(rising[-1], "ep", up))
        falling.append(lax.ppermute(falling[-1], "ep", down))
    parts, place = weight_parts(down_weight.T, width)
    gain = attn_gain.reshape(1, -1)

    def add(pairs, carried):
        wheres = []
        for _, offset in pairs:
            block = ep_index + offset
            valid = (block >= 0) & (block < ep)
            block = jnp.clip(block, 0, ep - 1)
            part, inside = place(block)
            wheres.append(jnp.stack([valid.astype(jnp.int32), block, part, inside]))
        where = jnp.stack(wheres, axis=1).astype(jnp.int32)
        return multiply([block for block, _ in pairs], where, parts, gain, carried)

    near = [(hidden, 0)]
    for step in range(1, ep - 1):
        near += [(rising[step], -step), (falling[step], step)]
    total, squares = add(near, None)
    total, squares = add([(rising[-1], 1 - ep), (falling[-1], ep - 1)], (total, squares))
    mine = (total * lax.rsqrt(squares / (ep * width) + epsilon)).astype(jnp.bfloat16)
    quarter = row_count // ep
    columns = mine.shape[1]
    latent = jnp.zeros((ep, quarter, columns), jnp.bfloat16)
    for turn in range(ep):
        target = (ep_index + turn) % ep
        piece = lax.dynamic_slice(mine, (target * quarter, 0), (quarter, columns))
        moves = [
            (s * ep + e, (s + 1) % section * ep + (e + turn) % ep)
            for s in range(section)
            for e in range(ep)
        ]
        piece = lax.ppermute(piece, ("section", "ep"), moves)
        source = (ep_index + ep - turn) % ep
        latent = lax.dynamic_update_slice(latent, piece[None], (source, 0, 0))
    latent = latent.astype(jnp.float32).transpose(1, 0, 2).reshape(quarter, ep * columns)
    query = root_scale(latent[:, :QL], q_gain).astype(jnp.bfloat16)
    key_value = root_scale(latent[:, QL : QL + KVL], kv_gain)
    row_index = lax.axis_index("fsdp") * row_count + ep_index * quarter + jnp.arange(quarter)
    position = row_index % LENGTH
    cache = jnp.concatenate([key_value, rotate(latent, position)], axis=1).astype(jnp.bfloat16)
    return (query, cache)


def solution(mesh):
    placed = (P(("section", "fsdp"), "ep"), P(), P(), P(), P("fsdp", "ep"))
    return jax.shard_map(
        on_device,
        mesh=mesh,
        in_specs=placed,
        out_specs=(P(("section", "fsdp", "ep"), None), P(("section", "fsdp", "ep"), None)),
        check_vma=False,
    )
```

time: 220 us -> 100 us (0.45)
  waiting for transfers between devices: 187 us -> 49.3 us
  starting transfers between devices: 4.67 us -> 27 us
  between operations: 14.1 us -> 1.02 us
  Pallas kernels: 0 us -> 10.9 us
  matrix products: 8.15 us -> 0 us
  local copies, waits for them, and re-layouts: 3.09 us -> 8.97 us
    all_gather x2 -> x0, waiting for transfers between devices: 125 us -> none  [the longest x1 75.8 us: on_device(): sender = lax.all_gather(hidden, 'ep', axis=1, tiled=True)]
    ppermute x1 -> x14, starting transfers between devices: 0.01 us -> 27 us  [the longest x3 16.4 us: on_device(): rising.append(lax.ppermute(rising[-1], 'ep', up))]
    all_to_all x1 -> x0, waiting for transfers between devices: 17.3 us -> none  [on_device(): lax.all_to_all(partial_latent, 'ep', split_axis=0, concat_axis=1, tiled=T...]
    pallas_call x0 -> x2, Pallas kernels: none -> 10.9 us  [multiply(): pl.pallas_call(functools.partial(accumulate, layout, len(blocks), carried...]
    dot_general x1 -> x0, matrix products: 8.15 us -> none  [on_device(): jnp.dot(normed, lax.all_gather(down_weight, 'fsdp', axis=0, tiled=True),...]
    ppermute x1 -> x14, waiting for transfers between devices: 42.5 us -> 49.3 us  [the longest x3 19.8 us: on_device(): rising.append(lax.ppermute(rising[-1], 'ep', up))]
    all_to_all x1 -> x0, starting transfers between devices: 4.59 us -> none  [on_device(): lax.all_to_all(partial_latent, 'ep', split_axis=0, concat_axis=1, tiled=T...]
    unnamed x10 -> x12, local copies, waits for them, and re-layouts: 2.06 us -> 5.15 us
  transfers between devices with their start and end apart: 4 -> 14, of which waited for: 4 -> 8; matrix products, arithmetic and copies ran while one was open for 0% -> 4% of each run, Pallas kernels for 0% -> 7%
where the time goes in v2:
time: 100 us; the launch traced here: 98.8 us
  waiting for transfers between devices  49.3 us (49%)
  starting transfers between devices  27 us (27%)
  Pallas kernels  10.9 us (11%)
  local copies, waits for them, and re-layouts  8.97 us (9%)
  other arithmetic  1.6 us (2%)
  between operations  1.02 us (1%)
    ppermute x3, waiting for transfers between devices, on_device(): rising.append(lax.ppermute(rising[-1], 'ep', up))  19.8 us
    ppermute x2, waiting for transfers between devices, weight_parts(): here.append(lax.ppermute(own, 'fsdp', [(0, 1), (1, 0)]))  19.7 us
    ppermute x3, starting transfers between devices, on_device(): rising.append(lax.ppermute(rising[-1], 'ep', up))  16.4 us
    pallas_call x2, Pallas kernels, multiply(): pl.pallas_call(functools.partial(accumulate, layout, len(blocks), carried...  10.9 us
    unnamed x12, local copies, waits for them, and re-layouts  5.15 us
    ppermute x3, waiting for transfers between devices, on_device(): falling.append(lax.ppermute(falling[-1], 'ep', down))  5.04 us
    ppermute x4, waiting for transfers between devices, on_device(): piece = lax.ppermute(piece, ('section', 'ep'), moves)  4.7 us
    ppermute x4, starting transfers between devices, on_device(): piece = lax.ppermute(piece, ('section', 'ep'), moves)  4.58 us
  transfers between devices with their start and end apart: 14, of which 8 were waited for; matrix products, arithmetic and copies ran while one was open for 4% of the time, Pallas kernels for 7%

profile of v2, /device:TPU:0, one launch (start us, length us, event | category | flops | bytes accessed | tf_op | source)
XLA Modules:
  0.0 98.8 jit_solution(4084407149015030940)
XLA Ops:
  0.6 5.9 %collective-permute-start = (bf16[256,1792]{1,0:T(8,128)(2,1)}, bf16[256,1792]{1,0:T(8,128)(2,1)}, u32[]{:S(2)}, u32[]{:S(2)}) collective-permute-start(bf16[256,1792]{1,0:T(8,128)(2,1)} %refs_0_.1), channel_id=1, source_target_pairs={{0,1},{1,2},{2,3},{4,5},{5,6},{6,7},{8,9},{9,10},{10,11},{12,13},{... | collective-permute-start | bytes 2752520 | tf_op jit(solution)/shard_map/ppermute | solution.py:160
  6.5 1.3 %collective-permute-start.3 = (bf16[256,1792]{1,0:T(8,128)(2,1)}, bf16[256,1792]{1,0:T(8,128)(2,1)}, u32[]{:S(2)}, u32[]{:S(2)}) collective-permute-start(bf16[256,1792]{1,0:T(8,128)(2,1)} %refs_0_.1), channel_id=1, source_target_pairs={{1,0},{2,1},{3,2},{5,4},{6,5},{7,6},{9,8},{10,9},{11,10},{13,12},{... | collective-permute-start | bytes 2752520 | tf_op jit(solution)/shard_map/ppermute | solution.py:161
  7.8 1.3 %dynamic-slice_bitcast_fusion = bf16[272,1792]{1,0:T(8,128)(2,1)S(1)} fusion(bf16[3584,528]{0,1:T(8,128)(2,1)} %param.9, s32[]{:T(128)S(6)} %select_n.212), kind=kLoop, calls=%fused_computation | loop fusion | bytes 1949700 | tf_op jit(solution)/shard_map/dynamic_slice | solution.py:48
  9.1 0.0 copy-start.2
  9.1 1.6 %collective-permute-start.6 = (bf16[272,1792]{1,0:T(8,128)(2,1)S(1)}, bf16[272,1792]{1,0:T(8,128)(2,1)S(1)}, u32[]{:S(2)}, u32[]{:S(2)}) collective-permute-start(bf16[272,1792]{1,0:T(8,128)(2,1)S(1)} %dynamic-slice_bitcast_fusion), channel_id=1, source_target_pairs={{0,4},{4,0},{1,5},{5,1},{2,6},{6,2},{3,7},{7,3},{8,12},{12,8},{9,1... | collective-permute-start | bytes 2924552 | tf_op jit(solution)/shard_map/ppermute | solution.py:49
  10.7 1.2 %dynamic-slice_bitcast_fusion.1 = bf16[256,1792]{1,0:T(8,128)(2,1)S(1)} fusion(bf16[3584,528]{0,1:T(8,128)(2,1)} %param.9, s32[]{:T(128)S(6)} %select_n.212), kind=kLoop, calls=%fused_computation.1 | loop fusion | bytes 1835012 | tf_op jit(solution)/shard_map/dynamic_slice | solution.py:48
  11.9 0.6 collective-permute-start.7
  12.5 13.0 %collective-permute-done.refs_1_ = bf16[256,1792]{1,0:T(8,128)(2,1)} collective-permute-done((bf16[256,1792]{1,0:T(8,128)(2,1)}, bf16[256,1792]{1,0:T(8,128)(2,1)}, u32[]{:S(2)}, u32[]{:S(2)}) %collective-permute-start) | collective-permute-done | bytes 917536 | tf_op jit(solution)/shard_map/ppermute | solution.py:160
  25.5 5.4 %collective-permute-start.1 = (bf16[256,1792]{1,0:T(8,128)(2,1)}, bf16[256,1792]{1,0:T(8,128)(2,1)}, u32[]{:S(2)}, u32[]{:S(2)}) collective-permute-start(bf16[256,1792]{1,0:T(8,128)(2,1)} %collective-permute-done.refs_1_), channel_id=1, source_target_pairs={{0,1},{1,2},{2,3},{4,5},{5,6},{6,7},{8,9},{9,10},{10,11},{12,13},{... | collective-permute-start | bytes 2752520 | tf_op jit(solution)/shard_map/ppermute | solution.py:160
  30.8 0.0 collective-permute-done.3.refs_2_
  30.8 1.3 %collective-permute-start.4 = (bf16[256,1792]{1,0:T(8,128)(2,1)}, bf16[256,1792]{1,0:T(8,128)(2,1)}, u32[]{:S(2)}, u32[]{:S(2)}) collective-permute-start(bf16[256,1792]{1,0:T(8,128)(2,1)} %collective-permute-done.3.refs_2_), channel_id=1, source_target_pairs={{1,0},{2,1},{3,2},{5,4},{6,5},{7,6},{9,8},{10,9},{11,10},{13,12},{... | collective-permute-start | bytes 2752520 | tf_op jit(solution)/shard_map/ppermute | solution.py:161
  32.1 1.5 %collective-permute-done.6.refs_6_.refs_3_ = bf16[272,1792]{1,0:T(8,128)(2,1)S(1)} collective-permute-done((bf16[272,1792]{1,0:T(8,128)(2,1)S(1)}, bf16[272,1792]{1,0:T(8,128)(2,1)S(1)}, u32[]{:S(2)}, u32[]{:S(2)}) %collective-permute-start.6) | collective-permute-done | bytes 974880 | tf_op jit(solution)/shard_map/ppermute | solution.py:49
  33.6 0.0 collective-permute-start.8
  33.6 18.2 %collective-permute-done.7.refs_7_.refs_4_ = bf16[256,1792]{1,0:T(8,128)(2,1)S(1)} collective-permute-done((bf16[256,1792]{1,0:T(8,128)(2,1)S(1)}, bf16[256,1792]{1,0:T(8,128)(2,1)S(1)}, u32[]{:S(2)}, u32[]{:S(2)}) %collective-permute-start.7) | collective-permute-done | bytes 917536 | tf_op jit(solution)/shard_map/ppermute | solution.py:49
  51.8 0.0 collective-permute-start.9
  51.8 0.0 collective-permute-done.1.refs_3_
  51.8 5.2 %collective-permute-start.2 = (bf16[256,1792]{1,0:T(8,128)(2,1)}, bf16[256,1792]{1,0:T(8,128)(2,1)}, u32[]{:S(2)}, u32[]{:S(2)}) collective-permute-start(bf16[256,1792]{1,0:T(8,128)(2,1)} %collective-permute-done.1.refs_3_), channel_id=1, source_target_pairs={{0,1},{1,2},{2,3},{4,5},{5,6},{6,7},{8,9},{9,10},{10,11},{12,13},{... | collective-permute-start | bytes 2752520 | tf_op jit(solution)/shard_map/ppermute | solution.py:160
  57.0 0.0 collective-permute-done.4.refs_4_
  57.0 1.3 %collective-permute-start.5 = (bf16[256,1792]{1,0:T(8,128)(2,1)}, bf16[256,1792]{1,0:T(8,128)(2,1)}, u32[]{:S(2)}, u32[]{:S(2)}) collective-permute-start(bf16[256,1792]{1,0:T(8,128)(2,1)} %collective-permute-done.4.refs_4_), channel_id=1, source_target_pairs={{1,0},{2,1},{3,2},{5,4},{6,5},{7,6},{9,8},{10,9},{11,10},{13,12},{... | collective-permute-start | bytes 2752520 | tf_op jit(solution)/shard_map/ppermute | solution.py:161
  58.5 0.1 add_bitcast_fusion.4
  58.6 0.1 copy.29
  58.7 0.1 copy.30
  58.8 0.1 add_bitcast_fusion.2
  58.8 0.1 copy.27
  58.9 0.1 copy.28
  59.0 0.1 add_bitcast_fusion.6
  59.1 0.1 copy.31
  59.2 0.1 add_bitcast_fusion
  59.3 0.1 copy.25
  59.4 0.1 copy.26
  59.5 0.1 stack.203.where
  59.6 0.1 pad_add_fusion.where
  59.7 0.0 collective-permute-done.9.refs_9_.refs_6_
  59.7 0.0 collective-permute-done.8.refs_8_.refs_5_
  59.7 0.0 copy-done.2
  59.7 0.0 copy-start
  59.7 2.1 %copy-done = bf16[3584,528]{0,1:T(8,128)(2,1)S(1)} copy-done((bf16[3584,528]{0,1:T(8,128)(2,1)S(1)}, bf16[3584,528]{0,1:T(8,128)(2,1)}, u32[]{:S(2)}) %copy-start) | copy-done | bytes 3784728
  61.8 1.2 %copy-done.1 = bf16[256,1792]{1,0:T(8,128)(2,1)S(1)} copy-done((bf16[256,1792]{1,0:T(8,128)(2,1)S(1)}, bf16[256,1792]{1,0:T(8,128)(2,1)}, u32[]{:S(2)}) %copy-start.1) | copy-done | bytes 917528
  62.9 6.9 %shard_map.68 = (f32[256,528]{1,0:T(8,128)S(1)}, f32[256,1]{1,0:T(8,128)S(1)}) custom-call(s32[4,5]{1,0:T(4,128)S(1)} %stack.203.where, bf16[256,1792]{1,0:T(8,128)(2,1)S(1)} %copy-done.1, bf16[256,1792]{1,0:T(8,128)(2,1)} %collective-permute-done.refs_1_, bf16[256,1792]{1,0:T(8,128)(2,1)} %collective-permute-done.3.refs_2_, ...), custom_call_target="tpu_custom_call" | custom-call | flops 2422210560 | bytes 14049280 | tf_op jit(solution)/shard_map/pallas_call | solution.py:127
  69.9 6.8 %collective-permute-done.2.refs_0_ = bf16[256,1792]{1,0:T(8,128)(2,1)} collective-permute-done((bf16[256,1792]{1,0:T(8,128)(2,1)}, bf16[256,1792]{1,0:T(8,128)(2,1)}, u32[]{:S(2)}, u32[]{:S(2)}) %collective-permute-start.2) | collective-permute-done | bytes 917536 | tf_op jit(solution)/shard_map/ppermute | solution.py:160
  76.7 5.0 %collective-permute-done.5.refs_1_ = bf16[256,1792]{1,0:T(8,128)(2,1)} collective-permute-done((bf16[256,1792]{1,0:T(8,128)(2,1)}, bf16[256,1792]{1,0:T(8,128)(2,1)}, u32[]{:S(2)}, u32[]{:S(2)}) %collective-permute-start.5) | collective-permute-done | bytes 917536 | tf_op jit(solution)/shard_map/ppermute | solution.py:161
  81.7 4.0 %shard_map.69 = (f32[256,528]{1,0:T(8,128)S(1)}, f32[256,1]{1,0:T(8,128)S(1)}) custom-call(s32[4,2]{1,0:T(4,128)S(1)} %pad_add_fusion.where, bf16[256,1792]{1,0:T(8,128)(2,1)} %collective-permute-done.2.refs_0_, bf16[256,1792]{1,0:T(8,128)(2,1)} %collective-permute-done.5.refs_1_, bf16[528,3584]{1,0:T(8,128)(2,1)S(1)} %bitcast.59, ...), custom_call_target="tpu_custom_call" | custom-call | flops 968884224 | bytes 5619712 | tf_op jit(solution)/shard_map/pallas_call | solution.py:127
  85.7 0.1 rsqrt_reduce_fusion
  85.8 0.1 multiply_convert_fusion.1
  86.0 0.1 collective-permute-start.10
  86.1 0.1 collective-permute-start.11
  86.2 0.9 collective-permute-start.12
  87.0 3.6 %collective-permute-start.13 = (bf16[64,528]{1,0:T(8,128)(2,1)S(1)}, bf16[64,528]{1,0:T(8,128)(2,1)S(1)}, u32[]{:S(2)}, u32[]{:S(2)}) collective-permute-start(bf16[64,528]{1,0:T(8,128)(2,1)S(1)} %get-tuple-element.14), channel_id=1, source_target_pairs={{0,11},{1,8},{2,9},{3,10},{8,19},{9,16},{10,17},{11,18},{16,27},{1... | collective-permute-start | bytes 202760 | tf_op jit(solution)/shard_map/ppermute | solution.py:193
  90.7 2.2 %collective-permute-done.11 = bf16[64,528]{1,0:T(8,128)(2,1)S(1)} collective-permute-done((bf16[64,528]{1,0:T(8,128)(2,1)S(1)}, bf16[64,528]{1,0:T(8,128)(2,1)S(1)}, u32[]{:S(2)}, u32[]{:S(2)}) %collective-permute-start.11) | collective-permute-done | bytes 67616 | tf_op jit(solution)/shard_map/ppermute | solution.py:193
  92.9 1.8 %collective-permute-done.12 = bf16[64,528]{1,0:T(8,128)(2,1)S(1)} collective-permute-done((bf16[64,528]{1,0:T(8,128)(2,1)S(1)}, bf16[64,528]{1,0:T(8,128)(2,1)S(1)}, u32[]{:S(2)}, u32[]{:S(2)}) %collective-permute-start.12) | collective-permute-done | bytes 67616 | tf_op jit(solution)/shard_map/ppermute | solution.py:193
  94.7 0.3 copy.32
  95.0 0.7 collective-permute-done.13
  95.7 0.1 copy.33
  95.9 0.0 copy-start.4
  95.9 0.1 reshape.66
  96.0 0.0 copy-start.3
  96.0 0.1 multiply_reduce_fusion.1
  96.1 0.2 multiply_reduce_fusion
  96.3 0.3 copy-done.4
  96.6 0.1 multiply_convert_fusion.2
  96.7 0.1 fusion.5
  96.9 0.8 copy.35
  97.7 0.3 multiply_convert_fusion
  97.9 0.8 copy.34
  (14 shorter events, 0.2 us)
Async XLA Ops:
  0.6 24.8 %collective-permute-start = (bf16[256,1792]{1,0:T(8,128)(2,1)}, bf16[256,1792]{1,0:T(8,128)(2,1)}, u32[]{:S(2)}, u32[]{:S(2)}) collective-permute-start(bf16[256,1792]{1,0:T(8,128)(2,1)} %refs_0_.1), channel_id=1, source_target_pairs={{0,1},{1,2},{2,3},{4,5},{5,6},{6,7},{8,9},{9,10},{10,11},{12,13},{... | collective-permute-start | bytes 2752520 | tf_op jit(solution)/shard_map/ppermute | solution.py:160
  6.5 24.4 %collective-permute-start.3 = (bf16[256,1792]{1,0:T(8,128)(2,1)}, bf16[256,1792]{1,0:T(8,128)(2,1)}, u32[]{:S(2)}, u32[]{:S(2)}) collective-permute-start(bf16[256,1792]{1,0:T(8,128)(2,1)} %refs_0_.1), channel_id=1, source_target_pairs={{1,0},{2,1},{3,2},{5,4},{6,5},{7,6},{9,8},{10,9},{11,10},{13,12},{... | collective-permute-start | bytes 2752520 | tf_op jit(solution)/shard_map/ppermute | solution.py:161
  9.1 50.6 %copy-start.2 = (f32[7168]{0:T(1024)S(1)}, f32[7168]{0:T(1024)}, u32[]{:S(2)}) copy-start(f32[7168]{0:T(1024)} %param.6) | copy-start | bytes 86020
  9.1 24.6 %collective-permute-start.6 = (bf16[272,1792]{1,0:T(8,128)(2,1)S(1)}, bf16[272,1792]{1,0:T(8,128)(2,1)S(1)}, u32[]{:S(2)}, u32[]{:S(2)}) collective-permute-start(bf16[272,1792]{1,0:T(8,128)(2,1)S(1)} %dynamic-slice_bitcast_fusion), channel_id=1, source_target_pairs={{0,4},{4,0},{1,5},{5,1},{2,6},{6,2},{3,7},{7,3},{8,12},{12,8},{9,1... | collective-permute-start | bytes 2924552 | tf_op jit(solution)/shard_map/ppermute | solution.py:49
  11.9 39.9 %collective-permute-start.7 = (bf16[256,1792]{1,0:T(8,128)(2,1)S(1)}, bf16[256,1792]{1,0:T(8,128)(2,1)S(1)}, u32[]{:S(2)}, u32[]{:S(2)}) collective-permute-start(bf16[256,1792]{1,0:T(8,128)(2,1)S(1)} %dynamic-slice_bitcast_fusion.1), channel_id=1, source_target_pairs={{0,4},{4,0},{1,5},{5,1},{2,6},{6,2},{3,7},{7,3},{8,12},{12,8},{9,1... | collective-permute-start | bytes 2752520 | tf_op jit(solution)/shard_map/ppermute | solution.py:49
  25.5 26.4 %collective-permute-start.1 = (bf16[256,1792]{1,0:T(8,128)(2,1)}, bf16[256,1792]{1,0:T(8,128)(2,1)}, u32[]{:S(2)}, u32[]{:S(2)}) collective-permute-start(bf16[256,1792]{1,0:T(8,128)(2,1)} %collective-permute-done.refs_1_), channel_id=1, source_target_pairs={{0,1},{1,2},{2,3},{4,5},{5,6},{6,7},{8,9},{9,10},{10,11},{12,13},{... | collective-permute-start | bytes 2752520 | tf_op jit(solution)/shard_map/ppermute | solution.py:160
  30.8 26.2 %collective-permute-start.4 = (bf16[256,1792]{1,0:T(8,128)(2,1)}, bf16[256,1792]{1,0:T(8,128)(2,1)}, u32[]{:S(2)}, u32[]{:S(2)}) collective-permute-start(bf16[256,1792]{1,0:T(8,128)(2,1)} %collective-permute-done.3.refs_2_), channel_id=1, source_target_pairs={{1,0},{2,1},{3,2},{5,4},{6,5},{7,6},{9,8},{10,9},{11,10},{13,12},{... | collective-permute-start | bytes 2752520 | tf_op jit(solution)/shard_map/ppermute | solution.py:161
  33.6 26.0 %collective-permute-start.8 = (bf16[272,1792]{1,0:T(8,128)(2,1)S(1)}, bf16[272,1792]{1,0:T(8,128)(2,1)S(1)}, u32[]{:S(2)}, u32[]{:S(2)}) collective-permute-start(bf16[272,1792]{1,0:T(8,128)(2,1)S(1)} %collective-permute-done.6.refs_6_.refs_3_), channel_id=1, source_target_pairs={{0,8},{8,0},{16,24},{24,16},{1,9},{9,1},{17,25},{25,17},{2,10},{10... | collective-permute-start | bytes 2924552 | tf_op jit(solution)/shard_map/ppermute | solution.py:50
  51.8 7.8 %collective-permute-start.9 = (bf16[256,1792]{1,0:T(8,128)(2,1)S(1)}, bf16[256,1792]{1,0:T(8,128)(2,1)}, u32[]{:S(2)}, u32[]{:S(2)}) collective-permute-start(bf16[256,1792]{1,0:T(8,128)(2,1)S(1)} %collective-permute-done.7.refs_7_.refs_4_), channel_id=1, source_target_pairs={{0,8},{8,0},{16,24},{24,16},{1,9},{9,1},{17,25},{25,17},{2,10},{10... | collective-permute-start | bytes 2752520 | tf_op jit(solution)/shard_map/ppermute | solution.py:50
  51.8 24.8 %collective-permute-start.2 = (bf16[256,1792]{1,0:T(8,128)(2,1)}, bf16[256,1792]{1,0:T(8,128)(2,1)}, u32[]{:S(2)}, u32[]{:S(2)}) collective-permute-start(bf16[256,1792]{1,0:T(8,128)(2,1)} %collective-permute-done.1.refs_3_), channel_id=1, source_target_pairs={{0,1},{1,2},{2,3},{4,5},{5,6},{6,7},{8,9},{9,10},{10,11},{12,13},{... | collective-permute-start | bytes 2752520 | tf_op jit(solution)/shard_map/ppermute | solution.py:160
  57.0 24.7 %collective-permute-start.5 = (bf16[256,1792]{1,0:T(8,128)(2,1)}, bf16[256,1792]{1,0:T(8,128)(2,1)}, u32[]{:S(2)}, u32[]{:S(2)}) collective-permute-start(bf16[256,1792]{1,0:T(8,128)(2,1)} %collective-permute-done.4.refs_4_), channel_id=1, source_target_pairs={{1,0},{2,1},{3,2},{5,4},{6,5},{7,6},{9,8},{10,9},{11,10},{13,12},{... | collective-permute-start | bytes 2752520 | tf_op jit(solution)/shard_map/ppermute | solution.py:161
  59.7 2.1 %copy-start = (bf16[3584,528]{0,1:T(8,128)(2,1)S(1)}, bf16[3584,528]{0,1:T(8,128)(2,1)}, u32[]{:S(2)}) copy-start(bf16[3584,528]{0,1:T(8,128)(2,1)} %param.9) | copy-start | bytes 11354116
  61.8 1.2 %copy-start.1 = (bf16[256,1792]{1,0:T(8,128)(2,1)S(1)}, bf16[256,1792]{1,0:T(8,128)(2,1)}, u32[]{:S(2)}) copy-start(bf16[256,1792]{1,0:T(8,128)(2,1)} %refs_0_.1) | copy-start | bytes 2752516
  86.0 4.6 %collective-permute-start.10 = (bf16[64,528]{1,0:T(8,128)(2,1)S(1)}, bf16[64,528]{1,0:T(8,128)(2,1)S(1)}, u32[]{:S(2)}, u32[]{:S(2)}) collective-permute-start(bf16[64,528]{1,0:T(8,128)(2,1)S(1)} %get-tuple-element.17), channel_id=1, source_target_pairs={{0,8},{1,9},{2,10},{3,11},{8,16},{9,17},{10,18},{11,19},{16,24},{1... | collective-permute-start | bytes 202760 | tf_op jit(solution)/shard_map/ppermute | solution.py:193
  86.1 6.8 %collective-permute-start.11 = (bf16[64,528]{1,0:T(8,128)(2,1)S(1)}, bf16[64,528]{1,0:T(8,128)(2,1)S(1)}, u32[]{:S(2)}, u32[]{:S(2)}) collective-permute-start(bf16[64,528]{1,0:T(8,128)(2,1)S(1)} %get-tuple-element.16), channel_id=1, source_target_pairs={{0,9},{1,10},{2,11},{3,8},{8,17},{9,18},{10,19},{11,16},{16,25},{1... | collective-permute-start | bytes 202760 | tf_op jit(solution)/shard_map/ppermute | solution.py:193
  86.2 8.6 %collective-permute-start.12 = (bf16[64,528]{1,0:T(8,128)(2,1)S(1)}, bf16[64,528]{1,0:T(8,128)(2,1)S(1)}, u32[]{:S(2)}, u32[]{:S(2)}) collective-permute-start(bf16[64,528]{1,0:T(8,128)(2,1)S(1)} %get-tuple-element.15), channel_id=1, source_target_pairs={{0,10},{1,11},{2,8},{3,9},{8,18},{9,19},{10,16},{11,17},{16,26},{1... | collective-permute-start | bytes 202760 | tf_op jit(solution)/shard_map/ppermute | solution.py:193
  87.0 8.7 %collective-permute-start.13 = (bf16[64,528]{1,0:T(8,128)(2,1)S(1)}, bf16[64,528]{1,0:T(8,128)(2,1)S(1)}, u32[]{:S(2)}, u32[]{:S(2)}) collective-permute-start(bf16[64,528]{1,0:T(8,128)(2,1)S(1)} %get-tuple-element.14), channel_id=1, source_target_pairs={{0,11},{1,8},{2,9},{3,10},{8,19},{9,16},{10,17},{11,18},{16,27},{1... | collective-permute-start | bytes 202760 | tf_op jit(solution)/shard_map/ppermute | solution.py:193
  95.9 0.7 copy-start.4
  96.0 1.7 %copy-start.3 = (f32[1536]{0:T(1024)S(1)}, f32[1536]{0:T(1024)}, u32[]{:S(2)}) copy-start(f32[1536]{0:T(1024)} %param.7) | copy-start | bytes 18436

commit v3 on v0

v3 whole, which is shorter than its diff:
```python
import functools

import jax
import jax.numpy as jnp
from jax import lax
from jax.experimental import pallas as pl
from jax.experimental.pallas import tpu as pltpu
from jax.sharding import PartitionSpec as P

QL = 1536
KVL = 512
ROPE = 64
LENGTH = 4096


epsilon = 1e-06
rope_base = 10000.0
ROW_CHUNKS = 2
PACK = 16
LANES = 128
VMEM_LIMIT = 48 * 1024 * 1024

vmem = pl.BlockSpec(memory_space=pltpu.VMEM)
smem = pl.BlockSpec(memory_space=pltpu.SMEM)
anywhere = pl.BlockSpec(memory_space=pl.ANY)


def section_spread(piece, pairs_of):
    across = lax.ppermute(piece, *pairs_of(2))
    beside = lax.ppermute(piece, *pairs_of(1))
    beside_across = lax.ppermute(across, *pairs_of(1))
    return [piece, beside, across, beside_across]


def far_weight(weight, width):
    columns = weight.shape[0]
    section_index, fsdp_index = lax.axis_index("section"), lax.axis_index("fsdp")
    low = section_index * LANES
    own = lax.dynamic_slice(weight, (low, fsdp_index * width), (columns - 3 * LANES, width))
    own = lax.ppermute(own, ("fsdp", "ep"), [(4, 5), (3, 2)])
    other = lax.ppermute(own, ("fsdp", "ep"), [(5, 1), (2, 6)])
    home = (lax.axis_index("ep") == 1) == (fsdp_index == 1)
    piece = jnp.where(home, own, other)

    def pairs_of(flip):
        return ("section", "ep"), [(s * 4 + z, (s ^ flip) * 4 + z) for s in range(4) for z in (1, 2)]

    return section_spread(piece, pairs_of)


def other_weight(weight, width):
    columns, depth = weight.shape
    section_index = lax.axis_index("section")
    quarter = depth // 4
    cut = (columns // 2 + PACK - 1) // PACK * PACK
    pieces = []
    for low, high in ((0, cut), (cut, columns)):
        own = lax.dynamic_slice(weight, (low, section_index * quarter), (high - low, quarter))
        own = lax.ppermute(own, "fsdp", [(0, 1), (1, 0)])
        pieces.append(
            section_spread(own, lambda flip: ("section", [(s, s ^ flip) for s in range(4)]))
        )
    return [[pieces[cut][flip] for cut in range(2)] for flip in range(4)]


def weight_copies(where, index, local_ref, piece_refs, target, arrived, act):
    width = target.shape[1]

    @pl.when(where[2, index] == 1)
    def _():
        start = pl.multiple_of(where[3, index] * width, width)
        act(pltpu.make_async_copy(local_ref.at[:, pl.ds(start, width)], target, arrived.at[0]))

    if piece_refs:
        for half in range(2):
            for flip in range(4):

                @pl.when((where[2, index] == 0) & (where[4 + half, index] == flip))
                def _():
                    row = 0
                    for cut, ref in enumerate(piece_refs[flip]):
                        rows, columns = ref.shape
                        into = target.at[pl.ds(row, rows), pl.ds(half * columns, columns)]
                        act(pltpu.make_async_copy(ref, into, arrived.at[2 * half + cut]))
                        row += rows


def start(copy):
    copy.start()


def wait(copy):
    copy.wait()


def product(values, gain, weight):
    gained = (values * gain).astype(jnp.bfloat16)
    return lax.dot_general(
        gained, weight, (((1,), (1,)), ((), ())), preferred_element_type=jnp.float32
    )


def near_kernel(groups, chunks, pieces, where, *refs):
    refs = list(refs)
    block_refs = [[refs.pop(0) for _ in range(chunks)] for _ in range(groups)]
    gain_ref, local_ref = refs.pop(0), refs.pop(0)
    piece_refs = [[refs.pop(0) for _ in range(2)] for _ in range(pieces)]
    total_ref, squares_ref, blocks, weights, block_arrived, weight_arrived = refs
    rows, width = block_refs[0][0].shape

    def block_copies(index, act):
        for chunk, ref in enumerate(block_refs[index]):
            into = blocks.at[index, pl.ds(chunk * rows, rows)]
            act(pltpu.make_async_copy(ref, into, block_arrived.at[index, chunk]))

    for index in range(groups):

        @pl.when(where[0, index] == 1)
        def _():
            block_copies(index, start)
            weight_copies(
                where, index, local_ref, piece_refs, weights.at[index], weight_arrived.at[index], start
            )

    total_ref[...] = jnp.zeros_like(total_ref)
    squares_ref[...] = jnp.zeros_like(squares_ref)
    for index in range(groups):

        @pl.when(where[0, index] == 1)
        def _():
            block_copies(index, wait)
            weight_copies(
                where, index, local_ref, piece_refs, weights.at[index], weight_arrived.at[index], wait
            )
            values = blocks[index].astype(jnp.float32)
            squares_ref[...] += jnp.sum(values * values, axis=1, keepdims=True)
            at = pl.multiple_of(where[1, index] * width, width)
            total_ref[...] += product(values, gain_ref[:, pl.ds(at, width)], weights[index])


def far_kernel(chunks, pieces, far_pieces, where, *refs):
    refs = list(refs)
    block_refs = [[refs.pop(0) for _ in range(chunks)] for _ in range(2)]
    gain_ref, total_in, squares_in, local_ref = [refs.pop(0) for _ in range(4)]
    piece_refs = [[refs.pop(0) for _ in range(2)] for _ in range(pieces)]
    far_refs = [refs.pop(0) for _ in range(far_pieces)]
    out_refs = [refs.pop(0) for _ in range(4)]
    total, extra, squares, block, weight, far, block_arrived, weight_arrived, far_arrived = refs
    rows, width = block_refs[0][0].shape

    def block_copies(act):
        for side in range(2):

            @pl.when(where[0, 0] == side)
            def _():
                for chunk, ref in enumerate(block_refs[side]):
                    into = block.at[pl.ds(chunk * rows, rows)]
                    act(pltpu.make_async_copy(ref, into, block_arrived.at[chunk]))

    def far_copies(act):
        if far_pieces == 1:
            act(pltpu.make_async_copy(far_refs[0], far, far_arrived.at[0]))
            return
        for flip in range(far_pieces):
            for place in range(4):
                count = LANES if place < 3 else far.shape[0] - 3 * LANES

                @pl.when(where[7, 0] == flip ^ place)
                def _():
                    act(
                        pltpu.make_async_copy(
                            far_refs[flip].at[pl.ds(0, count)],
                            far.at[pl.ds(place * LANES, count)],
                            far_arrived.at[flip],
                        )
                    )

    inner = where[6, 0] == 1
    block_copies(start)
    weight_copies(where, 0, local_ref, piece_refs, weight, weight_arrived, start)

    @pl.when(inner)
    def _():
        far_copies(start)

    block_copies(wait)
    values = block[...].astype(jnp.float32)
    squares[...] = squares_in[...] + jnp.sum(values * values, axis=1, keepdims=True)
    at = pl.multiple_of(where[1, 0] * width, width)
    gained = (values * gain_ref[:, pl.ds(at, width)]).astype(jnp.bfloat16)
    contract = (((1,), (1,)), ((), ()))
    weight_copies(where, 0, local_ref, piece_refs, weight, weight_arrived, wait)
    total[...] = total_in[...] + lax.dot_general(
        gained, weight[...], contract, preferred_element_type=jnp.float32
    )
    extra[...] = jnp.zeros_like(extra)

    @pl.when(inner)
    def _():
        far_copies(wait)
        extra[...] = lax.dot_general(
            gained, far[...], contract, preferred_element_type=jnp.float32
        )

    quarter, columns = out_refs[0].shape[0], total.shape[1]
    main = columns // LANES * LANES
    for turn, out_ref in enumerate(out_refs):
        piece = pl.ds(pl.multiple_of(where[8, turn] * quarter, quarter), quarter)
        own, more, square = total[piece, :], extra[piece, :], squares[piece, :]
        high = square.astype(jnp.bfloat16).astype(jnp.float32)
        rest = LANES - 2 * (columns - main) - 2
        out_ref[:, :main] = own[:, :main].astype(jnp.bfloat16)
        out_ref[:, main : 2 * main] = more[:, :main].astype(jnp.bfloat16)
        out_ref[:, 2 * main :] = jnp.concatenate(
            [own[:, main:], more[:, main:], high, square - high, jnp.zeros((quarter, rest))],
            axis=1,
        ).astype(jnp.bfloat16)


def finish_kernel(depth, columns, where, *refs):
    refs = list(refs)
    part_refs = [refs.pop(0) for _ in range(4)]
    q_gain_ref, kv_gain_ref, cosine_ref, sine_ref, query_ref, cache_ref, parts = refs
    main = columns // LANES * LANES
    tail = columns - main
    for turn, ref in enumerate(part_refs):
        parts[where[turn]] = ref[...].astype(jnp.float32)
    added = {0: 1, 3: 2}
    pieces = []
    for plane in range(4):
        body, end = parts[plane, :, :main], parts[plane, :, 2 * main : 2 * main + tail]
        if plane in added:
            other = added[plane]
            body = body + parts[other, :, main : 2 * main]
            end = end + parts[other, :, 2 * main + tail : 2 * main + 2 * tail]
        pieces += [body, end]
    at = 2 * main + 2 * tail
    squares = parts[1, :, at : at + 1] + parts[1, :, at + 1 : at + 2]
    latent = jnp.concatenate(pieces, axis=1) * lax.rsqrt(squares / depth + epsilon)

    def normed(values, gain):
        mean_square = jnp.mean(values * values, axis=-1, keepdims=True)
        return (values * lax.rsqrt(mean_square + epsilon) * gain).astype(jnp.bfloat16)

    query_ref[...] = normed(latent[:, :QL], q_gain_ref[...])
    cache_ref[:, :KVL] = normed(latent[:, QL : QL + KVL], kv_gain_ref[...])
    half = ROPE // 2
    key = latent[:, QL + KVL :]
    turned = jnp.concatenate([key[:, half:], key[:, :half]], axis=1)
    cache_ref[:, KVL:] = (key * cosine_ref[...] + turned * sine_ref[...]).astype(jnp.bfloat16)


def on_device(hidden, attn_gain, q_gain, kv_gain, down_weight):
    row_count, width = hidden.shape
    ep, section, fsdp = lax.axis_size("ep"), lax.axis_size("section"), lax.axis_size("fsdp")
    assert ep == 4
    ep_index, section_index = lax.axis_index("ep"), lax.axis_index("section")
    fsdp_index = lax.axis_index("fsdp")
    quarter = row_count // ep
    rows = row_count // ROW_CHUNKS
    weight = down_weight.T
    columns = weight.shape[0]
    shared = fsdp == 2 and section == 4

    if shared:
        far = far_weight(weight, width)
    own = [hidden[i * rows : (i + 1) * rows] for i in range(ROW_CHUNKS)]
    up, down = [(0, 1), (1, 2), (2, 3)], [(3, 2), (2, 1), (1, 0)]
    rising = [lax.ppermute(block, "ep", up) for block in own]
    falling = [lax.ppermute(block, "ep", down) for block in own]
    rising_far = [lax.ppermute(block, "ep", up[1:]) for block in rising]
    falling_far = [lax.ppermute(block, "ep", down[1:]) for block in falling]
    if shared:
        pieces = other_weight(weight, width)
    else:
        weight = lax.all_gather(weight, "fsdp", axis=1, tiled=True)
        pieces = []
        block = lax.dynamic_slice(weight, (0, (3 - ep_index) * width), (columns, width))
        far = [lax.ppermute(block, "ep", [(0, 1), (3, 2)])]
    gain = attn_gain.reshape(1, -1)
    flat_pieces = [array for piece in pieces for array in piece]

    def place(block, valid):
        local = (block // 2 == fsdp_index) if shared else True
        inside = block % 2 if shared else block
        flips = [section_index ^ (2 * (block % 2) + half) for half in range(2)]
        fields = [valid, block, local, inside] + flips
        return [jnp.asarray(field).astype(jnp.int32) for field in fields]

    wheres = []
    for offset in (0, -1, 1):
        block = ep_index + offset
        wheres.append(jnp.stack(place(jnp.clip(block, 0, 3), (block >= 0) & (block < 4))))
    limits = pltpu.CompilerParams(vmem_limit_bytes=VMEM_LIMIT)
    total, squares = pl.pallas_call(
        functools.partial(near_kernel, 3, ROW_CHUNKS, len(pieces)),
        out_shape=(
            jax.ShapeDtypeStruct((row_count, columns), jnp.float32),
            jax.ShapeDtypeStruct((row_count, 1), jnp.float32),
        ),
        in_specs=[smem]
        + [anywhere] * (3 * ROW_CHUNKS)
        + [vmem]
        + [anywhere] * (1 + len(flat_pieces)),
        out_specs=(vmem, vmem),
        scratch_shapes=[
            pltpu.VMEM((3, row_count, width), jnp.bfloat16),
            pltpu.VMEM((3, columns, width), jnp.bfloat16),
            pltpu.SemaphoreType.DMA((3, ROW_CHUNKS)),
            pltpu.SemaphoreType.DMA((3, 4)),
        ],
        compiler_params=limits,
        cost_estimate=pl.CostEstimate(
            flops=6 * row_count * width * columns,
            bytes_accessed=6 * width * (row_count + columns),
            transcendentals=0,
        ),
    )(jnp.stack(wheres, axis=1), *own, *rising, *falling, gain, weight, *flat_pieces)

    far_block = ep_index ^ 2
    inner = ((ep_index == 1) | (ep_index == 2)).astype(jnp.int32)
    fields = place(far_block, (ep_index < 2)) + [inner, section_index]
    turns = jnp.stack([ep_index ^ turn for turn in range(4)])
    where = jnp.concatenate([jnp.stack([jnp.broadcast_to(f, (4,)) for f in fields]), turns[None]])
    main = columns // LANES * LANES
    message = jax.ShapeDtypeStruct((quarter, 2 * main + LANES), jnp.bfloat16)
    messages = pl.pallas_call(
        functools.partial(far_kernel, ROW_CHUNKS, len(pieces), len(far)),
        out_shape=(message,) * 4,
        in_specs=[smem]
        + [anywhere] * (2 * ROW_CHUNKS)
        + [vmem] * 3
        + [anywhere] * (1 + len(flat_pieces) + len(far)),
        out_specs=(vmem,) * 4,
        scratch_shapes=[
            pltpu.VMEM((row_count, columns), jnp.float32),
            pltpu.VMEM((row_count, columns), jnp.float32),
            pltpu.VMEM((row_count, 1), jnp.float32),
            pltpu.VMEM((row_count, width), jnp.bfloat16),
            pltpu.VMEM((columns, width), jnp.bfloat16),
            pltpu.VMEM((columns, width), jnp.bfloat16),
            pltpu.SemaphoreType.DMA((ROW_CHUNKS,)),
            pltpu.SemaphoreType.DMA((4,)),
            pltpu.SemaphoreType.DMA((4,)),
        ],
        compiler_params=limits,
        cost_estimate=pl.CostEstimate(
            flops=4 * row_count * width * columns,
            bytes_accessed=2 * width * (row_count + 2 * columns),
            transcendentals=0,
        ),
    )(
        where,
        *rising_far,
        *falling_far,
        gain,
        total,
        squares,
        weight,
        *flat_pieces,
        *far,
    )
    received = []
    for turn in range(4):
        moves = [
            (s * 4 + z, (s + 1) % section * 4 + (z ^ turn)) for s in range(section) for z in range(4)
        ]
        received.append(lax.ppermute(messages[turn], ("section", "ep"), moves))

    half = ROPE // 2
    position = (fsdp_index * row_count + ep_index * quarter + jnp.arange(quarter)) % LENGTH
    frequency = rope_base ** (-(jnp.arange(half).astype(jnp.float32) / half))
    angle = position.astype(jnp.float32)[:, None] * frequency[None, :]
    cosine, sine = jnp.cos(angle), jnp.sin(angle)
    return pl.pallas_call(
        functools.partial(finish_kernel, ep * width, columns),
        out_shape=(
            jax.ShapeDtypeStruct((quarter, QL), jnp.bfloat16),
            jax.ShapeDtypeStruct((quarter, KVL + ROPE), jnp.bfloat16),
        ),
        in_specs=[smem] + [vmem] * 8,
        out_specs=(vmem, vmem),
        scratch_shapes=[pltpu.VMEM((4, quarter, 2 * main + LANES), jnp.float32)],
        compiler_params=limits,
    )(
        turns,
        *received,
        q_gain.reshape(1, -1),
        kv_gain.reshape(1, -1),
        jnp.concatenate([cosine, cosine], axis=1),
        jnp.concatenate([-sine, sine], axis=1),
    )


def solution(mesh):
    placed = (P(("section", "fsdp"), "ep"), P(), P(), P(), P("fsdp", "ep"))
    return jax.shard_map(
        on_device,
        mesh=mesh,
        in_specs=placed,
        out_specs=(P(("section", "fsdp", "ep"), None), P(("section", "fsdp", "ep"), None)),
        check_vma=False,
    )
```

time: 220 us -> 132 us (0.60)
  waiting for transfers between devices: 187 us -> 63.4 us
  starting transfers between devices: 4.67 us -> 44.8 us
  between operations: 14.1 us -> 0.94 us
  Pallas kernels: 0 us -> 10.9 us
  matrix products: 8.15 us -> 0 us
  local copies, waits for them, and re-layouts: 3.09 us -> 8.88 us
    all_gather x2 -> x0, waiting for transfers between devices: 125 us -> none  [the longest x1 75.8 us: on_device(): sender = lax.all_gather(hidden, 'ep', axis=1, tiled=True)]
    ppermute x1 -> x25, starting transfers between devices: 0.01 us -> 44.8 us  [the longest x2 16.4 us: on_device(): rising = [lax.ppermute(block, 'ep', up) for block in own]]
    ppermute x1 -> x25, waiting for transfers between devices: 42.5 us -> 63.4 us  [the longest x2 31.7 us: on_device(): falling_far = [lax.ppermute(block, 'ep', down[1:]) for block in falling]]
    all_to_all x1 -> x0, waiting for transfers between devices: 17.3 us -> none  [on_device(): lax.all_to_all(partial_latent, 'ep', split_axis=0, concat_axis=1, tiled=T...]
    pallas_call x0 -> x3, Pallas kernels: none -> 10.9 us  [the longest x1 5.7 us: on_device(): pl.pallas_call(functools.partial(near_kernel, 3, ROW_CHUNKS, len(pieces))...]
    dot_general x1 -> x0, matrix products: 8.15 us -> none  [on_device(): jnp.dot(normed, lax.all_gather(down_weight, 'fsdp', axis=0, tiled=True),...]
    all_to_all x1 -> x0, starting transfers between devices: 4.59 us -> none  [on_device(): lax.all_to_all(partial_latent, 'ep', split_axis=0, concat_axis=1, tiled=T...]
    dynamic_slice x0 -> x3, local copies, waits for them, and re-layouts: none -> 3.21 us  [the longest x2 2.13 us: other_weight(): lax.dynamic_slice(weight, (low, section_index * quarter), (high - low, qu...]
  transfers between devices with their start and end apart: 4 -> 25, of which waited for: 4 -> 9; matrix products, arithmetic and copies ran while one was open for 0% -> 4% of each run, Pallas kernels for 0% -> 4%
where the time goes in v3:
time: 132 us; the launch traced here: 130 us
  waiting for transfers between devices  63.4 us (48%)
  starting transfers between devices  44.8 us (34%)
  Pallas kernels  10.9 us (8%)
  local copies, waits for them, and re-layouts  8.88 us (7%)
  other arithmetic  1.46 us (1%)
    ppermute x2, waiting for transfers between devices, on_device(): falling_far = [lax.ppermute(block, 'ep', down[1:]) for block in falling]  31.7 us
    ppermute x2, starting transfers between devices, on_device(): rising = [lax.ppermute(block, 'ep', up) for block in own]  16.4 us
    ppermute x4, waiting for transfers between devices, on_device(): received.append(lax.ppermute(messages[turn], ('section', 'ep'), moves))  11.8 us
    ppermute x2, waiting for transfers between devices, on_device(): falling = [lax.ppermute(block, 'ep', down) for block in own]  11.2 us
    ppermute x4, starting transfers between devices, on_device(): received.append(lax.ppermute(messages[turn], ('section', 'ep'), moves))  5.98 us
    ppermute x2, starting transfers between devices, other_weight(): own = lax.ppermute(own, 'fsdp', [(0, 1), (1, 0)])  5.94 us
    pallas_call x1, Pallas kernels, on_device(): pl.pallas_call(functools.partial(near_kernel, 3, ROW_CHUNKS, len(pieces))...  5.7 us
    ppermute x2, waiting for transfers between devices, on_device(): rising = [lax.ppermute(block, 'ep', up) for block in own]  4.81 us
  transfers between devices with their start and end apart: 25, of which 9 were waited for; matrix products, arithmetic and copies ran while one was open for 4% of the time, Pallas kernels for 4%

profile of v3, /device:TPU:0, one launch (start us, length us, event | category | flops | bytes accessed | tf_op | source)
XLA Modules:
  0.0 130.4 jit_solution(16885001418987399410)
XLA Ops:
  0.6 1.1 dynamic-slice_bitcast_fusion
  1.7 0.7 collective-permute-start.16
  2.4 1.1 dynamic-slice_bitcast_fusion.1
  3.5 5.9 %collective-permute-start.8 = (bf16[272,896]{1,0:T(8,128)(2,1)S(1)}, bf16[272,896]{1,0:T(8,128)(2,1)S(1)}, u32[]{:S(2)}, u32[]{:S(2)}) collective-permute-start(bf16[272,896]{1,0:T(8,128)(2,1)S(1)} %dynamic-slice_bitcast_fusion.1), channel_id=1, source_target_pairs={{0,4},{4,0},{1,5},{5,1},{2,6},{6,2},{3,7},{7,3},{8,12},{12,8},{9,1... | collective-permute-start | bytes 1462280 | tf_op jit(solution)/shard_map/ppermute | solution.py:59
  9.4 1.1 dynamic-slice_bitcast_fusion.2
  10.4 0.1 collective-permute-start.9
  10.5 1.5 %collective-permute-start.17 = (bf16[144,1792]{1,0:T(8,128)(2,1)S(1)}, bf16[144,1792]{1,0:T(8,128)(2,1)}, u32[]{:S(2)}, u32[]{:S(2)}) collective-permute-start(bf16[144,1792]{1,0:T(8,128)(2,1)S(1)} %collective-permute-done.16), channel_id=1, source_target_pairs={{5,1},{2,6},{13,9},{10,14},{21,17},{18,22},{29,25},{26,30}} | collective-permute-start | bytes 1548296 | tf_op jit(solution)/shard_map/ppermute | solution.py:41
  12.0 1.2 fusion.3
  13.2 2.1 %collective-permute-start = (bf16[128,1792]{1,0:T(8,128)(2,1)S(1)}, bf16[128,1792]{1,0:T(8,128)(2,1)}, u32[]{:S(2)}, u32[]{:S(2)}) collective-permute-start(bf16[128,1792]{1,0:T(8,128)(2,1)S(1)} %get-tuple-element.15.refs_0_), channel_id=1, source_target_pairs={{0,1},{1,2},{2,3},{4,5},{5,6},{6,7},{8,9},{9,10},{10,11},{12,13},{... | collective-permute-start | bytes 1376264 | tf_op jit(solution)/shard_map/ppermute | solution.py:269
  15.3 14.4 %collective-permute-start.2 = (bf16[128,1792]{1,0:T(8,128)(2,1)S(1)}, bf16[128,1792]{1,0:T(8,128)(2,1)}, u32[]{:S(2)}, u32[]{:S(2)}) collective-permute-start(bf16[128,1792]{1,0:T(8,128)(2,1)S(1)} %get-tuple-element.14.refs_1_), channel_id=1, source_target_pairs={{0,1},{1,2},{2,3},{4,5},{5,6},{6,7},{8,9},{9,10},{10,11},{12,13},{... | collective-permute-start | bytes 1376264 | tf_op jit(solution)/shard_map/ppermute | solution.py:269
  29.6 0.4 collective-permute-done.9.refs_9_
  30.0 1.3 collective-permute-start.4
  31.3 0.0 collective-permute-done.refs_2_
  31.3 1.3 collective-permute-start.6
  32.6 4.8 %collective-permute-done.2.refs_3_ = bf16[128,1792]{1,0:T(8,128)(2,1)} collective-permute-done((bf16[128,1792]{1,0:T(8,128)(2,1)S(1)}, bf16[128,1792]{1,0:T(8,128)(2,1)}, u32[]{:S(2)}, u32[]{:S(2)}) %collective-permute-start.2) | collective-permute-done | bytes 458784 | tf_op jit(solution)/shard_map/ppermute | solution.py:269
  37.4 1.5 %collective-permute-start.13 = (bf16[256,896]{1,0:T(8,128)(2,1)S(1)}, bf16[256,896]{1,0:T(8,128)(2,1)S(1)}, u32[]{:S(2)}, u32[]{:S(2)}) collective-permute-start(bf16[256,896]{1,0:T(8,128)(2,1)S(1)} %collective-permute-done.9.refs_9_), channel_id=1, source_target_pairs={{0,16},{8,24},{16,0},{24,8},{1,17},{9,25},{17,1},{25,9},{2,18},{10... | collective-permute-start | bytes 1376264 | tf_op jit(solution)/shard_map/ppermute | solution.py:29
  38.9 0.0 collective-permute-done.8.refs_8_
  38.9 0.0 collective-permute-start.11
  38.9 0.0 collective-permute-done.17
  39.0 0.6 collective-permute-start.12
  39.6 0.9 broadcast_select_fusion.refs_16_
  40.5 4.9 %collective-permute-done.4.refs_4_ = bf16[128,1792]{1,0:T(8,128)(2,1)S(1)} collective-permute-done((bf16[128,1792]{1,0:T(8,128)(2,1)S(1)}, bf16[128,1792]{1,0:T(8,128)(2,1)S(1)}, u32[]{:S(2)}, u32[]{:S(2)}) %collective-permute-start.4) | collective-permute-done | bytes 458784 | tf_op jit(solution)/shard_map/ppermute | solution.py:270
  45.4 1.5 %collective-permute-start.19 = (bf16[144,1792]{1,0:T(8,128)(2,1)}, bf16[144,1792]{1,0:T(8,128)(2,1)}, u32[]{:S(2)}, u32[]{:S(2)}) collective-permute-start(bf16[144,1792]{1,0:T(8,128)(2,1)} %broadcast_select_fusion.refs_16_), channel_id=1, source_target_pairs={{1,17},{2,18},{9,25},{10,26},{17,1},{18,2},{25,9},{26,10},{5,21},{... | collective-permute-start | bytes 1548296 | tf_op jit(solution)/shard_map/ppermute | solution.py:29
  46.8 6.3 %collective-permute-done.6.refs_5_ = bf16[128,1792]{1,0:T(8,128)(2,1)S(1)} collective-permute-done((bf16[128,1792]{1,0:T(8,128)(2,1)S(1)}, bf16[128,1792]{1,0:T(8,128)(2,1)S(1)}, u32[]{:S(2)}, u32[]{:S(2)}) %collective-permute-start.6) | collective-permute-done | bytes 458784 | tf_op jit(solution)/shard_map/ppermute | solution.py:270
  53.1 1.4 %collective-permute-start.1 = (bf16[128,1792]{1,0:T(8,128)(2,1)}, bf16[128,1792]{1,0:T(8,128)(2,1)}, u32[]{:S(2)}, u32[]{:S(2)}) collective-permute-start(bf16[128,1792]{1,0:T(8,128)(2,1)} %collective-permute-done.refs_2_), channel_id=1, source_target_pairs={{1,2},{2,3},{5,6},{6,7},{9,10},{10,11},{13,14},{14,15},{17,18},{18... | collective-permute-start | bytes 1376264 | tf_op jit(solution)/shard_map/ppermute | solution.py:271
  54.6 0.0 collective-permute-done.13.refs_13_
  54.6 0.0 collective-permute-start.10
  54.6 3.5 %collective-permute-done.12.refs_12_ = bf16[272,896]{1,0:T(8,128)(2,1)S(1)} collective-permute-done((bf16[272,896]{1,0:T(8,128)(2,1)S(1)}, bf16[272,896]{1,0:T(8,128)(2,1)S(1)}, u32[]{:S(2)}, u32[]{:S(2)}) %collective-permute-start.12) | collective-permute-done | bytes 487456 | tf_op jit(solution)/shard_map/ppermute | solution.py:29
  58.1 0.0 collective-permute-start.14
  58.1 0.0 collective-permute-done.11.refs_11_
  58.1 0.8 copy-done
  58.9 0.5 collective-permute-start.15
  59.4 0.1 stack.131
  59.5 0.1 copy.16
  59.6 0.1 stack.141
  59.7 0.1 copy.17
  59.7 0.1 stack.121
  59.8 0.1 copy.15
  59.9 0.1 pad_add_fusion.where
  60.0 0.0 collective-permute-done.1.refs_0_
  60.0 1.5 %collective-permute-start.18 = (bf16[144,1792]{1,0:T(8,128)(2,1)}, bf16[144,1792]{1,0:T(8,128)(2,1)}, u32[]{:S(2)}, u32[]{:S(2)}) collective-permute-start(bf16[144,1792]{1,0:T(8,128)(2,1)} %broadcast_select_fusion.refs_16_), channel_id=1, source_target_pairs={{1,9},{2,10},{9,1},{10,2},{17,25},{18,26},{25,17},{26,18},{5,13},{... | collective-permute-start | bytes 1548296 | tf_op jit(solution)/shard_map/ppermute | solution.py:30
  61.5 1.5 %collective-permute-start.20 = (bf16[144,1792]{1,0:T(8,128)(2,1)}, bf16[144,1792]{1,0:T(8,128)(2,1)}, u32[]{:S(2)}, u32[]{:S(2)}) collective-permute-start(bf16[144,1792]{1,0:T(8,128)(2,1)} %collective-permute-done.19.refs_18_), channel_id=1, source_target_pairs={{1,9},{2,10},{9,1},{10,2},{17,25},{18,26},{25,17},{26,18},{5,13},{... | collective-permute-start | bytes 1548296 | tf_op jit(solution)/shard_map/ppermute | solution.py:31
  63.0 0.1 fusion.4
  63.2 0.7 collective-permute-start.3
  63.9 1.3 collective-permute-start.5
  65.2 1.3 collective-permute-start.7
  66.5 0.2 fusion
  66.7 1.0 copy-done.1
  67.7 1.0 copy-done.4
  68.8 1.0 copy-done.6
  69.8 5.7 %shard_map.68 = (f32[256,528]{1,0:T(8,128)}, f32[256,1]{1,0:T(8,128)S(1)}) custom-call(s32[6,3]{1,0:T(8,128)S(1)} %pad_add_fusion.where, bf16[128,1792]{1,0:T(8,128)(2,1)S(1)} %get-tuple-element.15.refs_0_, bf16[128,1792]{1,0:T(8,128)(2,1)S(1)} %get-tuple-element.14.refs_1_, bf16[128,1792]{1,0:T(8,128)(2,1)} %collective-permute-done.refs_2_, ...), custom_call_target="tpu_custom_call" | custom-call | flops 1453326336 | bytes 8429568 | tf_op jit(solution)/shard_map/pallas_call | solution.py:295
  75.5 22.3 %collective-permute-done.5.refs_2_ = bf16[128,1792]{1,0:T(8,128)(2,1)S(1)} collective-permute-done((bf16[128,1792]{1,0:T(8,128)(2,1)}, bf16[128,1792]{1,0:T(8,128)(2,1)S(1)}, u32[]{:S(2)}, u32[]{:S(2)}) %collective-permute-start.5) | collective-permute-done | bytes 458784 | tf_op jit(solution)/shard_map/ppermute | solution.py:272
  97.8 9.4 %collective-permute-done.7.refs_3_ = bf16[128,1792]{1,0:T(8,128)(2,1)S(1)} collective-permute-done((bf16[128,1792]{1,0:T(8,128)(2,1)}, bf16[128,1792]{1,0:T(8,128)(2,1)S(1)}, u32[]{:S(2)}, u32[]{:S(2)}) %collective-permute-start.7) | collective-permute-done | bytes 458784 | tf_op jit(solution)/shard_map/ppermute | solution.py:272
  107.2 0.0 copy-start.9
  107.3 0.0 copy-start.8
  107.3 3.5 %shard_map.69 = (bf16[64,1152]{1,0:T(8,128)(2,1)S(1)}, bf16[64,1152]{1,0:T(8,128)(2,1)S(1)}, bf16[64,1152]{1,0:T(8,128)(2,1)S(1)}, bf16[64,1152]{1,0:T(8,128)(2,1)S(1)}) custom-call(s32[9,4]{1,0:T(8,128)S(1)} %concatenate.9.where, bf16[128,1792]{1,0:T(8,128)(2,1)} %collective-permute-done.1.refs_0_, bf16[128,1792]{1,0:T(8,128)(2,1)S(1)} %collective-permute-done.3.refs_1_, ...), custom_call_target="tpu_custom_call" | custom-call | flops 968884224 | bytes 4702208 | tf_op jit(solution)/shard_map/pallas_call | solution.py:327
  110.8 0.1 collective-permute-start.21
  110.9 4.0 %collective-permute-start.22 = (bf16[64,1152]{1,0:T(8,128)(2,1)S(1)}, bf16[64,1152]{1,0:T(8,128)(2,1)S(1)}, u32[]{:S(2)}, u32[]{:S(2)}) collective-permute-start(bf16[64,1152]{1,0:T(8,128)(2,1)S(1)} %get-tuple-element.11), channel_id=1, source_target_pairs={{0,9},{1,8},{2,11},{3,10},{8,17},{9,16},{10,19},{11,18},{16,25},{1... | collective-permute-start | bytes 442376 | tf_op jit(solution)/shard_map/ppermute | solution.py:368
  114.9 1.9 %collective-permute-start.24 = (bf16[64,1152]{1,0:T(8,128)(2,1)S(1)}, bf16[64,1152]{1,0:T(8,128)(2,1)S(1)}, u32[]{:S(2)}, u32[]{:S(2)}) collective-permute-start(bf16[64,1152]{1,0:T(8,128)(2,1)S(1)} %get-tuple-element.13), channel_id=1, source_target_pairs={{0,11},{1,10},{2,9},{3,8},{8,19},{9,18},{10,17},{11,16},{16,27},{1... | collective-permute-start | bytes 442376 | tf_op jit(solution)/shard_map/ppermute | solution.py:368
  116.8 0.1 pad_add_fusion.1.where
  116.9 0.1 pad_maximum_fusion
  117.0 2.4 %collective-permute-done.22.refs_1_ = bf16[64,1152]{1,0:T(8,128)(2,1)S(1)} collective-permute-done((bf16[64,1152]{1,0:T(8,128)(2,1)S(1)}, bf16[64,1152]{1,0:T(8,128)(2,1)S(1)}, u32[]{:S(2)}, u32[]{:S(2)}) %collective-permute-start.22) | collective-permute-done | bytes 147488 | tf_op jit(solution)/shard_map/ppermute | solution.py:368
  119.3 9.4 %collective-permute-done.23.refs_2_ = bf16[64,1152]{1,0:T(8,128)(2,1)S(1)} collective-permute-done((bf16[64,1152]{1,0:T(8,128)(2,1)S(1)}, bf16[64,1152]{1,0:T(8,128)(2,1)S(1)}, u32[]{:S(2)}, u32[]{:S(2)}) %collective-permute-start.23) | collective-permute-done | bytes 147488 | tf_op jit(solution)/shard_map/ppermute | solution.py:368
  128.7 1.7 %shard_map.70 = (bf16[64,1536]{1,0:T(8,128)(2,1)}, bf16[64,576]{1,0:T(8,128)(2,1)}) custom-call(s32[4]{0:T(128)S(1)} %pad_add_fusion.1.where, bf16[64,1152]{1,0:T(8,128)(2,1)S(1)} %collective-permute-done.21.refs_0_, bf16[64,1152]{1,0:T(8,128)(2,1)S(1)} %collective-permute-done.22.refs_1_, bf16[64,1152]{1,0:T(8,128)(2,1)S(1)} %collective-permute-done.23.refs_2_, ...), custom_call_target="tpu_custom_call" | custom-call | tf_op jit(solution)/shard_map/pallas_call | solution.py:375
  (37 shorter events, 0.1 us)
Async XLA Ops:
  0.6 66.1 %copy-start.7 = (f32[7168]{0:T(1024)S(1)}, f32[7168]{0:T(1024)}, u32[]{:S(2)}) copy-start(f32[7168]{0:T(1024)} %param.6) | copy-start | bytes 86020
  1.7 8.8 %collective-permute-start.16 = (bf16[144,1792]{1,0:T(8,128)(2,1)S(1)}, bf16[144,1792]{1,0:T(8,128)(2,1)S(1)}, u32[]{:S(2)}, u32[]{:S(2)}) collective-permute-start(bf16[144,1792]{1,0:T(8,128)(2,1)S(1)} %dynamic-slice_bitcast_fusion), channel_id=1, source_target_pairs={{4,5},{3,2},{12,13},{11,10},{20,21},{19,18},{28,29},{27,26}} | collective-permute-start | bytes 1548296 | tf_op jit(solution)/shard_map/ppermute | solution.py:40
  3.5 35.4 %collective-permute-start.8 = (bf16[272,896]{1,0:T(8,128)(2,1)S(1)}, bf16[272,896]{1,0:T(8,128)(2,1)S(1)}, u32[]{:S(2)}, u32[]{:S(2)}) collective-permute-start(bf16[272,896]{1,0:T(8,128)(2,1)S(1)} %dynamic-slice_bitcast_fusion.1), channel_id=1, source_target_pairs={{0,4},{4,0},{1,5},{5,1},{2,6},{6,2},{3,7},{7,3},{8,12},{12,8},{9,1... | collective-permute-start | bytes 1462280 | tf_op jit(solution)/shard_map/ppermute | solution.py:59
  10.4 19.6 %collective-permute-start.9 = (bf16[256,896]{1,0:T(8,128)(2,1)S(1)}, bf16[256,896]{1,0:T(8,128)(2,1)S(1)}, u32[]{:S(2)}, u32[]{:S(2)}) collective-permute-start(bf16[256,896]{1,0:T(8,128)(2,1)S(1)} %dynamic-slice_bitcast_fusion.2), channel_id=1, source_target_pairs={{0,4},{4,0},{1,5},{5,1},{2,6},{6,2},{3,7},{7,3},{8,12},{12,8},{9,1... | collective-permute-start | bytes 1376264 | tf_op jit(solution)/shard_map/ppermute | solution.py:59
  10.5 28.4 %collective-permute-start.17 = (bf16[144,1792]{1,0:T(8,128)(2,1)S(1)}, bf16[144,1792]{1,0:T(8,128)(2,1)}, u32[]{:S(2)}, u32[]{:S(2)}) collective-permute-start(bf16[144,1792]{1,0:T(8,128)(2,1)S(1)} %collective-permute-done.16), channel_id=1, source_target_pairs={{5,1},{2,6},{13,9},{10,14},{21,17},{18,22},{29,25},{26,30}} | collective-permute-start | bytes 1548296 | tf_op jit(solution)/shard_map/ppermute | solution.py:41
  13.2 18.1 %collective-permute-start = (bf16[128,1792]{1,0:T(8,128)(2,1)S(1)}, bf16[128,1792]{1,0:T(8,128)(2,1)}, u32[]{:S(2)}, u32[]{:S(2)}) collective-permute-start(bf16[128,1792]{1,0:T(8,128)(2,1)S(1)} %get-tuple-element.15.refs_0_), channel_id=1, source_target_pairs={{0,1},{1,2},{2,3},{4,5},{5,6},{6,7},{8,9},{9,10},{10,11},{12,13},{... | collective-permute-start | bytes 1376264 | tf_op jit(solution)/shard_map/ppermute | solution.py:269
  15.3 22.2 %collective-permute-start.2 = (bf16[128,1792]{1,0:T(8,128)(2,1)S(1)}, bf16[128,1792]{1,0:T(8,128)(2,1)}, u32[]{:S(2)}, u32[]{:S(2)}) collective-permute-start(bf16[128,1792]{1,0:T(8,128)(2,1)S(1)} %get-tuple-element.14.refs_1_), channel_id=1, source_target_pairs={{0,1},{1,2},{2,3},{4,5},{5,6},{6,7},{8,9},{9,10},{10,11},{12,13},{... | collective-permute-start | bytes 1376264 | tf_op jit(solution)/shard_map/ppermute | solution.py:269
  30.0 15.3 %collective-permute-start.4 = (bf16[128,1792]{1,0:T(8,128)(2,1)S(1)}, bf16[128,1792]{1,0:T(8,128)(2,1)S(1)}, u32[]{:S(2)}, u32[]{:S(2)}) collective-permute-start(bf16[128,1792]{1,0:T(8,128)(2,1)S(1)} %get-tuple-element.15.refs_0_), channel_id=1, source_target_pairs={{3,2},{2,1},{1,0},{7,6},{6,5},{5,4},{11,10},{10,9},{9,8},{15,14},{... | collective-permute-start | bytes 1376264 | tf_op jit(solution)/shard_map/ppermute | solution.py:270
  31.3 21.8 %collective-permute-start.6 = (bf16[128,1792]{1,0:T(8,128)(2,1)S(1)}, bf16[128,1792]{1,0:T(8,128)(2,1)S(1)}, u32[]{:S(2)}, u32[]{:S(2)}) collective-permute-start(bf16[128,1792]{1,0:T(8,128)(2,1)S(1)} %get-tuple-element.14.refs_1_), channel_id=1, source_target_pairs={{3,2},{2,1},{1,0},{7,6},{6,5},{5,4},{11,10},{10,9},{9,8},{15,14},{... | collective-permute-start | bytes 1376264 | tf_op jit(solution)/shard_map/ppermute | solution.py:270
  37.4 17.1 %collective-permute-start.13 = (bf16[256,896]{1,0:T(8,128)(2,1)S(1)}, bf16[256,896]{1,0:T(8,128)(2,1)S(1)}, u32[]{:S(2)}, u32[]{:S(2)}) collective-permute-start(bf16[256,896]{1,0:T(8,128)(2,1)S(1)} %collective-permute-done.9.refs_9_), channel_id=1, source_target_pairs={{0,16},{8,24},{16,0},{24,8},{1,17},{9,25},{17,1},{25,9},{2,18},{10... | collective-permute-start | bytes 1376264 | tf_op jit(solution)/shard_map/ppermute | solution.py:29
  38.9 19.1 %collective-permute-start.11 = (bf16[256,896]{1,0:T(8,128)(2,1)S(1)}, bf16[256,896]{1,0:T(8,128)(2,1)S(1)}, u32[]{:S(2)}, u32[]{:S(2)}) collective-permute-start(bf16[256,896]{1,0:T(8,128)(2,1)S(1)} %collective-permute-done.9.refs_9_), channel_id=1, source_target_pairs={{0,8},{8,0},{16,24},{24,16},{1,9},{9,1},{17,25},{25,17},{2,10},{10... | collective-permute-start | bytes 1376264 | tf_op jit(solution)/shard_map/ppermute | solution.py:30
  39.0 19.1 %collective-permute-start.12 = (bf16[272,896]{1,0:T(8,128)(2,1)S(1)}, bf16[272,896]{1,0:T(8,128)(2,1)S(1)}, u32[]{:S(2)}, u32[]{:S(2)}) collective-permute-start(bf16[272,896]{1,0:T(8,128)(2,1)S(1)} %collective-permute-done.8.refs_8_), channel_id=1, source_target_pairs={{0,16},{8,24},{16,0},{24,8},{1,17},{9,25},{17,1},{25,9},{2,18},{10... | collective-permute-start | bytes 1462280 | tf_op jit(solution)/shard_map/ppermute | solution.py:29
  45.4 12.7 %copy-start.3 = (bf16[128,1792]{1,0:T(8,128)(2,1)}, bf16[128,1792]{1,0:T(8,128)(2,1)S(1)}, u32[]{:S(2)}) copy-start(bf16[128,1792]{1,0:T(8,128)(2,1)S(1)} %collective-permute-done.4.refs_4_) | copy-start | bytes 1376260
  45.4 16.1 %collective-permute-start.19 = (bf16[144,1792]{1,0:T(8,128)(2,1)}, bf16[144,1792]{1,0:T(8,128)(2,1)}, u32[]{:S(2)}, u32[]{:S(2)}) collective-permute-start(bf16[144,1792]{1,0:T(8,128)(2,1)} %broadcast_select_fusion.refs_16_), channel_id=1, source_target_pairs={{1,17},{2,18},{9,25},{10,26},{17,1},{18,2},{25,9},{26,10},{5,21},{... | collective-permute-start | bytes 1548296 | tf_op jit(solution)/shard_map/ppermute | solution.py:29
  53.1 5.0 %copy-start.5 = (bf16[128,1792]{1,0:T(8,128)(2,1)}, bf16[128,1792]{1,0:T(8,128)(2,1)S(1)}, u32[]{:S(2)}) copy-start(bf16[128,1792]{1,0:T(8,128)(2,1)S(1)} %collective-permute-done.6.refs_5_) | copy-start | bytes 1376260
  53.1 6.9 %collective-permute-start.1 = (bf16[128,1792]{1,0:T(8,128)(2,1)}, bf16[128,1792]{1,0:T(8,128)(2,1)}, u32[]{:S(2)}, u32[]{:S(2)}) collective-permute-start(bf16[128,1792]{1,0:T(8,128)(2,1)} %collective-permute-done.refs_2_), channel_id=1, source_target_pairs={{1,2},{2,3},{5,6},{6,7},{9,10},{10,11},{13,14},{14,15},{17,18},{18... | collective-permute-start | bytes 1376264 | tf_op jit(solution)/shard_map/ppermute | solution.py:271
  54.6 8.6 %collective-permute-start.10 = (bf16[272,896]{1,0:T(8,128)(2,1)S(1)}, bf16[272,896]{1,0:T(8,128)(2,1)S(1)}, u32[]{:S(2)}, u32[]{:S(2)}) collective-permute-start(bf16[272,896]{1,0:T(8,128)(2,1)S(1)} %collective-permute-done.8.refs_8_), channel_id=1, source_target_pairs={{0,8},{8,0},{16,24},{24,16},{1,9},{9,1},{17,25},{25,17},{2,10},{10... | collective-permute-start | bytes 1462280 | tf_op jit(solution)/shard_map/ppermute | solution.py:30
  58.1 7.1 %collective-permute-start.14 = (bf16[272,896]{1,0:T(8,128)(2,1)S(1)}, bf16[272,896]{1,0:T(8,128)(2,1)}, u32[]{:S(2)}, u32[]{:S(2)}) collective-permute-start(bf16[272,896]{1,0:T(8,128)(2,1)S(1)} %collective-permute-done.12.refs_12_), channel_id=1, source_target_pairs={{0,8},{8,0},{16,24},{24,16},{1,9},{9,1},{17,25},{25,17},{2,10},{10... | collective-permute-start | bytes 1462280 | tf_op jit(solution)/shard_map/ppermute | solution.py:31
  58.1 0.8 copy-start
  58.9 5.0 %collective-permute-start.15 = (bf16[256,896]{1,0:T(8,128)(2,1)S(1)}, bf16[256,896]{1,0:T(8,128)(2,1)}, u32[]{:S(2)}, u32[]{:S(2)}) collective-permute-start(bf16[256,896]{1,0:T(8,128)(2,1)S(1)} %collective-permute-done.13.refs_13_), channel_id=1, source_target_pairs={{0,8},{8,0},{16,24},{24,16},{1,9},{9,1},{17,25},{25,17},{2,10},{10... | collective-permute-start | bytes 1376264 | tf_op jit(solution)/shard_map/ppermute | solution.py:31
  60.0 47.2 %collective-permute-start.18 = (bf16[144,1792]{1,0:T(8,128)(2,1)}, bf16[144,1792]{1,0:T(8,128)(2,1)}, u32[]{:S(2)}, u32[]{:S(2)}) collective-permute-start(bf16[144,1792]{1,0:T(8,128)(2,1)} %broadcast_select_fusion.refs_16_), channel_id=1, source_target_pairs={{1,9},{2,10},{9,1},{10,2},{17,25},{18,26},{25,17},{26,18},{5,13},{... | collective-permute-start | bytes 1548296 | tf_op jit(solution)/shard_map/ppermute | solution.py:30
  61.5 45.7 %collective-permute-start.20 = (bf16[144,1792]{1,0:T(8,128)(2,1)}, bf16[144,1792]{1,0:T(8,128)(2,1)}, u32[]{:S(2)}, u32[]{:S(2)}) collective-permute-start(bf16[144,1792]{1,0:T(8,128)(2,1)} %collective-permute-done.19.refs_18_), channel_id=1, source_target_pairs={{1,9},{2,10},{9,1},{10,2},{17,25},{18,26},{25,17},{26,18},{5,13},{... | collective-permute-start | bytes 1548296 | tf_op jit(solution)/shard_map/ppermute | solution.py:31
  63.2 12.3 %collective-permute-start.3 = (bf16[128,1792]{1,0:T(8,128)(2,1)}, bf16[128,1792]{1,0:T(8,128)(2,1)S(1)}, u32[]{:S(2)}, u32[]{:S(2)}) collective-permute-start(bf16[128,1792]{1,0:T(8,128)(2,1)} %collective-permute-done.2.refs_3_), channel_id=1, source_target_pairs={{1,2},{2,3},{5,6},{6,7},{9,10},{10,11},{13,14},{14,15},{17,18},{18... | collective-permute-start | bytes 1376264 | tf_op jit(solution)/shard_map/ppermute | solution.py:271
  63.9 33.9 %collective-permute-start.5 = (bf16[128,1792]{1,0:T(8,128)(2,1)}, bf16[128,1792]{1,0:T(8,128)(2,1)S(1)}, u32[]{:S(2)}, u32[]{:S(2)}) collective-permute-start(bf16[128,1792]{1,0:T(8,128)(2,1)} %copy-done.3), channel_id=1, source_target_pairs={{2,1},{1,0},{6,5},{5,4},{10,9},{9,8},{14,13},{13,12},{18,17},{17,1... | collective-permute-start | bytes 1376264 | tf_op jit(solution)/shard_map/ppermute | solution.py:272
  65.2 42.0 %collective-permute-start.7 = (bf16[128,1792]{1,0:T(8,128)(2,1)}, bf16[128,1792]{1,0:T(8,128)(2,1)S(1)}, u32[]{:S(2)}, u32[]{:S(2)}) collective-permute-start(bf16[128,1792]{1,0:T(8,128)(2,1)} %copy-done.5), channel_id=1, source_target_pairs={{2,1},{1,0},{6,5},{5,4},{10,9},{9,8},{14,13},{13,12},{18,17},{17,1... | collective-permute-start | bytes 1376264 | tf_op jit(solution)/shard_map/ppermute | solution.py:272
  66.7 1.0 copy-start.1
  67.7 1.0 copy-start.4
  68.8 1.0 copy-start.6
  69.8 37.5 %copy-start.2 = (bf16[256,896]{1,0:T(8,128)(2,1)S(1)}, bf16[256,896]{1,0:T(8,128)(2,1)}, u32[]{:S(2)}) copy-start(bf16[256,896]{1,0:T(8,128)(2,1)} %copy-done) | copy-start | bytes 1376260
  107.2 9.6 %copy-start.9 = (f32[1536]{0:T(1024)S(1)}, f32[1536]{0:T(1024)}, u32[]{:S(2)}) copy-start(f32[1536]{0:T(1024)} %param.7) | copy-start | bytes 18436
  107.3 21.5 %copy-start.8 = (f32[512]{0:T(512)S(1)}, f32[512]{0:T(512)}, u32[]{:S(2)}) copy-start(f32[512]{0:T(512)} %param.8) | copy-start | bytes 6148
  110.8 6.2 %collective-permute-start.21 = (bf16[64,1152]{1,0:T(8,128)(2,1)S(1)}, bf16[64,1152]{1,0:T(8,128)(2,1)S(1)}, u32[]{:S(2)}, u32[]{:S(2)}) collective-permute-start(bf16[64,1152]{1,0:T(8,128)(2,1)S(1)} %get-tuple-element.10), channel_id=1, source_target_pairs={{0,8},{1,9},{2,10},{3,11},{8,16},{9,17},{10,18},{11,19},{16,24},{1... | collective-permute-start | bytes 442376 | tf_op jit(solution)/shard_map/ppermute | solution.py:368
  110.9 8.5 %collective-permute-start.22 = (bf16[64,1152]{1,0:T(8,128)(2,1)S(1)}, bf16[64,1152]{1,0:T(8,128)(2,1)S(1)}, u32[]{:S(2)}, u32[]{:S(2)}) collective-permute-start(bf16[64,1152]{1,0:T(8,128)(2,1)S(1)} %get-tuple-element.11), channel_id=1, source_target_pairs={{0,9},{1,8},{2,11},{3,10},{8,17},{9,16},{10,19},{11,18},{16,25},{1... | collective-permute-start | bytes 442376 | tf_op jit(solution)/shard_map/ppermute | solution.py:368
  114.9 13.9 %collective-permute-start.23 = (bf16[64,1152]{1,0:T(8,128)(2,1)S(1)}, bf16[64,1152]{1,0:T(8,128)(2,1)S(1)}, u32[]{:S(2)}, u32[]{:S(2)}) collective-permute-start(bf16[64,1152]{1,0:T(8,128)(2,1)S(1)} %get-tuple-element.12), channel_id=1, source_target_pairs={{0,10},{1,11},{2,8},{3,9},{8,18},{9,19},{10,16},{11,17},{16,26},{1... | collective-permute-start | bytes 442376 | tf_op jit(solution)/shard_map/ppermute | solution.py:368
  114.9 13.9 %collective-permute-start.24 = (bf16[64,1152]{1,0:T(8,128)(2,1)S(1)}, bf16[64,1152]{1,0:T(8,128)(2,1)S(1)}, u32[]{:S(2)}, u32[]{:S(2)}) collective-permute-start(bf16[64,1152]{1,0:T(8,128)(2,1)S(1)} %get-tuple-element.13), channel_id=1, source_target_pairs={{0,11},{1,10},{2,9},{3,8},{8,19},{9,18},{10,17},{11,16},{16,27},{1... | collective-permute-start | bytes 442376 | tf_op jit(solution)/shard_map/ppermute | solution.py:368

commit v4 on v0

v4 whole, which is shorter than its diff:
```python
import functools

import jax
import jax.numpy as jnp
import numpy as np
from jax import lax
from jax.experimental import pallas as pl
from jax.experimental.pallas import tpu as pltpu
from jax.sharding import PartitionSpec as P

QL = 1536
KVL = 512
ROPE = 64
LENGTH = 4096


epsilon = 1e-06
rope_base = 10000.0
CHUNKS = 2
PLANES = 4
NEAR_COST, LAST_COSTS = 15, (8, 2)
VMEM_LIMIT = 20 * 1024 * 1024

vmem = pl.BlockSpec(memory_space=pltpu.VMEM)
smem = pl.BlockSpec(memory_space=pltpu.SMEM)
anywhere = pl.BlockSpec(memory_space=pl.ANY)


def square_sums(values):
    return jnp.sum(values * values, axis=1, keepdims=True)


def product(gained, weight):
    return lax.dot_general(
        gained, weight, (((1,), (1,)), ((), ())), preferred_element_type=jnp.float32
    )


def near_kernel(chunks, sources, where, *refs):
    refs = list(refs)
    block_refs = [[refs.pop(0) for _ in range(chunks)] for _ in range(3)]
    gain_ref = refs.pop(0)
    source_refs = [refs.pop(0) for _ in range(sources)]
    total, squares, last_weight, blocks, weights, block_arrived, weight_arrived = refs
    rows, width = block_refs[0][0].shape

    def weight_copy(entry, act):
        into = weights.at[entry] if entry < 3 else last_weight
        for source, ref in enumerate(source_refs):

            @pl.when(where[1, entry] == source)
            def _():
                at = pl.multiple_of(where[2, entry] * width, width)
                copy = pltpu.make_async_copy(ref.at[:, pl.ds(at, width)], into, weight_arrived.at[entry])
                getattr(copy, act)()

    def block_copies(entry, act):
        for chunk, ref in enumerate(block_refs[entry]):
            into = blocks.at[entry, pl.ds(chunk * rows, rows)]
            copy = pltpu.make_async_copy(ref, into, block_arrived.at[entry, chunk])
            getattr(copy, act)()

    for entry in range(3):
        block_copies(entry, "start")
        weight_copy(entry, "start")
    weight_copy(3, "start")
    for entry in range(3):
        block_copies(entry, "wait")
        values = blocks[entry].astype(jnp.float32)
        at = pl.multiple_of(where[0, entry] * width, width)
        gained = (values * gain_ref[:, pl.ds(at, width)]).astype(jnp.bfloat16)
        weight_copy(entry, "wait")
        if entry == 0:
            squares[...] = square_sums(values)
            total[...] = product(gained, weights[entry])
        else:
            squares[...] += square_sums(values)
            total[...] += product(gained, weights[entry])
    weight_copy(3, "wait")


def last_kernel(first_row, depth, where, *refs):
    refs = list(refs)
    sides = [refs.pop(0) for _ in range(2)]
    gain_ref, weight_ref, total_ref, squares_ref = [refs.pop(0) for _ in range(4)]
    scaled = refs.pop(-1)
    rows, width = sides[0].shape
    values = jnp.where(where[3, 0] == 0, sides[0][...], sides[1][...]).astype(jnp.float32)
    squares = squares_ref[first_row : first_row + rows, :] + square_sums(values)
    at = pl.multiple_of(where[0, 3] * width, width)
    gained = (values * gain_ref[:, pl.ds(at, width)]).astype(jnp.bfloat16)
    total = total_ref[first_row : first_row + rows, :] + product(gained, weight_ref[...])
    scaled[...] = total * lax.rsqrt(squares / depth + epsilon)
    share = refs[0].shape[0]
    for turn, out_ref in enumerate(refs):
        at = pl.multiple_of(where[4, turn] * share, share)
        out_ref[...] = scaled[pl.ds(at, share), :].astype(jnp.bfloat16)


def finish_kernel(where, *refs):
    refs = list(refs)
    part_refs = [refs.pop(0) for _ in range(len(refs) - 7)]
    q_gain_ref, kv_gain_ref, cosine_ref, sine_ref, query_ref, cache_ref, parts = refs
    share = part_refs[0].shape[0]
    for index, ref in enumerate(part_refs):
        chunk, turn = index // PLANES, index % PLANES
        parts[where[4, turn], chunk * share : (chunk + 1) * share] = ref[...].astype(jnp.float32)
    latent = jnp.concatenate([parts[plane] for plane in range(PLANES)], axis=1)

    def normed(values, gain):
        mean_square = jnp.mean(values * values, axis=-1, keepdims=True)
        return (values * lax.rsqrt(mean_square + epsilon) * gain).astype(jnp.bfloat16)

    query_ref[...] = normed(latent[:, :QL], q_gain_ref[...])
    cache_ref[:, :KVL] = normed(latent[:, QL : QL + KVL], kv_gain_ref[...])
    half = ROPE // 2
    key = latent[:, QL + KVL :]
    turned = jnp.concatenate([key[:, half:], key[:, :half]], axis=1)
    cache_ref[:, KVL:] = (key * cosine_ref[...] + turned * sine_ref[...]).astype(jnp.bfloat16)


def tables(fsdp, shared):
    made = np.zeros((2, fsdp, PLANES, 5, PLANES), np.int32)
    per = PLANES // fsdp if shared else PLANES
    for core, y, z in np.ndindex(2, fsdp, PLANES):
        for column, block in enumerate((z, (z - 1) % PLANES, (z + 1) % PLANES, z ^ 2)):
            source, inside = 0, block % per
            if shared and block // per != y:
                source, inside = (1 if inside == core else 2), 0
            made[core, y, z, :4, column] = [block, source, inside, int(z < 2)]
        made[core, y, z, 4] = [z ^ turn for turn in range(PLANES)]
    return made


def on_device(hidden, attn_gain, q_gain, kv_gain, down_weight):
    row_count, width = hidden.shape
    section, fsdp = lax.axis_size("section"), lax.axis_size("fsdp")
    ep_index, fsdp_index = lax.axis_index("ep"), lax.axis_index("fsdp")
    assert lax.axis_size("ep") == PLANES
    quarter = row_count // PLANES
    share = quarter // CHUNKS
    rows = row_count // CHUNKS
    weight = down_weight.T
    columns = weight.shape[0]
    shared = fsdp == 2 and section % 2 == 0
    place = (lax.axis_index("section") % 2, fsdp_index, ep_index, 0, 0)
    where = lax.dynamic_slice(tables(fsdp, shared), place, (1, 1, 1, 5, PLANES)).reshape(5, PLANES)
    gain = attn_gain.reshape(1, -1)

    chunks = hidden.reshape(PLANES, CHUNKS, share, width)
    own = [chunks[:, chunk].reshape(rows, width) for chunk in range(CHUNKS)]
    up = [(z, (z + 1) % PLANES) for z in range(PLANES)]
    down = [(z, (z - 1) % PLANES) for z in range(PLANES)]
    below = [lax.ppermute(block, "ep", up) for block in own]
    above = [lax.ppermute(block, "ep", down) for block in own]
    if shared:
        core = lax.axis_index("section") % 2
        sent = lax.dynamic_slice(weight, (0, core * width), (columns, width))
        here = lax.ppermute(sent, "fsdp", [(0, 1), (1, 0)])
        below, above, here, where = lax.optimization_barrier((below, above, here, where))
        beside = lax.ppermute(here, "section", [(s, s ^ 1) for s in range(section)])
        sources = [weight, here, beside]
    else:
        sources = [lax.all_gather(weight, "fsdp", axis=1, tiled=True)]
    below_far = [lax.ppermute(block, "ep", [(1, 2), (2, 3)]) for block in below]
    above_far = [lax.ppermute(block, "ep", [(2, 1), (1, 0)]) for block in above]

    limits = pltpu.CompilerParams(vmem_limit_bytes=VMEM_LIMIT)

    def cost(microseconds):
        return pl.CostEstimate(
            flops=int(microseconds * 1.15e9), bytes_accessed=2 * row_count * width, transcendentals=0
        )

    total, squares, last_weight = pl.pallas_call(
        functools.partial(near_kernel, CHUNKS, len(sources)),
        out_shape=(
            jax.ShapeDtypeStruct((row_count, columns), jnp.float32),
            jax.ShapeDtypeStruct((row_count, 1), jnp.float32),
            jax.ShapeDtypeStruct((columns, width), jnp.bfloat16),
        ),
        in_specs=[smem] + [anywhere] * (3 * CHUNKS) + [vmem] + [anywhere] * len(sources),
        out_specs=(vmem, vmem, anywhere),
        scratch_shapes=[
            pltpu.VMEM((3, row_count, width), jnp.bfloat16),
            pltpu.VMEM((3, columns, width), jnp.bfloat16),
            pltpu.SemaphoreType.DMA((3, CHUNKS)),
            pltpu.SemaphoreType.DMA((4,)),
        ],
        compiler_params=limits,
        cost_estimate=cost(NEAR_COST),
    )(where, *own, *below, *above, gain, *sources)

    received = []
    for chunk in range(CHUNKS):
        messages = pl.pallas_call(
            functools.partial(last_kernel, chunk * rows, PLANES * width),
            out_shape=(jax.ShapeDtypeStruct((share, columns), jnp.bfloat16),) * PLANES,
            in_specs=[smem] + [vmem] * 6,
            out_specs=(vmem,) * PLANES,
            scratch_shapes=[pltpu.VMEM((rows, columns), jnp.float32)],
            compiler_params=limits,
            cost_estimate=cost(LAST_COSTS[chunk]),
        )(where, below_far[chunk], above_far[chunk], gain, last_weight, total, squares)
        for turn in range(PLANES):
            moves = [
                (s * PLANES + z, (s + 1) % section * PLANES + (z ^ turn))
                for s in range(section)
                for z in range(PLANES)
            ]
            received.append(lax.ppermute(messages[turn], ("section", "ep"), moves))

    half = ROPE // 2
    position = (fsdp_index * row_count + ep_index * quarter + jnp.arange(quarter)) % LENGTH
    frequency = rope_base ** (-(jnp.arange(half).astype(jnp.float32) / half))
    angle = position.astype(jnp.float32)[:, None] * frequency[None, :]
    cosine, sine = jnp.cos(angle), jnp.sin(angle)
    return pl.pallas_call(
        finish_kernel,
        out_shape=(
            jax.ShapeDtypeStruct((quarter, QL), jnp.bfloat16),
            jax.ShapeDtypeStruct((quarter, KVL + ROPE), jnp.bfloat16),
        ),
        in_specs=[smem] + [vmem] * (len(received) + 4),
        out_specs=(vmem, vmem),
        scratch_shapes=[pltpu.VMEM((PLANES, quarter, columns), jnp.float32)],
        compiler_params=limits,
    )(
        where,
        *received,
        q_gain.reshape(1, -1),
        kv_gain.reshape(1, -1),
        jnp.concatenate([cosine, cosine], axis=1),
        jnp.concatenate([-sine, sine], axis=1),
    )


def solution(mesh):
    placed = (P(("section", "fsdp"), "ep"), P(), P(), P(), P("fsdp", "ep"))
    return jax.shard_map(
        on_device,
        mesh=mesh,
        in_specs=placed,
        out_specs=(P(("section", "fsdp", "ep"), None), P(("section", "fsdp", "ep"), None)),
        check_vma=False,
    )
```

time: 220 us -> 91.7 us (0.42)
  waiting for transfers between devices: 187 us -> 46 us
  starting transfers between devices: 4.67 us -> 27.5 us
  between operations: 14.1 us -> 0.85 us
  Pallas kernels: 0 us -> 10.9 us
  matrix products: 8.15 us -> 0 us
  local copies, waits for them, and re-layouts: 3.09 us -> 5.89 us
  other arithmetic: 2.83 us -> 0.3 us
    all_gather x2 -> x0, waiting for transfers between devices: 125 us -> none  [the longest x1 75.8 us: on_device(): sender = lax.all_gather(hidden, 'ep', axis=1, tiled=True)]
    ppermute x1 -> x18, starting transfers between devices: 0.01 us -> 27.5 us  [the longest x8 14.7 us: on_device(): received.append(lax.ppermute(messages[turn], ('section', 'ep'), moves))]
    all_to_all x1 -> x0, waiting for transfers between devices: 17.3 us -> none  [on_device(): lax.all_to_all(partial_latent, 'ep', split_axis=0, concat_axis=1, tiled=T...]
    pallas_call x0 -> x4, Pallas kernels: none -> 10.9 us  [the longest x1 6.28 us: on_device(): pl.pallas_call(functools.partial(near_kernel, CHUNKS, len(sources)), out_...]
    dot_general x1 -> x0, matrix products: 8.15 us -> none  [on_device(): jnp.dot(normed, lax.all_gather(down_weight, 'fsdp', axis=0, tiled=True),...]
    all_to_all x1 -> x0, starting transfers between devices: 4.59 us -> none  [on_device(): lax.all_to_all(partial_latent, 'ep', split_axis=0, concat_axis=1, tiled=T...]
    ppermute x1 -> x18, waiting for transfers between devices: 42.5 us -> 46 us  [the longest x2 18.7 us: on_device(): below = [lax.ppermute(block, 'ep', up) for block in own]]
    dynamic_slice x0 -> x1, local copies, waits for them, and re-layouts: none -> 2.97 us  [on_device(): sent = lax.dynamic_slice(weight, (0, core * width), (columns, width))]
  transfers between devices with their start and end apart: 4 -> 18, of which waited for: 4 -> 9; matrix products, arithmetic and copies ran while one was open for 0% -> 1% of each run, Pallas kernels for 0% -> 10%
where the time goes in v4:
time: 91.7 us; the launch traced here: 91.4 us
  waiting for transfers between devices  46 us (50%)
  starting transfers between devices  27.5 us (30%)
  Pallas kernels  10.9 us (12%)
  local copies, waits for them, and re-layouts  5.89 us (6%)
    ppermute x2, waiting for transfers between devices, on_device(): below = [lax.ppermute(block, 'ep', up) for block in own]  18.7 us
    ppermute x2, waiting for transfers between devices, on_device(): above = [lax.ppermute(block, 'ep', down) for block in own]  18.2 us
    ppermute x8, starting transfers between devices, on_device(): received.append(lax.ppermute(messages[turn], ('section', 'ep'), moves))  14.7 us
    pallas_call x1, Pallas kernels, on_device(): pl.pallas_call(functools.partial(near_kernel, CHUNKS, len(sources)), out_...  6.28 us
    ppermute x2, waiting for transfers between devices, on_device(): above_far = [lax.ppermute(block, 'ep', [(2, 1), (1, 0)]) for block in above]  4.91 us
    ppermute x8, waiting for transfers between devices, on_device(): received.append(lax.ppermute(messages[turn], ('section', 'ep'), moves))  4.19 us
    ppermute x2, starting transfers between devices, on_device(): below = [lax.ppermute(block, 'ep', up) for block in own]  3.21 us
    pallas_call x2, Pallas kernels, on_device(): pl.pallas_call(functools.partial(last_kernel, chunk * rows, PLANES * widt...  3 us
  transfers between devices with their start and end apart: 18, of which 9 were waited for; matrix products, arithmetic and copies ran while one was open for 1% of the time, Pallas kernels for 10%

profile of v4, /device:TPU:0, one launch (start us, length us, event | category | flops | bytes accessed | tf_op | source)
XLA Modules:
  0.0 91.4 jit_solution(9020727101998672091)
XLA Ops:
  0.6 0.0 copy-start.3
  0.7 3.0 %dynamic-slice_bitcast_fusion = bf16[528,1792]{1,0:T(8,128)(2,1)} fusion(bf16[3584,528]{0,1:T(8,128)(2,1)} %param.10, s32[]{:T(128)S(6)} %select_n.32), kind=kLoop, calls=%fused_computation | loop fusion | bytes 3784708 | tf_op jit(solution)/shard_map/dynamic_slice | solution.py:158
  3.6 0.0 copy-start.2
  3.6 3.0 %collective-permute-start.4 = (bf16[528,1792]{1,0:T(8,128)(2,1)}, bf16[528,1792]{1,0:T(8,128)(2,1)S(1)}, u32[]{:S(2)}, u32[]{:S(2)}) collective-permute-start(bf16[528,1792]{1,0:T(8,128)(2,1)} %dynamic-slice_bitcast_fusion), channel_id=1, source_target_pairs={{0,4},{4,0},{1,5},{5,1},{2,6},{6,2},{3,7},{7,3},{8,12},{12,8},{9,1... | collective-permute-start | bytes 5677064 | tf_op jit(solution)/shard_map/ppermute | solution.py:159
  6.6 0.0 copy-done.3
  6.6 0.1 fusion.3
  6.7 1.6 %collective-permute-start = (bf16[128,1792]{1,0:T(8,128)(2,1)S(1)}, bf16[128,1792]{1,0:T(8,128)(2,1)S(1)}, u32[]{:S(2)}, u32[]{:S(2)}) collective-permute-start(bf16[128,1792]{1,0:T(8,128)(2,1)S(1)} %bitcast.18), channel_id=1, source_target_pairs={{0,1},{1,2},{2,3},{3,0},{4,5},{5,6},{6,7},{7,4},{8,9},{9,10},{10,1... | collective-permute-start | bytes 1376264 | tf_op jit(solution)/shard_map/ppermute | solution.py:154
  8.3 1.6 %collective-permute-start.1 = (bf16[128,1792]{1,0:T(8,128)(2,1)S(1)}, bf16[128,1792]{1,0:T(8,128)(2,1)}, u32[]{:S(2)}, u32[]{:S(2)}) collective-permute-start(bf16[128,1792]{1,0:T(8,128)(2,1)S(1)} %bitcast.15), channel_id=1, source_target_pairs={{0,1},{1,2},{2,3},{3,0},{4,5},{5,6},{6,7},{7,4},{8,9},{9,10},{10,1... | collective-permute-start | bytes 1376264 | tf_op jit(solution)/shard_map/ppermute | solution.py:154
  9.9 2.2 %collective-permute-start.2 = (bf16[128,1792]{1,0:T(8,128)(2,1)S(1)}, bf16[128,1792]{1,0:T(8,128)(2,1)}, u32[]{:S(2)}, u32[]{:S(2)}) collective-permute-start(bf16[128,1792]{1,0:T(8,128)(2,1)S(1)} %bitcast.19), channel_id=1, source_target_pairs={{0,3},{1,0},{2,1},{3,2},{4,7},{5,4},{6,5},{7,6},{8,11},{9,8},{10,9... | collective-permute-start | bytes 1376264 | tf_op jit(solution)/shard_map/ppermute | solution.py:155
  12.1 0.4 collective-permute-start.3
  12.6 0.7 dynamic-slice_bitcast_fusion.1
  13.2 8.9 %collective-permute-done.refs_2_ = bf16[128,1792]{1,0:T(8,128)(2,1)S(1)} collective-permute-done((bf16[128,1792]{1,0:T(8,128)(2,1)S(1)}, bf16[128,1792]{1,0:T(8,128)(2,1)S(1)}, u32[]{:S(2)}, u32[]{:S(2)}) %collective-permute-start) | collective-permute-done | bytes 458784 | tf_op jit(solution)/shard_map/ppermute | solution.py:154
  22.1 9.8 %collective-permute-done.1.refs_3_ = bf16[128,1792]{1,0:T(8,128)(2,1)} collective-permute-done((bf16[128,1792]{1,0:T(8,128)(2,1)S(1)}, bf16[128,1792]{1,0:T(8,128)(2,1)}, u32[]{:S(2)}, u32[]{:S(2)}) %collective-permute-start.1) | collective-permute-done | bytes 458784 | tf_op jit(solution)/shard_map/ppermute | solution.py:154
  31.9 8.5 %collective-permute-done.2.refs_4_ = bf16[128,1792]{1,0:T(8,128)(2,1)} collective-permute-done((bf16[128,1792]{1,0:T(8,128)(2,1)S(1)}, bf16[128,1792]{1,0:T(8,128)(2,1)}, u32[]{:S(2)}, u32[]{:S(2)}) %collective-permute-start.2) | collective-permute-done | bytes 458784 | tf_op jit(solution)/shard_map/ppermute | solution.py:155
  40.5 9.7 %collective-permute-done.3.refs_5_ = bf16[128,1792]{1,0:T(8,128)(2,1)} collective-permute-done((bf16[128,1792]{1,0:T(8,128)(2,1)S(1)}, bf16[128,1792]{1,0:T(8,128)(2,1)}, u32[]{:S(2)}, u32[]{:S(2)}) %collective-permute-start.3) | collective-permute-done | bytes 458784 | tf_op jit(solution)/shard_map/ppermute | solution.py:155
  50.2 0.0 collective-permute-done.4.refs_8_
  50.2 0.0 collective-permute-start.7
  50.2 0.2 fusion
  50.4 0.1 copy.13.where
  50.5 0.7 collective-permute-start.12
  51.2 1.3 %collective-permute-start.13 = (bf16[128,1792]{1,0:T(8,128)(2,1)}, bf16[128,1792]{1,0:T(8,128)(2,1)S(1)}, u32[]{:S(2)}, u32[]{:S(2)}) collective-permute-start(bf16[128,1792]{1,0:T(8,128)(2,1)} %collective-permute-done.3.refs_5_), channel_id=1, source_target_pairs={{2,1},{1,0},{6,5},{5,4},{10,9},{9,8},{14,13},{13,12},{18,17},{17,1... | collective-permute-start | bytes 1376264 | tf_op jit(solution)/shard_map/ppermute | solution.py:166
  52.5 0.7 collective-permute-start.5
  53.2 1.3 %collective-permute-start.6 = (bf16[128,1792]{1,0:T(8,128)(2,1)}, bf16[128,1792]{1,0:T(8,128)(2,1)S(1)}, u32[]{:S(2)}, u32[]{:S(2)}) collective-permute-start(bf16[128,1792]{1,0:T(8,128)(2,1)} %collective-permute-done.2.refs_4_), channel_id=1, source_target_pairs={{2,1},{1,0},{6,5},{5,4},{10,9},{9,8},{14,13},{13,12},{18,17},{17,1... | collective-permute-start | bytes 1376264 | tf_op jit(solution)/shard_map/ppermute | solution.py:166
  54.5 0.0 collective-permute-done.7.refs_9_
  54.5 0.0 copy-done.2
  54.5 0.0 copy-start
  54.5 2.1 %copy-done = bf16[3584,528]{0,1:T(8,128)(2,1)S(1)} copy-done((bf16[3584,528]{0,1:T(8,128)(2,1)S(1)}, bf16[3584,528]{0,1:T(8,128)(2,1)}, u32[]{:S(2)}) %copy-start) | copy-done | bytes 3784728
  56.6 6.3 %shard_map.77 = (f32[256,528]{1,0:T(8,128)S(1)}, f32[256,1]{1,0:T(8,128)S(1)}, bf16[528,1792]{1,0:T(8,128)(2,1)S(1)}) custom-call(s32[5,4]{1,0:T(8,128)S(1)} %copy.13.where, bf16[128,1792]{1,0:T(8,128)(2,1)S(1)} %bitcast.20, bf16[128,1792]{1,0:T(8,128)(2,1)S(1)} %bitcast.17, bf16[128,1792]{1,0:T(8,128)(2,1)S(1)} %collective-permute-done.refs_2_, ...), custom_call_target="tpu_custom_call" | custom-call | flops 17250000896 | bytes 917504 | tf_op jit(solution)/shard_map/pallas_call | solution.py:175
  62.8 0.0 collective-permute-done.12.refs_0_
  62.9 4.3 %collective-permute-done.13.refs_1_ = bf16[128,1792]{1,0:T(8,128)(2,1)S(1)} collective-permute-done((bf16[128,1792]{1,0:T(8,128)(2,1)}, bf16[128,1792]{1,0:T(8,128)(2,1)S(1)}, u32[]{:S(2)}, u32[]{:S(2)}) %collective-permute-start.13) | collective-permute-done | bytes 458784 | tf_op jit(solution)/shard_map/ppermute | solution.py:166
  67.2 1.5 %shard_map.79 = (bf16[32,528]{1,0:T(8,128)(2,1)S(1)}, bf16[32,528]{1,0:T(8,128)(2,1)S(1)}, bf16[32,528]{1,0:T(8,128)(2,1)S(1)}, bf16[32,528]{1,0:T(8,128)(2,1)S(1)}) custom-call(s32[5,4]{1,0:T(8,128)S(1)} %copy.13.where, bf16[128,1792]{1,0:T(8,128)(2,1)S(1)} %collective-permute-done.12.refs_0_, bf16[128,1792]{1,0:T(8,128)(2,1)S(1)} %collective-permute-done.13.refs_1_, ...), custom_call_target="tpu_custom_call" | custom-call | flops 2300000000 | bytes 917504 | tf_op jit(solution)/shard_map/pallas_call | solution.py:196
  68.7 0.1 collective-permute-start.14
  68.8 4.0 %collective-permute-start.15 = (bf16[32,528]{1,0:T(8,128)(2,1)S(1)}, bf16[32,528]{1,0:T(8,128)(2,1)S(1)}, u32[]{:S(2)}, u32[]{:S(2)}) collective-permute-start(bf16[32,528]{1,0:T(8,128)(2,1)S(1)} %get-tuple-element.33), channel_id=1, source_target_pairs={{0,9},{1,8},{2,11},{3,10},{8,17},{9,16},{10,19},{11,18},{16,25},{1... | collective-permute-start | bytes 101384 | tf_op jit(solution)/shard_map/ppermute | solution.py:211
  72.8 1.5 %collective-permute-start.16 = (bf16[32,528]{1,0:T(8,128)(2,1)S(1)}, bf16[32,528]{1,0:T(8,128)(2,1)S(1)}, u32[]{:S(2)}, u32[]{:S(2)}) collective-permute-start(bf16[32,528]{1,0:T(8,128)(2,1)S(1)} %get-tuple-element.34), channel_id=1, source_target_pairs={{0,10},{1,11},{2,8},{3,9},{8,18},{9,19},{10,16},{11,17},{16,26},{1... | collective-permute-start | bytes 101384 | tf_op jit(solution)/shard_map/ppermute | solution.py:211
  74.3 0.0 collective-permute-done.5.refs_0_
  74.3 0.0 copy-start.4
  74.3 0.0 copy-start.1
  74.3 2.2 %collective-permute-start.17 = (bf16[32,528]{1,0:T(8,128)(2,1)S(1)}, bf16[32,528]{1,0:T(8,128)(2,1)S(1)}, u32[]{:S(2)}, u32[]{:S(2)}) collective-permute-start(bf16[32,528]{1,0:T(8,128)(2,1)S(1)} %get-tuple-element.35), channel_id=1, source_target_pairs={{0,11},{1,10},{2,9},{3,8},{8,19},{9,18},{10,17},{11,16},{16,27},{1... | collective-permute-start | bytes 101384 | tf_op jit(solution)/shard_map/ppermute | solution.py:211
  76.5 0.6 collective-permute-done.6.refs_1_
  77.0 1.5 %shard_map.78 = (bf16[32,528]{1,0:T(8,128)(2,1)S(1)}, bf16[32,528]{1,0:T(8,128)(2,1)S(1)}, bf16[32,528]{1,0:T(8,128)(2,1)S(1)}, bf16[32,528]{1,0:T(8,128)(2,1)S(1)}) custom-call(s32[5,4]{1,0:T(8,128)S(1)} %copy.13.where, bf16[128,1792]{1,0:T(8,128)(2,1)S(1)} %collective-permute-done.5.refs_0_, bf16[128,1792]{1,0:T(8,128)(2,1)S(1)} %collective-permute-done.6.refs_1_, ...), custom_call_target="tpu_custom_call" | custom-call | flops 9200000000 | bytes 917504 | tf_op jit(solution)/shard_map/pallas_call | solution.py:196
  78.5 0.1 collective-permute-start.10
  78.6 0.0 collective-permute-done.14.refs_4_
  78.6 6.8 %collective-permute-start.11 = (bf16[32,528]{1,0:T(8,128)(2,1)S(1)}, bf16[32,528]{1,0:T(8,128)(2,1)S(1)}, u32[]{:S(2)}, u32[]{:S(2)}) collective-permute-start(bf16[32,528]{1,0:T(8,128)(2,1)S(1)} %get-tuple-element.31), channel_id=1, source_target_pairs={{0,11},{1,10},{2,9},{3,8},{8,19},{9,18},{10,17},{11,16},{16,27},{1... | collective-permute-start | bytes 101384 | tf_op jit(solution)/shard_map/ppermute | solution.py:211
  85.4 0.0 collective-permute-done.15.refs_5_
  85.4 0.0 collective-permute-start.8
  85.4 0.0 collective-permute-done.16.refs_6_
  85.4 0.1 collective-permute-start.9
  85.5 0.1 pad_maximum_fusion
  85.6 0.0 copy-done.4
  85.6 0.0 collective-permute-done.17.refs_7_
  85.6 0.0 collective-permute-done.10.refs_2_
  85.6 2.3 %collective-permute-done.11.refs_3_ = bf16[32,528]{1,0:T(8,128)(2,1)S(1)} collective-permute-done((bf16[32,528]{1,0:T(8,128)(2,1)S(1)}, bf16[32,528]{1,0:T(8,128)(2,1)S(1)}, u32[]{:S(2)}, u32[]{:S(2)}) %collective-permute-start.11) | collective-permute-done | bytes 33824 | tf_op jit(solution)/shard_map/ppermute | solution.py:211
  87.9 0.9 collective-permute-done.8.refs_0_
  88.9 1.0 %collective-permute-done.9.refs_1_ = bf16[32,528]{1,0:T(8,128)(2,1)S(1)} collective-permute-done((bf16[32,528]{1,0:T(8,128)(2,1)S(1)}, bf16[32,528]{1,0:T(8,128)(2,1)S(1)}, u32[]{:S(2)}, u32[]{:S(2)}) %collective-permute-start.9) | collective-permute-done | bytes 33824 | tf_op jit(solution)/shard_map/ppermute | solution.py:211
  89.8 0.0 copy-done.1
  89.8 1.6 %shard_map.80 = (bf16[64,1536]{1,0:T(8,128)(2,1)}, bf16[64,576]{1,0:T(8,128)(2,1)}) custom-call(s32[5,4]{1,0:T(8,128)S(1)} %copy.13.where, bf16[32,528]{1,0:T(8,128)(2,1)S(1)} %collective-permute-done.8.refs_0_, bf16[32,528]{1,0:T(8,128)(2,1)S(1)} %collective-permute-done.9.refs_1_, bf16[32,528]{1,0:T(8,128)(2,1)S(1)} %collective-permute-done.10.refs_2_, ...), custom_call_target="tpu_custom_call" | custom-call | tf_op jit(solution)/shard_map/pallas_call | solution.py:218
  (3 shorter events, 0.0 us)
Async XLA Ops:
  0.6 5.9 %copy-start.3 = (bf16[256,1792]{1,0:T(8,128)(2,1)S(1)}, bf16[256,1792]{1,0:T(8,128)(2,1)}, u32[]{:S(2)}) copy-start(bf16[256,1792]{1,0:T(8,128)(2,1)} %param.6) | copy-start | bytes 2752516
  3.6 50.9 %copy-start.2 = (f32[7168]{0:T(1024)S(1)}, f32[7168]{0:T(1024)}, u32[]{:S(2)}) copy-start(f32[7168]{0:T(1024)} %param.7) | copy-start | bytes 86020
  3.6 46.5 %collective-permute-start.4 = (bf16[528,1792]{1,0:T(8,128)(2,1)}, bf16[528,1792]{1,0:T(8,128)(2,1)S(1)}, u32[]{:S(2)}, u32[]{:S(2)}) collective-permute-start(bf16[528,1792]{1,0:T(8,128)(2,1)} %dynamic-slice_bitcast_fusion), channel_id=1, source_target_pairs={{0,4},{4,0},{1,5},{5,1},{2,6},{6,2},{3,7},{7,3},{8,12},{12,8},{9,1... | collective-permute-start | bytes 5677064 | tf_op jit(solution)/shard_map/ppermute | solution.py:159
  6.7 15.4 %collective-permute-start = (bf16[128,1792]{1,0:T(8,128)(2,1)S(1)}, bf16[128,1792]{1,0:T(8,128)(2,1)S(1)}, u32[]{:S(2)}, u32[]{:S(2)}) collective-permute-start(bf16[128,1792]{1,0:T(8,128)(2,1)S(1)} %bitcast.18), channel_id=1, source_target_pairs={{0,1},{1,2},{2,3},{3,0},{4,5},{5,6},{6,7},{7,4},{8,9},{9,10},{10,1... | collective-permute-start | bytes 1376264 | tf_op jit(solution)/shard_map/ppermute | solution.py:154
  8.3 23.6 %collective-permute-start.1 = (bf16[128,1792]{1,0:T(8,128)(2,1)S(1)}, bf16[128,1792]{1,0:T(8,128)(2,1)}, u32[]{:S(2)}, u32[]{:S(2)}) collective-permute-start(bf16[128,1792]{1,0:T(8,128)(2,1)S(1)} %bitcast.15), channel_id=1, source_target_pairs={{0,1},{1,2},{2,3},{3,0},{4,5},{5,6},{6,7},{7,4},{8,9},{9,10},{10,1... | collective-permute-start | bytes 1376264 | tf_op jit(solution)/shard_map/ppermute | solution.py:154
  9.9 30.6 %collective-permute-start.2 = (bf16[128,1792]{1,0:T(8,128)(2,1)S(1)}, bf16[128,1792]{1,0:T(8,128)(2,1)}, u32[]{:S(2)}, u32[]{:S(2)}) collective-permute-start(bf16[128,1792]{1,0:T(8,128)(2,1)S(1)} %bitcast.19), channel_id=1, source_target_pairs={{0,3},{1,0},{2,1},{3,2},{4,7},{5,4},{6,5},{7,6},{8,11},{9,8},{10,9... | collective-permute-start | bytes 1376264 | tf_op jit(solution)/shard_map/ppermute | solution.py:155
  12.1 38.0 %collective-permute-start.3 = (bf16[128,1792]{1,0:T(8,128)(2,1)S(1)}, bf16[128,1792]{1,0:T(8,128)(2,1)}, u32[]{:S(2)}, u32[]{:S(2)}) collective-permute-start(bf16[128,1792]{1,0:T(8,128)(2,1)S(1)} %bitcast.16), channel_id=1, source_target_pairs={{0,3},{1,0},{2,1},{3,2},{4,7},{5,4},{6,5},{7,6},{8,11},{9,8},{10,9... | collective-permute-start | bytes 1376264 | tf_op jit(solution)/shard_map/ppermute | solution.py:155
  50.2 4.3 %collective-permute-start.7 = (bf16[528,1792]{1,0:T(8,128)(2,1)S(1)}, bf16[528,1792]{1,0:T(8,128)(2,1)}, u32[]{:S(2)}, u32[]{:S(2)}) collective-permute-start(bf16[528,1792]{1,0:T(8,128)(2,1)S(1)} %collective-permute-done.4.refs_8_), channel_id=1, source_target_pairs={{0,8},{8,0},{16,24},{24,16},{1,9},{9,1},{17,25},{25,17},{2,10},{10... | collective-permute-start | bytes 5677064 | tf_op jit(solution)/shard_map/ppermute | solution.py:161
  50.5 12.4 %collective-permute-start.12 = (bf16[128,1792]{1,0:T(8,128)(2,1)}, bf16[128,1792]{1,0:T(8,128)(2,1)S(1)}, u32[]{:S(2)}, u32[]{:S(2)}) collective-permute-start(bf16[128,1792]{1,0:T(8,128)(2,1)} %collective-permute-done.1.refs_3_), channel_id=1, source_target_pairs={{1,2},{2,3},{5,6},{6,7},{9,10},{10,11},{13,14},{14,15},{17,18},{18... | collective-permute-start | bytes 1376264 | tf_op jit(solution)/shard_map/ppermute | solution.py:165
  51.2 16.0 %collective-permute-start.13 = (bf16[128,1792]{1,0:T(8,128)(2,1)}, bf16[128,1792]{1,0:T(8,128)(2,1)S(1)}, u32[]{:S(2)}, u32[]{:S(2)}) collective-permute-start(bf16[128,1792]{1,0:T(8,128)(2,1)} %collective-permute-done.3.refs_5_), channel_id=1, source_target_pairs={{2,1},{1,0},{6,5},{5,4},{10,9},{9,8},{14,13},{13,12},{18,17},{17,1... | collective-permute-start | bytes 1376264 | tf_op jit(solution)/shard_map/ppermute | solution.py:166
  52.5 21.8 %collective-permute-start.5 = (bf16[128,1792]{1,0:T(8,128)(2,1)S(1)}, bf16[128,1792]{1,0:T(8,128)(2,1)S(1)}, u32[]{:S(2)}, u32[]{:S(2)}) collective-permute-start(bf16[128,1792]{1,0:T(8,128)(2,1)S(1)} %collective-permute-done.refs_2_), channel_id=1, source_target_pairs={{1,2},{2,3},{5,6},{6,7},{9,10},{10,11},{13,14},{14,15},{17,18},{18... | collective-permute-start | bytes 1376264 | tf_op jit(solution)/shard_map/ppermute | solution.py:165
  53.2 23.9 %collective-permute-start.6 = (bf16[128,1792]{1,0:T(8,128)(2,1)}, bf16[128,1792]{1,0:T(8,128)(2,1)S(1)}, u32[]{:S(2)}, u32[]{:S(2)}) collective-permute-start(bf16[128,1792]{1,0:T(8,128)(2,1)} %collective-permute-done.2.refs_4_), channel_id=1, source_target_pairs={{2,1},{1,0},{6,5},{5,4},{10,9},{9,8},{14,13},{13,12},{18,17},{17,1... | collective-permute-start | bytes 1376264 | tf_op jit(solution)/shard_map/ppermute | solution.py:166
  54.5 2.1 %copy-start = (bf16[3584,528]{0,1:T(8,128)(2,1)S(1)}, bf16[3584,528]{0,1:T(8,128)(2,1)}, u32[]{:S(2)}) copy-start(bf16[3584,528]{0,1:T(8,128)(2,1)} %param.10) | copy-start | bytes 11354116
  68.7 9.9 %collective-permute-start.14 = (bf16[32,528]{1,0:T(8,128)(2,1)S(1)}, bf16[32,528]{1,0:T(8,128)(2,1)S(1)}, u32[]{:S(2)}, u32[]{:S(2)}) collective-permute-start(bf16[32,528]{1,0:T(8,128)(2,1)S(1)} %get-tuple-element.32), channel_id=1, source_target_pairs={{0,8},{1,9},{2,10},{3,11},{8,16},{9,17},{10,18},{11,19},{16,24},{1... | collective-permute-start | bytes 101384 | tf_op jit(solution)/shard_map/ppermute | solution.py:211
  68.8 16.7 %collective-permute-start.15 = (bf16[32,528]{1,0:T(8,128)(2,1)S(1)}, bf16[32,528]{1,0:T(8,128)(2,1)S(1)}, u32[]{:S(2)}, u32[]{:S(2)}) collective-permute-start(bf16[32,528]{1,0:T(8,128)(2,1)S(1)} %get-tuple-element.33), channel_id=1, source_target_pairs={{0,9},{1,8},{2,11},{3,10},{8,17},{9,16},{10,19},{11,18},{16,25},{1... | collective-permute-start | bytes 101384 | tf_op jit(solution)/shard_map/ppermute | solution.py:211
  72.8 12.6 %collective-permute-start.16 = (bf16[32,528]{1,0:T(8,128)(2,1)S(1)}, bf16[32,528]{1,0:T(8,128)(2,1)S(1)}, u32[]{:S(2)}, u32[]{:S(2)}) collective-permute-start(bf16[32,528]{1,0:T(8,128)(2,1)S(1)} %get-tuple-element.34), channel_id=1, source_target_pairs={{0,10},{1,11},{2,8},{3,9},{8,18},{9,19},{10,16},{11,17},{16,26},{1... | collective-permute-start | bytes 101384 | tf_op jit(solution)/shard_map/ppermute | solution.py:211
  74.3 11.3 %copy-start.4 = (f32[1536]{0:T(1024)S(1)}, f32[1536]{0:T(1024)}, u32[]{:S(2)}) copy-start(f32[1536]{0:T(1024)} %param.8) | copy-start | bytes 18436
  74.3 15.5 %copy-start.1 = (f32[512]{0:T(512)S(1)}, f32[512]{0:T(512)}, u32[]{:S(2)}) copy-start(f32[512]{0:T(512)} %param.9) | copy-start | bytes 6148
  74.3 11.3 %collective-permute-start.17 = (bf16[32,528]{1,0:T(8,128)(2,1)S(1)}, bf16[32,528]{1,0:T(8,128)(2,1)S(1)}, u32[]{:S(2)}, u32[]{:S(2)}) collective-permute-start(bf16[32,528]{1,0:T(8,128)(2,1)S(1)} %get-tuple-element.35), channel_id=1, source_target_pairs={{0,11},{1,10},{2,9},{3,8},{8,19},{9,18},{10,17},{11,16},{16,27},{1... | collective-permute-start | bytes 101384 | tf_op jit(solution)/shard_map/ppermute | solution.py:211
  78.5 7.1 %collective-permute-start.10 = (bf16[32,528]{1,0:T(8,128)(2,1)S(1)}, bf16[32,528]{1,0:T(8,128)(2,1)S(1)}, u32[]{:S(2)}, u32[]{:S(2)}) collective-permute-start(bf16[32,528]{1,0:T(8,128)(2,1)S(1)} %get-tuple-element.30), channel_id=1, source_target_pairs={{0,10},{1,11},{2,8},{3,9},{8,18},{9,19},{10,16},{11,17},{16,26},{1... | collective-permute-start | bytes 101384 | tf_op jit(solution)/shard_map/ppermute | solution.py:211
  78.6 9.3 %collective-permute-start.11 = (bf16[32,528]{1,0:T(8,128)(2,1)S(1)}, bf16[32,528]{1,0:T(8,128)(2,1)S(1)}, u32[]{:S(2)}, u32[]{:S(2)}) collective-permute-start(bf16[32,528]{1,0:T(8,128)(2,1)S(1)} %get-tuple-element.31), channel_id=1, source_target_pairs={{0,11},{1,10},{2,9},{3,8},{8,19},{9,18},{10,17},{11,16},{16,27},{1... | collective-permute-start | bytes 101384 | tf_op jit(solution)/shard_map/ppermute | solution.py:211
  85.4 3.4 %collective-permute-start.8 = (bf16[32,528]{1,0:T(8,128)(2,1)S(1)}, bf16[32,528]{1,0:T(8,128)(2,1)S(1)}, u32[]{:S(2)}, u32[]{:S(2)}) collective-permute-start(bf16[32,528]{1,0:T(8,128)(2,1)S(1)} %get-tuple-element.28), channel_id=1, source_target_pairs={{0,8},{1,9},{2,10},{3,11},{8,16},{9,17},{10,18},{11,19},{16,24},{1... | collective-permute-start | bytes 101384 | tf_op jit(solution)/shard_map/ppermute | solution.py:211
  85.4 4.4 %collective-permute-start.9 = (bf16[32,528]{1,0:T(8,128)(2,1)S(1)}, bf16[32,528]{1,0:T(8,128)(2,1)S(1)}, u32[]{:S(2)}, u32[]{:S(2)}) collective-permute-start(bf16[32,528]{1,0:T(8,128)(2,1)S(1)} %get-tuple-element.29), channel_id=1, source_target_pairs={{0,9},{1,8},{2,11},{3,10},{8,17},{9,16},{10,19},{11,18},{16,25},{1... | collective-permute-start | bytes 101384 | tf_op jit(solution)/shard_map/ppermute | solution.py:211

commit v5 on v4

--- a/solution.py
+++ b/solution.py
@@ -16,9 +16,10 @@
 
 epsilon = 1e-06
 rope_base = 10000.0
-CHUNKS = 2
+CHUNKS = 1
 PLANES = 4
-NEAR_COST, LAST_COSTS = 15, (8, 2)
+PARTS = 3
+NEAR_COST, LAST_COSTS = 1, (2, 2)
 VMEM_LIMIT = 20 * 1024 * 1024
 
 vmem = pl.BlockSpec(memory_space=pltpu.VMEM)
@@ -36,23 +37,29 @@
     )
 
 
-def near_kernel(chunks, sources, where, *refs):
+def near_kernel(chunks, layout, where, *refs):
     refs = list(refs)
     block_refs = [[refs.pop(0) for _ in range(chunks)] for _ in range(3)]
     gain_ref = refs.pop(0)
-    source_refs = [refs.pop(0) for _ in range(sources)]
+    source_refs = [[refs.pop(0) for _ in range(parts)] for parts in layout]
     total, squares, last_weight, blocks, weights, block_arrived, weight_arrived = refs
     rows, width = block_refs[0][0].shape
 
     def weight_copy(entry, act):
         into = weights.at[entry] if entry < 3 else last_weight
-        for source, ref in enumerate(source_refs):
+        for source, parts in enumerate(source_refs):
 
             @pl.when(where[1, entry] == source)
             def _():
                 at = pl.multiple_of(where[2, entry] * width, width)
-                copy = pltpu.make_async_copy(ref.at[:, pl.ds(at, width)], into, weight_arrived.at[entry])
-                getattr(copy, act)()
+                for part, ref in enumerate(parts):
+                    height = ref.shape[0]
+                    copy = pltpu.make_async_copy(
+                        ref.at[:, pl.ds(at, width)],
+                        into.at[pl.ds(part * height, height)],
+                        weight_arrived.at[entry, part],
+                    )
+                    getattr(copy, act)()
 
     def block_copies(entry, act):
         for chunk, ref in enumerate(block_refs[entry]):
@@ -155,13 +162,16 @@
     above = [lax.ppermute(block, "ep", down) for block in own]
     if shared:
         core = lax.axis_index("section") % 2
-        sent = lax.dynamic_slice(weight, (0, core * width), (columns, width))
-        here = lax.ppermute(sent, "fsdp", [(0, 1), (1, 0)])
-        below, above, here, where = lax.optimization_barrier((below, above, here, where))
-        beside = lax.ppermute(here, "section", [(s, s ^ 1) for s in range(section)])
-        sources = [weight, here, beside]
+        height = columns // PARTS
+        here = [
+            lax.dynamic_slice(weight, (part * height, core * width), (height, width))
+            for part in range(PARTS)
+        ]
+        here = [lax.ppermute(part, "fsdp", [(0, 1), (1, 0)]) for part in here]
+        cores = [(s, s ^ 1) for s in range(section)]
+        sources = [[weight], here, [lax.ppermute(part, "section", cores) for part in here]]
     else:
-        sources = [lax.all_gather(weight, "fsdp", axis=1, tiled=True)]
+        sources = [[lax.all_gather(weight, "fsdp", axis=1, tiled=True)]]
     below_far = [lax.ppermute(block, "ep", [(1, 2), (2, 3)]) for block in below]
     above_far = [lax.ppermute(block, "ep", [(2, 1), (1, 0)]) for block in above]
 
@@ -173,23 +183,23 @@
         )
 
     total, squares, last_weight = pl.pallas_call(
-        functools.partial(near_kernel, CHUNKS, len(sources)),
+        functools.partial(near_kernel, CHUNKS, [len(parts) for parts in sources]),
         out_shape=(
             jax.ShapeDtypeStruct((row_count, columns), jnp.float32),
             jax.ShapeDtypeStruct((row_count, 1), jnp.float32),
             jax.ShapeDtypeStruct((columns, width), jnp.bfloat16),
         ),
-        in_specs=[smem] + [anywhere] * (3 * CHUNKS) + [vmem] + [anywhere] * len(sources),
+        in_specs=[smem] + [anywhere] * (3 * CHUNKS) + [vmem] + [anywhere] * sum(len(parts) for parts in sources),
         out_specs=(vmem, vmem, anywhere),
         scratch_shapes=[
             pltpu.VMEM((3, row_count, width), jnp.bfloat16),
             pltpu.VMEM((3, columns, width), jnp.bfloat16),
             pltpu.SemaphoreType.DMA((3, CHUNKS)),
-            pltpu.SemaphoreType.DMA((4,)),
+            pltpu.SemaphoreType.DMA((4, PARTS)),
         ],
         compiler_params=limits,
         cost_estimate=cost(NEAR_COST),
-    )(where, *own, *below, *above, gain, *sources)
+    )(where, *own, *below, *above, gain, *[part for parts in sources for part in parts])
 
     received = []
     for chunk in range(CHUNKS):

time: 91.7 us -> 85.8 us (0.936)
  starting transfers between devices: 27.5 us -> 17.7 us
  waiting for transfers between devices: 46 us -> 52 us
  local copies, waits for them, and re-layouts: 5.89 us -> 4.45 us
    ppermute x8 -> x4, starting transfers between devices: 14.7 us -> 5.33 us  [on_device(): received.append(lax.ppermute(messages[turn], ('section', 'ep'), moves))]
    ppermute x2 -> x6, waiting for transfers between devices: 0.01 us -> 4.35 us  [the longest x3 2.99 us: on_device(): here = [lax.ppermute(part, 'fsdp', [(0, 1), (1, 0)]) for part in here]]
    ppermute x2 -> x1, waiting for transfers between devices: 4.91 us -> 8.22 us  [on_device(): above_far = [lax.ppermute(block, 'ep', [(2, 1), (1, 0)]) for block in above]]
    ppermute x2 -> x1, waiting for transfers between devices: 18.7 us -> 16 us  [on_device(): below = [lax.ppermute(block, 'ep', up) for block in own]]
    ppermute x8 -> x4, waiting for transfers between devices: 4.19 us -> 6.78 us  [on_device(): received.append(lax.ppermute(messages[turn], ('section', 'ep'), moves))]
    ppermute x2 -> x1, waiting for transfers between devices: 18.2 us -> 16.6 us  [on_device(): above = [lax.ppermute(block, 'ep', down) for block in own]]
    dynamic_slice x1, local copies, waits for them, and re-layouts: 2.97 us -> 1.58 us  [on_device(): lax.dynamic_slice(weight, (part * height, core * width), (height, width))]
    ppermute x2 -> x6, starting transfers between devices: 2.97 us -> 4.33 us  [the longest x3 3.77 us: on_device(): here = [lax.ppermute(part, 'fsdp', [(0, 1), (1, 0)]) for part in here]]
  transfers between devices with their start and end apart: 18 -> 14, of which waited for: 9 -> 7; matrix products, arithmetic and copies ran while one was open for 1% -> 3% of each run, Pallas kernels for 10% -> 7%
where the time goes in v5:
time: 85.8 us; the launch traced here: 85.5 us
  waiting for transfers between devices  52 us (61%)
  starting transfers between devices  17.7 us (21%)
  Pallas kernels  10.3 us (12%)
  local copies, waits for them, and re-layouts  4.45 us (5%)
    ppermute x1, waiting for transfers between devices, on_device(): above = [lax.ppermute(block, 'ep', down) for block in own]  16.6 us
    ppermute x1, waiting for transfers between devices, on_device(): below = [lax.ppermute(block, 'ep', up) for block in own]  16 us
    ppermute x1, waiting for transfers between devices, on_device(): above_far = [lax.ppermute(block, 'ep', [(2, 1), (1, 0)]) for block in above]  8.22 us
    ppermute x4, waiting for transfers between devices, on_device(): received.append(lax.ppermute(messages[turn], ('section', 'ep'), moves))  6.78 us
    pallas_call x1, Pallas kernels, on_device(): pl.pallas_call(functools.partial(near_kernel, CHUNKS, [len(parts) for par...  6.17 us
    ppermute x4, starting transfers between devices, on_device(): received.append(lax.ppermute(messages[turn], ('section', 'ep'), moves))  5.33 us
    ppermute x3, starting transfers between devices, on_device(): here = [lax.ppermute(part, 'fsdp', [(0, 1), (1, 0)]) for part in here]  3.77 us
    ppermute x1, starting transfers between devices, on_device(): below = [lax.ppermute(block, 'ep', up) for block in own]  3.08 us
  transfers between devices with their start and end apart: 14, of which 7 were waited for; matrix products, arithmetic and copies ran while one was open for 3% of the time, Pallas kernels for 7%

profile of v5, /device:TPU:0, one launch (start us, length us, event | category | flops | bytes accessed | tf_op | source)
XLA Modules:
  0.0 85.5 jit_solution(12023754900458908279)
XLA Ops:
  0.6 0.0 copy-start.1
  0.6 0.0 copy-start.4
  0.6 0.0 copy-start.2
  0.7 3.1 %collective-permute-start = (bf16[256,1792]{1,0:T(8,128)(2,1)}, bf16[256,1792]{1,0:T(8,128)(2,1)S(1)}, u32[]{:S(2)}, u32[]{:S(2)}) collective-permute-start(bf16[256,1792]{1,0:T(8,128)(2,1)} %refs_0_.1), channel_id=1, source_target_pairs={{0,1},{1,2},{2,3},{3,0},{4,5},{5,6},{6,7},{7,4},{8,9},{9,10},{10,1... | collective-permute-start | bytes 2752520 | tf_op jit(solution)/shard_map/ppermute | solution.py:161
  3.7 2.1 %collective-permute-start.2 = (bf16[256,1792]{1,0:T(8,128)(2,1)}, bf16[256,1792]{1,0:T(8,128)(2,1)S(1)}, u32[]{:S(2)}, u32[]{:S(2)}) collective-permute-start(bf16[256,1792]{1,0:T(8,128)(2,1)} %refs_0_.1), channel_id=1, source_target_pairs={{0,3},{1,0},{2,1},{3,2},{4,7},{5,4},{6,5},{7,6},{8,11},{9,8},{10,9... | collective-permute-start | bytes 2752520 | tf_op jit(solution)/shard_map/ppermute | solution.py:162
  5.8 1.6 %dynamic-slice_bitcast_fusion = (bf16[176,1792]{1,0:T(8,128)(2,1)S(1)}, bf16[176,1792]{1,0:T(8,128)(2,1)S(1)}, bf16[176,1792]{1,0:T(8,128)(2,1)S(1)}) fusion(bf16[3584,528]{0,1:T(8,128)(2,1)} %param.10, s32[]{:T(128)S(6)} %select_n.37), kind=kLoop, calls=%fused_computation | loop fusion | bytes 3784708 | tf_op jit(solution)/shard_map/dynamic_slice | solution.py:167
  7.4 1.7 %collective-permute-start.4 = (bf16[176,1792]{1,0:T(8,128)(2,1)S(1)}, bf16[176,1792]{1,0:T(8,128)(2,1)S(1)}, u32[]{:S(2)}, u32[]{:S(2)}) collective-permute-start(bf16[176,1792]{1,0:T(8,128)(2,1)S(1)} %get-tuple-element.17), channel_id=1, source_target_pairs={{0,4},{4,0},{1,5},{5,1},{2,6},{6,2},{3,7},{7,3},{8,12},{12,8},{9,1... | collective-permute-start | bytes 1892360 | tf_op jit(solution)/shard_map/ppermute | solution.py:170
  9.2 0.3 collective-permute-start.5
  9.5 1.7 %collective-permute-start.6 = (bf16[176,1792]{1,0:T(8,128)(2,1)S(1)}, bf16[176,1792]{1,0:T(8,128)(2,1)}, u32[]{:S(2)}, u32[]{:S(2)}) collective-permute-start(bf16[176,1792]{1,0:T(8,128)(2,1)S(1)} %get-tuple-element.16), channel_id=1, source_target_pairs={{0,4},{4,0},{1,5},{5,1},{2,6},{6,2},{3,7},{7,3},{8,12},{12,8},{9,1... | collective-permute-start | bytes 1892360 | tf_op jit(solution)/shard_map/ppermute | solution.py:170
  11.2 16.0 %collective-permute-done.refs_1_ = bf16[256,1792]{1,0:T(8,128)(2,1)S(1)} collective-permute-done((bf16[256,1792]{1,0:T(8,128)(2,1)}, bf16[256,1792]{1,0:T(8,128)(2,1)S(1)}, u32[]{:S(2)}, u32[]{:S(2)}) %collective-permute-start) | collective-permute-done | bytes 917536 | tf_op jit(solution)/shard_map/ppermute | solution.py:161
  27.2 1.6 %collective-permute-start.1 = (bf16[256,1792]{1,0:T(8,128)(2,1)S(1)}, bf16[256,1792]{1,0:T(8,128)(2,1)}, u32[]{:S(2)}, u32[]{:S(2)}) collective-permute-start(bf16[256,1792]{1,0:T(8,128)(2,1)S(1)} %collective-permute-done.refs_1_), channel_id=1, source_target_pairs={{1,2},{2,3},{5,6},{6,7},{9,10},{10,11},{13,14},{14,15},{17,18},{18... | collective-permute-start | bytes 2752520 | tf_op jit(solution)/shard_map/ppermute | solution.py:175
  28.8 16.6 %collective-permute-done.2.refs_2_ = bf16[256,1792]{1,0:T(8,128)(2,1)S(1)} collective-permute-done((bf16[256,1792]{1,0:T(8,128)(2,1)}, bf16[256,1792]{1,0:T(8,128)(2,1)S(1)}, u32[]{:S(2)}, u32[]{:S(2)}) %collective-permute-start.2) | collective-permute-done | bytes 917536 | tf_op jit(solution)/shard_map/ppermute | solution.py:162
  45.4 1.3 %collective-permute-start.3 = (bf16[256,1792]{1,0:T(8,128)(2,1)S(1)}, bf16[256,1792]{1,0:T(8,128)(2,1)}, u32[]{:S(2)}, u32[]{:S(2)}) collective-permute-start(bf16[256,1792]{1,0:T(8,128)(2,1)S(1)} %collective-permute-done.2.refs_2_), channel_id=1, source_target_pairs={{2,1},{1,0},{6,5},{5,4},{10,9},{9,8},{14,13},{13,12},{18,17},{17,1... | collective-permute-start | bytes 2752520 | tf_op jit(solution)/shard_map/ppermute | solution.py:176
  46.7 0.0 collective-permute-done.4.refs_5_
  46.7 0.1 collective-permute-start.7
  46.8 0.0 collective-permute-done.5.refs_6_
  46.8 0.5 collective-permute-start.8
  47.3 3.0 %collective-permute-done.6.refs_7_ = bf16[176,1792]{1,0:T(8,128)(2,1)} collective-permute-done((bf16[176,1792]{1,0:T(8,128)(2,1)S(1)}, bf16[176,1792]{1,0:T(8,128)(2,1)}, u32[]{:S(2)}, u32[]{:S(2)}) %collective-permute-start.6) | collective-permute-done | bytes 630816 | tf_op jit(solution)/shard_map/ppermute | solution.py:170
  50.3 0.0 collective-permute-start.9
  50.3 0.7 dynamic-slice_bitcast_fusion.3
  51.0 0.1 copy.10.where
  51.1 0.0 copy-done.4
  51.1 0.2 fusion
  51.3 0.0 collective-permute-done.7.refs_8_
  51.3 0.0 collective-permute-done.8.refs_9_
  51.3 1.4 %collective-permute-done.9.refs_10_ = bf16[176,1792]{1,0:T(8,128)(2,1)} collective-permute-done((bf16[176,1792]{1,0:T(8,128)(2,1)}, bf16[176,1792]{1,0:T(8,128)(2,1)}, u32[]{:S(2)}, u32[]{:S(2)}) %collective-permute-start.9) | collective-permute-done | bytes 630816 | tf_op jit(solution)/shard_map/ppermute | solution.py:172
  52.7 0.0 copy-done.1
  52.7 0.0 copy-done.2
  52.7 0.0 copy-start
  52.7 2.1 %copy-done = bf16[3584,528]{0,1:T(8,128)(2,1)S(1)} copy-done((bf16[3584,528]{0,1:T(8,128)(2,1)S(1)}, bf16[3584,528]{0,1:T(8,128)(2,1)}, u32[]{:S(2)}) %copy-start) | copy-done | bytes 3784728
  54.8 6.2 %shard_map.77 = (f32[256,528]{1,0:T(8,128)S(1)}, f32[256,1]{1,0:T(8,128)S(1)}, bf16[528,1792]{1,0:T(8,128)(2,1)S(1)}) custom-call(s32[5,4]{1,0:T(8,128)S(1)} %copy.10.where, bf16[256,1792]{1,0:T(8,128)(2,1)S(1)} %copy-done.1, bf16[256,1792]{1,0:T(8,128)(2,1)S(1)} %collective-permute-done.refs_1_, bf16[256,1792]{1,0:T(8,128)(2,1)S(1)} %collective-permute-done.2.refs_2_, ...), custom_call_target="tpu_custom_call" | custom-call | flops 1150000000 | bytes 917504 | tf_op jit(solution)/shard_map/pallas_call | solution.py:185
  60.9 0.0 collective-permute-done.1.refs_0_
  61.0 8.2 %collective-permute-done.3.refs_1_ = bf16[256,1792]{1,0:T(8,128)(2,1)} collective-permute-done((bf16[256,1792]{1,0:T(8,128)(2,1)S(1)}, bf16[256,1792]{1,0:T(8,128)(2,1)}, u32[]{:S(2)}, u32[]{:S(2)}) %collective-permute-start.3) | collective-permute-done | bytes 917536 | tf_op jit(solution)/shard_map/ppermute | solution.py:176
  69.2 0.0 copy-start.3
  69.2 2.5 %shard_map.78 = (bf16[64,528]{1,0:T(8,128)(2,1)S(1)}, bf16[64,528]{1,0:T(8,128)(2,1)S(1)}, bf16[64,528]{1,0:T(8,128)(2,1)S(1)}, bf16[64,528]{1,0:T(8,128)(2,1)S(1)}) custom-call(s32[5,4]{1,0:T(8,128)S(1)} %copy.10.where, bf16[256,1792]{1,0:T(8,128)(2,1)} %collective-permute-done.1.refs_0_, bf16[256,1792]{1,0:T(8,128)(2,1)} %collective-permute-done.3.refs_1_, ...), custom_call_target="tpu_custom_call" | custom-call | flops 2300000000 | bytes 917504 | tf_op jit(solution)/shard_map/pallas_call | solution.py:206
  71.7 0.1 collective-permute-start.10
  71.8 2.9 %collective-permute-start.11 = (bf16[64,528]{1,0:T(8,128)(2,1)S(1)}, bf16[64,528]{1,0:T(8,128)(2,1)S(1)}, u32[]{:S(2)}, u32[]{:S(2)}) collective-permute-start(bf16[64,528]{1,0:T(8,128)(2,1)S(1)} %get-tuple-element.13), channel_id=1, source_target_pairs={{0,9},{1,8},{2,11},{3,10},{8,17},{9,16},{10,19},{11,18},{16,25},{1... | collective-permute-start | bytes 202760 | tf_op jit(solution)/shard_map/ppermute | solution.py:221
  74.7 0.0 collective-permute-start.12
  74.7 2.3 %collective-permute-start.13 = (bf16[64,528]{1,0:T(8,128)(2,1)S(1)}, bf16[64,528]{1,0:T(8,128)(2,1)S(1)}, u32[]{:S(2)}, u32[]{:S(2)}) collective-permute-start(bf16[64,528]{1,0:T(8,128)(2,1)S(1)} %get-tuple-element.15), channel_id=1, source_target_pairs={{0,11},{1,10},{2,9},{3,8},{8,19},{9,18},{10,17},{11,16},{16,27},{1... | collective-permute-start | bytes 202760 | tf_op jit(solution)/shard_map/ppermute | solution.py:221
  77.0 0.1 pad_maximum_fusion
  77.1 0.0 collective-permute-done.10.refs_0_
  77.1 0.4 collective-permute-done.11.refs_1_
  77.5 6.4 %collective-permute-done.12.refs_2_ = bf16[64,528]{1,0:T(8,128)(2,1)S(1)} collective-permute-done((bf16[64,528]{1,0:T(8,128)(2,1)S(1)}, bf16[64,528]{1,0:T(8,128)(2,1)S(1)}, u32[]{:S(2)}, u32[]{:S(2)}) %collective-permute-start.12) | collective-permute-done | bytes 67616 | tf_op jit(solution)/shard_map/ppermute | solution.py:221
  83.9 0.0 collective-permute-done.13.refs_3_
  83.9 0.0 copy-done.3
  83.9 1.6 %shard_map.79 = (bf16[64,1536]{1,0:T(8,128)(2,1)}, bf16[64,576]{1,0:T(8,128)(2,1)}) custom-call(s32[5,4]{1,0:T(8,128)S(1)} %copy.10.where, bf16[64,528]{1,0:T(8,128)(2,1)S(1)} %collective-permute-done.10.refs_0_, bf16[64,528]{1,0:T(8,128)(2,1)S(1)} %collective-permute-done.11.refs_1_, bf16[64,528]{1,0:T(8,128)(2,1)S(1)} %collective-permute-done.12.refs_2_, ...), custom_call_target="tpu_custom_call" | custom-call | tf_op jit(solution)/shard_map/pallas_call | solution.py:228
  (3 shorter events, 0.0 us)
Async XLA Ops:
  0.6 52.1 %copy-start.1 = (bf16[256,1792]{1,0:T(8,128)(2,1)S(1)}, bf16[256,1792]{1,0:T(8,128)(2,1)}, u32[]{:S(2)}) copy-start(bf16[256,1792]{1,0:T(8,128)(2,1)} %refs_0_.1) | copy-start | bytes 2752516
  0.6 50.4 %copy-start.4 = (f32[1536]{0:T(1024)S(1)}, f32[1536]{0:T(1024)}, u32[]{:S(2)}) copy-start(f32[1536]{0:T(1024)} %param.8) | copy-start | bytes 18436
  0.6 52.0 %copy-start.2 = (f32[7168]{0:T(1024)S(1)}, f32[7168]{0:T(1024)}, u32[]{:S(2)}) copy-start(f32[7168]{0:T(1024)} %param.7) | copy-start | bytes 86020
  0.7 26.5 %collective-permute-start = (bf16[256,1792]{1,0:T(8,128)(2,1)}, bf16[256,1792]{1,0:T(8,128)(2,1)S(1)}, u32[]{:S(2)}, u32[]{:S(2)}) collective-permute-start(bf16[256,1792]{1,0:T(8,128)(2,1)} %refs_0_.1), channel_id=1, source_target_pairs={{0,1},{1,2},{2,3},{3,0},{4,5},{5,6},{6,7},{7,4},{8,9},{9,10},{10,1... | collective-permute-start | bytes 2752520 | tf_op jit(solution)/shard_map/ppermute | solution.py:161
  3.7 41.7 %collective-permute-start.2 = (bf16[256,1792]{1,0:T(8,128)(2,1)}, bf16[256,1792]{1,0:T(8,128)(2,1)S(1)}, u32[]{:S(2)}, u32[]{:S(2)}) collective-permute-start(bf16[256,1792]{1,0:T(8,128)(2,1)} %refs_0_.1), channel_id=1, source_target_pairs={{0,3},{1,0},{2,1},{3,2},{4,7},{5,4},{6,5},{7,6},{8,11},{9,8},{10,9... | collective-permute-start | bytes 2752520 | tf_op jit(solution)/shard_map/ppermute | solution.py:162
  7.4 39.3 %collective-permute-start.4 = (bf16[176,1792]{1,0:T(8,128)(2,1)S(1)}, bf16[176,1792]{1,0:T(8,128)(2,1)S(1)}, u32[]{:S(2)}, u32[]{:S(2)}) collective-permute-start(bf16[176,1792]{1,0:T(8,128)(2,1)S(1)} %get-tuple-element.17), channel_id=1, source_target_pairs={{0,4},{4,0},{1,5},{5,1},{2,6},{6,2},{3,7},{7,3},{8,12},{12,8},{9,1... | collective-permute-start | bytes 1892360 | tf_op jit(solution)/shard_map/ppermute | solution.py:170
  9.2 37.6 %collective-permute-start.5 = (bf16[176,1792]{1,0:T(8,128)(2,1)S(1)}, bf16[176,1792]{1,0:T(8,128)(2,1)}, u32[]{:S(2)}, u32[]{:S(2)}) collective-permute-start(bf16[176,1792]{1,0:T(8,128)(2,1)S(1)} %get-tuple-element.18), channel_id=1, source_target_pairs={{0,4},{4,0},{1,5},{5,1},{2,6},{6,2},{3,7},{7,3},{8,12},{12,8},{9,1... | collective-permute-start | bytes 1892360 | tf_op jit(solution)/shard_map/ppermute | solution.py:170
  9.5 40.8 %collective-permute-start.6 = (bf16[176,1792]{1,0:T(8,128)(2,1)S(1)}, bf16[176,1792]{1,0:T(8,128)(2,1)}, u32[]{:S(2)}, u32[]{:S(2)}) collective-permute-start(bf16[176,1792]{1,0:T(8,128)(2,1)S(1)} %get-tuple-element.16), channel_id=1, source_target_pairs={{0,4},{4,0},{1,5},{5,1},{2,6},{6,2},{3,7},{7,3},{8,12},{12,8},{9,1... | collective-permute-start | bytes 1892360 | tf_op jit(solution)/shard_map/ppermute | solution.py:170
  27.2 33.8 %collective-permute-start.1 = (bf16[256,1792]{1,0:T(8,128)(2,1)S(1)}, bf16[256,1792]{1,0:T(8,128)(2,1)}, u32[]{:S(2)}, u32[]{:S(2)}) collective-permute-start(bf16[256,1792]{1,0:T(8,128)(2,1)S(1)} %collective-permute-done.refs_1_), channel_id=1, source_target_pairs={{1,2},{2,3},{5,6},{6,7},{9,10},{10,11},{13,14},{14,15},{17,18},{18... | collective-permute-start | bytes 2752520 | tf_op jit(solution)/shard_map/ppermute | solution.py:175
  45.4 23.8 %collective-permute-start.3 = (bf16[256,1792]{1,0:T(8,128)(2,1)S(1)}, bf16[256,1792]{1,0:T(8,128)(2,1)}, u32[]{:S(2)}, u32[]{:S(2)}) collective-permute-start(bf16[256,1792]{1,0:T(8,128)(2,1)S(1)} %collective-permute-done.2.refs_2_), channel_id=1, source_target_pairs={{2,1},{1,0},{6,5},{5,4},{10,9},{9,8},{14,13},{13,12},{18,17},{17,1... | collective-permute-start | bytes 2752520 | tf_op jit(solution)/shard_map/ppermute | solution.py:176
  46.7 4.6 %collective-permute-start.7 = (bf16[176,1792]{1,0:T(8,128)(2,1)S(1)}, bf16[176,1792]{1,0:T(8,128)(2,1)}, u32[]{:S(2)}, u32[]{:S(2)}) collective-permute-start(bf16[176,1792]{1,0:T(8,128)(2,1)S(1)} %collective-permute-done.4.refs_5_), channel_id=1, source_target_pairs={{0,8},{8,0},{16,24},{24,16},{1,9},{9,1},{17,25},{25,17},{2,10},{10... | collective-permute-start | bytes 1892360 | tf_op jit(solution)/shard_map/ppermute | solution.py:172
  46.8 4.5 %collective-permute-start.8 = (bf16[176,1792]{1,0:T(8,128)(2,1)}, bf16[176,1792]{1,0:T(8,128)(2,1)}, u32[]{:S(2)}, u32[]{:S(2)}) collective-permute-start(bf16[176,1792]{1,0:T(8,128)(2,1)} %collective-permute-done.5.refs_6_), channel_id=1, source_target_pairs={{0,8},{8,0},{16,24},{24,16},{1,9},{9,1},{17,25},{25,17},{2,10},{10... | collective-permute-start | bytes 1892360 | tf_op jit(solution)/shard_map/ppermute | solution.py:172
  50.3 2.4 %collective-permute-start.9 = (bf16[176,1792]{1,0:T(8,128)(2,1)}, bf16[176,1792]{1,0:T(8,128)(2,1)}, u32[]{:S(2)}, u32[]{:S(2)}) collective-permute-start(bf16[176,1792]{1,0:T(8,128)(2,1)} %collective-permute-done.6.refs_7_), channel_id=1, source_target_pairs={{0,8},{8,0},{16,24},{24,16},{1,9},{9,1},{17,25},{25,17},{2,10},{10... | collective-permute-start | bytes 1892360 | tf_op jit(solution)/shard_map/ppermute | solution.py:172
  52.7 2.1 %copy-start = (bf16[3584,528]{0,1:T(8,128)(2,1)S(1)}, bf16[3584,528]{0,1:T(8,128)(2,1)}, u32[]{:S(2)}) copy-start(bf16[3584,528]{0,1:T(8,128)(2,1)} %param.10) | copy-start | bytes 11354116
  69.2 14.8 %copy-start.3 = (f32[512]{0:T(512)S(1)}, f32[512]{0:T(512)}, u32[]{:S(2)}) copy-start(f32[512]{0:T(512)} %param.9) | copy-start | bytes 6148
  71.7 5.4 %collective-permute-start.10 = (bf16[64,528]{1,0:T(8,128)(2,1)S(1)}, bf16[64,528]{1,0:T(8,128)(2,1)S(1)}, u32[]{:S(2)}, u32[]{:S(2)}) collective-permute-start(bf16[64,528]{1,0:T(8,128)(2,1)S(1)} %get-tuple-element.12), channel_id=1, source_target_pairs={{0,8},{1,9},{2,10},{3,11},{8,16},{9,17},{10,18},{11,19},{16,24},{1... | collective-permute-start | bytes 202760 | tf_op jit(solution)/shard_map/ppermute | solution.py:221
  71.8 5.7 %collective-permute-start.11 = (bf16[64,528]{1,0:T(8,128)(2,1)S(1)}, bf16[64,528]{1,0:T(8,128)(2,1)S(1)}, u32[]{:S(2)}, u32[]{:S(2)}) collective-permute-start(bf16[64,528]{1,0:T(8,128)(2,1)S(1)} %get-tuple-element.13), channel_id=1, source_target_pairs={{0,9},{1,8},{2,11},{3,10},{8,17},{9,16},{10,19},{11,18},{16,25},{1... | collective-permute-start | bytes 202760 | tf_op jit(solution)/shard_map/ppermute | solution.py:221
  74.7 9.2 %collective-permute-start.12 = (bf16[64,528]{1,0:T(8,128)(2,1)S(1)}, bf16[64,528]{1,0:T(8,128)(2,1)S(1)}, u32[]{:S(2)}, u32[]{:S(2)}) collective-permute-start(bf16[64,528]{1,0:T(8,128)(2,1)S(1)} %get-tuple-element.14), channel_id=1, source_target_pairs={{0,10},{1,11},{2,8},{3,9},{8,18},{9,19},{10,16},{11,17},{16,26},{1... | collective-permute-start | bytes 202760 | tf_op jit(solution)/shard_map/ppermute | solution.py:221
  74.7 9.2 %collective-permute-start.13 = (bf16[64,528]{1,0:T(8,128)(2,1)S(1)}, bf16[64,528]{1,0:T(8,128)(2,1)S(1)}, u32[]{:S(2)}, u32[]{:S(2)}) collective-permute-start(bf16[64,528]{1,0:T(8,128)(2,1)S(1)} %get-tuple-element.15), channel_id=1, source_target_pairs={{0,11},{1,10},{2,9},{3,8},{8,19},{9,18},{10,17},{11,16},{16,27},{1... | collective-permute-start | bytes 202760 | tf_op jit(solution)/shard_map/ppermute | solution.py:221

commit v6 on v5

--- a/solution.py
+++ b/solution.py
@@ -110,7 +110,7 @@
     q_gain_ref, kv_gain_ref, cosine_ref, sine_ref, query_ref, cache_ref, parts = refs
     share = part_refs[0].shape[0]
     for index, ref in enumerate(part_refs):
-        chunk, turn = index // PLANES, index % PLANES
+        chunk, turn = index // PLANES, PLANES - 1 - index % PLANES
         parts[where[4, turn], chunk * share : (chunk + 1) * share] = ref[...].astype(jnp.float32)
     latent = jnp.concatenate([parts[plane] for plane in range(PLANES)], axis=1)
 
@@ -212,13 +212,15 @@
             compiler_params=limits,
             cost_estimate=cost(LAST_COSTS[chunk]),
         )(where, below_far[chunk], above_far[chunk], gain, last_weight, total, squares)
-        for turn in range(PLANES):
+        arrived = {}
+        for turn in reversed(range(PLANES)):
             moves = [
                 (s * PLANES + z, (s + 1) % section * PLANES + (z ^ turn))
                 for s in range(section)
                 for z in range(PLANES)
             ]
-            received.append(lax.ppermute(messages[turn], ("section", "ep"), moves))
+            arrived[turn] = lax.ppermute(messages[turn], ("section", "ep"), moves)
+        received += list(arrived.values())
 
     half = ROPE // 2
     position = (fsdp_index * row_count + ep_index * quarter + jnp.arange(quarter)) % LENGTH

time: 85.8 us -> 83.8 us (0.977)
  waiting for transfers between devices: 52 us -> 50.1 us
    ppermute x4, waiting for transfers between devices: 6.78 us -> 4.93 us  [on_device(): arrived[turn] = lax.ppermute(messages[turn], ('section', 'ep'), moves)]
  transfers between devices with their start and end apart: 14 -> 14, of which waited for: 7 -> 9; matrix products, arithmetic and copies ran while one was open for 3% -> 3% of each run, Pallas kernels for 7% -> 7%
where the time goes in v6:
time: 83.8 us; the launch traced here: 83.5 us
  waiting for transfers between devices  50.1 us (60%)
  starting transfers between devices  17.5 us (21%)
  Pallas kernels  10.3 us (12%)
  local copies, waits for them, and re-layouts  4.45 us (5%)
    ppermute x1, waiting for transfers between devices, on_device(): above = [lax.ppermute(block, 'ep', down) for block in own]  16.6 us
    ppermute x1, waiting for transfers between devices, on_device(): below = [lax.ppermute(block, 'ep', up) for block in own]  16 us
    ppermute x1, waiting for transfers between devices, on_device(): above_far = [lax.ppermute(block, 'ep', [(2, 1), (1, 0)]) for block in above]  8.22 us
    pallas_call x1, Pallas kernels, on_device(): pl.pallas_call(functools.partial(near_kernel, CHUNKS, [len(parts) for par...  6.17 us
    ppermute x4, starting transfers between devices, on_device(): arrived[turn] = lax.ppermute(messages[turn], ('section', 'ep'), moves)  5.17 us
    ppermute x4, waiting for transfers between devices, on_device(): arrived[turn] = lax.ppermute(messages[turn], ('section', 'ep'), moves)  4.93 us
    ppermute x3, starting transfers between devices, on_device(): here = [lax.ppermute(part, 'fsdp', [(0, 1), (1, 0)]) for part in here]  3.77 us
    ppermute x1, starting transfers between devices, on_device(): below = [lax.ppermute(block, 'ep', up) for block in own]  3.08 us
  transfers between devices with their start and end apart: 14, of which 9 were waited for; matrix products, arithmetic and copies ran while one was open for 3% of the time, Pallas kernels for 7%

profile of v6, /device:TPU:0, one launch (start us, length us, event | category | flops | bytes accessed | tf_op | source)
XLA Modules:
  0.0 83.5 jit_solution(11478036797342443355)
XLA Ops:
  0.6 0.0 copy-start.1
  0.6 0.0 copy-start.4
  0.6 0.0 copy-start.2
  0.7 3.1 %collective-permute-start = (bf16[256,1792]{1,0:T(8,128)(2,1)}, bf16[256,1792]{1,0:T(8,128)(2,1)S(1)}, u32[]{:S(2)}, u32[]{:S(2)}) collective-permute-start(bf16[256,1792]{1,0:T(8,128)(2,1)} %refs_0_.1), channel_id=1, source_target_pairs={{0,1},{1,2},{2,3},{3,0},{4,5},{5,6},{6,7},{7,4},{8,9},{9,10},{10,1... | collective-permute-start | bytes 2752520 | tf_op jit(solution)/shard_map/ppermute | solution.py:161
  3.7 2.1 %collective-permute-start.2 = (bf16[256,1792]{1,0:T(8,128)(2,1)}, bf16[256,1792]{1,0:T(8,128)(2,1)S(1)}, u32[]{:S(2)}, u32[]{:S(2)}) collective-permute-start(bf16[256,1792]{1,0:T(8,128)(2,1)} %refs_0_.1), channel_id=1, source_target_pairs={{0,3},{1,0},{2,1},{3,2},{4,7},{5,4},{6,5},{7,6},{8,11},{9,8},{10,9... | collective-permute-start | bytes 2752520 | tf_op jit(solution)/shard_map/ppermute | solution.py:162
  5.8 1.6 %dynamic-slice_bitcast_fusion = (bf16[176,1792]{1,0:T(8,128)(2,1)S(1)}, bf16[176,1792]{1,0:T(8,128)(2,1)S(1)}, bf16[176,1792]{1,0:T(8,128)(2,1)S(1)}) fusion(bf16[3584,528]{0,1:T(8,128)(2,1)} %param.10, s32[]{:T(128)S(6)} %select_n.37), kind=kLoop, calls=%fused_computation | loop fusion | bytes 3784708 | tf_op jit(solution)/shard_map/dynamic_slice | solution.py:167
  7.4 1.7 %collective-permute-start.4 = (bf16[176,1792]{1,0:T(8,128)(2,1)S(1)}, bf16[176,1792]{1,0:T(8,128)(2,1)S(1)}, u32[]{:S(2)}, u32[]{:S(2)}) collective-permute-start(bf16[176,1792]{1,0:T(8,128)(2,1)S(1)} %get-tuple-element.17), channel_id=1, source_target_pairs={{0,4},{4,0},{1,5},{5,1},{2,6},{6,2},{3,7},{7,3},{8,12},{12,8},{9,1... | collective-permute-start | bytes 1892360 | tf_op jit(solution)/shard_map/ppermute | solution.py:170
  9.2 0.3 collective-permute-start.5
  9.5 1.7 %collective-permute-start.6 = (bf16[176,1792]{1,0:T(8,128)(2,1)S(1)}, bf16[176,1792]{1,0:T(8,128)(2,1)}, u32[]{:S(2)}, u32[]{:S(2)}) collective-permute-start(bf16[176,1792]{1,0:T(8,128)(2,1)S(1)} %get-tuple-element.16), channel_id=1, source_target_pairs={{0,4},{4,0},{1,5},{5,1},{2,6},{6,2},{3,7},{7,3},{8,12},{12,8},{9,1... | collective-permute-start | bytes 1892360 | tf_op jit(solution)/shard_map/ppermute | solution.py:170
  11.2 16.0 %collective-permute-done.refs_1_ = bf16[256,1792]{1,0:T(8,128)(2,1)S(1)} collective-permute-done((bf16[256,1792]{1,0:T(8,128)(2,1)}, bf16[256,1792]{1,0:T(8,128)(2,1)S(1)}, u32[]{:S(2)}, u32[]{:S(2)}) %collective-permute-start) | collective-permute-done | bytes 917536 | tf_op jit(solution)/shard_map/ppermute | solution.py:161
  27.2 1.6 %collective-permute-start.1 = (bf16[256,1792]{1,0:T(8,128)(2,1)S(1)}, bf16[256,1792]{1,0:T(8,128)(2,1)}, u32[]{:S(2)}, u32[]{:S(2)}) collective-permute-start(bf16[256,1792]{1,0:T(8,128)(2,1)S(1)} %collective-permute-done.refs_1_), channel_id=1, source_target_pairs={{1,2},{2,3},{5,6},{6,7},{9,10},{10,11},{13,14},{14,15},{17,18},{18... | collective-permute-start | bytes 2752520 | tf_op jit(solution)/shard_map/ppermute | solution.py:175
  28.8 16.6 %collective-permute-done.2.refs_2_ = bf16[256,1792]{1,0:T(8,128)(2,1)S(1)} collective-permute-done((bf16[256,1792]{1,0:T(8,128)(2,1)}, bf16[256,1792]{1,0:T(8,128)(2,1)S(1)}, u32[]{:S(2)}, u32[]{:S(2)}) %collective-permute-start.2) | collective-permute-done | bytes 917536 | tf_op jit(solution)/shard_map/ppermute | solution.py:162
  45.4 1.3 %collective-permute-start.3 = (bf16[256,1792]{1,0:T(8,128)(2,1)S(1)}, bf16[256,1792]{1,0:T(8,128)(2,1)}, u32[]{:S(2)}, u32[]{:S(2)}) collective-permute-start(bf16[256,1792]{1,0:T(8,128)(2,1)S(1)} %collective-permute-done.2.refs_2_), channel_id=1, source_target_pairs={{2,1},{1,0},{6,5},{5,4},{10,9},{9,8},{14,13},{13,12},{18,17},{17,1... | collective-permute-start | bytes 2752520 | tf_op jit(solution)/shard_map/ppermute | solution.py:176
  46.7 0.0 collective-permute-done.4.refs_5_
  46.7 0.1 collective-permute-start.7
  46.8 0.0 collective-permute-done.5.refs_6_
  46.8 0.5 collective-permute-start.8
  47.3 3.0 %collective-permute-done.6.refs_7_ = bf16[176,1792]{1,0:T(8,128)(2,1)} collective-permute-done((bf16[176,1792]{1,0:T(8,128)(2,1)S(1)}, bf16[176,1792]{1,0:T(8,128)(2,1)}, u32[]{:S(2)}, u32[]{:S(2)}) %collective-permute-start.6) | collective-permute-done | bytes 630816 | tf_op jit(solution)/shard_map/ppermute | solution.py:170
  50.3 0.0 collective-permute-start.9
  50.3 0.7 dynamic-slice_bitcast_fusion.3
  51.0 0.1 copy.10.where
  51.1 0.0 copy-done.4
  51.1 0.2 fusion
  51.3 0.0 collective-permute-done.7.refs_8_
  51.3 0.0 collective-permute-done.8.refs_9_
  51.3 1.4 %collective-permute-done.9.refs_10_ = bf16[176,1792]{1,0:T(8,128)(2,1)} collective-permute-done((bf16[176,1792]{1,0:T(8,128)(2,1)}, bf16[176,1792]{1,0:T(8,128)(2,1)}, u32[]{:S(2)}, u32[]{:S(2)}) %collective-permute-start.9) | collective-permute-done | bytes 630816 | tf_op jit(solution)/shard_map/ppermute | solution.py:172
  52.7 0.0 copy-done.1
  52.7 0.0 copy-done.2
  52.7 0.0 copy-start
  52.7 2.1 %copy-done = bf16[3584,528]{0,1:T(8,128)(2,1)S(1)} copy-done((bf16[3584,528]{0,1:T(8,128)(2,1)S(1)}, bf16[3584,528]{0,1:T(8,128)(2,1)}, u32[]{:S(2)}) %copy-start) | copy-done | bytes 3784728
  54.8 6.2 %shard_map.77 = (f32[256,528]{1,0:T(8,128)S(1)}, f32[256,1]{1,0:T(8,128)S(1)}, bf16[528,1792]{1,0:T(8,128)(2,1)S(1)}) custom-call(s32[5,4]{1,0:T(8,128)S(1)} %copy.10.where, bf16[256,1792]{1,0:T(8,128)(2,1)S(1)} %copy-done.1, bf16[256,1792]{1,0:T(8,128)(2,1)S(1)} %collective-permute-done.refs_1_, bf16[256,1792]{1,0:T(8,128)(2,1)S(1)} %collective-permute-done.2.refs_2_, ...), custom_call_target="tpu_custom_call" | custom-call | flops 1150000000 | bytes 917504 | tf_op jit(solution)/shard_map/pallas_call | solution.py:185
  60.9 0.0 collective-permute-done.1.refs_0_
  61.0 8.2 %collective-permute-done.3.refs_1_ = bf16[256,1792]{1,0:T(8,128)(2,1)} collective-permute-done((bf16[256,1792]{1,0:T(8,128)(2,1)S(1)}, bf16[256,1792]{1,0:T(8,128)(2,1)}, u32[]{:S(2)}, u32[]{:S(2)}) %collective-permute-start.3) | collective-permute-done | bytes 917536 | tf_op jit(solution)/shard_map/ppermute | solution.py:176
  69.2 0.0 copy-start.3
  69.2 2.5 %shard_map.78 = (bf16[64,528]{1,0:T(8,128)(2,1)S(1)}, bf16[64,528]{1,0:T(8,128)(2,1)S(1)}, bf16[64,528]{1,0:T(8,128)(2,1)S(1)}, bf16[64,528]{1,0:T(8,128)(2,1)S(1)}) custom-call(s32[5,4]{1,0:T(8,128)S(1)} %copy.10.where, bf16[256,1792]{1,0:T(8,128)(2,1)} %collective-permute-done.1.refs_0_, bf16[256,1792]{1,0:T(8,128)(2,1)} %collective-permute-done.3.refs_1_, ...), custom_call_target="tpu_custom_call" | custom-call | flops 2300000000 | bytes 917504 | tf_op jit(solution)/shard_map/pallas_call | solution.py:206
  71.7 0.1 collective-permute-start.10
  71.8 3.8 %collective-permute-start.11 = (bf16[64,528]{1,0:T(8,128)(2,1)S(1)}, bf16[64,528]{1,0:T(8,128)(2,1)S(1)}, u32[]{:S(2)}, u32[]{:S(2)}) collective-permute-start(bf16[64,528]{1,0:T(8,128)(2,1)S(1)} %get-tuple-element.13), channel_id=1, source_target_pairs={{0,10},{1,11},{2,8},{3,9},{8,18},{9,19},{10,16},{11,17},{16,26},{1... | collective-permute-start | bytes 202760 | tf_op jit(solution)/shard_map/ppermute | solution.py:222
  75.6 0.0 collective-permute-start.12
  75.6 1.3 %collective-permute-start.13 = (bf16[64,528]{1,0:T(8,128)(2,1)S(1)}, bf16[64,528]{1,0:T(8,128)(2,1)S(1)}, u32[]{:S(2)}, u32[]{:S(2)}) collective-permute-start(bf16[64,528]{1,0:T(8,128)(2,1)S(1)} %get-tuple-element.15), channel_id=1, source_target_pairs={{0,8},{1,9},{2,10},{3,11},{8,16},{9,17},{10,18},{11,19},{16,24},{1... | collective-permute-start | bytes 202760 | tf_op jit(solution)/shard_map/ppermute | solution.py:222
  76.9 0.1 pad_maximum_fusion
  77.0 2.3 %collective-permute-done.10.refs_0_ = bf16[64,528]{1,0:T(8,128)(2,1)S(1)} collective-permute-done((bf16[64,528]{1,0:T(8,128)(2,1)S(1)}, bf16[64,528]{1,0:T(8,128)(2,1)S(1)}, u32[]{:S(2)}, u32[]{:S(2)}) %collective-permute-start.10) | collective-permute-done | bytes 67616 | tf_op jit(solution)/shard_map/ppermute | solution.py:222
  79.3 2.1 %collective-permute-done.11.refs_1_ = bf16[64,528]{1,0:T(8,128)(2,1)S(1)} collective-permute-done((bf16[64,528]{1,0:T(8,128)(2,1)S(1)}, bf16[64,528]{1,0:T(8,128)(2,1)S(1)}, u32[]{:S(2)}, u32[]{:S(2)}) %collective-permute-start.11) | collective-permute-done | bytes 67616 | tf_op jit(solution)/shard_map/ppermute | solution.py:222
  81.4 0.1 collective-permute-done.12.refs_2_
  81.5 0.4 collective-permute-done.13.refs_3_
  81.9 0.0 copy-done.3
  81.9 1.6 %shard_map.79 = (bf16[64,1536]{1,0:T(8,128)(2,1)}, bf16[64,576]{1,0:T(8,128)(2,1)}) custom-call(s32[5,4]{1,0:T(8,128)S(1)} %copy.10.where, bf16[64,528]{1,0:T(8,128)(2,1)S(1)} %collective-permute-done.10.refs_0_, bf16[64,528]{1,0:T(8,128)(2,1)S(1)} %collective-permute-done.11.refs_1_, bf16[64,528]{1,0:T(8,128)(2,1)S(1)} %collective-permute-done.12.refs_2_, ...), custom_call_target="tpu_custom_call" | custom-call | tf_op jit(solution)/shard_map/pallas_call | solution.py:230
  (3 shorter events, 0.0 us)
Async XLA Ops:
  0.6 52.1 %copy-start.1 = (bf16[256,1792]{1,0:T(8,128)(2,1)S(1)}, bf16[256,1792]{1,0:T(8,128)(2,1)}, u32[]{:S(2)}) copy-start(bf16[256,1792]{1,0:T(8,128)(2,1)} %refs_0_.1) | copy-start | bytes 2752516
  0.6 50.4 %copy-start.4 = (f32[1536]{0:T(1024)S(1)}, f32[1536]{0:T(1024)}, u32[]{:S(2)}) copy-start(f32[1536]{0:T(1024)} %param.8) | copy-start | bytes 18436
  0.6 52.0 %copy-start.2 = (f32[7168]{0:T(1024)S(1)}, f32[7168]{0:T(1024)}, u32[]{:S(2)}) copy-start(f32[7168]{0:T(1024)} %param.7) | copy-start | bytes 86020
  0.7 26.5 %collective-permute-start = (bf16[256,1792]{1,0:T(8,128)(2,1)}, bf16[256,1792]{1,0:T(8,128)(2,1)S(1)}, u32[]{:S(2)}, u32[]{:S(2)}) collective-permute-start(bf16[256,1792]{1,0:T(8,128)(2,1)} %refs_0_.1), channel_id=1, source_target_pairs={{0,1},{1,2},{2,3},{3,0},{4,5},{5,6},{6,7},{7,4},{8,9},{9,10},{10,1... | collective-permute-start | bytes 2752520 | tf_op jit(solution)/shard_map/ppermute | solution.py:161
  3.7 41.7 %collective-permute-start.2 = (bf16[256,1792]{1,0:T(8,128)(2,1)}, bf16[256,1792]{1,0:T(8,128)(2,1)S(1)}, u32[]{:S(2)}, u32[]{:S(2)}) collective-permute-start(bf16[256,1792]{1,0:T(8,128)(2,1)} %refs_0_.1), channel_id=1, source_target_pairs={{0,3},{1,0},{2,1},{3,2},{4,7},{5,4},{6,5},{7,6},{8,11},{9,8},{10,9... | collective-permute-start | bytes 2752520 | tf_op jit(solution)/shard_map/ppermute | solution.py:162
  7.4 39.3 %collective-permute-start.4 = (bf16[176,1792]{1,0:T(8,128)(2,1)S(1)}, bf16[176,1792]{1,0:T(8,128)(2,1)S(1)}, u32[]{:S(2)}, u32[]{:S(2)}) collective-permute-start(bf16[176,1792]{1,0:T(8,128)(2,1)S(1)} %get-tuple-element.17), channel_id=1, source_target_pairs={{0,4},{4,0},{1,5},{5,1},{2,6},{6,2},{3,7},{7,3},{8,12},{12,8},{9,1... | collective-permute-start | bytes 1892360 | tf_op jit(solution)/shard_map/ppermute | solution.py:170
  9.2 37.6 %collective-permute-start.5 = (bf16[176,1792]{1,0:T(8,128)(2,1)S(1)}, bf16[176,1792]{1,0:T(8,128)(2,1)}, u32[]{:S(2)}, u32[]{:S(2)}) collective-permute-start(bf16[176,1792]{1,0:T(8,128)(2,1)S(1)} %get-tuple-element.18), channel_id=1, source_target_pairs={{0,4},{4,0},{1,5},{5,1},{2,6},{6,2},{3,7},{7,3},{8,12},{12,8},{9,1... | collective-permute-start | bytes 1892360 | tf_op jit(solution)/shard_map/ppermute | solution.py:170
  9.5 40.8 %collective-permute-start.6 = (bf16[176,1792]{1,0:T(8,128)(2,1)S(1)}, bf16[176,1792]{1,0:T(8,128)(2,1)}, u32[]{:S(2)}, u32[]{:S(2)}) collective-permute-start(bf16[176,1792]{1,0:T(8,128)(2,1)S(1)} %get-tuple-element.16), channel_id=1, source_target_pairs={{0,4},{4,0},{1,5},{5,1},{2,6},{6,2},{3,7},{7,3},{8,12},{12,8},{9,1... | collective-permute-start | bytes 1892360 | tf_op jit(solution)/shard_map/ppermute | solution.py:170
  27.2 33.8 %collective-permute-start.1 = (bf16[256,1792]{1,0:T(8,128)(2,1)S(1)}, bf16[256,1792]{1,0:T(8,128)(2,1)}, u32[]{:S(2)}, u32[]{:S(2)}) collective-permute-start(bf16[256,1792]{1,0:T(8,128)(2,1)S(1)} %collective-permute-done.refs_1_), channel_id=1, source_target_pairs={{1,2},{2,3},{5,6},{6,7},{9,10},{10,11},{13,14},{14,15},{17,18},{18... | collective-permute-start | bytes 2752520 | tf_op jit(solution)/shard_map/ppermute | solution.py:175
  45.4 23.8 %collective-permute-start.3 = (bf16[256,1792]{1,0:T(8,128)(2,1)S(1)}, bf16[256,1792]{1,0:T(8,128)(2,1)}, u32[]{:S(2)}, u32[]{:S(2)}) collective-permute-start(bf16[256,1792]{1,0:T(8,128)(2,1)S(1)} %collective-permute-done.2.refs_2_), channel_id=1, source_target_pairs={{2,1},{1,0},{6,5},{5,4},{10,9},{9,8},{14,13},{13,12},{18,17},{17,1... | collective-permute-start | bytes 2752520 | tf_op jit(solution)/shard_map/ppermute | solution.py:176
  46.7 4.6 %collective-permute-start.7 = (bf16[176,1792]{1,0:T(8,128)(2,1)S(1)}, bf16[176,1792]{1,0:T(8,128)(2,1)}, u32[]{:S(2)}, u32[]{:S(2)}) collective-permute-start(bf16[176,1792]{1,0:T(8,128)(2,1)S(1)} %collective-permute-done.4.refs_5_), channel_id=1, source_target_pairs={{0,8},{8,0},{16,24},{24,16},{1,9},{9,1},{17,25},{25,17},{2,10},{10... | collective-permute-start | bytes 1892360 | tf_op jit(solution)/shard_map/ppermute | solution.py:172
  46.8 4.5 %collective-permute-start.8 = (bf16[176,1792]{1,0:T(8,128)(2,1)}, bf16[176,1792]{1,0:T(8,128)(2,1)}, u32[]{:S(2)}, u32[]{:S(2)}) collective-permute-start(bf16[176,1792]{1,0:T(8,128)(2,1)} %collective-permute-done.5.refs_6_), channel_id=1, source_target_pairs={{0,8},{8,0},{16,24},{24,16},{1,9},{9,1},{17,25},{25,17},{2,10},{10... | collective-permute-start | bytes 1892360 | tf_op jit(solution)/shard_map/ppermute | solution.py:172
  50.3 2.4 %collective-permute-start.9 = (bf16[176,1792]{1,0:T(8,128)(2,1)}, bf16[176,1792]{1,0:T(8,128)(2,1)}, u32[]{:S(2)}, u32[]{:S(2)}) collective-permute-start(bf16[176,1792]{1,0:T(8,128)(2,1)} %collective-permute-done.6.refs_7_), channel_id=1, source_target_pairs={{0,8},{8,0},{16,24},{24,16},{1,9},{9,1},{17,25},{25,17},{2,10},{10... | collective-permute-start | bytes 1892360 | tf_op jit(solution)/shard_map/ppermute | solution.py:172
  52.7 2.1 %copy-start = (bf16[3584,528]{0,1:T(8,128)(2,1)S(1)}, bf16[3584,528]{0,1:T(8,128)(2,1)}, u32[]{:S(2)}) copy-start(bf16[3584,528]{0,1:T(8,128)(2,1)} %param.10) | copy-start | bytes 11354116
  69.2 12.7 %copy-start.3 = (f32[512]{0:T(512)S(1)}, f32[512]{0:T(512)}, u32[]{:S(2)}) copy-start(f32[512]{0:T(512)} %param.9) | copy-start | bytes 6148
  71.7 7.6 %collective-permute-start.10 = (bf16[64,528]{1,0:T(8,128)(2,1)S(1)}, bf16[64,528]{1,0:T(8,128)(2,1)S(1)}, u32[]{:S(2)}, u32[]{:S(2)}) collective-permute-start(bf16[64,528]{1,0:T(8,128)(2,1)S(1)} %get-tuple-element.12), channel_id=1, source_target_pairs={{0,11},{1,10},{2,9},{3,8},{8,19},{9,18},{10,17},{11,16},{16,27},{1... | collective-permute-start | bytes 202760 | tf_op jit(solution)/shard_map/ppermute | solution.py:222
  71.8 9.6 %collective-permute-start.11 = (bf16[64,528]{1,0:T(8,128)(2,1)S(1)}, bf16[64,528]{1,0:T(8,128)(2,1)S(1)}, u32[]{:S(2)}, u32[]{:S(2)}) collective-permute-start(bf16[64,528]{1,0:T(8,128)(2,1)S(1)} %get-tuple-element.13), channel_id=1, source_target_pairs={{0,10},{1,11},{2,8},{3,9},{8,18},{9,19},{10,16},{11,17},{16,26},{1... | collective-permute-start | bytes 202760 | tf_op jit(solution)/shard_map/ppermute | solution.py:222
  75.6 5.9 %collective-permute-start.12 = (bf16[64,528]{1,0:T(8,128)(2,1)S(1)}, bf16[64,528]{1,0:T(8,128)(2,1)S(1)}, u32[]{:S(2)}, u32[]{:S(2)}) collective-permute-start(bf16[64,528]{1,0:T(8,128)(2,1)S(1)} %get-tuple-element.14), channel_id=1, source_target_pairs={{0,9},{1,8},{2,11},{3,10},{8,17},{9,16},{10,19},{11,18},{16,25},{1... | collective-permute-start | bytes 202760 | tf_op jit(solution)/shard_map/ppermute | solution.py:222
  75.6 6.3 %collective-permute-start.13 = (bf16[64,528]{1,0:T(8,128)(2,1)S(1)}, bf16[64,528]{1,0:T(8,128)(2,1)S(1)}, u32[]{:S(2)}, u32[]{:S(2)}) collective-permute-start(bf16[64,528]{1,0:T(8,128)(2,1)S(1)} %get-tuple-element.15), channel_id=1, source_target_pairs={{0,8},{1,9},{2,10},{3,11},{8,16},{9,17},{10,18},{11,19},{16,24},{1... | collective-permute-start | bytes 202760 | tf_op jit(solution)/shard_map/ppermute | solution.py:222

commit v7 on v5

v7 whole, which is shorter than its diff:
```python
import functools

import jax
import jax.numpy as jnp
import numpy as np
from jax import lax
from jax.experimental import pallas as pl
from jax.experimental.pallas import tpu as pltpu
from jax.sharding import PartitionSpec as P

QL = 1536
KVL = 512
ROPE = 64
LENGTH = 4096


epsilon = 1e-06
rope_base = 10000.0
PLANES = 4
PARTS = 3
NEAR_COST, LAST_COST = 1, 2
TURNS = 3, 2, 1, 0
VMEM_LIMIT = 20 * 1024 * 1024

vmem = pl.BlockSpec(memory_space=pltpu.VMEM)
smem = pl.BlockSpec(memory_space=pltpu.SMEM)
anywhere = pl.BlockSpec(memory_space=pl.ANY)


def square_sums(values):
    return jnp.sum(values * values, axis=1, keepdims=True)


def product(gained, weight):
    return lax.dot_general(
        gained, weight, (((1,), (1,)), ((), ())), preferred_element_type=jnp.float32
    )


def near_kernel(layout, where, *refs):
    refs = list(refs)
    block_refs = [refs.pop(0) for _ in range(3)]
    gain_ref = refs.pop(0)
    source_refs = [[refs.pop(0) for _ in range(parts)] for parts in layout]
    total, squares, last_weight, blocks, weights, block_arrived, weight_arrived = refs
    width = blocks.shape[2]

    def weight_copy(entry, act):
        into = weights.at[entry] if entry < 3 else last_weight
        for source, parts in enumerate(source_refs):

            @pl.when(where[1, entry] == source)
            def _():
                at = pl.multiple_of(where[2, entry] * width, width)
                for part, ref in enumerate(parts):
                    height = ref.shape[0]
                    copy = pltpu.make_async_copy(
                        ref.at[:, pl.ds(at, width)],
                        into.at[pl.ds(part * height, height)],
                        weight_arrived.at[entry, part],
                    )
                    getattr(copy, act)()

    def block_copy(entry, act):
        copy = pltpu.make_async_copy(block_refs[entry], blocks.at[entry], block_arrived.at[entry])
        getattr(copy, act)()

    for entry in range(3):
        block_copy(entry, "start")
        weight_copy(entry, "start")
    weight_copy(3, "start")
    for entry in range(3):
        block_copy(entry, "wait")
        values = blocks[entry].astype(jnp.float32)
        at = pl.multiple_of(where[0, entry] * width, width)
        gained = (values * gain_ref[:, pl.ds(at, width)]).astype(jnp.bfloat16)
        weight_copy(entry, "wait")
        if entry == 0:
            squares[...] = square_sums(values)
            total[...] = product(gained, weights[entry])
        else:
            squares[...] += square_sums(values)
            total[...] += product(gained, weights[entry])
    weight_copy(3, "wait")


def last_kernel(depth, where, *refs):
    refs = list(refs)
    block_ref, gain_ref, weight_ref, total_ref, squares_ref = [refs.pop(0) for _ in range(5)]
    scaled = refs.pop(-1)
    width = block_ref.shape[1]
    values = block_ref[...].astype(jnp.float32)
    squares = squares_ref[...] + square_sums(values)
    at = pl.multiple_of(where[0, 3] * width, width)
    gained = (values * gain_ref[:, pl.ds(at, width)]).astype(jnp.bfloat16)
    total = total_ref[...] + product(gained, weight_ref[...])
    scaled[...] = total * lax.rsqrt(squares / depth + epsilon)
    quarter = refs[0].shape[0]
    for turn, out_ref in zip(TURNS, refs):
        at = pl.multiple_of(where[3, turn] * quarter, quarter)
        out_ref[...] = scaled[pl.ds(at, quarter), :].astype(jnp.bfloat16)


def finish_kernel(where, *refs):
    refs = list(refs)
    part_refs = [refs.pop(0) for _ in range(len(refs) - 7)]
    q_gain_ref, kv_gain_ref, cosine_ref, sine_ref, query_ref, cache_ref, parts = refs
    for turn, ref in zip(TURNS, part_refs):
        parts[where[3, turn]] = ref[...].astype(jnp.float32)
    latent = jnp.concatenate([parts[plane] for plane in range(PLANES)], axis=1)

    def normed(values, gain):
        mean_square = jnp.mean(values * values, axis=-1, keepdims=True)
        return (values * lax.rsqrt(mean_square + epsilon) * gain).astype(jnp.bfloat16)

    query_ref[...] = normed(latent[:, :QL], q_gain_ref[...])
    cache_ref[:, :KVL] = normed(latent[:, QL : QL + KVL], kv_gain_ref[...])
    half = ROPE // 2
    key = latent[:, QL + KVL :]
    turned = jnp.concatenate([key[:, half:], key[:, :half]], axis=1)
    cache_ref[:, KVL:] = (key * cosine_ref[...] + turned * sine_ref[...]).astype(jnp.bfloat16)


def tables(fsdp, shared):
    made = np.zeros((2, fsdp, PLANES, 4, PLANES), np.int32)
    per = PLANES // fsdp if shared else PLANES
    for core, y, z in np.ndindex(2, fsdp, PLANES):
        for column, block in enumerate((z, PLANES - 1 - z, z ^ 1, z ^ 2)):
            source, inside = 0, block % per
            if shared and block // per != y:
                source, inside = (1 if inside == core else 2), 0
            made[core, y, z, :3, column] = [block, source, inside]
        made[core, y, z, 3] = [z ^ turn for turn in range(PLANES)]
    return made


def on_device(hidden, attn_gain, q_gain, kv_gain, down_weight):
    row_count, width = hidden.shape
    section, fsdp = lax.axis_size("section"), lax.axis_size("fsdp")
    ep_index, fsdp_index = lax.axis_index("ep"), lax.axis_index("fsdp")
    assert lax.axis_size("ep") == PLANES
    quarter = row_count // PLANES
    weight = down_weight.T
    columns = weight.shape[0]
    shared = fsdp == 2 and section % 2 == 0
    place = (lax.axis_index("section") % 2, fsdp_index, ep_index, 0, 0)
    where = lax.dynamic_slice(tables(fsdp, shared), place, (1, 1, 1, 4, PLANES)).reshape(4, PLANES)
    gain = attn_gain.reshape(1, -1)

    mirrored = lax.ppermute(hidden, "ep", [(z, PLANES - 1 - z) for z in range(PLANES)])
    paired = lax.ppermute(hidden, "ep", [(z, z ^ 1) for z in range(PLANES)])
    if shared:
        core = lax.axis_index("section") % 2
        height = columns // PARTS
        here = [
            lax.dynamic_slice(weight, (part * height, core * width), (height, width))
            for part in range(PARTS)
        ]
        here = [lax.ppermute(part, "fsdp", [(0, 1), (1, 0)]) for part in here]
        cores = [(s, s ^ 1) for s in range(section)]
        sources = [[weight], here, [lax.ppermute(part, "section", cores) for part in here]]
    else:
        sources = [[lax.all_gather(weight, "fsdp", axis=1, tiled=True)]]
    far = lax.ppermute(mirrored, "ep", [(z, z ^ 1) for z in range(PLANES)])

    limits = pltpu.CompilerParams(vmem_limit_bytes=VMEM_LIMIT)

    def cost(microseconds):
        return pl.CostEstimate(
            flops=int(microseconds * 1.15e9), bytes_accessed=2 * row_count * width, transcendentals=0
        )

    total, squares, last_weight = pl.pallas_call(
        functools.partial(near_kernel, [len(parts) for parts in sources]),
        out_shape=(
            jax.ShapeDtypeStruct((row_count, columns), jnp.float32),
            jax.ShapeDtypeStruct((row_count, 1), jnp.float32),
            jax.ShapeDtypeStruct((columns, width), jnp.bfloat16),
        ),
        in_specs=[smem] + [anywhere] * 3 + [vmem] + [anywhere] * sum(len(parts) for parts in sources),
        out_specs=(vmem, vmem, anywhere),
        scratch_shapes=[
            pltpu.VMEM((3, row_count, width), jnp.bfloat16),
            pltpu.VMEM((3, columns, width), jnp.bfloat16),
            pltpu.SemaphoreType.DMA((3,)),
            pltpu.SemaphoreType.DMA((4, PARTS)),
        ],
        compiler_params=limits,
        cost_estimate=cost(NEAR_COST),
    )(where, hidden, mirrored, paired, gain, *[part for parts in sources for part in parts])

    messages = pl.pallas_call(
        functools.partial(last_kernel, PLANES * width),
        out_shape=(jax.ShapeDtypeStruct((quarter, columns), jnp.bfloat16),) * PLANES,
        in_specs=[smem] + [vmem] * 5,
        out_specs=(vmem,) * PLANES,
        scratch_shapes=[pltpu.VMEM((row_count, columns), jnp.float32)],
        compiler_params=limits,
        cost_estimate=cost(LAST_COST),
    )(where, far, gain, last_weight, total, squares)
    received = []
    for turn, message in zip(TURNS, messages):
        moves = [
            (s * PLANES + z, (s + 1) % section * PLANES + (z ^ turn))
            for s in range(section)
            for z in range(PLANES)
        ]
        received.append(lax.ppermute(message, ("section", "ep"), moves))

    half = ROPE // 2
    position = (fsdp_index * row_count + ep_index * quarter + jnp.arange(quarter)) % LENGTH
    frequency = rope_base ** (-(jnp.arange(half).astype(jnp.float32) / half))
    angle = position.astype(jnp.float32)[:, None] * frequency[None, :]
    cosine, sine = jnp.cos(angle), jnp.sin(angle)
    return pl.pallas_call(
        finish_kernel,
        out_shape=(
            jax.ShapeDtypeStruct((quarter, QL), jnp.bfloat16),
            jax.ShapeDtypeStruct((quarter, KVL + ROPE), jnp.bfloat16),
        ),
        in_specs=[smem] + [vmem] * (len(received) + 4),
        out_specs=(vmem, vmem),
        scratch_shapes=[pltpu.VMEM((PLANES, quarter, columns), jnp.float32)],
        compiler_params=limits,
    )(
        where,
        *received,
        q_gain.reshape(1, -1),
        kv_gain.reshape(1, -1),
        jnp.concatenate([cosine, cosine], axis=1),
        jnp.concatenate([-sine, sine], axis=1),
    )


def solution(mesh):
    placed = (P(("section", "fsdp"), "ep"), P(), P(), P(), P("fsdp", "ep"))
    return jax.shard_map(
        on_device,
        mesh=mesh,
        in_specs=placed,
        out_specs=(P(("section", "fsdp", "ep"), None), P(("section", "fsdp", "ep"), None)),
        check_vma=False,
    )
```

time: 85.8 us -> 81.3 us (0.948)
  waiting for transfers between devices: 52 us -> 32.7 us
  starting transfers between devices: 17.7 us -> 33 us
    ppermute x8 -> x7, waiting for transfers between devices: 47.6 us -> 27.3 us  [the longest x1 16.3 us: on_device(): lax.ppermute(hidden, 'ep', [(z, PLANES - 1 - z) for z in range(PLANES)])]
    ppermute x8 -> x7, starting transfers between devices: 13.4 us -> 28.9 us  [the longest x1 18.5 us: on_device(): far = lax.ppermute(mirrored, 'ep', [(z, z ^ 1) for z in range(PLANES)])]
    ppermute x3, waiting for transfers between devices: 2.99 us -> 4 us  [on_device(): here = [lax.ppermute(part, 'fsdp', [(0, 1), (1, 0)]) for part in here]]
  transfers between devices with their start and end apart: 14 -> 13, of which waited for: 7 -> 7; matrix products, arithmetic and copies ran while one was open for 3% -> 3% of each run, Pallas kernels for 7% -> 8%
where the time goes in v7:
time: 81.3 us; the launch traced here: 81.1 us
  starting transfers between devices  33 us (41%)
  waiting for transfers between devices  32.7 us (40%)
  Pallas kernels  9.94 us (12%)
  local copies, waits for them, and re-layouts  4.37 us (5%)
    ppermute x1, starting transfers between devices, on_device(): far = lax.ppermute(mirrored, 'ep', [(z, z ^ 1) for z in range(PLANES)])  18.5 us
    ppermute x1, waiting for transfers between devices, on_device(): lax.ppermute(hidden, 'ep', [(z, PLANES - 1 - z) for z in range(PLANES)])  16.3 us
    pallas_call x1, Pallas kernels, on_device(): pl.pallas_call(functools.partial(near_kernel, [len(parts) for parts in so...  6.14 us
    ppermute x4, waiting for transfers between devices, on_device(): received.append(lax.ppermute(message, ('section', 'ep'), moves))  6 us
    ppermute x4, starting transfers between devices, on_device(): received.append(lax.ppermute(message, ('section', 'ep'), moves))  5.34 us
    ppermute x1, starting transfers between devices, on_device(): lax.ppermute(hidden, 'ep', [(z, PLANES - 1 - z) for z in range(PLANES)])  5.11 us
    ppermute x1, waiting for transfers between devices, on_device(): far = lax.ppermute(mirrored, 'ep', [(z, z ^ 1) for z in range(PLANES)])  5 us
    ppermute x3, waiting for transfers between devices, on_device(): here = [lax.ppermute(part, 'fsdp', [(0, 1), (1, 0)]) for part in here]  4 us
  transfers between devices with their start and end apart: 13, of which 7 were waited for; matrix products, arithmetic and copies ran while one was open for 3% of the time, Pallas kernels for 8%

profile of v7, /device:TPU:0, one launch (start us, length us, event | category | flops | bytes accessed | tf_op | source)
XLA Modules:
  0.0 81.1 jit_solution(4226572054196224640)
XLA Ops:
  0.6 0.0 copy-start.1
  0.6 0.0 copy-start.4
  0.6 0.0 copy-start.2
  0.7 5.1 %collective-permute-start = (bf16[256,1792]{1,0:T(8,128)(2,1)}, bf16[256,1792]{1,0:T(8,128)(2,1)S(1)}, u32[]{:S(2)}, u32[]{:S(2)}) collective-permute-start(bf16[256,1792]{1,0:T(8,128)(2,1)} %refs_0_.1), channel_id=1, source_target_pairs={{0,3},{1,2},{2,1},{3,0},{4,7},{5,6},{6,5},{7,4},{8,11},{9,10},{10,... | collective-permute-start | bytes 2752520 | tf_op jit(solution)/shard_map/ppermute | solution.py:150
  5.8 1.6 %dynamic-slice_bitcast_fusion = (bf16[176,1792]{1,0:T(8,128)(2,1)S(1)}, bf16[176,1792]{1,0:T(8,128)(2,1)S(1)}, bf16[176,1792]{1,0:T(8,128)(2,1)S(1)}) fusion(bf16[3584,528]{0,1:T(8,128)(2,1)} %param.10, s32[]{:T(128)S(6)} %select_n.37), kind=kLoop, calls=%fused_computation | loop fusion | bytes 3784708 | tf_op jit(solution)/shard_map/dynamic_slice | solution.py:156
  7.4 1.6 %collective-permute-start.3 = (bf16[176,1792]{1,0:T(8,128)(2,1)S(1)}, bf16[176,1792]{1,0:T(8,128)(2,1)S(1)}, u32[]{:S(2)}, u32[]{:S(2)}) collective-permute-start(bf16[176,1792]{1,0:T(8,128)(2,1)S(1)} %get-tuple-element.17), channel_id=1, source_target_pairs={{0,4},{4,0},{1,5},{5,1},{2,6},{6,2},{3,7},{7,3},{8,12},{12,8},{9,1... | collective-permute-start | bytes 1892360 | tf_op jit(solution)/shard_map/ppermute | solution.py:159
  8.9 0.5 collective-permute-start.4
  9.4 1.5 %collective-permute-start.5 = (bf16[176,1792]{1,0:T(8,128)(2,1)S(1)}, bf16[176,1792]{1,0:T(8,128)(2,1)}, u32[]{:S(2)}, u32[]{:S(2)}) collective-permute-start(bf16[176,1792]{1,0:T(8,128)(2,1)S(1)} %get-tuple-element.16), channel_id=1, source_target_pairs={{0,4},{4,0},{1,5},{5,1},{2,6},{6,2},{3,7},{7,3},{8,12},{12,8},{9,1... | collective-permute-start | bytes 1892360 | tf_op jit(solution)/shard_map/ppermute | solution.py:159
  11.0 0.0 copy-done.1
  11.0 0.0 collective-permute-start.2
  11.0 16.3 %collective-permute-done.refs_1_ = bf16[256,1792]{1,0:T(8,128)(2,1)S(1)} collective-permute-done((bf16[256,1792]{1,0:T(8,128)(2,1)}, bf16[256,1792]{1,0:T(8,128)(2,1)S(1)}, u32[]{:S(2)}, u32[]{:S(2)}) %collective-permute-start) | collective-permute-done | bytes 917536 | tf_op jit(solution)/shard_map/ppermute | solution.py:150
  27.3 18.5 %collective-permute-start.1 = (bf16[256,1792]{1,0:T(8,128)(2,1)S(1)}, bf16[256,1792]{1,0:T(8,128)(2,1)}, u32[]{:S(2)}, u32[]{:S(2)}) collective-permute-start(bf16[256,1792]{1,0:T(8,128)(2,1)S(1)} %collective-permute-done.refs_1_), channel_id=1, source_target_pairs={{0,1},{1,0},{2,3},{3,2},{4,5},{5,4},{6,7},{7,6},{8,9},{9,8},{10,11... | collective-permute-start | bytes 2752520 | tf_op jit(solution)/shard_map/ppermute | solution.py:164
  45.7 0.0 collective-permute-done.3.refs_5_
  45.7 0.0 collective-permute-start.6
  45.7 0.0 collective-permute-done.4.refs_6_
  45.7 0.5 collective-permute-start.7
  46.2 4.0 %collective-permute-done.5.refs_7_ = bf16[176,1792]{1,0:T(8,128)(2,1)} collective-permute-done((bf16[176,1792]{1,0:T(8,128)(2,1)S(1)}, bf16[176,1792]{1,0:T(8,128)(2,1)}, u32[]{:S(2)}, u32[]{:S(2)}) %collective-permute-start.5) | collective-permute-done | bytes 630816 | tf_op jit(solution)/shard_map/ppermute | solution.py:159
  50.2 0.0 collective-permute-start.8
  50.2 0.0 copy-done.4
  50.3 0.7 dynamic-slice_bitcast_fusion.3.where
  51.0 0.2 fusion
  51.2 0.0 collective-permute-done.2.refs_2_
  51.2 0.0 collective-permute-done.6.refs_8_
  51.2 0.0 collective-permute-done.7.refs_9_
  51.2 1.4 %collective-permute-done.8.refs_10_ = bf16[176,1792]{1,0:T(8,128)(2,1)} collective-permute-done((bf16[176,1792]{1,0:T(8,128)(2,1)}, bf16[176,1792]{1,0:T(8,128)(2,1)}, u32[]{:S(2)}, u32[]{:S(2)}) %collective-permute-start.8) | collective-permute-done | bytes 630816 | tf_op jit(solution)/shard_map/ppermute | solution.py:161
  52.6 0.0 copy-done.2
  52.6 0.0 copy-start
  52.6 2.1 %copy-done = bf16[3584,528]{0,1:T(8,128)(2,1)S(1)} copy-done((bf16[3584,528]{0,1:T(8,128)(2,1)S(1)}, bf16[3584,528]{0,1:T(8,128)(2,1)}, u32[]{:S(2)}) %copy-start) | copy-done | bytes 3784728
  54.7 6.1 %shard_map.77 = (f32[256,528]{1,0:T(8,128)S(1)}, f32[256,1]{1,0:T(8,128)S(1)}, bf16[528,1792]{1,0:T(8,128)(2,1)S(1)}) custom-call(s32[4,4]{1,0:T(4,128)S(1)} %dynamic-slice_bitcast_fusion.3.where, bf16[256,1792]{1,0:T(8,128)(2,1)S(1)} %copy-done.1, bf16[256,1792]{1,0:T(8,128)(2,1)S(1)} %collective-permute-done.refs_1_, ...), custom_call_target="tpu_custom_call" | custom-call | flops 1150000000 | bytes 917504 | tf_op jit(solution)/shard_map/pallas_call | solution.py:173
  60.9 5.0 %collective-permute-done.1.refs_0_ = bf16[256,1792]{1,0:T(8,128)(2,1)} collective-permute-done((bf16[256,1792]{1,0:T(8,128)(2,1)S(1)}, bf16[256,1792]{1,0:T(8,128)(2,1)}, u32[]{:S(2)}, u32[]{:S(2)}) %collective-permute-start.1) | collective-permute-done | bytes 917536 | tf_op jit(solution)/shard_map/ppermute | solution.py:164
  65.9 0.0 copy-start.3
  65.9 2.2 %shard_map.78 = (bf16[64,528]{1,0:T(8,128)(2,1)S(1)}, bf16[64,528]{1,0:T(8,128)(2,1)S(1)}, bf16[64,528]{1,0:T(8,128)(2,1)S(1)}, bf16[64,528]{1,0:T(8,128)(2,1)S(1)}) custom-call(s32[4,4]{1,0:T(4,128)S(1)} %dynamic-slice_bitcast_fusion.3.where, bf16[256,1792]{1,0:T(8,128)(2,1)} %collective-permute-done.1.refs_0_, f32[1,7168]{1,0:T(1,128)S(1)} %bitcast.13, ...), custom_call_target="tpu_custom_call" | custom-call | flops 2300000000 | bytes 917504 | tf_op jit(solution)/shard_map/pallas_call | solution.py:192
  68.1 1.2 %collective-permute-start.10 = (bf16[64,528]{1,0:T(8,128)(2,1)S(1)}, bf16[64,528]{1,0:T(8,128)(2,1)S(1)}, u32[]{:S(2)}, u32[]{:S(2)}) collective-permute-start(bf16[64,528]{1,0:T(8,128)(2,1)S(1)} %get-tuple-element.13), channel_id=1, source_target_pairs={{0,10},{1,11},{2,8},{3,9},{8,18},{9,19},{10,16},{11,17},{16,26},{1... | collective-permute-start | bytes 202760 | tf_op jit(solution)/shard_map/ppermute | solution.py:208
  69.3 3.6 %collective-permute-start.11 = (bf16[64,528]{1,0:T(8,128)(2,1)S(1)}, bf16[64,528]{1,0:T(8,128)(2,1)S(1)}, u32[]{:S(2)}, u32[]{:S(2)}) collective-permute-start(bf16[64,528]{1,0:T(8,128)(2,1)S(1)} %get-tuple-element.14), channel_id=1, source_target_pairs={{0,9},{1,8},{2,11},{3,10},{8,17},{9,16},{10,19},{11,18},{16,25},{1... | collective-permute-start | bytes 202760 | tf_op jit(solution)/shard_map/ppermute | solution.py:208
  72.9 0.0 collective-permute-start.12
  72.9 0.5 collective-permute-start.9
  73.4 0.1 pad_maximum_fusion
  73.5 3.0 %collective-permute-done.10.refs_1_ = bf16[64,528]{1,0:T(8,128)(2,1)S(1)} collective-permute-done((bf16[64,528]{1,0:T(8,128)(2,1)S(1)}, bf16[64,528]{1,0:T(8,128)(2,1)S(1)}, u32[]{:S(2)}, u32[]{:S(2)}) %collective-permute-start.10) | collective-permute-done | bytes 67616 | tf_op jit(solution)/shard_map/ppermute | solution.py:208
  76.5 0.0 collective-permute-done.11.refs_2_
  76.5 0.5 collective-permute-done.12.refs_3_
  77.0 2.5 %collective-permute-done.9.refs_0_ = bf16[64,528]{1,0:T(8,128)(2,1)S(1)} collective-permute-done((bf16[64,528]{1,0:T(8,128)(2,1)S(1)}, bf16[64,528]{1,0:T(8,128)(2,1)S(1)}, u32[]{:S(2)}, u32[]{:S(2)}) %collective-permute-start.9) | collective-permute-done | bytes 67616 | tf_op jit(solution)/shard_map/ppermute | solution.py:208
  79.5 0.0 copy-done.3
  79.5 1.6 %shard_map.79 = (bf16[64,1536]{1,0:T(8,128)(2,1)}, bf16[64,576]{1,0:T(8,128)(2,1)}) custom-call(s32[4,4]{1,0:T(4,128)S(1)} %dynamic-slice_bitcast_fusion.3.where, bf16[64,528]{1,0:T(8,128)(2,1)S(1)} %collective-permute-done.9.refs_0_, bf16[64,528]{1,0:T(8,128)(2,1)S(1)} %collective-permute-done.10.refs_1_, ...), custom_call_target="tpu_custom_call" | custom-call | tf_op jit(solution)/shard_map/pallas_call | solution.py:215
  (3 shorter events, 0.0 us)
Async XLA Ops:
  0.6 10.3 %copy-start.1 = (bf16[256,1792]{1,0:T(8,128)(2,1)S(1)}, bf16[256,1792]{1,0:T(8,128)(2,1)}, u32[]{:S(2)}) copy-start(bf16[256,1792]{1,0:T(8,128)(2,1)} %refs_0_.1) | copy-start | bytes 2752516
  0.6 49.6 %copy-start.4 = (f32[1536]{0:T(1024)S(1)}, f32[1536]{0:T(1024)}, u32[]{:S(2)}) copy-start(f32[1536]{0:T(1024)} %param.8) | copy-start | bytes 18436
  0.6 52.0 %copy-start.2 = (f32[7168]{0:T(1024)S(1)}, f32[7168]{0:T(1024)}, u32[]{:S(2)}) copy-start(f32[7168]{0:T(1024)} %param.7) | copy-start | bytes 86020
  0.7 26.6 %collective-permute-start = (bf16[256,1792]{1,0:T(8,128)(2,1)}, bf16[256,1792]{1,0:T(8,128)(2,1)S(1)}, u32[]{:S(2)}, u32[]{:S(2)}) collective-permute-start(bf16[256,1792]{1,0:T(8,128)(2,1)} %refs_0_.1), channel_id=1, source_target_pairs={{0,3},{1,2},{2,1},{3,0},{4,7},{5,6},{6,5},{7,4},{8,11},{9,10},{10,... | collective-permute-start | bytes 2752520 | tf_op jit(solution)/shard_map/ppermute | solution.py:150
  7.4 38.4 %collective-permute-start.3 = (bf16[176,1792]{1,0:T(8,128)(2,1)S(1)}, bf16[176,1792]{1,0:T(8,128)(2,1)S(1)}, u32[]{:S(2)}, u32[]{:S(2)}) collective-permute-start(bf16[176,1792]{1,0:T(8,128)(2,1)S(1)} %get-tuple-element.17), channel_id=1, source_target_pairs={{0,4},{4,0},{1,5},{5,1},{2,6},{6,2},{3,7},{7,3},{8,12},{12,8},{9,1... | collective-permute-start | bytes 1892360 | tf_op jit(solution)/shard_map/ppermute | solution.py:159
  8.9 36.8 %collective-permute-start.4 = (bf16[176,1792]{1,0:T(8,128)(2,1)S(1)}, bf16[176,1792]{1,0:T(8,128)(2,1)}, u32[]{:S(2)}, u32[]{:S(2)}) collective-permute-start(bf16[176,1792]{1,0:T(8,128)(2,1)S(1)} %get-tuple-element.18), channel_id=1, source_target_pairs={{0,4},{4,0},{1,5},{5,1},{2,6},{6,2},{3,7},{7,3},{8,12},{12,8},{9,1... | collective-permute-start | bytes 1892360 | tf_op jit(solution)/shard_map/ppermute | solution.py:159
  9.4 40.8 %collective-permute-start.5 = (bf16[176,1792]{1,0:T(8,128)(2,1)S(1)}, bf16[176,1792]{1,0:T(8,128)(2,1)}, u32[]{:S(2)}, u32[]{:S(2)}) collective-permute-start(bf16[176,1792]{1,0:T(8,128)(2,1)S(1)} %get-tuple-element.16), channel_id=1, source_target_pairs={{0,4},{4,0},{1,5},{5,1},{2,6},{6,2},{3,7},{7,3},{8,12},{12,8},{9,1... | collective-permute-start | bytes 1892360 | tf_op jit(solution)/shard_map/ppermute | solution.py:159
  11.0 40.2 %collective-permute-start.2 = (bf16[256,1792]{1,0:T(8,128)(2,1)S(1)}, bf16[256,1792]{1,0:T(8,128)(2,1)S(1)}, u32[]{:S(2)}, u32[]{:S(2)}) collective-permute-start(bf16[256,1792]{1,0:T(8,128)(2,1)S(1)} %copy-done.1), channel_id=1, source_target_pairs={{0,1},{1,0},{2,3},{3,2},{4,5},{5,4},{6,7},{7,6},{8,9},{9,8},{10,11... | collective-permute-start | bytes 2752520 | tf_op jit(solution)/shard_map/ppermute | solution.py:151
  27.3 38.6 %collective-permute-start.1 = (bf16[256,1792]{1,0:T(8,128)(2,1)S(1)}, bf16[256,1792]{1,0:T(8,128)(2,1)}, u32[]{:S(2)}, u32[]{:S(2)}) collective-permute-start(bf16[256,1792]{1,0:T(8,128)(2,1)S(1)} %collective-permute-done.refs_1_), channel_id=1, source_target_pairs={{0,1},{1,0},{2,3},{3,2},{4,5},{5,4},{6,7},{7,6},{8,9},{9,8},{10,11... | collective-permute-start | bytes 2752520 | tf_op jit(solution)/shard_map/ppermute | solution.py:164
  45.7 5.5 %collective-permute-start.6 = (bf16[176,1792]{1,0:T(8,128)(2,1)S(1)}, bf16[176,1792]{1,0:T(8,128)(2,1)}, u32[]{:S(2)}, u32[]{:S(2)}) collective-permute-start(bf16[176,1792]{1,0:T(8,128)(2,1)S(1)} %collective-permute-done.3.refs_5_), channel_id=1, source_target_pairs={{0,8},{8,0},{16,24},{24,16},{1,9},{9,1},{17,25},{25,17},{2,10},{10... | collective-permute-start | bytes 1892360 | tf_op jit(solution)/shard_map/ppermute | solution.py:161
  45.7 5.5 %collective-permute-start.7 = (bf16[176,1792]{1,0:T(8,128)(2,1)}, bf16[176,1792]{1,0:T(8,128)(2,1)}, u32[]{:S(2)}, u32[]{:S(2)}) collective-permute-start(bf16[176,1792]{1,0:T(8,128)(2,1)} %collective-permute-done.4.refs_6_), channel_id=1, source_target_pairs={{0,8},{8,0},{16,24},{24,16},{1,9},{9,1},{17,25},{25,17},{2,10},{10... | collective-permute-start | bytes 1892360 | tf_op jit(solution)/shard_map/ppermute | solution.py:161
  50.2 2.4 %collective-permute-start.8 = (bf16[176,1792]{1,0:T(8,128)(2,1)}, bf16[176,1792]{1,0:T(8,128)(2,1)}, u32[]{:S(2)}, u32[]{:S(2)}) collective-permute-start(bf16[176,1792]{1,0:T(8,128)(2,1)} %collective-permute-done.5.refs_7_), channel_id=1, source_target_pairs={{0,8},{8,0},{16,24},{24,16},{1,9},{9,1},{17,25},{25,17},{2,10},{10... | collective-permute-start | bytes 1892360 | tf_op jit(solution)/shard_map/ppermute | solution.py:161
  52.6 2.1 %copy-start = (bf16[3584,528]{0,1:T(8,128)(2,1)S(1)}, bf16[3584,528]{0,1:T(8,128)(2,1)}, u32[]{:S(2)}) copy-start(bf16[3584,528]{0,1:T(8,128)(2,1)} %param.10) | copy-start | bytes 11354116
  65.9 13.7 %copy-start.3 = (f32[512]{0:T(512)S(1)}, f32[512]{0:T(512)}, u32[]{:S(2)}) copy-start(f32[512]{0:T(512)} %param.9) | copy-start | bytes 6148
  68.1 8.4 %collective-permute-start.10 = (bf16[64,528]{1,0:T(8,128)(2,1)S(1)}, bf16[64,528]{1,0:T(8,128)(2,1)S(1)}, u32[]{:S(2)}, u32[]{:S(2)}) collective-permute-start(bf16[64,528]{1,0:T(8,128)(2,1)S(1)} %get-tuple-element.13), channel_id=1, source_target_pairs={{0,10},{1,11},{2,8},{3,9},{8,18},{9,19},{10,16},{11,17},{16,26},{1... | collective-permute-start | bytes 202760 | tf_op jit(solution)/shard_map/ppermute | solution.py:208
  69.3 7.2 %collective-permute-start.11 = (bf16[64,528]{1,0:T(8,128)(2,1)S(1)}, bf16[64,528]{1,0:T(8,128)(2,1)S(1)}, u32[]{:S(2)}, u32[]{:S(2)}) collective-permute-start(bf16[64,528]{1,0:T(8,128)(2,1)S(1)} %get-tuple-element.14), channel_id=1, source_target_pairs={{0,9},{1,8},{2,11},{3,10},{8,17},{9,16},{10,19},{11,18},{16,25},{1... | collective-permute-start | bytes 202760 | tf_op jit(solution)/shard_map/ppermute | solution.py:208
  72.9 4.1 %collective-permute-start.12 = (bf16[64,528]{1,0:T(8,128)(2,1)S(1)}, bf16[64,528]{1,0:T(8,128)(2,1)S(1)}, u32[]{:S(2)}, u32[]{:S(2)}) collective-permute-start(bf16[64,528]{1,0:T(8,128)(2,1)S(1)} %get-tuple-element.15), channel_id=1, source_target_pairs={{0,8},{1,9},{2,10},{3,11},{8,16},{9,17},{10,18},{11,19},{16,24},{1... | collective-permute-start | bytes 202760 | tf_op jit(solution)/shard_map/ppermute | solution.py:208
  72.9 6.6 %collective-permute-start.9 = (bf16[64,528]{1,0:T(8,128)(2,1)S(1)}, bf16[64,528]{1,0:T(8,128)(2,1)S(1)}, u32[]{:S(2)}, u32[]{:S(2)}) collective-permute-start(bf16[64,528]{1,0:T(8,128)(2,1)S(1)} %get-tuple-element.12), channel_id=1, source_target_pairs={{0,11},{1,10},{2,9},{3,8},{8,19},{9,18},{10,17},{11,16},{16,27},{1... | collective-permute-start | bytes 202760 | tf_op jit(solution)/shard_map/ppermute | solution.py:208

commit v8 on v7

--- a/solution.py
+++ b/solution.py
@@ -20,6 +20,8 @@
 PARTS = 3
 NEAR_COST, LAST_COST = 1, 2
 TURNS = 3, 2, 1, 0
+LANES = 128
+PACK = 16
 VMEM_LIMIT = 20 * 1024 * 1024
 
 vmem = pl.BlockSpec(memory_space=pltpu.VMEM)
@@ -46,7 +48,7 @@
     width = blocks.shape[2]
 
     def weight_copy(entry, act):
-        into = weights.at[entry] if entry < 3 else last_weight
+        into = weights.at[entry]
         for source, parts in enumerate(source_refs):
 
             @pl.when(where[1, entry] == source)
@@ -82,23 +84,47 @@
             squares[...] += square_sums(values)
             total[...] += product(gained, weights[entry])
     weight_copy(3, "wait")
-
-
-def last_kernel(depth, where, *refs):
+    at = pl.multiple_of(where[0, 3] * width, width)
+    gained = weights[3].astype(jnp.float32) * gain_ref[:, pl.ds(at, width)]
+    last_weight[...] = gained.astype(jnp.bfloat16)
+
+
+def pack(rows, out_ref):
+    count, columns = rows.shape
+    main = columns // LANES * LANES
+    for tile in range(main // LANES):
+        tile_rows = rows[:, tile * LANES : (tile + 1) * LANES]
+        out_ref[tile * count : (tile + 1) * count, :] = tile_rows.astype(jnp.bfloat16)
+    rest = [rows[at : at + PACK, main:] for at in range(0, count, PACK)]
+    spare = LANES - len(rest) * (columns - main)
+    rest = jnp.concatenate(rest + [jnp.zeros((PACK, spare), jnp.float32)], axis=1)
+    out_ref[main // LANES * count :, :] = rest.astype(jnp.bfloat16)
+
+
+def unpack(packed_ref, into):
+    count, columns = into.shape
+    main = columns // LANES * LANES
+    for tile in range(main // LANES):
+        tile_rows = packed_ref[tile * count : (tile + 1) * count, :]
+        into[:, tile * LANES : (tile + 1) * LANES] = tile_rows.astype(jnp.float32)
+    rest = packed_ref[main // LANES * count :, :].astype(jnp.float32)
+    width = columns - main
+    into[:, main:] = jnp.concatenate(
+        [rest[:, at * width : (at + 1) * width] for at in range(count // PACK)], axis=0
+    )
+
+
+def last_kernel(depth, quarter, where, *refs):
     refs = list(refs)
-    block_ref, gain_ref, weight_ref, total_ref, squares_ref = [refs.pop(0) for _ in range(5)]
+    block_ref, weight_ref, total_ref, squares_ref = [refs.pop(0) for _ in range(4)]
     scaled = refs.pop(-1)
-    width = block_ref.shape[1]
-    values = block_ref[...].astype(jnp.float32)
-    squares = squares_ref[...] + square_sums(values)
-    at = pl.multiple_of(where[0, 3] * width, width)
-    gained = (values * gain_ref[:, pl.ds(at, width)]).astype(jnp.bfloat16)
-    total = total_ref[...] + product(gained, weight_ref[...])
+    block = block_ref[...]
+    squares = squares_ref[...] + square_sums(block.astype(jnp.float32))
+    total = total_ref[...] + product(block, weight_ref[...])
     scaled[...] = total * lax.rsqrt(squares / depth + epsilon)
-    quarter = refs[0].shape[0]
     for turn, out_ref in zip(TURNS, refs):
         at = pl.multiple_of(where[3, turn] * quarter, quarter)
-        out_ref[...] = scaled[pl.ds(at, quarter), :].astype(jnp.bfloat16)
+        pack(scaled[pl.ds(at, quarter), :], out_ref)
 
 
 def finish_kernel(where, *refs):
@@ -106,7 +132,7 @@
     part_refs = [refs.pop(0) for _ in range(len(refs) - 7)]
     q_gain_ref, kv_gain_ref, cosine_ref, sine_ref, query_ref, cache_ref, parts = refs
     for turn, ref in zip(TURNS, part_refs):
-        parts[where[3, turn]] = ref[...].astype(jnp.float32)
+        unpack(ref, parts.at[where[3, turn]])
     latent = jnp.concatenate([parts[plane] for plane in range(PLANES)], axis=1)
 
     def normed(values, gain):
@@ -178,10 +204,10 @@
             jax.ShapeDtypeStruct((columns, width), jnp.bfloat16),
         ),
         in_specs=[smem] + [anywhere] * 3 + [vmem] + [anywhere] * sum(len(parts) for parts in sources),
-        out_specs=(vmem, vmem, anywhere),
+        out_specs=(vmem, vmem, vmem),
         scratch_shapes=[
             pltpu.VMEM((3, row_count, width), jnp.bfloat16),
-            pltpu.VMEM((3, columns, width), jnp.bfloat16),
+            pltpu.VMEM((4, columns, width), jnp.bfloat16),
             pltpu.SemaphoreType.DMA((3,)),
             pltpu.SemaphoreType.DMA((4, PARTS)),
         ],
@@ -189,15 +215,16 @@
         cost_estimate=cost(NEAR_COST),
     )(where, hidden, mirrored, paired, gain, *[part for parts in sources for part in parts])
 
+    packed = columns // LANES * quarter + PACK
     messages = pl.pallas_call(
-        functools.partial(last_kernel, PLANES * width),
-        out_shape=(jax.ShapeDtypeStruct((quarter, columns), jnp.bfloat16),) * PLANES,
-        in_specs=[smem] + [vmem] * 5,
+        functools.partial(last_kernel, PLANES * width, quarter),
+        out_shape=(jax.ShapeDtypeStruct((packed, LANES), jnp.bfloat16),) * PLANES,
+        in_specs=[smem] + [vmem] * 4,
         out_specs=(vmem,) * PLANES,
         scratch_shapes=[pltpu.VMEM((row_count, columns), jnp.float32)],
         compiler_params=limits,
         cost_estimate=cost(LAST_COST),
-    )(where, far, gain, last_weight, total, squares)
+    )(where, far, last_weight, total, squares)
     received = []
     for turn, message in zip(TURNS, messages):
         moves = [

time: 81.3 us -> 81.3 us (level)
  no operation moved by 1% of the time
where the time goes in v8:
time: 81.3 us; the launch traced here: 81.1 us
  starting transfers between devices  33 us (41%)
  waiting for transfers between devices  32.2 us (40%)
  Pallas kernels  10.4 us (13%)
  local copies, waits for them, and re-layouts  4.37 us (5%)
    ppermute x1, starting transfers between devices, on_device(): far = lax.ppermute(mirrored, 'ep', [(z, z ^ 1) for z in range(PLANES)])  18.5 us
    ppermute x1, waiting for transfers between devices, on_device(): lax.ppermute(hidden, 'ep', [(z, PLANES - 1 - z) for z in range(PLANES)])  16.3 us
    pallas_call x1, Pallas kernels, on_device(): pl.pallas_call(functools.partial(near_kernel, [len(parts) for parts in so...  6.45 us
    ppermute x4, waiting for transfers between devices, on_device(): received.append(lax.ppermute(message, ('section', 'ep'), moves))  5.82 us
    ppermute x4, starting transfers between devices, on_device(): received.append(lax.ppermute(message, ('section', 'ep'), moves))  5.34 us
    ppermute x1, starting transfers between devices, on_device(): lax.ppermute(hidden, 'ep', [(z, PLANES - 1 - z) for z in range(PLANES)])  5.11 us
    ppermute x1, waiting for transfers between devices, on_device(): far = lax.ppermute(mirrored, 'ep', [(z, z ^ 1) for z in range(PLANES)])  4.7 us
    ppermute x3, waiting for transfers between devices, on_device(): here = [lax.ppermute(part, 'fsdp', [(0, 1), (1, 0)]) for part in here]  4 us
  transfers between devices with their start and end apart: 13, of which 7 were waited for; matrix products, arithmetic and copies ran while one was open for 3% of the time, Pallas kernels for 8%

profile of v8, /device:TPU:0, one launch (start us, length us, event | category | flops | bytes accessed | tf_op | source)
XLA Modules:
  0.0 81.1 jit_solution(3320976524234715391)
XLA Ops:
  0.6 0.0 copy-start.1
  0.6 0.0 copy-start.4
  0.6 0.0 copy-start.2
  0.7 5.1 %collective-permute-start = (bf16[256,1792]{1,0:T(8,128)(2,1)}, bf16[256,1792]{1,0:T(8,128)(2,1)S(1)}, u32[]{:S(2)}, u32[]{:S(2)}) collective-permute-start(bf16[256,1792]{1,0:T(8,128)(2,1)} %refs_0_.1), channel_id=1, source_target_pairs={{0,3},{1,2},{2,1},{3,0},{4,7},{5,6},{6,5},{7,4},{8,11},{9,10},{10,... | collective-permute-start | bytes 2752520 | tf_op jit(solution)/shard_map/ppermute | solution.py:176
  5.8 1.6 %dynamic-slice_bitcast_fusion = (bf16[176,1792]{1,0:T(8,128)(2,1)S(1)}, bf16[176,1792]{1,0:T(8,128)(2,1)S(1)}, bf16[176,1792]{1,0:T(8,128)(2,1)S(1)}) fusion(bf16[3584,528]{0,1:T(8,128)(2,1)} %param.10, s32[]{:T(128)S(6)} %select_n.37), kind=kLoop, calls=%fused_computation | loop fusion | bytes 3784708 | tf_op jit(solution)/shard_map/dynamic_slice | solution.py:182
  7.4 1.6 %collective-permute-start.3 = (bf16[176,1792]{1,0:T(8,128)(2,1)S(1)}, bf16[176,1792]{1,0:T(8,128)(2,1)S(1)}, u32[]{:S(2)}, u32[]{:S(2)}) collective-permute-start(bf16[176,1792]{1,0:T(8,128)(2,1)S(1)} %get-tuple-element.17), channel_id=1, source_target_pairs={{0,4},{4,0},{1,5},{5,1},{2,6},{6,2},{3,7},{7,3},{8,12},{12,8},{9,1... | collective-permute-start | bytes 1892360 | tf_op jit(solution)/shard_map/ppermute | solution.py:185
  8.9 0.5 collective-permute-start.4
  9.4 1.5 %collective-permute-start.5 = (bf16[176,1792]{1,0:T(8,128)(2,1)S(1)}, bf16[176,1792]{1,0:T(8,128)(2,1)}, u32[]{:S(2)}, u32[]{:S(2)}) collective-permute-start(bf16[176,1792]{1,0:T(8,128)(2,1)S(1)} %get-tuple-element.16), channel_id=1, source_target_pairs={{0,4},{4,0},{1,5},{5,1},{2,6},{6,2},{3,7},{7,3},{8,12},{12,8},{9,1... | collective-permute-start | bytes 1892360 | tf_op jit(solution)/shard_map/ppermute | solution.py:185
  11.0 0.0 copy-done.1
  11.0 0.0 collective-permute-start.2
  11.0 16.3 %collective-permute-done.refs_1_ = bf16[256,1792]{1,0:T(8,128)(2,1)S(1)} collective-permute-done((bf16[256,1792]{1,0:T(8,128)(2,1)}, bf16[256,1792]{1,0:T(8,128)(2,1)S(1)}, u32[]{:S(2)}, u32[]{:S(2)}) %collective-permute-start) | collective-permute-done | bytes 917536 | tf_op jit(solution)/shard_map/ppermute | solution.py:176
  27.3 18.5 %collective-permute-start.1 = (bf16[256,1792]{1,0:T(8,128)(2,1)S(1)}, bf16[256,1792]{1,0:T(8,128)(2,1)}, u32[]{:S(2)}, u32[]{:S(2)}) collective-permute-start(bf16[256,1792]{1,0:T(8,128)(2,1)S(1)} %collective-permute-done.refs_1_), channel_id=1, source_target_pairs={{0,1},{1,0},{2,3},{3,2},{4,5},{5,4},{6,7},{7,6},{8,9},{9,8},{10,11... | collective-permute-start | bytes 2752520 | tf_op jit(solution)/shard_map/ppermute | solution.py:190
  45.7 0.0 collective-permute-done.3.refs_5_
  45.7 0.0 collective-permute-start.6
  45.7 0.0 collective-permute-done.4.refs_6_
  45.7 0.5 collective-permute-start.7
  46.2 4.0 %collective-permute-done.5.refs_7_ = bf16[176,1792]{1,0:T(8,128)(2,1)} collective-permute-done((bf16[176,1792]{1,0:T(8,128)(2,1)S(1)}, bf16[176,1792]{1,0:T(8,128)(2,1)}, u32[]{:S(2)}, u32[]{:S(2)}) %collective-permute-start.5) | collective-permute-done | bytes 630816 | tf_op jit(solution)/shard_map/ppermute | solution.py:185
  50.2 0.0 collective-permute-start.8
  50.2 0.0 copy-done.4
  50.3 0.7 dynamic-slice_bitcast_fusion.3.where
  51.0 0.2 fusion
  51.2 0.0 collective-permute-done.2.refs_2_
  51.2 0.0 collective-permute-done.6.refs_8_
  51.2 0.0 collective-permute-done.7.refs_9_
  51.2 1.4 %collective-permute-done.8.refs_10_ = bf16[176,1792]{1,0:T(8,128)(2,1)} collective-permute-done((bf16[176,1792]{1,0:T(8,128)(2,1)}, bf16[176,1792]{1,0:T(8,128)(2,1)}, u32[]{:S(2)}, u32[]{:S(2)}) %collective-permute-start.8) | collective-permute-done | bytes 630816 | tf_op jit(solution)/shard_map/ppermute | solution.py:187
  52.6 0.0 copy-done.2
  52.6 0.0 copy-start
  52.6 2.1 %copy-done = bf16[3584,528]{0,1:T(8,128)(2,1)S(1)} copy-done((bf16[3584,528]{0,1:T(8,128)(2,1)S(1)}, bf16[3584,528]{0,1:T(8,128)(2,1)}, u32[]{:S(2)}) %copy-start) | copy-done | bytes 3784728
  54.7 6.4 %shard_map.77 = (f32[256,528]{1,0:T(8,128)S(1)}, f32[256,1]{1,0:T(8,128)S(1)}, bf16[528,1792]{1,0:T(8,128)(2,1)S(1)}) custom-call(s32[4,4]{1,0:T(4,128)S(1)} %dynamic-slice_bitcast_fusion.3.where, bf16[256,1792]{1,0:T(8,128)(2,1)S(1)} %copy-done.1, bf16[256,1792]{1,0:T(8,128)(2,1)S(1)} %collective-permute-done.refs_1_, ...), custom_call_target="tpu_custom_call" | custom-call | flops 1150000000 | bytes 917504 | tf_op jit(solution)/shard_map/pallas_call | solution.py:199
  61.2 4.7 %collective-permute-done.1.refs_0_ = bf16[256,1792]{1,0:T(8,128)(2,1)} collective-permute-done((bf16[256,1792]{1,0:T(8,128)(2,1)S(1)}, bf16[256,1792]{1,0:T(8,128)(2,1)}, u32[]{:S(2)}, u32[]{:S(2)}) %collective-permute-start.1) | collective-permute-done | bytes 917536 | tf_op jit(solution)/shard_map/ppermute | solution.py:190
  65.9 0.0 copy-start.3
  65.9 2.3 %shard_map.78 = (bf16[272,128]{1,0:T(8,128)(2,1)S(1)}, bf16[272,128]{1,0:T(8,128)(2,1)S(1)}, bf16[272,128]{1,0:T(8,128)(2,1)S(1)}, bf16[272,128]{1,0:T(8,128)(2,1)S(1)}) custom-call(s32[4,4]{1,0:T(4,128)S(1)} %dynamic-slice_bitcast_fusion.3.where, bf16[256,1792]{1,0:T(8,128)(2,1)} %collective-permute-done.1.refs_0_, ...), custom_call_target="tpu_custom_call" | custom-call | flops 2300000000 | bytes 917504 | tf_op jit(solution)/shard_map/pallas_call | solution.py:219
  68.2 1.2 %collective-permute-start.10 = (bf16[272,128]{1,0:T(8,128)(2,1)S(1)}, bf16[272,128]{1,0:T(8,128)(2,1)S(1)}, u32[]{:S(2)}, u32[]{:S(2)}) collective-permute-start(bf16[272,128]{1,0:T(8,128)(2,1)S(1)} %get-tuple-element.13), channel_id=1, source_target_pairs={{0,10},{1,11},{2,8},{3,9},{8,18},{9,19},{10,16},{11,17},{16,26},{1... | collective-permute-start | bytes 208904 | tf_op jit(solution)/shard_map/ppermute | solution.py:235
  69.4 3.6 %collective-permute-start.11 = (bf16[272,128]{1,0:T(8,128)(2,1)S(1)}, bf16[272,128]{1,0:T(8,128)(2,1)S(1)}, u32[]{:S(2)}, u32[]{:S(2)}) collective-permute-start(bf16[272,128]{1,0:T(8,128)(2,1)S(1)} %get-tuple-element.14), channel_id=1, source_target_pairs={{0,9},{1,8},{2,11},{3,10},{8,17},{9,16},{10,19},{11,18},{16,25},{1... | collective-permute-start | bytes 208904 | tf_op jit(solution)/shard_map/ppermute | solution.py:235
  73.0 0.0 collective-permute-start.12
  73.0 0.5 collective-permute-start.9
  73.5 0.1 pad_maximum_fusion
  73.6 2.4 %collective-permute-done.10.refs_1_ = bf16[272,128]{1,0:T(8,128)(2,1)S(1)} collective-permute-done((bf16[272,128]{1,0:T(8,128)(2,1)S(1)}, bf16[272,128]{1,0:T(8,128)(2,1)S(1)}, u32[]{:S(2)}, u32[]{:S(2)}) %collective-permute-start.10) | collective-permute-done | bytes 69664 | tf_op jit(solution)/shard_map/ppermute | solution.py:235
  76.0 0.0 collective-permute-done.11.refs_2_
  76.0 0.7 collective-permute-done.12.refs_3_
  76.7 2.7 %collective-permute-done.9.refs_0_ = bf16[272,128]{1,0:T(8,128)(2,1)S(1)} collective-permute-done((bf16[272,128]{1,0:T(8,128)(2,1)S(1)}, bf16[272,128]{1,0:T(8,128)(2,1)S(1)}, u32[]{:S(2)}, u32[]{:S(2)}) %collective-permute-start.9) | collective-permute-done | bytes 69664 | tf_op jit(solution)/shard_map/ppermute | solution.py:235
  79.4 0.0 copy-done.3
  79.4 1.6 %shard_map.79 = (bf16[64,1536]{1,0:T(8,128)(2,1)}, bf16[64,576]{1,0:T(8,128)(2,1)}) custom-call(s32[4,4]{1,0:T(4,128)S(1)} %dynamic-slice_bitcast_fusion.3.where, bf16[272,128]{1,0:T(8,128)(2,1)S(1)} %collective-permute-done.9.refs_0_, bf16[272,128]{1,0:T(8,128)(2,1)S(1)} %collective-permute-done.10.refs_1_, ...), custom_call_target="tpu_custom_call" | custom-call | tf_op jit(solution)/shard_map/pallas_call | solution.py:242
  (3 shorter events, 0.0 us)
Async XLA Ops:
  0.6 10.3 %copy-start.1 = (bf16[256,1792]{1,0:T(8,128)(2,1)S(1)}, bf16[256,1792]{1,0:T(8,128)(2,1)}, u32[]{:S(2)}) copy-start(bf16[256,1792]{1,0:T(8,128)(2,1)} %refs_0_.1) | copy-start | bytes 2752516
  0.6 49.6 %copy-start.4 = (f32[1536]{0:T(1024)S(1)}, f32[1536]{0:T(1024)}, u32[]{:S(2)}) copy-start(f32[1536]{0:T(1024)} %param.8) | copy-start | bytes 18436
  0.6 52.0 %copy-start.2 = (f32[7168]{0:T(1024)S(1)}, f32[7168]{0:T(1024)}, u32[]{:S(2)}) copy-start(f32[7168]{0:T(1024)} %param.7) | copy-start | bytes 86020
  0.7 26.6 %collective-permute-start = (bf16[256,1792]{1,0:T(8,128)(2,1)}, bf16[256,1792]{1,0:T(8,128)(2,1)S(1)}, u32[]{:S(2)}, u32[]{:S(2)}) collective-permute-start(bf16[256,1792]{1,0:T(8,128)(2,1)} %refs_0_.1), channel_id=1, source_target_pairs={{0,3},{1,2},{2,1},{3,0},{4,7},{5,6},{6,5},{7,4},{8,11},{9,10},{10,... | collective-permute-start | bytes 2752520 | tf_op jit(solution)/shard_map/ppermute | solution.py:176
  7.4 38.4 %collective-permute-start.3 = (bf16[176,1792]{1,0:T(8,128)(2,1)S(1)}, bf16[176,1792]{1,0:T(8,128)(2,1)S(1)}, u32[]{:S(2)}, u32[]{:S(2)}) collective-permute-start(bf16[176,1792]{1,0:T(8,128)(2,1)S(1)} %get-tuple-element.17), channel_id=1, source_target_pairs={{0,4},{4,0},{1,5},{5,1},{2,6},{6,2},{3,7},{7,3},{8,12},{12,8},{9,1... | collective-permute-start | bytes 1892360 | tf_op jit(solution)/shard_map/ppermute | solution.py:185
  8.9 36.8 %collective-permute-start.4 = (bf16[176,1792]{1,0:T(8,128)(2,1)S(1)}, bf16[176,1792]{1,0:T(8,128)(2,1)}, u32[]{:S(2)}, u32[]{:S(2)}) collective-permute-start(bf16[176,1792]{1,0:T(8,128)(2,1)S(1)} %get-tuple-element.18), channel_id=1, source_target_pairs={{0,4},{4,0},{1,5},{5,1},{2,6},{6,2},{3,7},{7,3},{8,12},{12,8},{9,1... | collective-permute-start | bytes 1892360 | tf_op jit(solution)/shard_map/ppermute | solution.py:185
  9.4 40.8 %collective-permute-start.5 = (bf16[176,1792]{1,0:T(8,128)(2,1)S(1)}, bf16[176,1792]{1,0:T(8,128)(2,1)}, u32[]{:S(2)}, u32[]{:S(2)}) collective-permute-start(bf16[176,1792]{1,0:T(8,128)(2,1)S(1)} %get-tuple-element.16), channel_id=1, source_target_pairs={{0,4},{4,0},{1,5},{5,1},{2,6},{6,2},{3,7},{7,3},{8,12},{12,8},{9,1... | collective-permute-start | bytes 1892360 | tf_op jit(solution)/shard_map/ppermute | solution.py:185
  11.0 40.2 %collective-permute-start.2 = (bf16[256,1792]{1,0:T(8,128)(2,1)S(1)}, bf16[256,1792]{1,0:T(8,128)(2,1)S(1)}, u32[]{:S(2)}, u32[]{:S(2)}) collective-permute-start(bf16[256,1792]{1,0:T(8,128)(2,1)S(1)} %copy-done.1), channel_id=1, source_target_pairs={{0,1},{1,0},{2,3},{3,2},{4,5},{5,4},{6,7},{7,6},{8,9},{9,8},{10,11... | collective-permute-start | bytes 2752520 | tf_op jit(solution)/shard_map/ppermute | solution.py:177
  27.3 38.6 %collective-permute-start.1 = (bf16[256,1792]{1,0:T(8,128)(2,1)S(1)}, bf16[256,1792]{1,0:T(8,128)(2,1)}, u32[]{:S(2)}, u32[]{:S(2)}) collective-permute-start(bf16[256,1792]{1,0:T(8,128)(2,1)S(1)} %collective-permute-done.refs_1_), channel_id=1, source_target_pairs={{0,1},{1,0},{2,3},{3,2},{4,5},{5,4},{6,7},{7,6},{8,9},{9,8},{10,11... | collective-permute-start | bytes 2752520 | tf_op jit(solution)/shard_map/ppermute | solution.py:190
  45.7 5.5 %collective-permute-start.6 = (bf16[176,1792]{1,0:T(8,128)(2,1)S(1)}, bf16[176,1792]{1,0:T(8,128)(2,1)}, u32[]{:S(2)}, u32[]{:S(2)}) collective-permute-start(bf16[176,1792]{1,0:T(8,128)(2,1)S(1)} %collective-permute-done.3.refs_5_), channel_id=1, source_target_pairs={{0,8},{8,0},{16,24},{24,16},{1,9},{9,1},{17,25},{25,17},{2,10},{10... | collective-permute-start | bytes 1892360 | tf_op jit(solution)/shard_map/ppermute | solution.py:187
  45.7 5.5 %collective-permute-start.7 = (bf16[176,1792]{1,0:T(8,128)(2,1)}, bf16[176,1792]{1,0:T(8,128)(2,1)}, u32[]{:S(2)}, u32[]{:S(2)}) collective-permute-start(bf16[176,1792]{1,0:T(8,128)(2,1)} %collective-permute-done.4.refs_6_), channel_id=1, source_target_pairs={{0,8},{8,0},{16,24},{24,16},{1,9},{9,1},{17,25},{25,17},{2,10},{10... | collective-permute-start | bytes 1892360 | tf_op jit(solution)/shard_map/ppermute | solution.py:187
  50.2 2.4 %collective-permute-start.8 = (bf16[176,1792]{1,0:T(8,128)(2,1)}, bf16[176,1792]{1,0:T(8,128)(2,1)}, u32[]{:S(2)}, u32[]{:S(2)}) collective-permute-start(bf16[176,1792]{1,0:T(8,128)(2,1)} %collective-permute-done.5.refs_7_), channel_id=1, source_target_pairs={{0,8},{8,0},{16,24},{24,16},{1,9},{9,1},{17,25},{25,17},{2,10},{10... | collective-permute-start | bytes 1892360 | tf_op jit(solution)/shard_map/ppermute | solution.py:187
  52.6 2.1 %copy-start = (bf16[3584,528]{0,1:T(8,128)(2,1)S(1)}, bf16[3584,528]{0,1:T(8,128)(2,1)}, u32[]{:S(2)}) copy-start(bf16[3584,528]{0,1:T(8,128)(2,1)} %param.10) | copy-start | bytes 11354116
  65.9 13.6 %copy-start.3 = (f32[512]{0:T(512)S(1)}, f32[512]{0:T(512)}, u32[]{:S(2)}) copy-start(f32[512]{0:T(512)} %param.9) | copy-start | bytes 6148
  68.2 7.8 %collective-permute-start.10 = (bf16[272,128]{1,0:T(8,128)(2,1)S(1)}, bf16[272,128]{1,0:T(8,128)(2,1)S(1)}, u32[]{:S(2)}, u32[]{:S(2)}) collective-permute-start(bf16[272,128]{1,0:T(8,128)(2,1)S(1)} %get-tuple-element.13), channel_id=1, source_target_pairs={{0,10},{1,11},{2,8},{3,9},{8,18},{9,19},{10,16},{11,17},{16,26},{1... | collective-permute-start | bytes 208904 | tf_op jit(solution)/shard_map/ppermute | solution.py:235
  69.4 6.6 %collective-permute-start.11 = (bf16[272,128]{1,0:T(8,128)(2,1)S(1)}, bf16[272,128]{1,0:T(8,128)(2,1)S(1)}, u32[]{:S(2)}, u32[]{:S(2)}) collective-permute-start(bf16[272,128]{1,0:T(8,128)(2,1)S(1)} %get-tuple-element.14), channel_id=1, source_target_pairs={{0,9},{1,8},{2,11},{3,10},{8,17},{9,16},{10,19},{11,18},{16,25},{1... | collective-permute-start | bytes 208904 | tf_op jit(solution)/shard_map/ppermute | solution.py:235
  73.0 3.8 %collective-permute-start.12 = (bf16[272,128]{1,0:T(8,128)(2,1)S(1)}, bf16[272,128]{1,0:T(8,128)(2,1)S(1)}, u32[]{:S(2)}, u32[]{:S(2)}) collective-permute-start(bf16[272,128]{1,0:T(8,128)(2,1)S(1)} %get-tuple-element.15), channel_id=1, source_target_pairs={{0,8},{1,9},{2,10},{3,11},{8,16},{9,17},{10,18},{11,19},{16,24},{1... | collective-permute-start | bytes 208904 | tf_op jit(solution)/shard_map/ppermute | solution.py:235
  73.0 6.4 %collective-permute-start.9 = (bf16[272,128]{1,0:T(8,128)(2,1)S(1)}, bf16[272,128]{1,0:T(8,128)(2,1)S(1)}, u32[]{:S(2)}, u32[]{:S(2)}) collective-permute-start(bf16[272,128]{1,0:T(8,128)(2,1)S(1)} %get-tuple-element.12), channel_id=1, source_target_pairs={{0,11},{1,10},{2,9},{3,8},{8,19},{9,18},{10,17},{11,16},{16,27},{1... | collective-permute-start | bytes 208904 | tf_op jit(solution)/shard_map/ppermute | solution.py:235

commit v9 on v8

--- a/solution.py
+++ b/solution.py
@@ -173,8 +173,17 @@
     where = lax.dynamic_slice(tables(fsdp, shared), place, (1, 1, 1, 4, PLANES)).reshape(4, PLANES)
     gain = attn_gain.reshape(1, -1)
 
-    mirrored = lax.ppermute(hidden, "ep", [(z, PLANES - 1 - z) for z in range(PLANES)])
-    paired = lax.ppermute(hidden, "ep", [(z, z ^ 1) for z in range(PLANES)])
+    def onward(target_of):
+        moves = [
+            (s * PLANES + z, (s + 1) % section * PLANES + target_of(z))
+            for s in range(section)
+            for z in range(PLANES)
+        ]
+        return lax.ppermute(hidden, ("section", "ep"), moves)
+
+    mirrored = onward(lambda z: PLANES - 1 - z)
+    paired = onward(lambda z: z ^ 1)
+    own = onward(lambda z: z)
     if shared:
         core = lax.axis_index("section") % 2
         height = columns // PARTS
@@ -213,7 +222,7 @@
         ],
         compiler_params=limits,
         cost_estimate=cost(NEAR_COST),
-    )(where, hidden, mirrored, paired, gain, *[part for parts in sources for part in parts])
+    )(where, own, mirrored, paired, gain, *[part for parts in sources for part in parts])
 
     packed = columns // LANES * quarter + PACK
     messages = pl.pallas_call(
@@ -227,12 +236,9 @@
     )(where, far, last_weight, total, squares)
     received = []
     for turn, message in zip(TURNS, messages):
-        moves = [
-            (s * PLANES + z, (s + 1) % section * PLANES + (z ^ turn))
-            for s in range(section)
-            for z in range(PLANES)
-        ]
-        received.append(lax.ppermute(message, ("section", "ep"), moves))
+        if turn:
+            message = lax.ppermute(message, "ep", [(z, z ^ turn) for z in range(PLANES)])
+        received.append(message)
 
     half = ROPE // 2
     position = (fsdp_index * row_count + ep_index * quarter + jnp.arange(quarter)) % LENGTH

time: 81.3 us -> 80.6 us (level)
  waiting for transfers between devices: 32.2 us -> 28.9 us
  starting transfers between devices: 33 us -> 35.6 us
    ppermute x6, waiting for transfers between devices: 22.1 us -> 7 us  [the longest x3 4.37 us: on_device(): lax.ppermute(message, 'ep', [(z, z ^ turn) for z in range(PLANES)])]
    ppermute x3, waiting for transfers between devices: 4 us -> 15.1 us  [on_device(): here = [lax.ppermute(part, 'fsdp', [(0, 1), (1, 0)]) for part in here]]
    ppermute x1, starting transfers between devices: 18.5 us -> 20.5 us  [on_device(): far = lax.ppermute(mirrored, 'ep', [(z, z ^ 1) for z in range(PLANES)])]
    unnamed x10 -> x8, local copies, waits for them, and re-layouts: 2.09 us -> 2.08 us
  transfers between devices with their start and end apart: 13 -> 13, of which waited for: 7 -> 8; matrix products, arithmetic and copies ran while one was open for 3% -> 3% of each run, Pallas kernels for 8% -> 8%
where the time goes in v9:
time: 80.6 us; the launch traced here: 80.3 us
  starting transfers between devices  35.6 us (44%)
  waiting for transfers between devices  28.9 us (36%)
  Pallas kernels  10.4 us (13%)
  local copies, waits for them, and re-layouts  4.36 us (5%)
    ppermute x1, starting transfers between devices, on_device(): far = lax.ppermute(mirrored, 'ep', [(z, z ^ 1) for z in range(PLANES)])  20.5 us
    ppermute x3, waiting for transfers between devices, on_device(): here = [lax.ppermute(part, 'fsdp', [(0, 1), (1, 0)]) for part in here]  15.1 us
    pallas_call x1, Pallas kernels, on_device(): pl.pallas_call(functools.partial(near_kernel, [len(parts) for parts in so...  6.45 us
    ppermute x3, starting transfers between devices, onward(): return lax.ppermute(hidden, ('section', 'ep'), moves)  6.4 us
    ppermute x1, waiting for transfers between devices, on_device(): far = lax.ppermute(mirrored, 'ep', [(z, z ^ 1) for z in range(PLANES)])  4.83 us
    ppermute x3, starting transfers between devices, on_device(): lax.ppermute(message, 'ep', [(z, z ^ turn) for z in range(PLANES)])  4.45 us
    ppermute x3, waiting for transfers between devices, on_device(): lax.ppermute(message, 'ep', [(z, z ^ turn) for z in range(PLANES)])  4.37 us
    ppermute x3, starting transfers between devices, on_device(): here = [lax.ppermute(part, 'fsdp', [(0, 1), (1, 0)]) for part in here]  3.61 us
  transfers between devices with their start and end apart: 13, of which 8 were waited for; matrix products, arithmetic and copies ran while one was open for 3% of the time, Pallas kernels for 8%

profile of v9, /device:TPU:0, one launch (start us, length us, event | category | flops | bytes accessed | tf_op | source)
XLA Modules:
  0.0 80.3 jit_solution(4073268720092144722)
XLA Ops:
  0.6 0.0 copy-start.3
  0.6 0.0 copy-start.1
  0.6 4.5 %collective-permute-start = (bf16[256,1792]{1,0:T(8,128)(2,1)}, bf16[256,1792]{1,0:T(8,128)(2,1)S(1)}, u32[]{:S(2)}, u32[]{:S(2)}) collective-permute-start(bf16[256,1792]{1,0:T(8,128)(2,1)} %param.6), channel_id=1, source_target_pairs={{0,11},{1,10},{2,9},{3,8},{8,19},{9,18},{10,17},{11,16},{16,27},{1... | collective-permute-start | bytes 2752520 | tf_op jit(solution)/shard_map/ppermute | solution.py:182
  5.2 1.6 %dynamic-slice_bitcast_fusion = (bf16[176,1792]{1,0:T(8,128)(2,1)S(1)}, bf16[176,1792]{1,0:T(8,128)(2,1)S(1)}, bf16[176,1792]{1,0:T(8,128)(2,1)S(1)}) fusion(bf16[3584,528]{0,1:T(8,128)(2,1)} %param.10, s32[]{:T(128)S(6)} %select_n.37), kind=kLoop, calls=%fused_computation | loop fusion | bytes 3784708 | tf_op jit(solution)/shard_map/dynamic_slice | solution.py:191
  6.8 1.6 %collective-permute-start.4 = (bf16[176,1792]{1,0:T(8,128)(2,1)S(1)}, bf16[176,1792]{1,0:T(8,128)(2,1)S(1)}, u32[]{:S(2)}, u32[]{:S(2)}) collective-permute-start(bf16[176,1792]{1,0:T(8,128)(2,1)S(1)} %get-tuple-element.17), channel_id=1, source_target_pairs={{0,4},{4,0},{1,5},{5,1},{2,6},{6,2},{3,7},{7,3},{8,12},{12,8},{9,1... | collective-permute-start | bytes 1892360 | tf_op jit(solution)/shard_map/ppermute | solution.py:194
  8.4 1.3 %collective-permute-start.2 = (bf16[256,1792]{1,0:T(8,128)(2,1)}, bf16[256,1792]{1,0:T(8,128)(2,1)S(1)}, u32[]{:S(2)}, u32[]{:S(2)}) collective-permute-start(bf16[256,1792]{1,0:T(8,128)(2,1)} %param.6), channel_id=1, source_target_pairs={{0,8},{1,9},{2,10},{3,11},{8,16},{9,17},{10,18},{11,19},{16,24},{1... | collective-permute-start | bytes 2752520 | tf_op jit(solution)/shard_map/ppermute | solution.py:182
  9.7 0.5 collective-permute-start.5
  10.2 1.5 %collective-permute-start.6 = (bf16[176,1792]{1,0:T(8,128)(2,1)S(1)}, bf16[176,1792]{1,0:T(8,128)(2,1)}, u32[]{:S(2)}, u32[]{:S(2)}) collective-permute-start(bf16[176,1792]{1,0:T(8,128)(2,1)S(1)} %get-tuple-element.16), channel_id=1, source_target_pairs={{0,4},{4,0},{1,5},{5,1},{2,6},{6,2},{3,7},{7,3},{8,12},{12,8},{9,1... | collective-permute-start | bytes 1892360 | tf_op jit(solution)/shard_map/ppermute | solution.py:194
  11.7 11.6 %collective-permute-done.4.refs_5_ = bf16[176,1792]{1,0:T(8,128)(2,1)S(1)} collective-permute-done((bf16[176,1792]{1,0:T(8,128)(2,1)S(1)}, bf16[176,1792]{1,0:T(8,128)(2,1)S(1)}, u32[]{:S(2)}, u32[]{:S(2)}) %collective-permute-start.4) | collective-permute-done | bytes 630816 | tf_op jit(solution)/shard_map/ppermute | solution.py:194
  23.3 0.5 collective-permute-start.3
  23.9 2.6 %collective-permute-done.refs_1_ = bf16[256,1792]{1,0:T(8,128)(2,1)S(1)} collective-permute-done((bf16[256,1792]{1,0:T(8,128)(2,1)}, bf16[256,1792]{1,0:T(8,128)(2,1)S(1)}, u32[]{:S(2)}, u32[]{:S(2)}) %collective-permute-start) | collective-permute-done | bytes 917536 | tf_op jit(solution)/shard_map/ppermute | solution.py:182
  26.5 20.5 %collective-permute-start.1 = (bf16[256,1792]{1,0:T(8,128)(2,1)S(1)}, bf16[256,1792]{1,0:T(8,128)(2,1)}, u32[]{:S(2)}, u32[]{:S(2)}) collective-permute-start(bf16[256,1792]{1,0:T(8,128)(2,1)S(1)} %collective-permute-done.refs_1_), channel_id=1, source_target_pairs={{0,1},{1,0},{2,3},{3,2},{4,5},{5,4},{6,7},{7,6},{8,9},{9,8},{10,11... | collective-permute-start | bytes 2752520 | tf_op jit(solution)/shard_map/ppermute | solution.py:199
  47.0 0.0 collective-permute-done.5.refs_6_
  47.0 0.0 collective-permute-start.7
  47.0 3.5 %collective-permute-done.6.refs_7_ = bf16[176,1792]{1,0:T(8,128)(2,1)} collective-permute-done((bf16[176,1792]{1,0:T(8,128)(2,1)S(1)}, bf16[176,1792]{1,0:T(8,128)(2,1)}, u32[]{:S(2)}, u32[]{:S(2)}) %collective-permute-start.6) | collective-permute-done | bytes 630816 | tf_op jit(solution)/shard_map/ppermute | solution.py:194
  50.5 0.7 collective-permute-start.8
  51.2 0.0 collective-permute-done.2.refs_0_
  51.2 0.0 collective-permute-start.9
  51.2 0.0 copy-done.3
  51.2 0.7 dynamic-slice_bitcast_fusion.3.where
  51.9 0.2 fusion
  52.1 0.0 collective-permute-done.3.refs_2_
  52.1 0.0 collective-permute-done.7.refs_8_
  52.2 1.1 %collective-permute-done.8.refs_9_ = bf16[176,1792]{1,0:T(8,128)(2,1)} collective-permute-done((bf16[176,1792]{1,0:T(8,128)(2,1)}, bf16[176,1792]{1,0:T(8,128)(2,1)}, u32[]{:S(2)}, u32[]{:S(2)}) %collective-permute-start.8) | collective-permute-done | bytes 630816 | tf_op jit(solution)/shard_map/ppermute | solution.py:196
  53.2 0.9 %collective-permute-done.9.refs_10_ = bf16[176,1792]{1,0:T(8,128)(2,1)} collective-permute-done((bf16[176,1792]{1,0:T(8,128)(2,1)}, bf16[176,1792]{1,0:T(8,128)(2,1)}, u32[]{:S(2)}, u32[]{:S(2)}) %collective-permute-start.9) | collective-permute-done | bytes 630816 | tf_op jit(solution)/shard_map/ppermute | solution.py:196
  54.1 0.0 copy-done.1
  54.1 0.0 copy-start
  54.1 2.1 %copy-done = bf16[3584,528]{0,1:T(8,128)(2,1)S(1)} copy-done((bf16[3584,528]{0,1:T(8,128)(2,1)S(1)}, bf16[3584,528]{0,1:T(8,128)(2,1)}, u32[]{:S(2)}) %copy-start) | copy-done | bytes 3784728
  56.2 6.4 %shard_map.77 = (f32[256,528]{1,0:T(8,128)S(1)}, f32[256,1]{1,0:T(8,128)S(1)}, bf16[528,1792]{1,0:T(8,128)(2,1)S(1)}) custom-call(s32[4,4]{1,0:T(4,128)S(1)} %dynamic-slice_bitcast_fusion.3.where, bf16[256,1792]{1,0:T(8,128)(2,1)S(1)} %collective-permute-done.2.refs_0_, bf16[256,1792]{1,0:T(8,128)(2,1)S(1)} %collective-permute-done.refs_1_, ...), custom_call_target="tpu_custom_call" | custom-call | flops 1150000000 | bytes 917504 | tf_op jit(solution)/shard_map/pallas_call | solution.py:208
  62.6 4.8 %collective-permute-done.1.refs_0_ = bf16[256,1792]{1,0:T(8,128)(2,1)} collective-permute-done((bf16[256,1792]{1,0:T(8,128)(2,1)S(1)}, bf16[256,1792]{1,0:T(8,128)(2,1)}, u32[]{:S(2)}, u32[]{:S(2)}) %collective-permute-start.1) | collective-permute-done | bytes 917536 | tf_op jit(solution)/shard_map/ppermute | solution.py:199
  67.5 0.0 copy-start.2
  67.5 2.3 %shard_map.78 = (bf16[272,128]{1,0:T(8,128)(2,1)S(1)}, bf16[272,128]{1,0:T(8,128)(2,1)S(1)}, bf16[272,128]{1,0:T(8,128)(2,1)S(1)}, bf16[272,128]{1,0:T(8,128)(2,1)S(1)}) custom-call(s32[4,4]{1,0:T(4,128)S(1)} %dynamic-slice_bitcast_fusion.3.where, bf16[256,1792]{1,0:T(8,128)(2,1)} %collective-permute-done.1.refs_0_, ...), custom_call_target="tpu_custom_call" | custom-call | flops 2300000000 | bytes 917504 | tf_op jit(solution)/shard_map/pallas_call | solution.py:228
  69.8 2.5 %collective-permute-start.10 = (bf16[272,128]{1,0:T(8,128)(2,1)S(1)}, bf16[272,128]{1,0:T(8,128)(2,1)S(1)}, u32[]{:S(2)}, u32[]{:S(2)}) collective-permute-start(bf16[272,128]{1,0:T(8,128)(2,1)S(1)} %get-tuple-element.12), channel_id=1, source_target_pairs={{0,3},{1,2},{2,1},{3,0},{4,7},{5,6},{6,5},{7,4},{8,11},{9,10},{10,... | collective-permute-start | bytes 208904 | tf_op jit(solution)/shard_map/ppermute | solution.py:240
  72.3 0.0 collective-permute-start.11
  72.3 1.9 %collective-permute-start.12 = (bf16[272,128]{1,0:T(8,128)(2,1)S(1)}, bf16[272,128]{1,0:T(8,128)(2,1)S(1)}, u32[]{:S(2)}, u32[]{:S(2)}) collective-permute-start(bf16[272,128]{1,0:T(8,128)(2,1)S(1)} %get-tuple-element.14), channel_id=1, source_target_pairs={{0,1},{1,0},{2,3},{3,2},{4,5},{5,4},{6,7},{7,6},{8,9},{9,8},{10,11... | collective-permute-start | bytes 208904 | tf_op jit(solution)/shard_map/ppermute | solution.py:240
  74.2 0.1 pad_maximum_fusion
  74.3 1.8 %collective-permute-done.10.refs_0_ = bf16[272,128]{1,0:T(8,128)(2,1)S(1)} collective-permute-done((bf16[272,128]{1,0:T(8,128)(2,1)S(1)}, bf16[272,128]{1,0:T(8,128)(2,1)S(1)}, u32[]{:S(2)}, u32[]{:S(2)}) %collective-permute-start.10) | collective-permute-done | bytes 69664 | tf_op jit(solution)/shard_map/ppermute | solution.py:240
  76.2 2.5 %collective-permute-done.11.refs_1_ = bf16[272,128]{1,0:T(8,128)(2,1)S(1)} collective-permute-done((bf16[272,128]{1,0:T(8,128)(2,1)S(1)}, bf16[272,128]{1,0:T(8,128)(2,1)S(1)}, u32[]{:S(2)}, u32[]{:S(2)}) %collective-permute-start.11) | collective-permute-done | bytes 69664 | tf_op jit(solution)/shard_map/ppermute | solution.py:240
  78.7 0.0 collective-permute-done.12.refs_2_
  78.7 0.0 copy-done.2
  78.7 1.6 %shard_map.79 = (bf16[64,1536]{1,0:T(8,128)(2,1)}, bf16[64,576]{1,0:T(8,128)(2,1)}) custom-call(s32[4,4]{1,0:T(4,128)S(1)} %dynamic-slice_bitcast_fusion.3.where, bf16[272,128]{1,0:T(8,128)(2,1)S(1)} %collective-permute-done.10.refs_0_, bf16[272,128]{1,0:T(8,128)(2,1)S(1)} %collective-permute-done.11.refs_1_, ...), custom_call_target="tpu_custom_call" | custom-call | tf_op jit(solution)/shard_map/pallas_call | solution.py:248
  (3 shorter events, 0.0 us)
Async XLA Ops:
  0.6 50.6 %copy-start.3 = (f32[1536]{0:T(1024)S(1)}, f32[1536]{0:T(1024)}, u32[]{:S(2)}) copy-start(f32[1536]{0:T(1024)} %param.8) | copy-start | bytes 18436
  0.6 53.5 %copy-start.1 = (f32[7168]{0:T(1024)S(1)}, f32[7168]{0:T(1024)}, u32[]{:S(2)}) copy-start(f32[7168]{0:T(1024)} %param.7) | copy-start | bytes 86020
  0.6 25.9 %collective-permute-start = (bf16[256,1792]{1,0:T(8,128)(2,1)}, bf16[256,1792]{1,0:T(8,128)(2,1)S(1)}, u32[]{:S(2)}, u32[]{:S(2)}) collective-permute-start(bf16[256,1792]{1,0:T(8,128)(2,1)} %param.6), channel_id=1, source_target_pairs={{0,11},{1,10},{2,9},{3,8},{8,19},{9,18},{10,17},{11,16},{16,27},{1... | collective-permute-start | bytes 2752520 | tf_op jit(solution)/shard_map/ppermute | solution.py:182
  6.8 16.6 %collective-permute-start.4 = (bf16[176,1792]{1,0:T(8,128)(2,1)S(1)}, bf16[176,1792]{1,0:T(8,128)(2,1)S(1)}, u32[]{:S(2)}, u32[]{:S(2)}) collective-permute-start(bf16[176,1792]{1,0:T(8,128)(2,1)S(1)} %get-tuple-element.17), channel_id=1, source_target_pairs={{0,4},{4,0},{1,5},{5,1},{2,6},{6,2},{3,7},{7,3},{8,12},{12,8},{9,1... | collective-permute-start | bytes 1892360 | tf_op jit(solution)/shard_map/ppermute | solution.py:194
  8.4 42.8 %collective-permute-start.2 = (bf16[256,1792]{1,0:T(8,128)(2,1)}, bf16[256,1792]{1,0:T(8,128)(2,1)S(1)}, u32[]{:S(2)}, u32[]{:S(2)}) collective-permute-start(bf16[256,1792]{1,0:T(8,128)(2,1)} %param.6), channel_id=1, source_target_pairs={{0,8},{1,9},{2,10},{3,11},{8,16},{9,17},{10,18},{11,19},{16,24},{1... | collective-permute-start | bytes 2752520 | tf_op jit(solution)/shard_map/ppermute | solution.py:182
  9.7 37.3 %collective-permute-start.5 = (bf16[176,1792]{1,0:T(8,128)(2,1)S(1)}, bf16[176,1792]{1,0:T(8,128)(2,1)}, u32[]{:S(2)}, u32[]{:S(2)}) collective-permute-start(bf16[176,1792]{1,0:T(8,128)(2,1)S(1)} %get-tuple-element.18), channel_id=1, source_target_pairs={{0,4},{4,0},{1,5},{5,1},{2,6},{6,2},{3,7},{7,3},{8,12},{12,8},{9,1... | collective-permute-start | bytes 1892360 | tf_op jit(solution)/shard_map/ppermute | solution.py:194
  10.2 40.3 %collective-permute-start.6 = (bf16[176,1792]{1,0:T(8,128)(2,1)S(1)}, bf16[176,1792]{1,0:T(8,128)(2,1)}, u32[]{:S(2)}, u32[]{:S(2)}) collective-permute-start(bf16[176,1792]{1,0:T(8,128)(2,1)S(1)} %get-tuple-element.16), channel_id=1, source_target_pairs={{0,4},{4,0},{1,5},{5,1},{2,6},{6,2},{3,7},{7,3},{8,12},{12,8},{9,1... | collective-permute-start | bytes 1892360 | tf_op jit(solution)/shard_map/ppermute | solution.py:194
  23.3 28.8 %collective-permute-start.3 = (bf16[256,1792]{1,0:T(8,128)(2,1)}, bf16[256,1792]{1,0:T(8,128)(2,1)S(1)}, u32[]{:S(2)}, u32[]{:S(2)}) collective-permute-start(bf16[256,1792]{1,0:T(8,128)(2,1)} %param.6), channel_id=1, source_target_pairs={{0,9},{1,8},{2,11},{3,10},{8,17},{9,16},{10,19},{11,18},{16,25},{1... | collective-permute-start | bytes 2752520 | tf_op jit(solution)/shard_map/ppermute | solution.py:182
  26.5 41.0 %collective-permute-start.1 = (bf16[256,1792]{1,0:T(8,128)(2,1)S(1)}, bf16[256,1792]{1,0:T(8,128)(2,1)}, u32[]{:S(2)}, u32[]{:S(2)}) collective-permute-start(bf16[256,1792]{1,0:T(8,128)(2,1)S(1)} %collective-permute-done.refs_1_), channel_id=1, source_target_pairs={{0,1},{1,0},{2,3},{3,2},{4,5},{5,4},{6,7},{7,6},{8,9},{9,8},{10,11... | collective-permute-start | bytes 2752520 | tf_op jit(solution)/shard_map/ppermute | solution.py:199
  47.0 5.2 %collective-permute-start.7 = (bf16[176,1792]{1,0:T(8,128)(2,1)S(1)}, bf16[176,1792]{1,0:T(8,128)(2,1)}, u32[]{:S(2)}, u32[]{:S(2)}) collective-permute-start(bf16[176,1792]{1,0:T(8,128)(2,1)S(1)} %collective-permute-done.4.refs_5_), channel_id=1, source_target_pairs={{0,8},{8,0},{16,24},{24,16},{1,9},{9,1},{17,25},{25,17},{2,10},{10... | collective-permute-start | bytes 1892360 | tf_op jit(solution)/shard_map/ppermute | solution.py:196
  50.5 2.7 %collective-permute-start.8 = (bf16[176,1792]{1,0:T(8,128)(2,1)}, bf16[176,1792]{1,0:T(8,128)(2,1)}, u32[]{:S(2)}, u32[]{:S(2)}) collective-permute-start(bf16[176,1792]{1,0:T(8,128)(2,1)} %collective-permute-done.5.refs_6_), channel_id=1, source_target_pairs={{0,8},{8,0},{16,24},{24,16},{1,9},{9,1},{17,25},{25,17},{2,10},{10... | collective-permute-start | bytes 1892360 | tf_op jit(solution)/shard_map/ppermute | solution.py:196
  51.2 2.9 %collective-permute-start.9 = (bf16[176,1792]{1,0:T(8,128)(2,1)}, bf16[176,1792]{1,0:T(8,128)(2,1)}, u32[]{:S(2)}, u32[]{:S(2)}) collective-permute-start(bf16[176,1792]{1,0:T(8,128)(2,1)} %collective-permute-done.6.refs_7_), channel_id=1, source_target_pairs={{0,8},{8,0},{16,24},{24,16},{1,9},{9,1},{17,25},{25,17},{2,10},{10... | collective-permute-start | bytes 1892360 | tf_op jit(solution)/shard_map/ppermute | solution.py:196
  54.1 2.1 %copy-start = (bf16[3584,528]{0,1:T(8,128)(2,1)S(1)}, bf16[3584,528]{0,1:T(8,128)(2,1)}, u32[]{:S(2)}) copy-start(bf16[3584,528]{0,1:T(8,128)(2,1)} %param.10) | copy-start | bytes 11354116
  67.5 11.2 %copy-start.2 = (f32[512]{0:T(512)S(1)}, f32[512]{0:T(512)}, u32[]{:S(2)}) copy-start(f32[512]{0:T(512)} %param.9) | copy-start | bytes 6148
  69.8 6.4 %collective-permute-start.10 = (bf16[272,128]{1,0:T(8,128)(2,1)S(1)}, bf16[272,128]{1,0:T(8,128)(2,1)S(1)}, u32[]{:S(2)}, u32[]{:S(2)}) collective-permute-start(bf16[272,128]{1,0:T(8,128)(2,1)S(1)} %get-tuple-element.12), channel_id=1, source_target_pairs={{0,3},{1,2},{2,1},{3,0},{4,7},{5,6},{6,5},{7,4},{8,11},{9,10},{10,... | collective-permute-start | bytes 208904 | tf_op jit(solution)/shard_map/ppermute | solution.py:240
  72.3 6.4 %collective-permute-start.11 = (bf16[272,128]{1,0:T(8,128)(2,1)S(1)}, bf16[272,128]{1,0:T(8,128)(2,1)S(1)}, u32[]{:S(2)}, u32[]{:S(2)}) collective-permute-start(bf16[272,128]{1,0:T(8,128)(2,1)S(1)} %get-tuple-element.13), channel_id=1, source_target_pairs={{0,2},{1,3},{2,0},{3,1},{4,6},{5,7},{6,4},{7,5},{8,10},{9,11},{10,... | collective-permute-start | bytes 208904 | tf_op jit(solution)/shard_map/ppermute | solution.py:240
  72.3 6.4 %collective-permute-start.12 = (bf16[272,128]{1,0:T(8,128)(2,1)S(1)}, bf16[272,128]{1,0:T(8,128)(2,1)S(1)}, u32[]{:S(2)}, u32[]{:S(2)}) collective-permute-start(bf16[272,128]{1,0:T(8,128)(2,1)S(1)} %get-tuple-element.14), channel_id=1, source_target_pairs={{0,1},{1,0},{2,3},{3,2},{4,5},{5,4},{6,7},{7,6},{8,9},{9,8},{10,11... | collective-permute-start | bytes 208904 | tf_op jit(solution)/shard_map/ppermute | solution.py:240

commit v10 on v9

--- a/solution.py
+++ b/solution.py
@@ -173,17 +173,17 @@
     where = lax.dynamic_slice(tables(fsdp, shared), place, (1, 1, 1, 4, PLANES)).reshape(4, PLANES)
     gain = attn_gain.reshape(1, -1)
 
-    def onward(target_of):
+    def onward(block, target_of):
         moves = [
             (s * PLANES + z, (s + 1) % section * PLANES + target_of(z))
             for s in range(section)
             for z in range(PLANES)
         ]
-        return lax.ppermute(hidden, ("section", "ep"), moves)
-
-    mirrored = onward(lambda z: PLANES - 1 - z)
-    paired = onward(lambda z: z ^ 1)
-    own = onward(lambda z: z)
+        return lax.ppermute(block, ("section", "ep"), moves)
+
+    mirrored = onward(hidden, lambda z: PLANES - 1 - z)
+    paired = onward(hidden, lambda z: z ^ 1)
+    late = hidden
     if shared:
         core = lax.axis_index("section") % 2
         height = columns // PARTS
@@ -192,10 +192,12 @@
             for part in range(PARTS)
         ]
         here = [lax.ppermute(part, "fsdp", [(0, 1), (1, 0)]) for part in here]
+        late, here[0] = lax.optimization_barrier((hidden, here[0]))
         cores = [(s, s ^ 1) for s in range(section)]
         sources = [[weight], here, [lax.ppermute(part, "section", cores) for part in here]]
     else:
         sources = [[lax.all_gather(weight, "fsdp", axis=1, tiled=True)]]
+    own = onward(late, lambda z: z)
     far = lax.ppermute(mirrored, "ep", [(z, z ^ 1) for z in range(PLANES)])
 
     limits = pltpu.CompilerParams(vmem_limit_bytes=VMEM_LIMIT)

time: 80.6 us -> 79.6 us (0.988)
  waiting for transfers between devices: 28.9 us -> 28 us
where the time goes in v10:
time: 79.6 us; the launch traced here: 79.4 us
  starting transfers between devices  35.6 us (45%)
  waiting for transfers between devices  28 us (35%)
  Pallas kernels  10.4 us (13%)
  local copies, waits for them, and re-layouts  4.36 us (5%)
    ppermute x1, starting transfers between devices, on_device(): far = lax.ppermute(mirrored, 'ep', [(z, z ^ 1) for z in range(PLANES)])  20.5 us
    ppermute x3, waiting for transfers between devices, on_device(): here = [lax.ppermute(part, 'fsdp', [(0, 1), (1, 0)]) for part in here]  15.9 us
    pallas_call x1, Pallas kernels, on_device(): pl.pallas_call(functools.partial(near_kernel, [len(parts) for parts in so...  6.45 us
    ppermute x3, starting transfers between devices, onward(): return lax.ppermute(block, ('section', 'ep'), moves)  6.4 us
    ppermute x3, starting transfers between devices, on_device(): lax.ppermute(message, 'ep', [(z, z ^ turn) for z in range(PLANES)])  4.45 us
    ppermute x3, waiting for transfers between devices, on_device(): lax.ppermute(message, 'ep', [(z, z ^ turn) for z in range(PLANES)])  4.22 us
    ppermute x1, waiting for transfers between devices, on_device(): far = lax.ppermute(mirrored, 'ep', [(z, z ^ 1) for z in range(PLANES)])  4.05 us
    ppermute x3, starting transfers between devices, on_device(): here = [lax.ppermute(part, 'fsdp', [(0, 1), (1, 0)]) for part in here]  3.61 us
  transfers between devices with their start and end apart: 13, of which 8 were waited for; matrix products, arithmetic and copies ran while one was open for 3% of the time, Pallas kernels for 8%

profile of v10, /device:TPU:0, one launch (start us, length us, event | category | flops | bytes accessed | tf_op | source)
XLA Modules:
  0.0 79.4 jit_solution(1309589427686600945)
XLA Ops:
  0.6 0.0 copy-start.3
  0.6 0.0 copy-start.1
  0.6 4.5 %collective-permute-start = (bf16[256,1792]{1,0:T(8,128)(2,1)}, bf16[256,1792]{1,0:T(8,128)(2,1)S(1)}, u32[]{:S(2)}, u32[]{:S(2)}) collective-permute-start(bf16[256,1792]{1,0:T(8,128)(2,1)} %param.6), channel_id=1, source_target_pairs={{0,11},{1,10},{2,9},{3,8},{8,19},{9,18},{10,17},{11,16},{16,27},{1... | collective-permute-start | bytes 2752520 | tf_op jit(solution)/shard_map/ppermute | solution.py:182
  5.2 1.6 %dynamic-slice_bitcast_fusion = (bf16[176,1792]{1,0:T(8,128)(2,1)S(1)}, bf16[176,1792]{1,0:T(8,128)(2,1)S(1)}, bf16[176,1792]{1,0:T(8,128)(2,1)S(1)}) fusion(bf16[3584,528]{0,1:T(8,128)(2,1)} %param.10, s32[]{:T(128)S(6)} %select_n.37), kind=kLoop, calls=%fused_computation | loop fusion | bytes 3784708 | tf_op jit(solution)/shard_map/dynamic_slice | solution.py:191
  6.8 1.6 %collective-permute-start.2 = (bf16[176,1792]{1,0:T(8,128)(2,1)S(1)}, bf16[176,1792]{1,0:T(8,128)(2,1)S(1)}, u32[]{:S(2)}, u32[]{:S(2)}) collective-permute-start(bf16[176,1792]{1,0:T(8,128)(2,1)S(1)} %get-tuple-element.21), channel_id=1, source_target_pairs={{0,4},{4,0},{1,5},{5,1},{2,6},{6,2},{3,7},{7,3},{8,12},{12,8},{9,1... | collective-permute-start | bytes 1892360 | tf_op jit(solution)/shard_map/ppermute | solution.py:194
  8.4 0.5 collective-permute-start.4
  8.8 0.5 collective-permute-start.5
  9.3 1.5 %collective-permute-start.6 = (bf16[176,1792]{1,0:T(8,128)(2,1)S(1)}, bf16[176,1792]{1,0:T(8,128)(2,1)}, u32[]{:S(2)}, u32[]{:S(2)}) collective-permute-start(bf16[176,1792]{1,0:T(8,128)(2,1)S(1)} %get-tuple-element.20), channel_id=1, source_target_pairs={{0,4},{4,0},{1,5},{5,1},{2,6},{6,2},{3,7},{7,3},{8,12},{12,8},{9,1... | collective-permute-start | bytes 1892360 | tf_op jit(solution)/shard_map/ppermute | solution.py:194
  10.9 12.5 %collective-permute-done.2.refs_5_ = bf16[176,1792]{1,0:T(8,128)(2,1)S(1)} collective-permute-done((bf16[176,1792]{1,0:T(8,128)(2,1)S(1)}, bf16[176,1792]{1,0:T(8,128)(2,1)S(1)}, u32[]{:S(2)}, u32[]{:S(2)}) %collective-permute-start.2) | collective-permute-done | bytes 630816 | tf_op jit(solution)/shard_map/ppermute | solution.py:194
  23.3 1.4 %collective-permute-start.3 = (bf16[256,1792]{1,0:T(8,128)(2,1)}, bf16[256,1792]{1,0:T(8,128)(2,1)S(1)}, u32[]{:S(2)}, u32[]{:S(2)}) collective-permute-start(bf16[256,1792]{1,0:T(8,128)(2,1)} %param.6), channel_id=1, source_target_pairs={{0,8},{1,9},{2,10},{3,11},{8,16},{9,17},{10,18},{11,19},{16,24},{1... | collective-permute-start | bytes 2752520 | tf_op jit(solution)/shard_map/ppermute | solution.py:182
  24.7 1.9 %collective-permute-done.refs_1_ = bf16[256,1792]{1,0:T(8,128)(2,1)S(1)} collective-permute-done((bf16[256,1792]{1,0:T(8,128)(2,1)}, bf16[256,1792]{1,0:T(8,128)(2,1)S(1)}, u32[]{:S(2)}, u32[]{:S(2)}) %collective-permute-start) | collective-permute-done | bytes 917536 | tf_op jit(solution)/shard_map/ppermute | solution.py:182
  26.6 20.5 %collective-permute-start.1 = (bf16[256,1792]{1,0:T(8,128)(2,1)S(1)}, bf16[256,1792]{1,0:T(8,128)(2,1)}, u32[]{:S(2)}, u32[]{:S(2)}) collective-permute-start(bf16[256,1792]{1,0:T(8,128)(2,1)S(1)} %collective-permute-done.refs_1_), channel_id=1, source_target_pairs={{0,1},{1,0},{2,3},{3,2},{4,5},{5,4},{6,7},{7,6},{8,9},{9,8},{10,11... | collective-permute-start | bytes 2752520 | tf_op jit(solution)/shard_map/ppermute | solution.py:201
  47.1 0.0 collective-permute-done.5.refs_6_
  47.1 0.0 collective-permute-start.7
  47.1 3.4 %collective-permute-done.6.refs_7_ = bf16[176,1792]{1,0:T(8,128)(2,1)} collective-permute-done((bf16[176,1792]{1,0:T(8,128)(2,1)S(1)}, bf16[176,1792]{1,0:T(8,128)(2,1)}, u32[]{:S(2)}, u32[]{:S(2)}) %collective-permute-start.6) | collective-permute-done | bytes 630816 | tf_op jit(solution)/shard_map/ppermute | solution.py:194
  50.5 0.7 collective-permute-start.8
  51.2 0.0 collective-permute-done.4.refs_2_
  51.2 0.0 collective-permute-start.9
  51.2 0.0 copy-done.3
  51.2 0.7 dynamic-slice_bitcast_fusion.3.where
  51.9 0.2 fusion
  52.1 0.0 collective-permute-done.7.refs_8_
  52.1 1.1 %collective-permute-done.8.refs_9_ = bf16[176,1792]{1,0:T(8,128)(2,1)} collective-permute-done((bf16[176,1792]{1,0:T(8,128)(2,1)}, bf16[176,1792]{1,0:T(8,128)(2,1)}, u32[]{:S(2)}, u32[]{:S(2)}) %collective-permute-start.8) | collective-permute-done | bytes 630816 | tf_op jit(solution)/shard_map/ppermute | solution.py:197
  53.2 0.9 %collective-permute-done.9.refs_10_ = bf16[176,1792]{1,0:T(8,128)(2,1)} collective-permute-done((bf16[176,1792]{1,0:T(8,128)(2,1)}, bf16[176,1792]{1,0:T(8,128)(2,1)}, u32[]{:S(2)}, u32[]{:S(2)}) %collective-permute-start.9) | collective-permute-done | bytes 630816 | tf_op jit(solution)/shard_map/ppermute | solution.py:197
  54.1 0.0 collective-permute-done.3.refs_0_
  54.1 0.0 copy-done.1
  54.1 0.0 copy-start
  54.1 2.1 %copy-done = bf16[3584,528]{0,1:T(8,128)(2,1)S(1)} copy-done((bf16[3584,528]{0,1:T(8,128)(2,1)S(1)}, bf16[3584,528]{0,1:T(8,128)(2,1)}, u32[]{:S(2)}) %copy-start) | copy-done | bytes 3784728
  56.2 6.4 %shard_map.77 = (f32[256,528]{1,0:T(8,128)S(1)}, f32[256,1]{1,0:T(8,128)S(1)}, bf16[528,1792]{1,0:T(8,128)(2,1)S(1)}) custom-call(s32[4,4]{1,0:T(4,128)S(1)} %dynamic-slice_bitcast_fusion.3.where, bf16[256,1792]{1,0:T(8,128)(2,1)S(1)} %collective-permute-done.3.refs_0_, bf16[256,1792]{1,0:T(8,128)(2,1)S(1)} %collective-permute-done.refs_1_, ...), custom_call_target="tpu_custom_call" | custom-call | flops 1150000000 | bytes 917504 | tf_op jit(solution)/shard_map/pallas_call | solution.py:210
  62.6 4.1 %collective-permute-done.1.refs_0_ = bf16[256,1792]{1,0:T(8,128)(2,1)} collective-permute-done((bf16[256,1792]{1,0:T(8,128)(2,1)S(1)}, bf16[256,1792]{1,0:T(8,128)(2,1)}, u32[]{:S(2)}, u32[]{:S(2)}) %collective-permute-start.1) | collective-permute-done | bytes 917536 | tf_op jit(solution)/shard_map/ppermute | solution.py:201
  66.7 0.0 copy-start.2
  66.7 2.3 %shard_map.78 = (bf16[272,128]{1,0:T(8,128)(2,1)S(1)}, bf16[272,128]{1,0:T(8,128)(2,1)S(1)}, bf16[272,128]{1,0:T(8,128)(2,1)S(1)}, bf16[272,128]{1,0:T(8,128)(2,1)S(1)}) custom-call(s32[4,4]{1,0:T(4,128)S(1)} %dynamic-slice_bitcast_fusion.3.where, bf16[256,1792]{1,0:T(8,128)(2,1)} %collective-permute-done.1.refs_0_, ...), custom_call_target="tpu_custom_call" | custom-call | flops 2300000000 | bytes 917504 | tf_op jit(solution)/shard_map/pallas_call | solution.py:230
  69.0 3.3 %collective-permute-start.10 = (bf16[272,128]{1,0:T(8,128)(2,1)S(1)}, bf16[272,128]{1,0:T(8,128)(2,1)S(1)}, u32[]{:S(2)}, u32[]{:S(2)}) collective-permute-start(bf16[272,128]{1,0:T(8,128)(2,1)S(1)} %get-tuple-element.16), channel_id=1, source_target_pairs={{0,3},{1,2},{2,1},{3,0},{4,7},{5,6},{6,5},{7,4},{8,11},{9,10},{10,... | collective-permute-start | bytes 208904 | tf_op jit(solution)/shard_map/ppermute | solution.py:242
  72.3 0.0 collective-permute-start.11
  72.3 1.1 %collective-permute-start.12 = (bf16[272,128]{1,0:T(8,128)(2,1)S(1)}, bf16[272,128]{1,0:T(8,128)(2,1)S(1)}, u32[]{:S(2)}, u32[]{:S(2)}) collective-permute-start(bf16[272,128]{1,0:T(8,128)(2,1)S(1)} %get-tuple-element.18), channel_id=1, source_target_pairs={{0,1},{1,0},{2,3},{3,2},{4,5},{5,4},{6,7},{7,6},{8,9},{9,8},{10,11... | collective-permute-start | bytes 208904 | tf_op jit(solution)/shard_map/ppermute | solution.py:242
  73.5 0.1 pad_maximum_fusion
  73.6 1.7 %collective-permute-done.10.refs_0_ = bf16[272,128]{1,0:T(8,128)(2,1)S(1)} collective-permute-done((bf16[272,128]{1,0:T(8,128)(2,1)S(1)}, bf16[272,128]{1,0:T(8,128)(2,1)S(1)}, u32[]{:S(2)}, u32[]{:S(2)}) %collective-permute-start.10) | collective-permute-done | bytes 69664 | tf_op jit(solution)/shard_map/ppermute | solution.py:242
  75.3 2.5 %collective-permute-done.11.refs_1_ = bf16[272,128]{1,0:T(8,128)(2,1)S(1)} collective-permute-done((bf16[272,128]{1,0:T(8,128)(2,1)S(1)}, bf16[272,128]{1,0:T(8,128)(2,1)S(1)}, u32[]{:S(2)}, u32[]{:S(2)}) %collective-permute-start.11) | collective-permute-done | bytes 69664 | tf_op jit(solution)/shard_map/ppermute | solution.py:242
  77.8 0.0 collective-permute-done.12.refs_2_
  77.8 0.0 copy-done.2
  77.8 1.6 %shard_map.79 = (bf16[64,1536]{1,0:T(8,128)(2,1)}, bf16[64,576]{1,0:T(8,128)(2,1)}) custom-call(s32[4,4]{1,0:T(4,128)S(1)} %dynamic-slice_bitcast_fusion.3.where, bf16[272,128]{1,0:T(8,128)(2,1)S(1)} %collective-permute-done.10.refs_0_, bf16[272,128]{1,0:T(8,128)(2,1)S(1)} %collective-permute-done.11.refs_1_, ...), custom_call_target="tpu_custom_call" | custom-call | tf_op jit(solution)/shard_map/pallas_call | solution.py:250
  (3 shorter events, 0.0 us)
Async XLA Ops:
  0.6 50.6 %copy-start.3 = (f32[1536]{0:T(1024)S(1)}, f32[1536]{0:T(1024)}, u32[]{:S(2)}) copy-start(f32[1536]{0:T(1024)} %param.8) | copy-start | bytes 18436
  0.6 53.5 %copy-start.1 = (f32[7168]{0:T(1024)S(1)}, f32[7168]{0:T(1024)}, u32[]{:S(2)}) copy-start(f32[7168]{0:T(1024)} %param.7) | copy-start | bytes 86020
  0.6 26.0 %collective-permute-start = (bf16[256,1792]{1,0:T(8,128)(2,1)}, bf16[256,1792]{1,0:T(8,128)(2,1)S(1)}, u32[]{:S(2)}, u32[]{:S(2)}) collective-permute-start(bf16[256,1792]{1,0:T(8,128)(2,1)} %param.6), channel_id=1, source_target_pairs={{0,11},{1,10},{2,9},{3,8},{8,19},{9,18},{10,17},{11,16},{16,27},{1... | collective-permute-start | bytes 2752520 | tf_op jit(solution)/shard_map/ppermute | solution.py:182
  6.8 16.6 %collective-permute-start.2 = (bf16[176,1792]{1,0:T(8,128)(2,1)S(1)}, bf16[176,1792]{1,0:T(8,128)(2,1)S(1)}, u32[]{:S(2)}, u32[]{:S(2)}) collective-permute-start(bf16[176,1792]{1,0:T(8,128)(2,1)S(1)} %get-tuple-element.21), channel_id=1, source_target_pairs={{0,4},{4,0},{1,5},{5,1},{2,6},{6,2},{3,7},{7,3},{8,12},{12,8},{9,1... | collective-permute-start | bytes 1892360 | tf_op jit(solution)/shard_map/ppermute | solution.py:194
  8.4 42.8 %collective-permute-start.4 = (bf16[256,1792]{1,0:T(8,128)(2,1)}, bf16[256,1792]{1,0:T(8,128)(2,1)S(1)}, u32[]{:S(2)}, u32[]{:S(2)}) collective-permute-start(bf16[256,1792]{1,0:T(8,128)(2,1)} %param.6), channel_id=1, source_target_pairs={{0,9},{1,8},{2,11},{3,10},{8,17},{9,16},{10,19},{11,18},{16,25},{1... | collective-permute-start | bytes 2752520 | tf_op jit(solution)/shard_map/ppermute | solution.py:182
  8.8 38.3 %collective-permute-start.5 = (bf16[176,1792]{1,0:T(8,128)(2,1)S(1)}, bf16[176,1792]{1,0:T(8,128)(2,1)}, u32[]{:S(2)}, u32[]{:S(2)}) collective-permute-start(bf16[176,1792]{1,0:T(8,128)(2,1)S(1)} %get-tuple-element.22), channel_id=1, source_target_pairs={{0,4},{4,0},{1,5},{5,1},{2,6},{6,2},{3,7},{7,3},{8,12},{12,8},{9,1... | collective-permute-start | bytes 1892360 | tf_op jit(solution)/shard_map/ppermute | solution.py:194
  9.3 41.1 %collective-permute-start.6 = (bf16[176,1792]{1,0:T(8,128)(2,1)S(1)}, bf16[176,1792]{1,0:T(8,128)(2,1)}, u32[]{:S(2)}, u32[]{:S(2)}) collective-permute-start(bf16[176,1792]{1,0:T(8,128)(2,1)S(1)} %get-tuple-element.20), channel_id=1, source_target_pairs={{0,4},{4,0},{1,5},{5,1},{2,6},{6,2},{3,7},{7,3},{8,12},{12,8},{9,1... | collective-permute-start | bytes 1892360 | tf_op jit(solution)/shard_map/ppermute | solution.py:194
  23.3 30.8 %collective-permute-start.3 = (bf16[256,1792]{1,0:T(8,128)(2,1)}, bf16[256,1792]{1,0:T(8,128)(2,1)S(1)}, u32[]{:S(2)}, u32[]{:S(2)}) collective-permute-start(bf16[256,1792]{1,0:T(8,128)(2,1)} %param.6), channel_id=1, source_target_pairs={{0,8},{1,9},{2,10},{3,11},{8,16},{9,17},{10,18},{11,19},{16,24},{1... | collective-permute-start | bytes 2752520 | tf_op jit(solution)/shard_map/ppermute | solution.py:182
  26.6 40.1 %collective-permute-start.1 = (bf16[256,1792]{1,0:T(8,128)(2,1)S(1)}, bf16[256,1792]{1,0:T(8,128)(2,1)}, u32[]{:S(2)}, u32[]{:S(2)}) collective-permute-start(bf16[256,1792]{1,0:T(8,128)(2,1)S(1)} %collective-permute-done.refs_1_), channel_id=1, source_target_pairs={{0,1},{1,0},{2,3},{3,2},{4,5},{5,4},{6,7},{7,6},{8,9},{9,8},{10,11... | collective-permute-start | bytes 2752520 | tf_op jit(solution)/shard_map/ppermute | solution.py:201
  47.1 5.0 %collective-permute-start.7 = (bf16[176,1792]{1,0:T(8,128)(2,1)S(1)}, bf16[176,1792]{1,0:T(8,128)(2,1)}, u32[]{:S(2)}, u32[]{:S(2)}) collective-permute-start(bf16[176,1792]{1,0:T(8,128)(2,1)S(1)} %collective-permute-done.2.refs_5_), channel_id=1, source_target_pairs={{0,8},{8,0},{16,24},{24,16},{1,9},{9,1},{17,25},{25,17},{2,10},{10... | collective-permute-start | bytes 1892360 | tf_op jit(solution)/shard_map/ppermute | solution.py:197
  50.5 2.7 %collective-permute-start.8 = (bf16[176,1792]{1,0:T(8,128)(2,1)}, bf16[176,1792]{1,0:T(8,128)(2,1)}, u32[]{:S(2)}, u32[]{:S(2)}) collective-permute-start(bf16[176,1792]{1,0:T(8,128)(2,1)} %collective-permute-done.5.refs_6_), channel_id=1, source_target_pairs={{0,8},{8,0},{16,24},{24,16},{1,9},{9,1},{17,25},{25,17},{2,10},{10... | collective-permute-start | bytes 1892360 | tf_op jit(solution)/shard_map/ppermute | solution.py:197
  51.2 2.9 %collective-permute-start.9 = (bf16[176,1792]{1,0:T(8,128)(2,1)}, bf16[176,1792]{1,0:T(8,128)(2,1)}, u32[]{:S(2)}, u32[]{:S(2)}) collective-permute-start(bf16[176,1792]{1,0:T(8,128)(2,1)} %collective-permute-done.6.refs_7_), channel_id=1, source_target_pairs={{0,8},{8,0},{16,24},{24,16},{1,9},{9,1},{17,25},{25,17},{2,10},{10... | collective-permute-start | bytes 1892360 | tf_op jit(solution)/shard_map/ppermute | solution.py:197
  54.1 2.1 %copy-start = (bf16[3584,528]{0,1:T(8,128)(2,1)S(1)}, bf16[3584,528]{0,1:T(8,128)(2,1)}, u32[]{:S(2)}) copy-start(bf16[3584,528]{0,1:T(8,128)(2,1)} %param.10) | copy-start | bytes 11354116
  66.7 11.1 %copy-start.2 = (f32[512]{0:T(512)S(1)}, f32[512]{0:T(512)}, u32[]{:S(2)}) copy-start(f32[512]{0:T(512)} %param.9) | copy-start | bytes 6148
  69.0 6.3 %collective-permute-start.10 = (bf16[272,128]{1,0:T(8,128)(2,1)S(1)}, bf16[272,128]{1,0:T(8,128)(2,1)S(1)}, u32[]{:S(2)}, u32[]{:S(2)}) collective-permute-start(bf16[272,128]{1,0:T(8,128)(2,1)S(1)} %get-tuple-element.16), channel_id=1, source_target_pairs={{0,3},{1,2},{2,1},{3,0},{4,7},{5,6},{6,5},{7,4},{8,11},{9,10},{10,... | collective-permute-start | bytes 208904 | tf_op jit(solution)/shard_map/ppermute | solution.py:242
  72.3 5.4 %collective-permute-start.11 = (bf16[272,128]{1,0:T(8,128)(2,1)S(1)}, bf16[272,128]{1,0:T(8,128)(2,1)S(1)}, u32[]{:S(2)}, u32[]{:S(2)}) collective-permute-start(bf16[272,128]{1,0:T(8,128)(2,1)S(1)} %get-tuple-element.17), channel_id=1, source_target_pairs={{0,2},{1,3},{2,0},{3,1},{4,6},{5,7},{6,4},{7,5},{8,10},{9,11},{10,... | collective-permute-start | bytes 208904 | tf_op jit(solution)/shard_map/ppermute | solution.py:242
  72.3 5.4 %collective-permute-start.12 = (bf16[272,128]{1,0:T(8,128)(2,1)S(1)}, bf16[272,128]{1,0:T(8,128)(2,1)S(1)}, u32[]{:S(2)}, u32[]{:S(2)}) collective-permute-start(bf16[272,128]{1,0:T(8,128)(2,1)S(1)} %get-tuple-element.18), channel_id=1, source_target_pairs={{0,1},{1,0},{2,3},{3,2},{4,5},{5,4},{6,7},{7,6},{8,9},{9,8},{10,11... | collective-permute-start | bytes 208904 | tf_op jit(solution)/shard_map/ppermute | solution.py:242

commit v11 on v10

--- a/solution.py
+++ b/solution.py
@@ -124,7 +124,10 @@
     scaled[...] = total * lax.rsqrt(squares / depth + epsilon)
     for turn, out_ref in zip(TURNS, refs):
         at = pl.multiple_of(where[3, turn] * quarter, quarter)
-        pack(scaled[pl.ds(at, quarter), :], out_ref)
+        if turn:
+            pack(scaled[pl.ds(at, quarter), :], out_ref)
+        else:
+            out_ref[...] = scaled[pl.ds(at, quarter), :]
 
 
 def finish_kernel(where, *refs):
@@ -132,7 +135,10 @@
     part_refs = [refs.pop(0) for _ in range(len(refs) - 7)]
     q_gain_ref, kv_gain_ref, cosine_ref, sine_ref, query_ref, cache_ref, parts = refs
     for turn, ref in zip(TURNS, part_refs):
-        unpack(ref, parts.at[where[3, turn]])
+        if turn:
+            unpack(ref, parts.at[where[3, turn]])
+        else:
+            parts[where[3, turn]] = ref[...]
     latent = jnp.concatenate([parts[plane] for plane in range(PLANES)], axis=1)
 
     def normed(values, gain):
@@ -229,9 +235,14 @@
     packed = columns // LANES * quarter + PACK
     messages = pl.pallas_call(
         functools.partial(last_kernel, PLANES * width, quarter),
-        out_shape=(jax.ShapeDtypeStruct((packed, LANES), jnp.bfloat16),) * PLANES,
+        out_shape=[
+            jax.ShapeDtypeStruct((packed, LANES), jnp.bfloat16)
+            if turn
+            else jax.ShapeDtypeStruct((quarter, columns), jnp.float32)
+            for turn in TURNS
+        ],
         in_specs=[smem] + [vmem] * 4,
-        out_specs=(vmem,) * PLANES,
+        out_specs=[vmem] * PLANES,
         scratch_shapes=[pltpu.VMEM((row_count, columns), jnp.float32)],
         compiler_params=limits,
         cost_estimate=cost(LAST_COST),

time: 79.6 us -> 79.6 us (level)
  no operation moved by 1% of the time
where the time goes in v11:
time: 79.6 us; the launch traced here: 79.4 us
  starting transfers between devices  35.6 us (45%)
  waiting for transfers between devices  28 us (35%)
  Pallas kernels  10.4 us (13%)
  local copies, waits for them, and re-layouts  4.36 us (5%)
    ppermute x1, starting transfers between devices, on_device(): far = lax.ppermute(mirrored, 'ep', [(z, z ^ 1) for z in range(PLANES)])  20.5 us
    ppermute x3, waiting for transfers between devices, on_device(): here = [lax.ppermute(part, 'fsdp', [(0, 1), (1, 0)]) for part in here]  15.9 us
    pallas_call x1, Pallas kernels, on_device(): pl.pallas_call(functools.partial(near_kernel, [len(parts) for parts in so...  6.44 us
    ppermute x3, starting transfers between devices, onward(): return lax.ppermute(block, ('section', 'ep'), moves)  6.4 us
    ppermute x3, starting transfers between devices, on_device(): lax.ppermute(message, 'ep', [(z, z ^ turn) for z in range(PLANES)])  4.45 us
    ppermute x3, waiting for transfers between devices, on_device(): lax.ppermute(message, 'ep', [(z, z ^ turn) for z in range(PLANES)])  4.21 us
    ppermute x1, waiting for transfers between devices, on_device(): far = lax.ppermute(mirrored, 'ep', [(z, z ^ 1) for z in range(PLANES)])  4.06 us
    ppermute x3, starting transfers between devices, on_device(): here = [lax.ppermute(part, 'fsdp', [(0, 1), (1, 0)]) for part in here]  3.61 us
  transfers between devices with their start and end apart: 13, of which 8 were waited for; matrix products, arithmetic and copies ran while one was open for 3% of the time, Pallas kernels for 8%

profile of v11, /device:TPU:0, one launch (start us, length us, event | category | flops | bytes accessed | tf_op | source)
XLA Modules:
  0.0 79.4 jit_solution(15176357486674173663)
XLA Ops:
  0.6 0.0 copy-start.3
  0.6 0.0 copy-start.1
  0.6 4.5 %collective-permute-start = (bf16[256,1792]{1,0:T(8,128)(2,1)}, bf16[256,1792]{1,0:T(8,128)(2,1)S(1)}, u32[]{:S(2)}, u32[]{:S(2)}) collective-permute-start(bf16[256,1792]{1,0:T(8,128)(2,1)} %param.6), channel_id=1, source_target_pairs={{0,11},{1,10},{2,9},{3,8},{8,19},{9,18},{10,17},{11,16},{16,27},{1... | collective-permute-start | bytes 2752520 | tf_op jit(solution)/shard_map/ppermute | solution.py:188
  5.2 1.6 %dynamic-slice_bitcast_fusion = (bf16[176,1792]{1,0:T(8,128)(2,1)S(1)}, bf16[176,1792]{1,0:T(8,128)(2,1)S(1)}, bf16[176,1792]{1,0:T(8,128)(2,1)S(1)}) fusion(bf16[3584,528]{0,1:T(8,128)(2,1)} %param.10, s32[]{:T(128)S(6)} %select_n.37), kind=kLoop, calls=%fused_computation | loop fusion | bytes 3784708 | tf_op jit(solution)/shard_map/dynamic_slice | solution.py:197
  6.8 1.6 %collective-permute-start.2 = (bf16[176,1792]{1,0:T(8,128)(2,1)S(1)}, bf16[176,1792]{1,0:T(8,128)(2,1)S(1)}, u32[]{:S(2)}, u32[]{:S(2)}) collective-permute-start(bf16[176,1792]{1,0:T(8,128)(2,1)S(1)} %get-tuple-element.21), channel_id=1, source_target_pairs={{0,4},{4,0},{1,5},{5,1},{2,6},{6,2},{3,7},{7,3},{8,12},{12,8},{9,1... | collective-permute-start | bytes 1892360 | tf_op jit(solution)/shard_map/ppermute | solution.py:200
  8.4 0.5 collective-permute-start.4
  8.8 0.5 collective-permute-start.5
  9.3 1.5 %collective-permute-start.6 = (bf16[176,1792]{1,0:T(8,128)(2,1)S(1)}, bf16[176,1792]{1,0:T(8,128)(2,1)}, u32[]{:S(2)}, u32[]{:S(2)}) collective-permute-start(bf16[176,1792]{1,0:T(8,128)(2,1)S(1)} %get-tuple-element.20), channel_id=1, source_target_pairs={{0,4},{4,0},{1,5},{5,1},{2,6},{6,2},{3,7},{7,3},{8,12},{12,8},{9,1... | collective-permute-start | bytes 1892360 | tf_op jit(solution)/shard_map/ppermute | solution.py:200
  10.9 12.5 %collective-permute-done.2.refs_5_ = bf16[176,1792]{1,0:T(8,128)(2,1)S(1)} collective-permute-done((bf16[176,1792]{1,0:T(8,128)(2,1)S(1)}, bf16[176,1792]{1,0:T(8,128)(2,1)S(1)}, u32[]{:S(2)}, u32[]{:S(2)}) %collective-permute-start.2) | collective-permute-done | bytes 630816 | tf_op jit(solution)/shard_map/ppermute | solution.py:200
  23.3 1.4 %collective-permute-start.3 = (bf16[256,1792]{1,0:T(8,128)(2,1)}, bf16[256,1792]{1,0:T(8,128)(2,1)S(1)}, u32[]{:S(2)}, u32[]{:S(2)}) collective-permute-start(bf16[256,1792]{1,0:T(8,128)(2,1)} %param.6), channel_id=1, source_target_pairs={{0,8},{1,9},{2,10},{3,11},{8,16},{9,17},{10,18},{11,19},{16,24},{1... | collective-permute-start | bytes 2752520 | tf_op jit(solution)/shard_map/ppermute | solution.py:188
  24.7 1.9 %collective-permute-done.refs_1_ = bf16[256,1792]{1,0:T(8,128)(2,1)S(1)} collective-permute-done((bf16[256,1792]{1,0:T(8,128)(2,1)}, bf16[256,1792]{1,0:T(8,128)(2,1)S(1)}, u32[]{:S(2)}, u32[]{:S(2)}) %collective-permute-start) | collective-permute-done | bytes 917536 | tf_op jit(solution)/shard_map/ppermute | solution.py:188
  26.6 20.5 %collective-permute-start.1 = (bf16[256,1792]{1,0:T(8,128)(2,1)S(1)}, bf16[256,1792]{1,0:T(8,128)(2,1)}, u32[]{:S(2)}, u32[]{:S(2)}) collective-permute-start(bf16[256,1792]{1,0:T(8,128)(2,1)S(1)} %collective-permute-done.refs_1_), channel_id=1, source_target_pairs={{0,1},{1,0},{2,3},{3,2},{4,5},{5,4},{6,7},{7,6},{8,9},{9,8},{10,11... | collective-permute-start | bytes 2752520 | tf_op jit(solution)/shard_map/ppermute | solution.py:207
  47.1 0.0 collective-permute-done.5.refs_6_
  47.1 0.0 collective-permute-start.7
  47.1 3.4 %collective-permute-done.6.refs_7_ = bf16[176,1792]{1,0:T(8,128)(2,1)} collective-permute-done((bf16[176,1792]{1,0:T(8,128)(2,1)S(1)}, bf16[176,1792]{1,0:T(8,128)(2,1)}, u32[]{:S(2)}, u32[]{:S(2)}) %collective-permute-start.6) | collective-permute-done | bytes 630816 | tf_op jit(solution)/shard_map/ppermute | solution.py:200
  50.5 0.7 collective-permute-start.8
  51.2 0.0 collective-permute-done.4.refs_2_
  51.2 0.0 collective-permute-start.9
  51.2 0.0 copy-done.3
  51.2 0.7 dynamic-slice_bitcast_fusion.3.where
  51.9 0.2 fusion
  52.1 0.0 collective-permute-done.7.refs_8_
  52.1 1.1 %collective-permute-done.8.refs_9_ = bf16[176,1792]{1,0:T(8,128)(2,1)} collective-permute-done((bf16[176,1792]{1,0:T(8,128)(2,1)}, bf16[176,1792]{1,0:T(8,128)(2,1)}, u32[]{:S(2)}, u32[]{:S(2)}) %collective-permute-start.8) | collective-permute-done | bytes 630816 | tf_op jit(solution)/shard_map/ppermute | solution.py:203
  53.2 0.9 %collective-permute-done.9.refs_10_ = bf16[176,1792]{1,0:T(8,128)(2,1)} collective-permute-done((bf16[176,1792]{1,0:T(8,128)(2,1)}, bf16[176,1792]{1,0:T(8,128)(2,1)}, u32[]{:S(2)}, u32[]{:S(2)}) %collective-permute-start.9) | collective-permute-done | bytes 630816 | tf_op jit(solution)/shard_map/ppermute | solution.py:203
  54.1 0.0 collective-permute-done.3.refs_0_
  54.1 0.0 copy-done.1
  54.1 0.0 copy-start
  54.1 2.1 %copy-done = bf16[3584,528]{0,1:T(8,128)(2,1)S(1)} copy-done((bf16[3584,528]{0,1:T(8,128)(2,1)S(1)}, bf16[3584,528]{0,1:T(8,128)(2,1)}, u32[]{:S(2)}) %copy-start) | copy-done | bytes 3784728
  56.2 6.4 %shard_map.77 = (f32[256,528]{1,0:T(8,128)S(1)}, f32[256,1]{1,0:T(8,128)S(1)}, bf16[528,1792]{1,0:T(8,128)(2,1)S(1)}) custom-call(s32[4,4]{1,0:T(4,128)S(1)} %dynamic-slice_bitcast_fusion.3.where, bf16[256,1792]{1,0:T(8,128)(2,1)S(1)} %collective-permute-done.3.refs_0_, bf16[256,1792]{1,0:T(8,128)(2,1)S(1)} %collective-permute-done.refs_1_, ...), custom_call_target="tpu_custom_call" | custom-call | flops 1150000000 | bytes 917504 | tf_op jit(solution)/shard_map/pallas_call | solution.py:216
  62.6 4.1 %collective-permute-done.1.refs_0_ = bf16[256,1792]{1,0:T(8,128)(2,1)} collective-permute-done((bf16[256,1792]{1,0:T(8,128)(2,1)S(1)}, bf16[256,1792]{1,0:T(8,128)(2,1)}, u32[]{:S(2)}, u32[]{:S(2)}) %collective-permute-start.1) | collective-permute-done | bytes 917536 | tf_op jit(solution)/shard_map/ppermute | solution.py:207
  66.7 0.0 copy-start.2
  66.7 2.3 %shard_map.78 = (bf16[272,128]{1,0:T(8,128)(2,1)S(1)}, bf16[272,128]{1,0:T(8,128)(2,1)S(1)}, bf16[272,128]{1,0:T(8,128)(2,1)S(1)}, f32[64,528]{1,0:T(8,128)S(1)}) custom-call(s32[4,4]{1,0:T(4,128)S(1)} %dynamic-slice_bitcast_fusion.3.where, bf16[256,1792]{1,0:T(8,128)(2,1)} %collective-permute-done.1.refs_0_, ...), custom_call_target="tpu_custom_call" | custom-call | flops 2300000000 | bytes 917504 | tf_op jit(solution)/shard_map/pallas_call | solution.py:236
  69.0 3.3 %collective-permute-start.10 = (bf16[272,128]{1,0:T(8,128)(2,1)S(1)}, bf16[272,128]{1,0:T(8,128)(2,1)S(1)}, u32[]{:S(2)}, u32[]{:S(2)}) collective-permute-start(bf16[272,128]{1,0:T(8,128)(2,1)S(1)} %get-tuple-element.16), channel_id=1, source_target_pairs={{0,3},{1,2},{2,1},{3,0},{4,7},{5,6},{6,5},{7,4},{8,11},{9,10},{10,... | collective-permute-start | bytes 208904 | tf_op jit(solution)/shard_map/ppermute | solution.py:253
  72.3 0.0 collective-permute-start.11
  72.3 1.1 %collective-permute-start.12 = (bf16[272,128]{1,0:T(8,128)(2,1)S(1)}, bf16[272,128]{1,0:T(8,128)(2,1)S(1)}, u32[]{:S(2)}, u32[]{:S(2)}) collective-permute-start(bf16[272,128]{1,0:T(8,128)(2,1)S(1)} %get-tuple-element.18), channel_id=1, source_target_pairs={{0,1},{1,0},{2,3},{3,2},{4,5},{5,4},{6,7},{7,6},{8,9},{9,8},{10,11... | collective-permute-start | bytes 208904 | tf_op jit(solution)/shard_map/ppermute | solution.py:253
  73.5 0.1 pad_maximum_fusion
  73.6 1.7 %collective-permute-done.10.refs_0_ = bf16[272,128]{1,0:T(8,128)(2,1)S(1)} collective-permute-done((bf16[272,128]{1,0:T(8,128)(2,1)S(1)}, bf16[272,128]{1,0:T(8,128)(2,1)S(1)}, u32[]{:S(2)}, u32[]{:S(2)}) %collective-permute-start.10) | collective-permute-done | bytes 69664 | tf_op jit(solution)/shard_map/ppermute | solution.py:253
  75.3 2.5 %collective-permute-done.11.refs_1_ = bf16[272,128]{1,0:T(8,128)(2,1)S(1)} collective-permute-done((bf16[272,128]{1,0:T(8,128)(2,1)S(1)}, bf16[272,128]{1,0:T(8,128)(2,1)S(1)}, u32[]{:S(2)}, u32[]{:S(2)}) %collective-permute-start.11) | collective-permute-done | bytes 69664 | tf_op jit(solution)/shard_map/ppermute | solution.py:253
  77.8 0.0 collective-permute-done.12.refs_2_
  77.8 0.0 copy-done.2
  77.8 1.6 %shard_map.79 = (bf16[64,1536]{1,0:T(8,128)(2,1)}, bf16[64,576]{1,0:T(8,128)(2,1)}) custom-call(s32[4,4]{1,0:T(4,128)S(1)} %dynamic-slice_bitcast_fusion.3.where, bf16[272,128]{1,0:T(8,128)(2,1)S(1)} %collective-permute-done.10.refs_0_, bf16[272,128]{1,0:T(8,128)(2,1)S(1)} %collective-permute-done.11.refs_1_, ...), custom_call_target="tpu_custom_call" | custom-call | tf_op jit(solution)/shard_map/pallas_call | solution.py:261
  (3 shorter events, 0.0 us)
Async XLA Ops:
  0.6 50.6 %copy-start.3 = (f32[1536]{0:T(1024)S(1)}, f32[1536]{0:T(1024)}, u32[]{:S(2)}) copy-start(f32[1536]{0:T(1024)} %param.8) | copy-start | bytes 18436
  0.6 53.5 %copy-start.1 = (f32[7168]{0:T(1024)S(1)}, f32[7168]{0:T(1024)}, u32[]{:S(2)}) copy-start(f32[7168]{0:T(1024)} %param.7) | copy-start | bytes 86020
  0.6 26.0 %collective-permute-start = (bf16[256,1792]{1,0:T(8,128)(2,1)}, bf16[256,1792]{1,0:T(8,128)(2,1)S(1)}, u32[]{:S(2)}, u32[]{:S(2)}) collective-permute-start(bf16[256,1792]{1,0:T(8,128)(2,1)} %param.6), channel_id=1, source_target_pairs={{0,11},{1,10},{2,9},{3,8},{8,19},{9,18},{10,17},{11,16},{16,27},{1... | collective-permute-start | bytes 2752520 | tf_op jit(solution)/shard_map/ppermute | solution.py:188
  6.8 16.6 %collective-permute-start.2 = (bf16[176,1792]{1,0:T(8,128)(2,1)S(1)}, bf16[176,1792]{1,0:T(8,128)(2,1)S(1)}, u32[]{:S(2)}, u32[]{:S(2)}) collective-permute-start(bf16[176,1792]{1,0:T(8,128)(2,1)S(1)} %get-tuple-element.21), channel_id=1, source_target_pairs={{0,4},{4,0},{1,5},{5,1},{2,6},{6,2},{3,7},{7,3},{8,12},{12,8},{9,1... | collective-permute-start | bytes 1892360 | tf_op jit(solution)/shard_map/ppermute | solution.py:200
  8.4 42.8 %collective-permute-start.4 = (bf16[256,1792]{1,0:T(8,128)(2,1)}, bf16[256,1792]{1,0:T(8,128)(2,1)S(1)}, u32[]{:S(2)}, u32[]{:S(2)}) collective-permute-start(bf16[256,1792]{1,0:T(8,128)(2,1)} %param.6), channel_id=1, source_target_pairs={{0,9},{1,8},{2,11},{3,10},{8,17},{9,16},{10,19},{11,18},{16,25},{1... | collective-permute-start | bytes 2752520 | tf_op jit(solution)/shard_map/ppermute | solution.py:188
  8.8 38.3 %collective-permute-start.5 = (bf16[176,1792]{1,0:T(8,128)(2,1)S(1)}, bf16[176,1792]{1,0:T(8,128)(2,1)}, u32[]{:S(2)}, u32[]{:S(2)}) collective-permute-start(bf16[176,1792]{1,0:T(8,128)(2,1)S(1)} %get-tuple-element.22), channel_id=1, source_target_pairs={{0,4},{4,0},{1,5},{5,1},{2,6},{6,2},{3,7},{7,3},{8,12},{12,8},{9,1... | collective-permute-start | bytes 1892360 | tf_op jit(solution)/shard_map/ppermute | solution.py:200
  9.3 41.1 %collective-permute-start.6 = (bf16[176,1792]{1,0:T(8,128)(2,1)S(1)}, bf16[176,1792]{1,0:T(8,128)(2,1)}, u32[]{:S(2)}, u32[]{:S(2)}) collective-permute-start(bf16[176,1792]{1,0:T(8,128)(2,1)S(1)} %get-tuple-element.20), channel_id=1, source_target_pairs={{0,4},{4,0},{1,5},{5,1},{2,6},{6,2},{3,7},{7,3},{8,12},{12,8},{9,1... | collective-permute-start | bytes 1892360 | tf_op jit(solution)/shard_map/ppermute | solution.py:200
  23.3 30.8 %collective-permute-start.3 = (bf16[256,1792]{1,0:T(8,128)(2,1)}, bf16[256,1792]{1,0:T(8,128)(2,1)S(1)}, u32[]{:S(2)}, u32[]{:S(2)}) collective-permute-start(bf16[256,1792]{1,0:T(8,128)(2,1)} %param.6), channel_id=1, source_target_pairs={{0,8},{1,9},{2,10},{3,11},{8,16},{9,17},{10,18},{11,19},{16,24},{1... | collective-permute-start | bytes 2752520 | tf_op jit(solution)/shard_map/ppermute | solution.py:188
  26.6 40.1 %collective-permute-start.1 = (bf16[256,1792]{1,0:T(8,128)(2,1)S(1)}, bf16[256,1792]{1,0:T(8,128)(2,1)}, u32[]{:S(2)}, u32[]{:S(2)}) collective-permute-start(bf16[256,1792]{1,0:T(8,128)(2,1)S(1)} %collective-permute-done.refs_1_), channel_id=1, source_target_pairs={{0,1},{1,0},{2,3},{3,2},{4,5},{5,4},{6,7},{7,6},{8,9},{9,8},{10,11... | collective-permute-start | bytes 2752520 | tf_op jit(solution)/shard_map/ppermute | solution.py:207
  47.1 5.0 %collective-permute-start.7 = (bf16[176,1792]{1,0:T(8,128)(2,1)S(1)}, bf16[176,1792]{1,0:T(8,128)(2,1)}, u32[]{:S(2)}, u32[]{:S(2)}) collective-permute-start(bf16[176,1792]{1,0:T(8,128)(2,1)S(1)} %collective-permute-done.2.refs_5_), channel_id=1, source_target_pairs={{0,8},{8,0},{16,24},{24,16},{1,9},{9,1},{17,25},{25,17},{2,10},{10... | collective-permute-start | bytes 1892360 | tf_op jit(solution)/shard_map/ppermute | solution.py:203
  50.5 2.7 %collective-permute-start.8 = (bf16[176,1792]{1,0:T(8,128)(2,1)}, bf16[176,1792]{1,0:T(8,128)(2,1)}, u32[]{:S(2)}, u32[]{:S(2)}) collective-permute-start(bf16[176,1792]{1,0:T(8,128)(2,1)} %collective-permute-done.5.refs_6_), channel_id=1, source_target_pairs={{0,8},{8,0},{16,24},{24,16},{1,9},{9,1},{17,25},{25,17},{2,10},{10... | collective-permute-start | bytes 1892360 | tf_op jit(solution)/shard_map/ppermute | solution.py:203
  51.2 2.9 %collective-permute-start.9 = (bf16[176,1792]{1,0:T(8,128)(2,1)}, bf16[176,1792]{1,0:T(8,128)(2,1)}, u32[]{:S(2)}, u32[]{:S(2)}) collective-permute-start(bf16[176,1792]{1,0:T(8,128)(2,1)} %collective-permute-done.6.refs_7_), channel_id=1, source_target_pairs={{0,8},{8,0},{16,24},{24,16},{1,9},{9,1},{17,25},{25,17},{2,10},{10... | collective-permute-start | bytes 1892360 | tf_op jit(solution)/shard_map/ppermute | solution.py:203
  54.1 2.1 %copy-start = (bf16[3584,528]{0,1:T(8,128)(2,1)S(1)}, bf16[3584,528]{0,1:T(8,128)(2,1)}, u32[]{:S(2)}) copy-start(bf16[3584,528]{0,1:T(8,128)(2,1)} %param.10) | copy-start | bytes 11354116
  66.7 11.1 %copy-start.2 = (f32[512]{0:T(512)S(1)}, f32[512]{0:T(512)}, u32[]{:S(2)}) copy-start(f32[512]{0:T(512)} %param.9) | copy-start | bytes 6148
  69.0 6.3 %collective-permute-start.10 = (bf16[272,128]{1,0:T(8,128)(2,1)S(1)}, bf16[272,128]{1,0:T(8,128)(2,1)S(1)}, u32[]{:S(2)}, u32[]{:S(2)}) collective-permute-start(bf16[272,128]{1,0:T(8,128)(2,1)S(1)} %get-tuple-element.16), channel_id=1, source_target_pairs={{0,3},{1,2},{2,1},{3,0},{4,7},{5,6},{6,5},{7,4},{8,11},{9,10},{10,... | collective-permute-start | bytes 208904 | tf_op jit(solution)/shard_map/ppermute | solution.py:253
  72.3 5.4 %collective-permute-start.11 = (bf16[272,128]{1,0:T(8,128)(2,1)S(1)}, bf16[272,128]{1,0:T(8,128)(2,1)S(1)}, u32[]{:S(2)}, u32[]{:S(2)}) collective-permute-start(bf16[272,128]{1,0:T(8,128)(2,1)S(1)} %get-tuple-element.17), channel_id=1, source_target_pairs={{0,2},{1,3},{2,0},{3,1},{4,6},{5,7},{6,4},{7,5},{8,10},{9,11},{10,... | collective-permute-start | bytes 208904 | tf_op jit(solution)/shard_map/ppermute | solution.py:253
  72.3 5.4 %collective-permute-start.12 = (bf16[272,128]{1,0:T(8,128)(2,1)S(1)}, bf16[272,128]{1,0:T(8,128)(2,1)S(1)}, u32[]{:S(2)}, u32[]{:S(2)}) collective-permute-start(bf16[272,128]{1,0:T(8,128)(2,1)S(1)} %get-tuple-element.18), channel_id=1, source_target_pairs={{0,1},{1,0},{2,3},{3,2},{4,5},{5,4},{6,7},{7,6},{8,9},{9,8},{10,11... | collective-permute-start | bytes 208904 | tf_op jit(solution)/shard_map/ppermute | solution.py:253

commit v12 on v11

--- a/solution.py
+++ b/solution.py
@@ -22,7 +22,7 @@
 TURNS = 3, 2, 1, 0
 LANES = 128
 PACK = 16
-VMEM_LIMIT = 20 * 1024 * 1024
+VMEM_LIMIT = 40 * 1024 * 1024
 
 vmem = pl.BlockSpec(memory_space=pltpu.VMEM)
 smem = pl.BlockSpec(memory_space=pltpu.SMEM)

time: 79.6 us -> 79.6 us (level)
  no operation moved by 1% of the time
where the time goes in v12:
time: 79.6 us; the launch traced here: 79.4 us
  starting transfers between devices  35.6 us (45%)
  waiting for transfers between devices  28 us (35%)
  Pallas kernels  10.4 us (13%)
  local copies, waits for them, and re-layouts  4.36 us (5%)
    ppermute x1, starting transfers between devices, on_device(): far = lax.ppermute(mirrored, 'ep', [(z, z ^ 1) for z in range(PLANES)])  20.5 us
    ppermute x3, waiting for transfers between devices, on_device(): here = [lax.ppermute(part, 'fsdp', [(0, 1), (1, 0)]) for part in here]  15.9 us
    pallas_call x1, Pallas kernels, on_device(): pl.pallas_call(functools.partial(near_kernel, [len(parts) for parts in so...  6.44 us
    ppermute x3, starting transfers between devices, onward(): return lax.ppermute(block, ('section', 'ep'), moves)  6.4 us
    ppermute x3, starting transfers between devices, on_device(): lax.ppermute(message, 'ep', [(z, z ^ turn) for z in range(PLANES)])  4.45 us
    ppermute x3, waiting for transfers between devices, on_device(): lax.ppermute(message, 'ep', [(z, z ^ turn) for z in range(PLANES)])  4.21 us
    ppermute x1, waiting for transfers between devices, on_device(): far = lax.ppermute(mirrored, 'ep', [(z, z ^ 1) for z in range(PLANES)])  4.06 us
    ppermute x3, starting transfers between devices, on_device(): here = [lax.ppermute(part, 'fsdp', [(0, 1), (1, 0)]) for part in here]  3.61 us
  transfers between devices with their start and end apart: 13, of which 8 were waited for; matrix products, arithmetic and copies ran while one was open for 3% of the time, Pallas kernels for 8%

profile of v12, /device:TPU:0, one launch (start us, length us, event | category | flops | bytes accessed | tf_op | source)
XLA Modules:
  0.0 79.4 jit_solution(6750293976298059446)
XLA Ops:
  0.6 0.0 copy-start.3
  0.6 0.0 copy-start.1
  0.6 4.5 %collective-permute-start = (bf16[256,1792]{1,0:T(8,128)(2,1)}, bf16[256,1792]{1,0:T(8,128)(2,1)S(1)}, u32[]{:S(2)}, u32[]{:S(2)}) collective-permute-start(bf16[256,1792]{1,0:T(8,128)(2,1)} %param.6), channel_id=1, source_target_pairs={{0,11},{1,10},{2,9},{3,8},{8,19},{9,18},{10,17},{11,16},{16,27},{1... | collective-permute-start | bytes 2752520 | tf_op jit(solution)/shard_map/ppermute | solution.py:188
  5.2 1.6 %dynamic-slice_bitcast_fusion = (bf16[176,1792]{1,0:T(8,128)(2,1)S(1)}, bf16[176,1792]{1,0:T(8,128)(2,1)S(1)}, bf16[176,1792]{1,0:T(8,128)(2,1)S(1)}) fusion(bf16[3584,528]{0,1:T(8,128)(2,1)} %param.10, s32[]{:T(128)S(6)} %select_n.37), kind=kLoop, calls=%fused_computation | loop fusion | bytes 3784708 | tf_op jit(solution)/shard_map/dynamic_slice | solution.py:197
  6.8 1.6 %collective-permute-start.2 = (bf16[176,1792]{1,0:T(8,128)(2,1)S(1)}, bf16[176,1792]{1,0:T(8,128)(2,1)S(1)}, u32[]{:S(2)}, u32[]{:S(2)}) collective-permute-start(bf16[176,1792]{1,0:T(8,128)(2,1)S(1)} %get-tuple-element.21), channel_id=1, source_target_pairs={{0,4},{4,0},{1,5},{5,1},{2,6},{6,2},{3,7},{7,3},{8,12},{12,8},{9,1... | collective-permute-start | bytes 1892360 | tf_op jit(solution)/shard_map/ppermute | solution.py:200
  8.4 0.5 collective-permute-start.4
  8.8 0.5 collective-permute-start.5
  9.3 1.5 %collective-permute-start.6 = (bf16[176,1792]{1,0:T(8,128)(2,1)S(1)}, bf16[176,1792]{1,0:T(8,128)(2,1)}, u32[]{:S(2)}, u32[]{:S(2)}) collective-permute-start(bf16[176,1792]{1,0:T(8,128)(2,1)S(1)} %get-tuple-element.20), channel_id=1, source_target_pairs={{0,4},{4,0},{1,5},{5,1},{2,6},{6,2},{3,7},{7,3},{8,12},{12,8},{9,1... | collective-permute-start | bytes 1892360 | tf_op jit(solution)/shard_map/ppermute | solution.py:200
  10.9 12.5 %collective-permute-done.2.refs_5_ = bf16[176,1792]{1,0:T(8,128)(2,1)S(1)} collective-permute-done((bf16[176,1792]{1,0:T(8,128)(2,1)S(1)}, bf16[176,1792]{1,0:T(8,128)(2,1)S(1)}, u32[]{:S(2)}, u32[]{:S(2)}) %collective-permute-start.2) | collective-permute-done | bytes 630816 | tf_op jit(solution)/shard_map/ppermute | solution.py:200
  23.3 1.4 %collective-permute-start.3 = (bf16[256,1792]{1,0:T(8,128)(2,1)}, bf16[256,1792]{1,0:T(8,128)(2,1)S(1)}, u32[]{:S(2)}, u32[]{:S(2)}) collective-permute-start(bf16[256,1792]{1,0:T(8,128)(2,1)} %param.6), channel_id=1, source_target_pairs={{0,8},{1,9},{2,10},{3,11},{8,16},{9,17},{10,18},{11,19},{16,24},{1... | collective-permute-start | bytes 2752520 | tf_op jit(solution)/shard_map/ppermute | solution.py:188
  24.7 1.9 %collective-permute-done.refs_1_ = bf16[256,1792]{1,0:T(8,128)(2,1)S(1)} collective-permute-done((bf16[256,1792]{1,0:T(8,128)(2,1)}, bf16[256,1792]{1,0:T(8,128)(2,1)S(1)}, u32[]{:S(2)}, u32[]{:S(2)}) %collective-permute-start) | collective-permute-done | bytes 917536 | tf_op jit(solution)/shard_map/ppermute | solution.py:188
  26.6 20.5 %collective-permute-start.1 = (bf16[256,1792]{1,0:T(8,128)(2,1)S(1)}, bf16[256,1792]{1,0:T(8,128)(2,1)}, u32[]{:S(2)}, u32[]{:S(2)}) collective-permute-start(bf16[256,1792]{1,0:T(8,128)(2,1)S(1)} %collective-permute-done.refs_1_), channel_id=1, source_target_pairs={{0,1},{1,0},{2,3},{3,2},{4,5},{5,4},{6,7},{7,6},{8,9},{9,8},{10,11... | collective-permute-start | bytes 2752520 | tf_op jit(solution)/shard_map/ppermute | solution.py:207
  47.1 0.0 collective-permute-done.5.refs_6_
  47.1 0.0 collective-permute-start.7
  47.1 3.4 %collective-permute-done.6.refs_7_ = bf16[176,1792]{1,0:T(8,128)(2,1)} collective-permute-done((bf16[176,1792]{1,0:T(8,128)(2,1)S(1)}, bf16[176,1792]{1,0:T(8,128)(2,1)}, u32[]{:S(2)}, u32[]{:S(2)}) %collective-permute-start.6) | collective-permute-done | bytes 630816 | tf_op jit(solution)/shard_map/ppermute | solution.py:200
  50.5 0.7 collective-permute-start.8
  51.2 0.0 collective-permute-done.4.refs_2_
  51.2 0.0 collective-permute-start.9
  51.2 0.0 copy-done.3
  51.2 0.7 dynamic-slice_bitcast_fusion.3.where
  51.9 0.2 fusion
  52.1 0.0 collective-permute-done.7.refs_8_
  52.1 1.1 %collective-permute-done.8.refs_9_ = bf16[176,1792]{1,0:T(8,128)(2,1)} collective-permute-done((bf16[176,1792]{1,0:T(8,128)(2,1)}, bf16[176,1792]{1,0:T(8,128)(2,1)}, u32[]{:S(2)}, u32[]{:S(2)}) %collective-permute-start.8) | collective-permute-done | bytes 630816 | tf_op jit(solution)/shard_map/ppermute | solution.py:203
  53.2 0.9 %collective-permute-done.9.refs_10_ = bf16[176,1792]{1,0:T(8,128)(2,1)} collective-permute-done((bf16[176,1792]{1,0:T(8,128)(2,1)}, bf16[176,1792]{1,0:T(8,128)(2,1)}, u32[]{:S(2)}, u32[]{:S(2)}) %collective-permute-start.9) | collective-permute-done | bytes 630816 | tf_op jit(solution)/shard_map/ppermute | solution.py:203
  54.1 0.0 collective-permute-done.3.refs_0_
  54.1 0.0 copy-done.1
  54.1 0.0 copy-start
  54.1 2.1 %copy-done = bf16[3584,528]{0,1:T(8,128)(2,1)S(1)} copy-done((bf16[3584,528]{0,1:T(8,128)(2,1)S(1)}, bf16[3584,528]{0,1:T(8,128)(2,1)}, u32[]{:S(2)}) %copy-start) | copy-done | bytes 3784728
  56.2 6.4 %shard_map.77 = (f32[256,528]{1,0:T(8,128)S(1)}, f32[256,1]{1,0:T(8,128)S(1)}, bf16[528,1792]{1,0:T(8,128)(2,1)S(1)}) custom-call(s32[4,4]{1,0:T(4,128)S(1)} %dynamic-slice_bitcast_fusion.3.where, bf16[256,1792]{1,0:T(8,128)(2,1)S(1)} %collective-permute-done.3.refs_0_, bf16[256,1792]{1,0:T(8,128)(2,1)S(1)} %collective-permute-done.refs_1_, ...), custom_call_target="tpu_custom_call" | custom-call | flops 1150000000 | bytes 917504 | tf_op jit(solution)/shard_map/pallas_call | solution.py:216
  62.6 4.1 %collective-permute-done.1.refs_0_ = bf16[256,1792]{1,0:T(8,128)(2,1)} collective-permute-done((bf16[256,1792]{1,0:T(8,128)(2,1)S(1)}, bf16[256,1792]{1,0:T(8,128)(2,1)}, u32[]{:S(2)}, u32[]{:S(2)}) %collective-permute-start.1) | collective-permute-done | bytes 917536 | tf_op jit(solution)/shard_map/ppermute | solution.py:207
  66.7 0.0 copy-start.2
  66.7 2.3 %shard_map.78 = (bf16[272,128]{1,0:T(8,128)(2,1)S(1)}, bf16[272,128]{1,0:T(8,128)(2,1)S(1)}, bf16[272,128]{1,0:T(8,128)(2,1)S(1)}, f32[64,528]{1,0:T(8,128)S(1)}) custom-call(s32[4,4]{1,0:T(4,128)S(1)} %dynamic-slice_bitcast_fusion.3.where, bf16[256,1792]{1,0:T(8,128)(2,1)} %collective-permute-done.1.refs_0_, ...), custom_call_target="tpu_custom_call" | custom-call | flops 2300000000 | bytes 917504 | tf_op jit(solution)/shard_map/pallas_call | solution.py:236
  69.0 3.3 %collective-permute-start.10 = (bf16[272,128]{1,0:T(8,128)(2,1)S(1)}, bf16[272,128]{1,0:T(8,128)(2,1)S(1)}, u32[]{:S(2)}, u32[]{:S(2)}) collective-permute-start(bf16[272,128]{1,0:T(8,128)(2,1)S(1)} %get-tuple-element.16), channel_id=1, source_target_pairs={{0,3},{1,2},{2,1},{3,0},{4,7},{5,6},{6,5},{7,4},{8,11},{9,10},{10,... | collective-permute-start | bytes 208904 | tf_op jit(solution)/shard_map/ppermute | solution.py:253
  72.3 0.0 collective-permute-start.11
  72.3 1.1 %collective-permute-start.12 = (bf16[272,128]{1,0:T(8,128)(2,1)S(1)}, bf16[272,128]{1,0:T(8,128)(2,1)S(1)}, u32[]{:S(2)}, u32[]{:S(2)}) collective-permute-start(bf16[272,128]{1,0:T(8,128)(2,1)S(1)} %get-tuple-element.18), channel_id=1, source_target_pairs={{0,1},{1,0},{2,3},{3,2},{4,5},{5,4},{6,7},{7,6},{8,9},{9,8},{10,11... | collective-permute-start | bytes 208904 | tf_op jit(solution)/shard_map/ppermute | solution.py:253
  73.5 0.1 pad_maximum_fusion
  73.6 1.7 %collective-permute-done.10.refs_0_ = bf16[272,128]{1,0:T(8,128)(2,1)S(1)} collective-permute-done((bf16[272,128]{1,0:T(8,128)(2,1)S(1)}, bf16[272,128]{1,0:T(8,128)(2,1)S(1)}, u32[]{:S(2)}, u32[]{:S(2)}) %collective-permute-start.10) | collective-permute-done | bytes 69664 | tf_op jit(solution)/shard_map/ppermute | solution.py:253
  75.3 2.5 %collective-permute-done.11.refs_1_ = bf16[272,128]{1,0:T(8,128)(2,1)S(1)} collective-permute-done((bf16[272,128]{1,0:T(8,128)(2,1)S(1)}, bf16[272,128]{1,0:T(8,128)(2,1)S(1)}, u32[]{:S(2)}, u32[]{:S(2)}) %collective-permute-start.11) | collective-permute-done | bytes 69664 | tf_op jit(solution)/shard_map/ppermute | solution.py:253
  77.8 0.0 collective-permute-done.12.refs_2_
  77.8 0.0 copy-done.2
  77.8 1.6 %shard_map.79 = (bf16[64,1536]{1,0:T(8,128)(2,1)}, bf16[64,576]{1,0:T(8,128)(2,1)}) custom-call(s32[4,4]{1,0:T(4,128)S(1)} %dynamic-slice_bitcast_fusion.3.where, bf16[272,128]{1,0:T(8,128)(2,1)S(1)} %collective-permute-done.10.refs_0_, bf16[272,128]{1,0:T(8,128)(2,1)S(1)} %collective-permute-done.11.refs_1_, ...), custom_call_target="tpu_custom_call" | custom-call | tf_op jit(solution)/shard_map/pallas_call | solution.py:261
  (3 shorter events, 0.0 us)
Async XLA Ops:
  0.6 50.6 %copy-start.3 = (f32[1536]{0:T(1024)S(1)}, f32[1536]{0:T(1024)}, u32[]{:S(2)}) copy-start(f32[1536]{0:T(1024)} %param.8) | copy-start | bytes 18436
  0.6 53.5 %copy-start.1 = (f32[7168]{0:T(1024)S(1)}, f32[7168]{0:T(1024)}, u32[]{:S(2)}) copy-start(f32[7168]{0:T(1024)} %param.7) | copy-start | bytes 86020
  0.6 26.0 %collective-permute-start = (bf16[256,1792]{1,0:T(8,128)(2,1)}, bf16[256,1792]{1,0:T(8,128)(2,1)S(1)}, u32[]{:S(2)}, u32[]{:S(2)}) collective-permute-start(bf16[256,1792]{1,0:T(8,128)(2,1)} %param.6), channel_id=1, source_target_pairs={{0,11},{1,10},{2,9},{3,8},{8,19},{9,18},{10,17},{11,16},{16,27},{1... | collective-permute-start | bytes 2752520 | tf_op jit(solution)/shard_map/ppermute | solution.py:188
  6.8 16.6 %collective-permute-start.2 = (bf16[176,1792]{1,0:T(8,128)(2,1)S(1)}, bf16[176,1792]{1,0:T(8,128)(2,1)S(1)}, u32[]{:S(2)}, u32[]{:S(2)}) collective-permute-start(bf16[176,1792]{1,0:T(8,128)(2,1)S(1)} %get-tuple-element.21), channel_id=1, source_target_pairs={{0,4},{4,0},{1,5},{5,1},{2,6},{6,2},{3,7},{7,3},{8,12},{12,8},{9,1... | collective-permute-start | bytes 1892360 | tf_op jit(solution)/shard_map/ppermute | solution.py:200
  8.4 42.8 %collective-permute-start.4 = (bf16[256,1792]{1,0:T(8,128)(2,1)}, bf16[256,1792]{1,0:T(8,128)(2,1)S(1)}, u32[]{:S(2)}, u32[]{:S(2)}) collective-permute-start(bf16[256,1792]{1,0:T(8,128)(2,1)} %param.6), channel_id=1, source_target_pairs={{0,9},{1,8},{2,11},{3,10},{8,17},{9,16},{10,19},{11,18},{16,25},{1... | collective-permute-start | bytes 2752520 | tf_op jit(solution)/shard_map/ppermute | solution.py:188
  8.8 38.3 %collective-permute-start.5 = (bf16[176,1792]{1,0:T(8,128)(2,1)S(1)}, bf16[176,1792]{1,0:T(8,128)(2,1)}, u32[]{:S(2)}, u32[]{:S(2)}) collective-permute-start(bf16[176,1792]{1,0:T(8,128)(2,1)S(1)} %get-tuple-element.22), channel_id=1, source_target_pairs={{0,4},{4,0},{1,5},{5,1},{2,6},{6,2},{3,7},{7,3},{8,12},{12,8},{9,1... | collective-permute-start | bytes 1892360 | tf_op jit(solution)/shard_map/ppermute | solution.py:200
  9.3 41.1 %collective-permute-start.6 = (bf16[176,1792]{1,0:T(8,128)(2,1)S(1)}, bf16[176,1792]{1,0:T(8,128)(2,1)}, u32[]{:S(2)}, u32[]{:S(2)}) collective-permute-start(bf16[176,1792]{1,0:T(8,128)(2,1)S(1)} %get-tuple-element.20), channel_id=1, source_target_pairs={{0,4},{4,0},{1,5},{5,1},{2,6},{6,2},{3,7},{7,3},{8,12},{12,8},{9,1... | collective-permute-start | bytes 1892360 | tf_op jit(solution)/shard_map/ppermute | solution.py:200
  23.3 30.8 %collective-permute-start.3 = (bf16[256,1792]{1,0:T(8,128)(2,1)}, bf16[256,1792]{1,0:T(8,128)(2,1)S(1)}, u32[]{:S(2)}, u32[]{:S(2)}) collective-permute-start(bf16[256,1792]{1,0:T(8,128)(2,1)} %param.6), channel_id=1, source_target_pairs={{0,8},{1,9},{2,10},{3,11},{8,16},{9,17},{10,18},{11,19},{16,24},{1... | collective-permute-start | bytes 2752520 | tf_op jit(solution)/shard_map/ppermute | solution.py:188
  26.6 40.1 %collective-permute-start.1 = (bf16[256,1792]{1,0:T(8,128)(2,1)S(1)}, bf16[256,1792]{1,0:T(8,128)(2,1)}, u32[]{:S(2)}, u32[]{:S(2)}) collective-permute-start(bf16[256,1792]{1,0:T(8,128)(2,1)S(1)} %collective-permute-done.refs_1_), channel_id=1, source_target_pairs={{0,1},{1,0},{2,3},{3,2},{4,5},{5,4},{6,7},{7,6},{8,9},{9,8},{10,11... | collective-permute-start | bytes 2752520 | tf_op jit(solution)/shard_map/ppermute | solution.py:207
  47.1 5.0 %collective-permute-start.7 = (bf16[176,1792]{1,0:T(8,128)(2,1)S(1)}, bf16[176,1792]{1,0:T(8,128)(2,1)}, u32[]{:S(2)}, u32[]{:S(2)}) collective-permute-start(bf16[176,1792]{1,0:T(8,128)(2,1)S(1)} %collective-permute-done.2.refs_5_), channel_id=1, source_target_pairs={{0,8},{8,0},{16,24},{24,16},{1,9},{9,1},{17,25},{25,17},{2,10},{10... | collective-permute-start | bytes 1892360 | tf_op jit(solution)/shard_map/ppermute | solution.py:203
  50.5 2.7 %collective-permute-start.8 = (bf16[176,1792]{1,0:T(8,128)(2,1)}, bf16[176,1792]{1,0:T(8,128)(2,1)}, u32[]{:S(2)}, u32[]{:S(2)}) collective-permute-start(bf16[176,1792]{1,0:T(8,128)(2,1)} %collective-permute-done.5.refs_6_), channel_id=1, source_target_pairs={{0,8},{8,0},{16,24},{24,16},{1,9},{9,1},{17,25},{25,17},{2,10},{10... | collective-permute-start | bytes 1892360 | tf_op jit(solution)/shard_map/ppermute | solution.py:203
  51.2 2.9 %collective-permute-start.9 = (bf16[176,1792]{1,0:T(8,128)(2,1)}, bf16[176,1792]{1,0:T(8,128)(2,1)}, u32[]{:S(2)}, u32[]{:S(2)}) collective-permute-start(bf16[176,1792]{1,0:T(8,128)(2,1)} %collective-permute-done.6.refs_7_), channel_id=1, source_target_pairs={{0,8},{8,0},{16,24},{24,16},{1,9},{9,1},{17,25},{25,17},{2,10},{10... | collective-permute-start | bytes 1892360 | tf_op jit(solution)/shard_map/ppermute | solution.py:203
  54.1 2.1 %copy-start = (bf16[3584,528]{0,1:T(8,128)(2,1)S(1)}, bf16[3584,528]{0,1:T(8,128)(2,1)}, u32[]{:S(2)}) copy-start(bf16[3584,528]{0,1:T(8,128)(2,1)} %param.10) | copy-start | bytes 11354116
  66.7 11.1 %copy-start.2 = (f32[512]{0:T(512)S(1)}, f32[512]{0:T(512)}, u32[]{:S(2)}) copy-start(f32[512]{0:T(512)} %param.9) | copy-start | bytes 6148
  69.0 6.3 %collective-permute-start.10 = (bf16[272,128]{1,0:T(8,128)(2,1)S(1)}, bf16[272,128]{1,0:T(8,128)(2,1)S(1)}, u32[]{:S(2)}, u32[]{:S(2)}) collective-permute-start(bf16[272,128]{1,0:T(8,128)(2,1)S(1)} %get-tuple-element.16), channel_id=1, source_target_pairs={{0,3},{1,2},{2,1},{3,0},{4,7},{5,6},{6,5},{7,4},{8,11},{9,10},{10,... | collective-permute-start | bytes 208904 | tf_op jit(solution)/shard_map/ppermute | solution.py:253
  72.3 5.4 %collective-permute-start.11 = (bf16[272,128]{1,0:T(8,128)(2,1)S(1)}, bf16[272,128]{1,0:T(8,128)(2,1)S(1)}, u32[]{:S(2)}, u32[]{:S(2)}) collective-permute-start(bf16[272,128]{1,0:T(8,128)(2,1)S(1)} %get-tuple-element.17), channel_id=1, source_target_pairs={{0,2},{1,3},{2,0},{3,1},{4,6},{5,7},{6,4},{7,5},{8,10},{9,11},{10,... | collective-permute-start | bytes 208904 | tf_op jit(solution)/shard_map/ppermute | solution.py:253
  72.3 5.4 %collective-permute-start.12 = (bf16[272,128]{1,0:T(8,128)(2,1)S(1)}, bf16[272,128]{1,0:T(8,128)(2,1)S(1)}, u32[]{:S(2)}, u32[]{:S(2)}) collective-permute-start(bf16[272,128]{1,0:T(8,128)(2,1)S(1)} %get-tuple-element.18), channel_id=1, source_target_pairs={{0,1},{1,0},{2,3},{3,2},{4,5},{5,4},{6,7},{7,6},{8,9},{9,8},{10,11... | collective-permute-start | bytes 208904 | tf_op jit(solution)/shard_map/ppermute | solution.py:253
